TPU v7x, 32 devices: a whole 2x2x4 slice. The times are simulated.
32 devices in a mesh: blk: 8 (over z, y), group: 4 (over x, core).
Axes of the slice: x: 2, y: 2, z: 4, core: 2. Of those that a mesh axis runs over, the one named last changes fastest.
Arguments:
- expression: bfloat16 [12288, 2048], P(('blk', 'group')), may hold values from -6 to 6
- observed: int32 [12288, 2048], P(('blk', 'group')), may hold values 0 or 1
- cell_factors: float32 [12288, 512], P(('blk', 'group')), may hold values from -1.2613447 to 1.2613447
- locus_factors: float32 [2048, 512], P('blk'), may hold values from -1.2613447 to 1.2613447
Outputs:
- cells_out: float32 [12288, 512], P(('blk', 'group'))
- loci_out: float32 [2048, 512], P('blk')
All inputs are finite; a program needn't handle non-finite values. No bound on the sum of `observed` on one device may be relied on, other than what follows from the above.
Results may differ from a plain program's by a relative error of at most 0.00095.
Values sent between devices are 32-bit elements; how exact they have to be, the bound alone decides.
No kernel may reach another device: no remote copies, remote signals or barrier semaphores. Data moves between devices by JAX's collectives and lax.ppermute only.
A program may use at most 64 MiB of HBM per device.

v0:
```python
import jax
import jax.numpy as jnp
from jax import lax
from jax.sharding import PartitionSpec as P

HOPS = 6
SWEEPS = 2


def shifted(block, axis, distance):
    devices = range(lax.axis_size(axis))
    route = [((i - distance) % len(devices), i) for i in devices]
    return lax.ppermute(block, axis, route)


def sweep(cell_rows, locus_rows, tile_data, weights):
    cell_half = cell_rows.astype(jnp.bfloat16)
    locus_half = locus_rows.astype(jnp.bfloat16)
    predicted = lax.dot_general(
        cell_half, locus_half, (((1,), (1,)), ((), ())), preferred_element_type=jnp.float32
    )
    residue = (weights * (tile_data.astype(jnp.float32) - predicted)).astype(jnp.bfloat16)
    grad_cells = jnp.dot(residue, locus_half, preferred_element_type=jnp.float32)
    grad_locus = lax.dot_general(
        residue, cell_half, (((0,), (0,)), ((), ())), preferred_element_type=jnp.float32
    )
    rank_width = cell_rows.shape[1]
    cell_step = 2.0 / (locus_rows.shape[0] + rank_width)
    locus_step = 2.0 / (cell_rows.shape[0] + rank_width)
    return (cell_rows + cell_step * grad_cells, locus_rows + locus_step * grad_locus)


def share_home(share):
    return shifted(share, "blk", 1 - HOPS)


def on_device(expression, observed, cell_factors, locus_factors):
    cycle_size = lax.axis_size("blk")
    group_size = lax.axis_size("group")
    position = lax.axis_index("blk")
    block_rows = locus_factors.shape[0]
    cell_rows = cell_factors
    locus_rows = locus_factors
    for hop_index in range(HOPS):
        offset = (position - hop_index) % cycle_size * block_rows
        tile_data = lax.dynamic_slice_in_dim(expression, offset, block_rows, 1)
        weights = lax.dynamic_slice_in_dim(observed, offset, block_rows, 1).astype(jnp.float32)
        for sweep_index in range(SWEEPS):
            cell_rows, locus_rows = sweep(cell_rows, locus_rows, tile_data, weights)
        if hop_index == HOPS // 2 - 1 or hop_index == HOPS - 1:
            share = (
                lax.psum_scatter(locus_rows, "group", scatter_dimension=0, tiled=True) / group_size
            )
            if hop_index < HOPS - 1:
                share = shifted(share, "blk", 1)
            else:
                share = share_home(share)
            locus_rows = lax.all_gather(share, "group", axis=0, tiled=True)
            continue
        locus_rows = shifted(locus_rows, "blk", 1)
    return (cell_rows, locus_rows)


def solution(mesh):
    placed = (
        P(("blk", "group"), None),
        P(("blk", "group"), None),
        P(("blk", "group"), None),
        P("blk", None),
    )
    return jax.shard_map(
        on_device,
        mesh=mesh,
        in_specs=placed,
        out_specs=(P(("blk", "group"), None), P("blk", None)),
        check_vma=False,
    )
```

profile of v0, /device:TPU:0, one launch (start us, length us, event | category | flops | bytes accessed | tf_op | source)
XLA Modules:
  0.0 180.3 jit_solution(2416250186251299536)
XLA Ops:
  7.2 1.8 %fusion.47 = bf16[384,256]{1,0:T(8,128)(2,1)S(1)} fusion(s32[384,2048]{1,0:T(8,128)} %param.5, s32[]{:T(128)S(6)} %select_n.52, f32[384,512]{1,0:T(8,128)} %param.6, bf16[384,2048]{1,0:T(8,128)(2,1)} %param.4, f32[256,512]{1,0:T(8,128)} %param.7), kind=kOutput, calls=%fused_computation.83 | convolution fusion | flops 101482496 | bytes 2097156 | tf_op jit(solution)/shard_map/dot_general | solution.py:19
  9.1 1.6 fusion.23
  10.7 0.3 fusion.11
  11.0 1.4 fusion.46
  12.4 0.3 fusion.22
  12.7 3.0 %collective-permute-start = (f32[256,512]{1,0:T(8,128)S(1)}, f32[256,512]{1,0:T(8,128)S(1)}, u32[]{:S(2)}, u32[]{:S(2)}) collective-permute-start(f32[256,512]{1,0:T(8,128)S(1)} %fusion.22), channel_id=1, source_target_pairs={{28,0},{0,4},{4,8},{8,12},{12,16},{16,20},{20,24},{24,28},{29,1},{... | collective-permute-start | bytes 1572872 | tf_op jit(solution)/shard_map/ppermute | solution.py:13
  16.0 14.7 %collective-permute-done = f32[256,512]{1,0:T(8,128)S(1)} collective-permute-done((f32[256,512]{1,0:T(8,128)S(1)}, f32[256,512]{1,0:T(8,128)S(1)}, u32[]{:S(2)}, u32[]{:S(2)}) %collective-permute-start) | collective-permute-done | bytes 524320 | tf_op jit(solution)/shard_map/ppermute | solution.py:13
  30.7 1.3 fusion.45
  32.0 0.3 fusion.21
  32.3 0.3 fusion.9
  32.6 1.4 fusion.44
  34.0 0.3 fusion.20
  34.7 15.5 %collective-permute-done.1 = f32[256,512]{1,0:T(8,128)S(1)} collective-permute-done((f32[256,512]{1,0:T(8,128)S(1)}, f32[256,512]{1,0:T(8,128)S(1)}, u32[]{:S(2)}, u32[]{:S(2)}) %collective-permute-start.1) | collective-permute-done | bytes 524320 | tf_op jit(solution)/shard_map/ppermute | solution.py:13
  50.2 1.3 fusion.43
  51.5 0.3 fusion.19
  51.9 0.3 fusion.7
  52.1 1.3 fusion.42
  53.4 1.1 fusion.18
  54.7 18.8 %reduce-scatter.3.cloned.1.call-done = f32[64,512]{1,0:T(8,128)} async-done(((f32[256,512]{1,0:T(8,128)}), f32[64,512]{1,0:T(8,128)}) %reduce-scatter.3.cloned.1.call-update) | async-done | bytes 131088 | tf_op jit(solution)/shard_map/reduce_scatter | solution.py:52
  73.4 0.9 broadcast_multiply_fusion.1
  74.4 1.5 collective-permute-start.2
  76.2 6.2 %collective-permute-done.2 = f32[64,512]{1,0:T(8,128)S(1)} collective-permute-done((f32[64,512]{1,0:T(8,128)S(1)}, f32[64,512]{1,0:T(8,128)S(1)}, u32[]{:S(2)}, u32[]{:S(2)}) %collective-permute-start.2) | collective-permute-done | bytes 131104 | tf_op jit(solution)/shard_map/ppermute | solution.py:13
  82.4 6.5 %all_gather.6 = f32[256,512]{1,0:T(8,128)S(1)} all-gather(f32[64,512]{1,0:T(8,128)S(1)} %collective-permute-done.2), channel_id=1, replica_groups=mesh['blk'=8,'group'=4] {'group'}, dimensions={0}, use_global_device_ids=true | all-gather | bytes 655360 | tf_op jit(solution)/shard_map/all_gather | solution.py:58
  88.9 1.3 fusion.41
  90.2 0.3 fusion.17
  90.8 1.3 fusion.40
  92.1 0.7 copy-done.4
  92.8 1.1 fusion.16
  93.9 1.2 fusion.4
  95.1 15.9 %collective-permute-done.3 = f32[256,512]{1,0:T(8,128)S(1)} collective-permute-done((f32[256,512]{1,0:T(8,128)}, f32[256,512]{1,0:T(8,128)S(1)}, u32[]{:S(2)}, u32[]{:S(2)}) %collective-permute-start.3) | collective-permute-done | bytes 524320 | tf_op jit(solution)/shard_map/ppermute | solution.py:13
  111.0 1.3 fusion.39
  112.3 0.3 fusion.15
  112.9 1.3 fusion.38
  114.2 0.7 copy-done.3
  114.9 1.1 fusion.14
  116.0 1.2 fusion.2
  117.2 15.1 %collective-permute-done.4 = f32[256,512]{1,0:T(8,128)S(1)} collective-permute-done((f32[256,512]{1,0:T(8,128)}, f32[256,512]{1,0:T(8,128)S(1)}, u32[]{:S(2)}, u32[]{:S(2)}) %collective-permute-start.4) | collective-permute-done | bytes 524320 | tf_op jit(solution)/shard_map/ppermute | solution.py:13
  132.3 1.3 fusion.37
  133.6 0.3 fusion.13
  134.2 1.3 fusion.36
  135.5 1.1 fusion.12
  136.6 18.8 %reduce-scatter.5.cloned.1.call-done = f32[64,512]{1,0:T(8,128)} async-done(((f32[256,512]{1,0:T(8,128)}), f32[64,512]{1,0:T(8,128)}) %reduce-scatter.5.cloned.1.call-update) | async-done | bytes 131088 | tf_op jit(solution)/shard_map/reduce_scatter | solution.py:52
  155.4 0.9 broadcast_multiply_fusion
  156.3 2.5 %collective-permute-start.5 = (f32[64,512]{1,0:T(8,128)S(1)}, f32[64,512]{1,0:T(8,128)S(1)}, u32[]{:S(2)}, u32[]{:S(2)}) collective-permute-start(f32[64,512]{1,0:T(8,128)S(1)} %broadcast_multiply_fusion), channel_id=1, source_target_pairs={{20,0},{24,4},{28,8},{0,12},{4,16},{8,20},{12,24},{16,28},{21,1},{... | collective-permute-start | bytes 393224 | tf_op jit(solution)/shard_map/ppermute | solution.py:13
  158.7 1.1 fusion
  159.9 6.3 %collective-permute-done.5 = f32[64,512]{1,0:T(8,128)S(1)} collective-permute-done((f32[64,512]{1,0:T(8,128)S(1)}, f32[64,512]{1,0:T(8,128)S(1)}, u32[]{:S(2)}, u32[]{:S(2)}) %collective-permute-start.5) | collective-permute-done | bytes 131104 | tf_op jit(solution)/shard_map/ppermute | solution.py:13
  166.2 6.5 %all_gather.7 = f32[256,512]{1,0:T(8,128)S(1)} all-gather(f32[64,512]{1,0:T(8,128)S(1)} %collective-permute-done.5), channel_id=1, replica_groups=mesh['blk'=8,'group'=4] {'group'}, dimensions={0}, use_global_device_ids=true | all-gather | bytes 655360 | tf_op jit(solution)/shard_map/all_gather | solution.py:58
  172.7 0.8 copy.7
  (21 shorter events, 1.8 us)
Async XLA Ops:
  7.2 3.5 %copy-start.1 = (f32[256,512]{1,0:T(8,128)S(1)}, f32[256,512]{1,0:T(8,128)}, u32[]{:S(2)}) copy-start(f32[256,512]{1,0:T(8,128)} %param.7) | copy-start | bytes 1572868
  7.2 3.5 %copy-start = (f32[384,512]{1,0:T(8,128)S(1)}, f32[384,512]{1,0:T(8,128)}, u32[]{:S(2)}) copy-start(f32[384,512]{1,0:T(8,128)} %param.6) | copy-start | bytes 2359300
  7.2 66.3 %reduce-scatter.3.cloned.1.call-start = ((), (), s32[]{:S(2)}) async-start(), calls=%async_computation.2 | async-start | bytes 655360 | tf_op jit(solution)/shard_map/reduce_scatter | solution.py:52
  12.7 18.0 %collective-permute-start = (f32[256,512]{1,0:T(8,128)S(1)}, f32[256,512]{1,0:T(8,128)S(1)}, u32[]{:S(2)}, u32[]{:S(2)}) collective-permute-start(f32[256,512]{1,0:T(8,128)S(1)} %fusion.22), channel_id=1, source_target_pairs={{28,0},{0,4},{4,8},{8,12},{12,16},{16,20},{20,24},{24,28},{29,1},{... | collective-permute-start | bytes 1572872 | tf_op jit(solution)/shard_map/ppermute | solution.py:13
  34.3 15.9 %collective-permute-start.1 = (f32[256,512]{1,0:T(8,128)S(1)}, f32[256,512]{1,0:T(8,128)S(1)}, u32[]{:S(2)}, u32[]{:S(2)}) collective-permute-start(f32[256,512]{1,0:T(8,128)S(1)} %fusion.20), channel_id=1, source_target_pairs={{28,0},{0,4},{4,8},{8,12},{12,16},{16,20},{20,24},{24,28},{29,1},{... | collective-permute-start | bytes 1572872 | tf_op jit(solution)/shard_map/ppermute | solution.py:13
  34.7 17.4 %copy-start.2 = (bf16[384,2048]{1,0:T(8,128)(2,1)S(1)}, bf16[384,2048]{1,0:T(8,128)(2,1)}, u32[]{:S(2)}) copy-start(bf16[384,2048]{1,0:T(8,128)(2,1)} %param.4) | copy-start | bytes 4718596
  54.6 100.8 %reduce-scatter.5.cloned.1.call-start = ((), (), s32[]{:S(2)}) async-start(), calls=%async_computation.3 | async-start | bytes 655360 | tf_op jit(solution)/shard_map/reduce_scatter | solution.py:52
  74.4 8.0 %collective-permute-start.2 = (f32[64,512]{1,0:T(8,128)S(1)}, f32[64,512]{1,0:T(8,128)S(1)}, u32[]{:S(2)}, u32[]{:S(2)}) collective-permute-start(f32[64,512]{1,0:T(8,128)S(1)} %broadcast_multiply_fusion.1), channel_id=1, source_target_pairs={{28,0},{0,4},{4,8},{8,12},{12,16},{16,20},{20,24},{24,28},{29,1},{... | collective-permute-start | bytes 393224 | tf_op jit(solution)/shard_map/ppermute | solution.py:13
  92.1 0.7 copy-start.4
  93.9 17.1 %collective-permute-start.3 = (f32[256,512]{1,0:T(8,128)}, f32[256,512]{1,0:T(8,128)S(1)}, u32[]{:S(2)}, u32[]{:S(2)}) collective-permute-start(f32[256,512]{1,0:T(8,128)} %fusion.16), channel_id=1, source_target_pairs={{28,0},{0,4},{4,8},{8,12},{12,16},{16,20},{20,24},{24,28},{29,1},{... | collective-permute-start | bytes 1572872 | tf_op jit(solution)/shard_map/ppermute | solution.py:13
  114.2 0.7 copy-start.3
  116.0 16.3 %collective-permute-start.4 = (f32[256,512]{1,0:T(8,128)}, f32[256,512]{1,0:T(8,128)S(1)}, u32[]{:S(2)}, u32[]{:S(2)}) collective-permute-start(f32[256,512]{1,0:T(8,128)} %fusion.14), channel_id=1, source_target_pairs={{28,0},{0,4},{4,8},{8,12},{12,16},{16,20},{20,24},{24,28},{29,1},{... | collective-permute-start | bytes 1572872 | tf_op jit(solution)/shard_map/ppermute | solution.py:13
  156.3 9.9 %collective-permute-start.5 = (f32[64,512]{1,0:T(8,128)S(1)}, f32[64,512]{1,0:T(8,128)S(1)}, u32[]{:S(2)}, u32[]{:S(2)}) collective-permute-start(f32[64,512]{1,0:T(8,128)S(1)} %broadcast_multiply_fusion), channel_id=1, source_target_pairs={{20,0},{24,4},{28,8},{0,12},{4,16},{8,20},{12,24},{16,28},{21,1},{... | collective-permute-start | bytes 393224 | tf_op jit(solution)/shard_map/ppermute | solution.py:13
Sparse Core Ops, SparseCore 0:
  54.7 18.6 reduce-scatter.2
  136.7 18.5 reduce-scatter.4
where the time goes:
time: 181 us; the launch traced here: 180 us
  waiting for transfers between devices  111 us (61%)
  matrix products  30.6 us (17%)
  between operations  14.4 us (8%)
  blocking collectives  13 us (7%)
  starting transfers between devices  7.15 us (4%)
  local copies, waits for them, and re-layouts  2.15 us (1%)
  other arithmetic  1.83 us (1%)
    ppermute x6, waiting for transfers between devices, shifted(): return lax.ppermute(block, axis, route)  73.7 us
    reduce_scatter x2, waiting for transfers between devices, on_device(): lax.psum_scatter(locus_rows, 'group', scatter_dimension=0, tiled=True)  37.5 us
    dot_general x12, matrix products, sweep(): lax.dot_general(cell_half, locus_half, (((1,), (1,)), ((), ())), preferre...  16.4 us
    all_gather x2, blocking collectives, on_device(): locus_rows = lax.all_gather(share, 'group', axis=0, tiled=True)  13 us
    dot_general x12, matrix products, sweep(): lax.dot_general(residue, cell_half, (((0,), (0,)), ((), ())), preferred_e...  8.3 us
    ppermute x6, starting transfers between devices, shifted(): return lax.ppermute(block, axis, route)  7.07 us
    dot_general x12, matrix products, sweep(): jnp.dot(residue, locus_half, preferred_element_type=jnp.float32)  5.9 us
  transfers between devices with their start and end apart: 8, of which 8 were waited for; matrix products, arithmetic and copies ran while one was open for 2% of the time, Pallas kernels for 0%

commit v1 on v0

v1 whole, which is shorter than its diff:
```python
import jax
import jax.numpy as jnp
from jax import lax
from jax.sharding import PartitionSpec as P

HOPS = 6
SWEEPS = 2
CHUNKS = 2
AXES = ("blk", "group")


def moved(block, blocks, groups, distance, flip=0):
    route = [
        (b * groups + g, (b + distance) % blocks * groups + (g ^ flip))
        for b in range(blocks)
        for g in range(groups)
    ]
    return lax.ppermute(block, AXES, route)


def halves(block):
    rows = block.shape[0] // 2
    return block[:rows], block[rows:]


def average(locus_rows, blocks, groups, distance):
    member = lax.axis_index("group")
    bits = [1 << i for i in range(groups.bit_length() - 1)]
    share = locus_rows
    for bit in bits:
        low, high = halves(share)
        upper = (member & bit) != 0
        share = jnp.where(upper, high, low) + moved(jnp.where(upper, low, high), blocks, groups, 0, bit)
    share = share / groups
    for place, bit in enumerate(reversed(bits)):
        upper = (member & bit) != 0
        if place == 0:
            mine = moved(share, blocks, groups, distance)
            other = moved(share, blocks, groups, distance, bit)
        else:
            mine = share
            other = moved(share, blocks, groups, 0, bit)
        share = jnp.where(
            upper, jnp.concatenate([other, mine], 0), jnp.concatenate([mine, other], 0)
        )
    return share


def visit(cell_rows, parts, tiles, masks):
    rank_width = cell_rows.shape[1]
    cell_step = 2.0 / (sum(p.shape[0] for p in parts) + rank_width)
    locus_step = 2.0 / (cell_rows.shape[0] + rank_width)
    for _ in range(SWEEPS):
        cell_half = cell_rows.astype(jnp.bfloat16)
        grad_cells = None
        updated = []
        for part, tile, mask in zip(parts, tiles, masks):
            half = part.astype(jnp.bfloat16)
            predicted = lax.dot_general(
                cell_half, half, (((1,), (1,)), ((), ())), preferred_element_type=jnp.float32
            )
            residue = (mask * (tile - predicted)).astype(jnp.bfloat16)
            term = jnp.dot(residue, half, preferred_element_type=jnp.float32)
            grad_cells = term if grad_cells is None else grad_cells + term
            grad_locus = lax.dot_general(
                residue, cell_half, (((0,), (0,)), ((), ())), preferred_element_type=jnp.float32
            )
            updated.append(part + locus_step * grad_locus)
        cell_rows = cell_rows + cell_step * grad_cells
        parts = updated
    return cell_rows, parts


def solution(mesh):
    blocks, groups = mesh.shape["blk"], mesh.shape["group"]

    def on_device(expression, observed, cell_factors, locus_factors):
        position = lax.axis_index("blk")
        block_rows = locus_factors.shape[0]
        size = block_rows // CHUNKS
        cell_rows = cell_factors
        parts = [locus_factors[c * size : (c + 1) * size] for c in range(CHUNKS)]
        for hop in range(HOPS):
            offset = (position - hop) % blocks * block_rows
            tiles = [
                lax.dynamic_slice_in_dim(expression, offset + c * size, size, 1).astype(jnp.float32)
                for c in range(CHUNKS)
            ]
            masks = [
                lax.dynamic_slice_in_dim(observed, offset + c * size, size, 1).astype(jnp.float32)
                for c in range(CHUNKS)
            ]
            cell_rows, parts = visit(cell_rows, parts, tiles, masks)
            if hop == HOPS // 2 - 1 or hop == HOPS - 1:
                distance = 1 if hop < HOPS - 1 else 1 - HOPS
                whole = average(jnp.concatenate(parts, 0), blocks, groups, distance)
                parts = [whole[c * size : (c + 1) * size] for c in range(CHUNKS)]
            else:
                parts = [moved(p, blocks, groups, 1) for p in parts]
        return cell_rows, jnp.concatenate(parts, 0)

    split = P(AXES, None)
    return jax.shard_map(
        on_device,
        mesh=mesh,
        in_specs=(split, split, split, P("blk", None)),
        out_specs=(split, P("blk", None)),
        check_vma=False,
    )
```

time: 181 us -> 138 us (0.76)
  waiting for transfers between devices: 111 us -> 81.6 us
  between operations: 14.4 us -> 1.38 us
  blocking collectives: 13 us -> 0 us
  matrix products: 30.6 us -> 39.6 us
  other arithmetic: 1.83 us -> 5.03 us
    reduce_scatter x2 -> x0, waiting for transfers between devices: 37.5 us -> none  [on_device(): lax.psum_scatter(locus_rows, 'group', scatter_dimension=0, tiled=True)]
    all_gather x2 -> x0, blocking collectives: 13 us -> none  [on_device(): locus_rows = lax.all_gather(share, 'group', axis=0, tiled=True)]
    dot_general x36 -> x72, matrix products: 30.6 us -> 39.6 us  [the longest x24 16 us: visit(): term = jnp.dot(residue, half, preferred_element_type=jnp.float32)]
    ppermute x6 -> x18, waiting for transfers between devices: 73.7 us -> 81.6 us  [moved(): return lax.ppermute(block, AXES, route)]
    ppermute x6 -> x18, starting transfers between devices: 7.07 us -> 8.62 us  [moved(): return lax.ppermute(block, AXES, route)]
  transfers between devices with their start and end apart: 8 -> 18, of which waited for: 8 -> 18; matrix products, arithmetic and copies ran while one was open for 2% -> 12% of each run, Pallas kernels for 0% -> 0%
where the time goes in v1:
time: 138 us; the launch traced here: 137 us
  waiting for transfers between devices  81.6 us (59%)
  matrix products  39.6 us (29%)
  starting transfers between devices  8.62 us (6%)
  other arithmetic  5.03 us (4%)
    ppermute x18, waiting for transfers between devices, moved(): return lax.ppermute(block, AXES, route)  81.6 us
    dot_general x24, matrix products, visit(): term = jnp.dot(residue, half, preferred_element_type=jnp.float32)  16 us
    dot_general x24, matrix products, visit(): lax.dot_general(cell_half, half, (((1,), (1,)), ((), ())), preferred_elem...  12.5 us
    dot_general x24, matrix products, visit(): lax.dot_general(residue, cell_half, (((0,), (0,)), ((), ())), preferred_e...  11.1 us
    ppermute x18, starting transfers between devices, moved(): return lax.ppermute(block, AXES, route)  8.62 us
  transfers between devices with their start and end apart: 18, of which 18 were waited for; matrix products, arithmetic and copies ran while one was open for 12% of the time, Pallas kernels for 0%

profile of v1, /device:TPU:0, one launch (start us, length us, event | category | flops | bytes accessed | tf_op | source)
XLA Modules:
  0.0 137.0 jit_solution(4186177001004067795)
XLA Ops:
  0.6 1.2 convert_element_type.254
  1.9 1.4 %fusion.73 = bf16[384,128]{1,0:T(8,128)(2,1)S(1)} fusion(bf16[384,512]{1,0:T(8,128)(2,1)S(1)} %convert_element_type.254, s32[384,2048]{1,0:T(8,128)} %param.5, s32[]{:T(128)S(6)} %select_n.139, bf16[384,2048]{1,0:T(8,128)(2,1)} %param.4, f32[256,512]{1,0:T(8,128)} %param.7), kind=kOutput, calls=%fused_computation.133 | convolution fusion | flops 50577408 | bytes 917508 | tf_op jit(solution)/shard_map/dot_general | solution.py:59
  3.3 1.5 %fusion.72 = bf16[384,128]{1,0:T(8,128)(2,1)S(1)} fusion(bf16[384,512]{1,0:T(8,128)(2,1)S(1)} %convert_element_type.254, s32[384,2048]{1,0:T(8,128)} %param.5, s32[]{:T(128)S(6)} %select_n.138, bf16[384,2048]{1,0:T(8,128)(2,1)} %param.4, f32[256,512]{1,0:T(8,128)} %param.7), kind=kOutput, calls=%fused_computation.132 | convolution fusion | flops 50577408 | bytes 917508 | tf_op jit(solution)/shard_map/dot_general | solution.py:59
  4.8 1.2 fusion.46
  6.3 1.1 fusion.148
  7.5 1.2 fusion.75
  8.6 1.0 fusion.44
  9.6 3.0 %collective-permute-start.1 = (f32[128,512]{1,0:T(8,128)}, f32[128,512]{1,0:T(8,128)}, u32[]{:S(2)}, u32[]{:S(2)}) collective-permute-start(f32[128,512]{1,0:T(8,128)} %fusion.44), channel_id=1, source_target_pairs={{0,4},{1,5},{2,6},{3,7},{4,8},{5,9},{6,10},{7,11},{8,12},{9,13},{1... | collective-permute-start | bytes 786440 | tf_op jit(solution)/shard_map/ppermute | solution.py:18
  12.8 1.3 fusion.74
  14.1 1.0 fusion.45
  15.1 1.5 %collective-permute-start = (f32[128,512]{1,0:T(8,128)}, f32[128,512]{1,0:T(8,128)}, u32[]{:S(2)}, u32[]{:S(2)}) collective-permute-start(f32[128,512]{1,0:T(8,128)} %fusion.45), channel_id=1, source_target_pairs={{0,4},{1,5},{2,6},{3,7},{4,8},{5,9},{6,10},{7,11},{8,12},{9,13},{1... | collective-permute-start | bytes 786440 | tf_op jit(solution)/shard_map/ppermute | solution.py:18
  16.6 2.1 %fusion.143 = f32[384,512]{1,0:T(8,128)} fusion(bf16[384,128]{1,0:T(8,128)(2,1)} %copy-done.14, f32[128,512]{1,0:T(8,128)} %copy-done.5), kind=kOutput, calls=%fused_computation.219 | convolution fusion | flops 50397184 | bytes 1146880 | tf_op jit(solution)/shard_map/dot_general | solution.py:63
  18.8 1.7 %fusion.149 = (bf16[384,512]{1,0:T(8,128)(2,1)S(1)}, f32[384,512]{1,0:T(8,128)S(1)}) fusion(f32[384,512]{1,0:T(8,128)} %get-tuple-element.3, f32[384,512]{1,0:T(8,128)} %fusion.143, bf16[384,128]{1,0:T(8,128)(2,1)S(1)} %copy-done.12, f32[128,512]{1,0:T(8,128)S(1)} %copy-done.3), kind=kOutput, calls=%fused_computation.225 | convolution fusion | flops 51183616 | bytes 3112960 | tf_op jit(solution)/shard_map/dot_general | solution.py:63
  20.5 2.5 %collective-permute-done.1 = f32[128,512]{1,0:T(8,128)} collective-permute-done((f32[128,512]{1,0:T(8,128)}, f32[128,512]{1,0:T(8,128)}, u32[]{:S(2)}, u32[]{:S(2)}) %collective-permute-start.1) | collective-permute-done | bytes 262176 | tf_op jit(solution)/shard_map/ppermute | solution.py:18
  23.0 1.2 fusion.77
  24.3 1.2 fusion.42
  25.5 1.2 fusion.136
  26.7 1.2 collective-permute-done
  27.8 1.2 fusion.76
  29.0 1.2 fusion.150
  31.0 1.2 fusion.43
  32.8 1.1 collective-permute-start.2
  34.2 10.6 %collective-permute-done.3 = f32[128,512]{1,0:T(8,128)S(1)} collective-permute-done((f32[128,512]{1,0:T(8,128)S(1)}, f32[128,512]{1,0:T(8,128)S(1)}, u32[]{:S(2)}, u32[]{:S(2)}) %collective-permute-start.3) | collective-permute-done | bytes 262176 | tf_op jit(solution)/shard_map/ppermute | solution.py:18
  45.5 3.1 %collective-permute-done.2 = f32[128,512]{1,0:T(8,128)S(1)} collective-permute-done((f32[128,512]{1,0:T(8,128)S(1)}, f32[128,512]{1,0:T(8,128)S(1)}, u32[]{:S(2)}, u32[]{:S(2)}) %collective-permute-start.2) | collective-permute-done | bytes 262176 | tf_op jit(solution)/shard_map/ppermute | solution.py:18
  48.9 1.1 fusion.152
  51.1 1.1 broadcast_select_fusion.1
  52.2 1.9 %collective-permute-done.4 = f32[128,512]{1,0:T(8,128)} collective-permute-done((f32[128,512]{1,0:T(8,128)}, f32[128,512]{1,0:T(8,128)}, u32[]{:S(2)}, u32[]{:S(2)}) %collective-permute-start.4) | collective-permute-done | bytes 262176 | tf_op jit(solution)/shard_map/ppermute | solution.py:18
  54.0 1.1 select_add_fusion.1
  55.1 0.7 copy-done.9
  55.8 0.7 slice_select_fusion.1
  56.5 1.3 collective-permute-start.5
  57.8 4.5 %collective-permute-done.5 = f32[64,512]{1,0:T(8,128)} collective-permute-done((f32[64,512]{1,0:T(8,128)}, f32[64,512]{1,0:T(8,128)}, u32[]{:S(2)}, u32[]{:S(2)}) %collective-permute-start.5) | collective-permute-done | bytes 131104 | tf_op jit(solution)/shard_map/ppermute | solution.py:18
  62.3 1.1 add_multiply_fusion.1
  63.5 1.2 fusion.121
  64.8 7.8 %collective-permute-done.7 = f32[64,512]{1,0:T(8,128)S(1)} collective-permute-done((f32[64,512]{1,0:T(8,128)S(1)}, f32[64,512]{1,0:T(8,128)S(1)}, u32[]{:S(2)}, u32[]{:S(2)}) %collective-permute-start.7) | collective-permute-done | bytes 131104 | tf_op jit(solution)/shard_map/ppermute | solution.py:18
  72.6 1.9 %collective-permute-done.6 = f32[64,512]{1,0:T(8,128)S(1)} collective-permute-done((f32[64,512]{1,0:T(8,128)S(1)}, f32[64,512]{1,0:T(8,128)S(1)}, u32[]{:S(2)}, u32[]{:S(2)}) %collective-permute-start.6) | collective-permute-done | bytes 131104 | tf_op jit(solution)/shard_map/ppermute | solution.py:18
  74.5 1.4 %fusion.153 = (bf16[384,512]{1,0:T(8,128)(2,1)S(1)}, f32[384,512]{1,0:T(8,128)S(1)}) fusion(f32[384,512]{1,0:T(8,128)} %get-tuple-element.11, f32[384,512]{1,0:T(8,128)S(1)} %fusion.121, bf16[384,128]{1,0:T(8,128)(2,1)S(1)} %fusion.82, f32[128,512]{1,0:T(8,128)S(1)} %fusion.39), kind=kOutput, calls=%fused_computation.229 | convolution fusion | flops 51183616 | bytes 3112960 | tf_op jit(solution)/shard_map/dot_general | solution.py:63
  79.4 11.5 %collective-permute-done.10 = f32[128,512]{1,0:T(8,128)S(1)} collective-permute-done((f32[128,512]{1,0:T(8,128)S(1)}, f32[128,512]{1,0:T(8,128)S(1)}, u32[]{:S(2)}, u32[]{:S(2)}) %collective-permute-start.10) | collective-permute-done | bytes 262176 | tf_op jit(solution)/shard_map/ppermute | solution.py:18
  91.7 4.3 %collective-permute-done.9 = f32[128,512]{1,0:T(8,128)S(1)} collective-permute-done((f32[128,512]{1,0:T(8,128)S(1)}, f32[128,512]{1,0:T(8,128)S(1)}, u32[]{:S(2)}, u32[]{:S(2)}) %collective-permute-start.9) | collective-permute-done | bytes 262176 | tf_op jit(solution)/shard_map/ppermute | solution.py:18
  98.6 11.4 %collective-permute-done.12 = f32[128,512]{1,0:T(8,128)S(1)} collective-permute-done((f32[128,512]{1,0:T(8,128)S(1)}, f32[128,512]{1,0:T(8,128)S(1)}, u32[]{:S(2)}, u32[]{:S(2)}) %collective-permute-start.12) | collective-permute-done | bytes 262176 | tf_op jit(solution)/shard_map/ppermute | solution.py:18
  110.8 3.4 %collective-permute-done.11 = f32[128,512]{1,0:T(8,128)S(1)} collective-permute-done((f32[128,512]{1,0:T(8,128)S(1)}, f32[128,512]{1,0:T(8,128)S(1)}, u32[]{:S(2)}, u32[]{:S(2)}) %collective-permute-start.11) | collective-permute-done | bytes 262176 | tf_op jit(solution)/shard_map/ppermute | solution.py:18
  116.1 1.5 %collective-permute-done.13 = f32[128,512]{1,0:T(8,128)S(1)} collective-permute-done((f32[128,512]{1,0:T(8,128)S(1)}, f32[128,512]{1,0:T(8,128)S(1)}, u32[]{:S(2)}, u32[]{:S(2)}) %collective-permute-start.13) | collective-permute-done | bytes 262176 | tf_op jit(solution)/shard_map/ppermute | solution.py:18
  117.7 0.8 collective-permute-start.14
  118.5 4.8 %collective-permute-done.14 = f32[64,512]{1,0:T(8,128)S(1)} collective-permute-done((f32[64,512]{1,0:T(8,128)S(1)}, f32[64,512]{1,0:T(8,128)S(1)}, u32[]{:S(2)}, u32[]{:S(2)}) %collective-permute-start.14) | collective-permute-done | bytes 131104 | tf_op jit(solution)/shard_map/ppermute | solution.py:18
  123.8 7.9 %collective-permute-done.16 = f32[64,512]{1,0:T(8,128)S(1)} collective-permute-done((f32[64,512]{1,0:T(8,128)S(1)}, f32[64,512]{1,0:T(8,128)S(1)}, u32[]{:S(2)}, u32[]{:S(2)}) %collective-permute-start.16) | collective-permute-done | bytes 131104 | tf_op jit(solution)/shard_map/ppermute | solution.py:18
  131.7 2.8 %collective-permute-done.15 = f32[64,512]{1,0:T(8,128)S(1)} collective-permute-done((f32[64,512]{1,0:T(8,128)S(1)}, f32[64,512]{1,0:T(8,128)S(1)}, u32[]{:S(2)}, u32[]{:S(2)}) %collective-permute-start.15) | collective-permute-done | bytes 131104 | tf_op jit(solution)/shard_map/ppermute | solution.py:18
  134.6 1.1 fusion.1
  136.1 0.8 maximum_select_fusion.1
  (101 shorter events, 14.7 us)
Async XLA Ops:
  1.9 4.2 %copy-start.1 = (f32[256,512]{1,0:T(8,128)S(1)}, f32[256,512]{1,0:T(8,128)}, u32[]{:S(2)}) copy-start(f32[256,512]{1,0:T(8,128)} %param.7) | copy-start | bytes 1572868
  1.9 4.4 %copy-start.8 = (f32[384,512]{1,0:T(8,128)S(1)}, f32[384,512]{1,0:T(8,128)}, u32[]{:S(2)}) copy-start(f32[384,512]{1,0:T(8,128)} %param.6) | copy-start | bytes 2359300
  3.3 4.1 %copy-start = (s32[384,2048]{1,0:T(8,128)S(1)}, s32[384,2048]{1,0:T(8,128)}, u32[]{:S(2)}) copy-start(s32[384,2048]{1,0:T(8,128)} %param.5) | copy-start | bytes 9437188
  6.0 3.5 %copy-start.2 = (f32[128,512]{1,0:T(8,128)}, f32[128,512]{1,0:T(8,128)S(1)}, u32[]{:S(2)}) copy-start(f32[128,512]{1,0:T(8,128)S(1)} %fusion.46) | copy-start | bytes 786436
  8.6 1.0 copy-start.11
  9.6 13.5 %collective-permute-start.1 = (f32[128,512]{1,0:T(8,128)}, f32[128,512]{1,0:T(8,128)}, u32[]{:S(2)}, u32[]{:S(2)}) collective-permute-start(f32[128,512]{1,0:T(8,128)} %fusion.44), channel_id=1, source_target_pairs={{0,4},{1,5},{2,6},{3,7},{4,8},{5,9},{6,10},{7,11},{8,12},{9,13},{1... | collective-permute-start | bytes 786440 | tf_op jit(solution)/shard_map/ppermute | solution.py:18
  12.8 2.3 %copy-start.5 = (f32[128,512]{1,0:T(8,128)}, f32[128,512]{1,0:T(8,128)S(1)}, u32[]{:S(2)}) copy-start(f32[128,512]{1,0:T(8,128)S(1)} %fusion.47) | copy-start | bytes 786436
  12.8 5.9 %copy-start.3 = (f32[128,512]{1,0:T(8,128)S(1)}, f32[128,512]{1,0:T(8,128)}, u32[]{:S(2)}) copy-start(f32[128,512]{1,0:T(8,128)} %copy-done.2) | copy-start | bytes 786436
  12.8 5.9 %copy-start.12 = (bf16[384,128]{1,0:T(8,128)(2,1)S(1)}, bf16[384,128]{1,0:T(8,128)(2,1)}, u32[]{:S(2)}) copy-start(bf16[384,128]{1,0:T(8,128)(2,1)} %copy-done.11) | copy-start | bytes 294916
  14.1 1.0 copy-start.14
  15.1 12.7 %collective-permute-start = (f32[128,512]{1,0:T(8,128)}, f32[128,512]{1,0:T(8,128)}, u32[]{:S(2)}, u32[]{:S(2)}) collective-permute-start(f32[128,512]{1,0:T(8,128)} %fusion.45), channel_id=1, source_target_pairs={{0,4},{1,5},{2,6},{3,7},{4,8},{5,9},{6,10},{7,11},{8,12},{9,13},{1... | collective-permute-start | bytes 786440 | tf_op jit(solution)/shard_map/ppermute | solution.py:18
  18.8 4.3 %copy-start.6 = (bf16[384,2048]{1,0:T(8,128)(2,1)S(1)}, bf16[384,2048]{1,0:T(8,128)(2,1)}, u32[]{:S(2)}) copy-start(bf16[384,2048]{1,0:T(8,128)(2,1)} %param.4) | copy-start | bytes 4718596
  32.8 12.0 %collective-permute-start.3 = (f32[128,512]{1,0:T(8,128)S(1)}, f32[128,512]{1,0:T(8,128)S(1)}, u32[]{:S(2)}, u32[]{:S(2)}) collective-permute-start(f32[128,512]{1,0:T(8,128)S(1)} %fusion.40), channel_id=1, source_target_pairs={{0,4},{1,5},{2,6},{3,7},{4,8},{5,9},{6,10},{7,11},{8,12},{9,13},{1... | collective-permute-start | bytes 786440 | tf_op jit(solution)/shard_map/ppermute | solution.py:18
  32.8 15.8 %collective-permute-start.2 = (f32[128,512]{1,0:T(8,128)S(1)}, f32[128,512]{1,0:T(8,128)S(1)}, u32[]{:S(2)}, u32[]{:S(2)}) collective-permute-start(f32[128,512]{1,0:T(8,128)S(1)} %fusion.41), channel_id=1, source_target_pairs={{0,4},{1,5},{2,6},{3,7},{4,8},{5,9},{6,10},{7,11},{8,12},{9,13},{1... | collective-permute-start | bytes 786440 | tf_op jit(solution)/shard_map/ppermute | solution.py:18
  45.3 5.6 %copy-start.4 = (f32[128,512]{1,0:T(8,128)}, f32[128,512]{1,0:T(8,128)S(1)}, u32[]{:S(2)}) copy-start(f32[128,512]{1,0:T(8,128)S(1)} %fusion.38) | copy-start | bytes 786436
  50.3 1.9 %copy-start.13 = (bf16[384,128]{1,0:T(8,128)(2,1)}, bf16[384,128]{1,0:T(8,128)(2,1)S(1)}, u32[]{:S(2)}) copy-start(bf16[384,128]{1,0:T(8,128)(2,1)S(1)} %fusion.83) | copy-start | bytes 294916
  51.1 1.1 copy-start.10
  52.2 1.9 %collective-permute-start.4 = (f32[128,512]{1,0:T(8,128)}, f32[128,512]{1,0:T(8,128)}, u32[]{:S(2)}, u32[]{:S(2)}) collective-permute-start(f32[128,512]{1,0:T(8,128)} %get-tuple-element.14), channel_id=1, source_target_pairs={{0,1},{1,0},{2,3},{3,2},{4,5},{5,4},{6,7},{7,6},{8,9},{9,8},{10,11... | collective-permute-start | bytes 786440 | tf_op jit(solution)/shard_map/ppermute | solution.py:18
  55.1 0.7 copy-start.9
  56.5 5.9 %collective-permute-start.5 = (f32[64,512]{1,0:T(8,128)}, f32[64,512]{1,0:T(8,128)}, u32[]{:S(2)}, u32[]{:S(2)}) collective-permute-start(f32[64,512]{1,0:T(8,128)} %slice_select_fusion.1), channel_id=1, source_target_pairs={{0,2},{1,3},{2,0},{3,1},{4,6},{5,7},{6,4},{7,5},{8,10},{9,11},{10,... | collective-permute-start | bytes 393224 | tf_op jit(solution)/shard_map/ppermute | solution.py:18
  57.8 18.3 %copy-start.7 = (bf16[384,2048]{1,0:T(8,128)(2,1)S(1)}, bf16[384,2048]{1,0:T(8,128)(2,1)}, u32[]{:S(2)}) copy-start(bf16[384,2048]{1,0:T(8,128)(2,1)} %param.4) | copy-start | bytes 4718596
  63.4 9.2 %collective-permute-start.7 = (f32[64,512]{1,0:T(8,128)S(1)}, f32[64,512]{1,0:T(8,128)S(1)}, u32[]{:S(2)}, u32[]{:S(2)}) collective-permute-start(f32[64,512]{1,0:T(8,128)S(1)} %add_multiply_fusion.1), channel_id=1, source_target_pairs={{0,4},{1,5},{2,6},{3,7},{4,8},{5,9},{6,10},{7,11},{8,12},{9,13},{1... | collective-permute-start | bytes 393224 | tf_op jit(solution)/shard_map/ppermute | solution.py:18
  63.5 11.0 %collective-permute-start.6 = (f32[64,512]{1,0:T(8,128)S(1)}, f32[64,512]{1,0:T(8,128)S(1)}, u32[]{:S(2)}, u32[]{:S(2)}) collective-permute-start(f32[64,512]{1,0:T(8,128)S(1)} %add_multiply_fusion.1), channel_id=1, source_target_pairs={{0,6},{1,7},{2,4},{3,5},{4,10},{5,11},{6,8},{7,9},{8,14},{9,15},{1... | collective-permute-start | bytes 393224 | tf_op jit(solution)/shard_map/ppermute | solution.py:18
  74.5 1.6 %collective-permute-start.8 = (f32[128,512]{1,0:T(8,128)S(1)}, f32[128,512]{1,0:T(8,128)S(1)}, u32[]{:S(2)}, u32[]{:S(2)}) collective-permute-start(f32[128,512]{1,0:T(8,128)S(1)} %maximum_select_fusion.2), channel_id=1, source_target_pairs={{0,1},{1,0},{2,3},{3,2},{4,5},{5,4},{6,7},{7,6},{8,9},{9,8},{10,11... | collective-permute-start | bytes 786440 | tf_op jit(solution)/shard_map/ppermute | solution.py:18
  79.0 11.9 %collective-permute-start.10 = (f32[128,512]{1,0:T(8,128)S(1)}, f32[128,512]{1,0:T(8,128)S(1)}, u32[]{:S(2)}, u32[]{:S(2)}) collective-permute-start(f32[128,512]{1,0:T(8,128)S(1)} %fusion.32), channel_id=1, source_target_pairs={{0,4},{1,5},{2,6},{3,7},{4,8},{5,9},{6,10},{7,11},{8,12},{9,13},{1... | collective-permute-start | bytes 786440 | tf_op jit(solution)/shard_map/ppermute | solution.py:18
  79.1 16.9 %collective-permute-start.9 = (f32[128,512]{1,0:T(8,128)S(1)}, f32[128,512]{1,0:T(8,128)S(1)}, u32[]{:S(2)}, u32[]{:S(2)}) collective-permute-start(f32[128,512]{1,0:T(8,128)S(1)} %fusion.33), channel_id=1, source_target_pairs={{0,4},{1,5},{2,6},{3,7},{4,8},{5,9},{6,10},{7,11},{8,12},{9,13},{1... | collective-permute-start | bytes 786440 | tf_op jit(solution)/shard_map/ppermute | solution.py:18
  98.1 12.0 %collective-permute-start.12 = (f32[128,512]{1,0:T(8,128)S(1)}, f32[128,512]{1,0:T(8,128)S(1)}, u32[]{:S(2)}, u32[]{:S(2)}) collective-permute-start(f32[128,512]{1,0:T(8,128)S(1)} %fusion.28), channel_id=1, source_target_pairs={{0,4},{1,5},{2,6},{3,7},{4,8},{5,9},{6,10},{7,11},{8,12},{9,13},{1... | collective-permute-start | bytes 786440 | tf_op jit(solution)/shard_map/ppermute | solution.py:18
  98.1 16.1 %collective-permute-start.11 = (f32[128,512]{1,0:T(8,128)S(1)}, f32[128,512]{1,0:T(8,128)S(1)}, u32[]{:S(2)}, u32[]{:S(2)}) collective-permute-start(f32[128,512]{1,0:T(8,128)S(1)} %fusion.29), channel_id=1, source_target_pairs={{0,4},{1,5},{2,6},{3,7},{4,8},{5,9},{6,10},{7,11},{8,12},{9,13},{1... | collective-permute-start | bytes 786440 | tf_op jit(solution)/shard_map/ppermute | solution.py:18
  116.0 1.6 %collective-permute-start.13 = (f32[128,512]{1,0:T(8,128)S(1)}, f32[128,512]{1,0:T(8,128)S(1)}, u32[]{:S(2)}, u32[]{:S(2)}) collective-permute-start(f32[128,512]{1,0:T(8,128)S(1)} %get-tuple-element.26), channel_id=1, source_target_pairs={{0,1},{1,0},{2,3},{3,2},{4,5},{5,4},{6,7},{7,6},{8,9},{9,8},{10,11... | collective-permute-start | bytes 786440 | tf_op jit(solution)/shard_map/ppermute | solution.py:18
  117.7 5.6 %collective-permute-start.14 = (f32[64,512]{1,0:T(8,128)S(1)}, f32[64,512]{1,0:T(8,128)S(1)}, u32[]{:S(2)}, u32[]{:S(2)}) collective-permute-start(f32[64,512]{1,0:T(8,128)S(1)} %slice_select_fusion), channel_id=1, source_target_pairs={{0,2},{1,3},{2,0},{3,1},{4,6},{5,7},{6,4},{7,5},{8,10},{9,11},{10,... | collective-permute-start | bytes 393224 | tf_op jit(solution)/shard_map/ppermute | solution.py:18
  123.4 8.3 %collective-permute-start.16 = (f32[64,512]{1,0:T(8,128)S(1)}, f32[64,512]{1,0:T(8,128)S(1)}, u32[]{:S(2)}, u32[]{:S(2)}) collective-permute-start(f32[64,512]{1,0:T(8,128)S(1)} %add_multiply_fusion), channel_id=1, source_target_pairs={{0,12},{1,13},{2,14},{3,15},{4,16},{5,17},{6,18},{7,19},{8,20},{9,... | collective-permute-start | bytes 393224 | tf_op jit(solution)/shard_map/ppermute | solution.py:18
  123.4 11.1 %collective-permute-start.15 = (f32[64,512]{1,0:T(8,128)S(1)}, f32[64,512]{1,0:T(8,128)S(1)}, u32[]{:S(2)}, u32[]{:S(2)}) collective-permute-start(f32[64,512]{1,0:T(8,128)S(1)} %add_multiply_fusion), channel_id=1, source_target_pairs={{0,14},{1,15},{2,12},{3,13},{4,18},{5,19},{6,16},{7,17},{8,22},{9,... | collective-permute-start | bytes 393224 | tf_op jit(solution)/shard_map/ppermute | solution.py:18
  134.5 1.6 %collective-permute-start.17 = (f32[128,512]{1,0:T(8,128)S(1)}, f32[128,512]{1,0:T(8,128)S(1)}, u32[]{:S(2)}, u32[]{:S(2)}) collective-permute-start(f32[128,512]{1,0:T(8,128)S(1)} %maximum_select_fusion.3), channel_id=1, source_target_pairs={{0,1},{1,0},{2,3},{3,2},{4,5},{5,4},{6,7},{7,6},{8,9},{9,8},{10,11... | collective-permute-start | bytes 786440 | tf_op jit(solution)/shard_map/ppermute | solution.py:18

commit v2 on v1

v2 whole, which is shorter than its diff:
```python
import functools

import jax
import jax.numpy as jnp
from jax import lax
from jax.experimental import pallas as pl
from jax.experimental.pallas import tpu as pltpu
from jax.sharding import PartitionSpec as P

HOPS = 6
AXES = ("blk", "group")
F32, HALF = jnp.float32, jnp.bfloat16


def across(a, b):
    return lax.dot_general(a, b, (((1,), (1,)), ((), ())), preferred_element_type=F32)


def along(a, b):
    return lax.dot_general(a, b, (((0,), (0,)), ((), ())), preferred_element_type=F32)


def times(a, b):
    return jnp.dot(a, b, preferred_element_type=F32)


def residue(x_ref, m_ref, cell_half, locus_half):
    difference = x_ref[...].astype(F32) - across(cell_half, locus_half)
    return (m_ref[...].astype(F32) * difference).astype(HALF)


def tile_copies(first, x_hbm, m_hbm, xa, ma, xb, mb, sems):
    width = xa.shape[1]
    copies = []
    for place, (x_out, m_out) in enumerate(((xa, ma), (xb, mb))):
        column = first if place == 0 else first + 1 - 2 * (first % 2)
        columns = pl.ds(pl.multiple_of(column * width, width), width)
        copies.append(pltpu.make_async_copy(x_hbm.at[:, columns], x_out, sems.at[2 * place]))
        copies.append(pltpu.make_async_copy(m_hbm.at[:, columns], m_out, sems.at[2 * place + 1]))
    return copies


def load_body(first, x_hbm, m_hbm, u_hbm, v_hbm, xa, ma, xb, mb, u, va, vb, sems):
    rows = va.shape[0]
    half = first[0] % 2
    copies = tile_copies(first[0], x_hbm, m_hbm, xa, ma, xb, mb, sems)
    copies.append(pltpu.make_async_copy(u_hbm, u, sems.at[4]))
    for place, (out, index) in enumerate(((va, half), (vb, 1 - half))):
        at = pl.ds(pl.multiple_of(index * rows, rows), rows)
        copies.append(pltpu.make_async_copy(v_hbm.at[at], out, sems.at[5 + place]))
    for copy in copies:
        copy.start()
    for copy in copies:
        copy.wait()


def open_body(steps, u, va, xa, ma, grad_u, va1):
    cell_half, locus_half = u[...].astype(HALF), va[...].astype(HALF)
    r = residue(xa, ma, cell_half, locus_half)
    grad_u[...] = times(r, locus_half)
    va1[...] = va[...] + steps[1] * along(r, cell_half)


def turn_body(steps, u, grad_u, va1, vb, xa, ma, xb, mb, u1, va2, r1b, r2a):
    cell_half, locus_half = u[...].astype(HALF), vb[...].astype(HALF)
    r = residue(xb, mb, cell_half, locus_half)
    r1b[...] = r
    moved_u = u[...] + steps[0] * (grad_u[...] + times(r, locus_half))
    u1[...] = moved_u
    cell_half, locus_half = moved_u.astype(HALF), va1[...].astype(HALF)
    r = residue(xa, ma, cell_half, locus_half)
    r2a[...] = r
    va2[...] = va1[...] + steps[1] * along(r, cell_half)


def close_body(
    steps, first, u, u1, r1b, r2a, va1, vb, xb, mb, x_hbm, m_hbm,
    vb2, u2, xa_next, ma_next, xb_next, mb_next, sems,
):
    copies = tile_copies(first[0], x_hbm, m_hbm, xa_next, ma_next, xb_next, mb_next, sems)
    for copy in copies:
        copy.start()
    vb1 = vb[...] + steps[1] * along(r1b[...], u[...].astype(HALF))
    cell_half, locus_half = u1[...].astype(HALF), vb1.astype(HALF)
    r = residue(xb, mb, cell_half, locus_half)
    vb2[...] = vb1 + steps[1] * along(r, cell_half)
    u2[...] = u1[...] + steps[0] * (times(r2a[...], va1[...].astype(HALF)) + times(r, locus_half))
    for copy in copies:
        copy.wait()


def call(body, args, spaces, outs, sems=0, flops=0):
    kinds = {"v": pltpu.VMEM, "h": pl.ANY, "s": pltpu.SMEM}
    pinned = [
        pltpu.with_memory_space_constraint(a, pltpu.VMEM) if s == "v" else a
        for a, s in zip(args, spaces)
    ]
    moved_bytes = sum(a.size * a.dtype.itemsize for a in args) if sems == 0 else 4 << 20
    return pl.pallas_call(
        body,
        out_shape=[pltpu.VMEM(shape, dtype) for shape, dtype in outs],
        in_specs=[pl.BlockSpec(memory_space=kinds[s]) for s in spaces],
        out_specs=[pl.BlockSpec(memory_space=pltpu.VMEM) for _ in outs],
        scratch_shapes=[pltpu.SemaphoreType.DMA((sems,))] if sems else [],
        compiler_params=pltpu.CompilerParams(vmem_limit_bytes=24 << 20),
        cost_estimate=pl.CostEstimate(flops=flops, bytes_accessed=moved_bytes, transcendentals=0),
    )(*pinned)


def moved(block, blocks, groups, distance, flip=0):
    route = [
        (b * groups + g, (b + distance) % blocks * groups + (g ^ flip))
        for b in range(blocks)
        for g in range(groups)
    ]
    return lax.ppermute(block, AXES, route)


def average(part_a, part_b, blocks, groups, distance):
    member = lax.axis_index("group")
    bits = [1 << i for i in range(1, groups.bit_length() - 1)]
    share = part_a + moved(part_b, blocks, groups, 0, 1)
    for bit in bits:
        rows = share.shape[0] // 2
        upper = (member & bit) != 0
        low, high = share[:rows], share[rows:]
        share = jnp.where(upper, high, low) + moved(jnp.where(upper, low, high), blocks, groups, 0, bit)
    share = share / groups
    for place, bit in enumerate(reversed(bits)):
        upper = (member & bit) != 0
        if place == 0:
            mine = moved(share, blocks, groups, distance)
            other = moved(share, blocks, groups, distance, bit)
        else:
            mine = share
            other = moved(share, blocks, groups, 0, bit)
        share = jnp.where(
            upper, jnp.concatenate([other, mine], 0), jnp.concatenate([mine, other], 0)
        )
    return share, moved(share, blocks, groups, 0, 1)


def solution(mesh):
    blocks, groups = mesh.shape["blk"], mesh.shape["group"]

    def on_device(expression, observed, cell_factors, locus_factors):
        position = lax.axis_index("blk")
        side = lax.axis_index("group") % 2
        cells, rank = cell_factors.shape
        rows = locus_factors.shape[0] // 2
        steps = (2.0 / (2 * rows + rank), 2.0 / (cells + rank))
        wide, tall = ((cells, rank), F32), ((rows, rank), F32)
        tiles = [((cells, rows), HALF), ((cells, rows), jnp.int32)] * 2
        small = ((cells, rows), HALF)
        work = 2 * cells * rows * rank

        def first(hop):
            return ((position - hop) % blocks * 2 + side).reshape(1).astype(jnp.int32)

        xa, ma, xb, mb, u, va, vb = call(
            load_body,
            (first(0), expression, observed, cell_factors, locus_factors),
            "shhhh",
            tiles + [wide, tall, tall],
            7,
        )
        for hop in range(HOPS):
            grad_u, va1 = call(
                functools.partial(open_body, steps), (u, va, xa, ma), "vvvv", [wide, tall], 0, 3 * work
            )
            u1, va2, r1b, r2a = call(
                functools.partial(turn_body, steps),
                (u, grad_u, va1, vb, xa, ma, xb, mb),
                "vvvvvvvv",
                [wide, tall, small, small],
                0,
                4 * work,
            )
            vb2, u, xa, ma, xb, mb = call(
                functools.partial(close_body, steps),
                (first(hop + 1), u, u1, r1b, r2a, va1, vb, xb, mb, expression, observed),
                "svvvvvvvvhh",
                [tall, wide] + tiles,
                4,
                5 * work,
            )
            if hop == HOPS // 2 - 1 or hop == HOPS - 1:
                distance = 1 if hop < HOPS - 1 else 1 - HOPS
                va, vb = average(va2, vb2, blocks, groups, distance)
            else:
                va, vb = (moved(part, blocks, groups, 1) for part in (va2, vb2))
        whole = jnp.where(side == 0, jnp.concatenate([va, vb], 0), jnp.concatenate([vb, va], 0))
        return u, whole

    split = P(AXES, None)
    return jax.shard_map(
        on_device,
        mesh=mesh,
        in_specs=(split, split, split, P("blk", None)),
        out_specs=(split, P("blk", None)),
        check_vma=False,
    )
```

time: 138 us -> 160 us (1.16)
  local copies, waits for them, and re-layouts: 0.76 us -> 52.7 us
  matrix products: 39.6 us -> 0 us
  Pallas kernels: 0 us -> 30.2 us
  waiting for transfers between devices: 81.6 us -> 61.7 us
  other arithmetic: 5.03 us -> 2.08 us
  starting transfers between devices: 8.62 us -> 10.9 us
    unnamed x30 -> x135, local copies, waits for them, and re-layouts: 0.76 us -> 52.7 us
    dot_general x72 -> x0, matrix products: 39.6 us -> none  [the longest x24 16 us: visit(): term = jnp.dot(residue, half, preferred_element_type=jnp.float32)]
    pallas_call x0 -> x19, Pallas kernels: none -> 30.2 us  [call(): pl.pallas_call(body, out_shape=[pltpu.VMEM(shape, dtype) for shape, dtype...]
    ppermute x18, waiting for transfers between devices: 81.6 us -> 61.7 us  [moved(): return lax.ppermute(block, AXES, route)]
    ppermute x18, starting transfers between devices: 8.62 us -> 10.9 us  [moved(): return lax.ppermute(block, AXES, route)]
  transfers between devices with their start and end apart: 18 -> 18, of which waited for: 18 -> 16; matrix products, arithmetic and copies ran while one was open for 12% -> 1% of each run, Pallas kernels for 0% -> 10%
where the time goes in v2:
time: 160 us; the launch traced here: 159 us
  waiting for transfers between devices  61.7 us (39%)
  local copies, waits for them, and re-layouts  52.7 us (33%)
  Pallas kernels  30.2 us (19%)
  starting transfers between devices  10.9 us (7%)
  other arithmetic  2.08 us (1%)
    ppermute x18, waiting for transfers between devices, moved(): return lax.ppermute(block, AXES, route)  61.7 us
    unnamed x135, local copies, waits for them, and re-layouts  52.7 us
    pallas_call x19, Pallas kernels, call(): pl.pallas_call(body, out_shape=[pltpu.VMEM(shape, dtype) for shape, dtype...  30.2 us
    ppermute x18, starting transfers between devices, moved(): return lax.ppermute(block, AXES, route)  10.9 us
  transfers between devices with their start and end apart: 18, of which 16 were waited for; matrix products, arithmetic and copies ran while one was open for 1% of the time, Pallas kernels for 10%

profile of v2, /device:TPU:0, one launch (start us, length us, event | category | flops | bytes accessed | tf_op | source)
XLA Modules:
  0.0 158.7 jit_solution(4748902858295532887)
XLA Ops:
  0.7 1.9 %copy-done = s32[384,2048]{1,0:T(8,128)S(1)} copy-done((s32[384,2048]{1,0:T(8,128)S(1)}, s32[384,2048]{1,0:T(8,128)}, u32[]{:S(2)}) %copy-start) | copy-done | bytes 3145752
  2.5 1.4 copy-done.3
  4.0 1.1 copy-done.24
  7.3 1.8 %shard_map.61 = (f32[384,512]{1,0:T(8,128)S(1)}, f32[128,512]{1,0:T(8,128)}, bf16[384,128]{1,0:T(8,128)(2,1)S(1)}, bf16[384,128]{1,0:T(8,128)(2,1)S(1)}) custom-call(f32[384,512]{1,0:T(8,128)S(1)} %get-tuple-element.77.u, f32[384,512]{1,0:T(8,128)S(1)} %get-tuple-element.81.grad_u, f32[128,512]{1,0:T(8,128)S(1)} %get-tuple-element.82.va1, ...), custom_call_target="tpu_custom_call" | custom-call | flops 201326592 | bytes 2686976 | tf_op jit(solution)/shard_map/pallas_call | solution.py:99
  11.2 3.0 %collective-permute-start = (f32[128,512]{1,0:T(8,128)}, f32[128,512]{1,0:T(8,128)}, u32[]{:S(2)}, u32[]{:S(2)}) collective-permute-start(f32[128,512]{1,0:T(8,128)} %get-tuple-element.90), channel_id=1, source_target_pairs={{0,4},{1,5},{2,6},{3,7},{4,8},{5,9},{6,10},{7,11},{8,12},{9,13},{1... | collective-permute-start | bytes 786440 | tf_op jit(solution)/shard_map/ppermute | solution.py:116
  14.2 1.4 copy-done.4
  15.6 1.1 copy-done.21
  17.7 1.1 copy-done.36
  22.4 1.9 %shard_map.62 = (f32[128,512]{1,0:T(8,128)}, f32[384,512]{1,0:T(8,128)S(1)}, bf16[384,128]{1,0:T(8,128)(2,1)S(1)}, s32[384,128]{1,0:T(8,128)S(1)}, bf16[384,128]{1,0:T(8,128)(2,1)S(1)}, /*index=5*/s32[384,128]{1,0:T(8,128)S(1)}) custom-call(s32[1]{0:T(128)} %bitcast.5.first, f32[384,512]{1,0:T(8,128)S(1)} %copy-done.21, f32[384,512]{1,0:T(8,128)S(1)} %copy-done.36, ...), custom_call_target="tpu_custom_call" | custom-call | flops 251658240 | bytes 4194304 | tf_op jit(solution)/shard_map/pallas_call | solution.py:99
  27.1 1.5 collective-permute-start.1
  28.7 1.3 copy-done.13
  30.9 1.6 %shard_map.63 = (f32[384,512]{1,0:T(8,128)S(1)}, f32[128,512]{1,0:T(8,128)S(1)}) custom-call(f32[384,512]{1,0:T(8,128)S(1)} %copy-done.13, f32[128,512]{1,0:T(8,128)} %collective-permute-done.va, bf16[384,128]{1,0:T(8,128)(2,1)S(1)} %get-tuple-element.91.xa, s32[384,128]{1,0:T(8,128)S(1)} %copy-done.30), custom_call_target="tpu_custom_call" | custom-call | flops 150994944 | bytes 1343488 | tf_op jit(solution)/shard_map/pallas_call | solution.py:99
  32.5 5.4 %collective-permute-done.1.vb = f32[128,512]{1,0:T(8,128)S(1)} collective-permute-done((f32[128,512]{1,0:T(8,128)}, f32[128,512]{1,0:T(8,128)S(1)}, u32[]{:S(2)}, u32[]{:S(2)}) %collective-permute-start.1) | collective-permute-done | bytes 262176 | tf_op jit(solution)/shard_map/ppermute | solution.py:116
  39.6 1.7 %shard_map.64 = (f32[384,512]{1,0:T(8,128)S(1)}, f32[128,512]{1,0:T(8,128)}, bf16[384,128]{1,0:T(8,128)(2,1)S(1)}, bf16[384,128]{1,0:T(8,128)(2,1)S(1)}) custom-call(f32[384,512]{1,0:T(8,128)S(1)} %copy-done.13, f32[384,512]{1,0:T(8,128)S(1)} %get-tuple-element.93.grad_u, f32[128,512]{1,0:T(8,128)S(1)} %get-tuple-element.94.va1, ...), custom_call_target="tpu_custom_call" | custom-call | flops 201326592 | bytes 2686976 | tf_op jit(solution)/shard_map/pallas_call | solution.py:99
  41.4 1.9 %shard_map.65 = (f32[128,512]{1,0:T(8,128)}, f32[384,512]{1,0:T(8,128)S(1)}, bf16[384,128]{1,0:T(8,128)(2,1)S(1)}, s32[384,128]{1,0:T(8,128)S(1)}, bf16[384,128]{1,0:T(8,128)(2,1)S(1)}, /*index=5*/s32[384,128]{1,0:T(8,128)S(1)}) custom-call(s32[1]{0:T(128)} %bitcast.4.first, f32[384,512]{1,0:T(8,128)S(1)} %copy-done.13, ...), custom_call_target="tpu_custom_call" | custom-call | flops 251658240 | bytes 4194304 | tf_op jit(solution)/shard_map/pallas_call | solution.py:99
  46.1 1.2 collective-permute-start.3
  47.4 4.7 %collective-permute-done.2.va = f32[128,512]{1,0:T(8,128)} collective-permute-done((f32[128,512]{1,0:T(8,128)}, f32[128,512]{1,0:T(8,128)}, u32[]{:S(2)}, u32[]{:S(2)}) %collective-permute-start.2) | collective-permute-done | bytes 262176 | tf_op jit(solution)/shard_map/ppermute | solution.py:116
  52.0 1.1 copy-done.19
  54.1 1.6 %shard_map.66 = (f32[384,512]{1,0:T(8,128)S(1)}, f32[128,512]{1,0:T(8,128)S(1)}) custom-call(f32[384,512]{1,0:T(8,128)S(1)} %copy-done.19, f32[128,512]{1,0:T(8,128)} %collective-permute-done.2.va, bf16[384,128]{1,0:T(8,128)(2,1)S(1)} %get-tuple-element.103.xa, s32[384,128]{1,0:T(8,128)S(1)} %copy-done.32), custom_call_target="tpu_custom_call" | custom-call | flops 150994944 | bytes 1343488 | tf_op jit(solution)/shard_map/pallas_call | solution.py:99
  55.7 1.0 collective-permute-done.3.vb
  59.6 1.9 %shard_map.68 = (f32[128,512]{1,0:T(8,128)}, f32[384,512]{1,0:T(8,128)S(1)}, bf16[384,128]{1,0:T(8,128)(2,1)S(1)}, s32[384,128]{1,0:T(8,128)S(1)}, bf16[384,128]{1,0:T(8,128)(2,1)S(1)}, /*index=5*/s32[384,128]{1,0:T(8,128)S(1)}) custom-call(s32[1]{0:T(128)} %bitcast.3.first, f32[384,512]{1,0:T(8,128)S(1)} %copy-done.19, ...), custom_call_target="tpu_custom_call" | custom-call | flops 251658240 | bytes 4194304 | tf_op jit(solution)/shard_map/pallas_call | solution.py:99
  64.4 1.9 %collective-permute-done.4 = f32[128,512]{1,0:T(8,128)} collective-permute-done((f32[128,512]{1,0:T(8,128)}, f32[128,512]{1,0:T(8,128)}, u32[]{:S(2)}, u32[]{:S(2)}) %collective-permute-start.4) | collective-permute-done | bytes 262176 | tf_op jit(solution)/shard_map/ppermute | solution.py:116
  66.3 1.1 add.79
  67.4 1.6 collective-permute-start.5
  68.9 4.0 %collective-permute-done.5 = f32[64,512]{1,0:T(8,128)S(1)} collective-permute-done((f32[64,512]{1,0:T(8,128)S(1)}, f32[64,512]{1,0:T(8,128)S(1)}, u32[]{:S(2)}, u32[]{:S(2)}) %collective-permute-start.5) | collective-permute-done | bytes 131104 | tf_op jit(solution)/shard_map/ppermute | solution.py:116
  73.4 9.4 %collective-permute-done.6 = f32[64,512]{1,0:T(8,128)S(1)} collective-permute-done((f32[64,512]{1,0:T(8,128)S(1)}, f32[64,512]{1,0:T(8,128)S(1)}, u32[]{:S(2)}, u32[]{:S(2)}) %collective-permute-start.6) | collective-permute-done | bytes 131104 | tf_op jit(solution)/shard_map/ppermute | solution.py:116
  82.8 1.4 collective-permute-done.7
  84.4 1.2 copy-done.11
  89.0 2.7 %shard_map.70 = (f32[384,512]{1,0:T(8,128)S(1)}, f32[128,512]{1,0:T(8,128)}, bf16[384,128]{1,0:T(8,128)(2,1)S(1)}, bf16[384,128]{1,0:T(8,128)(2,1)S(1)}) custom-call(f32[384,512]{1,0:T(8,128)S(1)} %copy-done.11, f32[384,512]{1,0:T(8,128)S(1)} %get-tuple-element.118.grad_u, f32[128,512]{1,0:T(8,128)S(1)} %get-tuple-element.119.va1, ...), custom_call_target="tpu_custom_call" | custom-call | flops 201326592 | bytes 2686976 | tf_op jit(solution)/shard_map/pallas_call | solution.py:99
  91.7 2.8 %shard_map.71 = (f32[128,512]{1,0:T(8,128)}, f32[384,512]{1,0:T(8,128)S(1)}, bf16[384,128]{1,0:T(8,128)(2,1)S(1)}, s32[384,128]{1,0:T(8,128)S(1)}, bf16[384,128]{1,0:T(8,128)(2,1)S(1)}, /*index=5*/s32[384,128]{1,0:T(8,128)S(1)}) custom-call(s32[1]{0:T(128)} %bitcast.2.first, f32[384,512]{1,0:T(8,128)S(1)} %copy-done.11, ...), custom_call_target="tpu_custom_call" | custom-call | flops 251658240 | bytes 4194304 | tf_op jit(solution)/shard_map/pallas_call | solution.py:99
  97.4 6.0 %collective-permute-done.9.va = f32[128,512]{1,0:T(8,128)} collective-permute-done((f32[128,512]{1,0:T(8,128)}, f32[128,512]{1,0:T(8,128)}, u32[]{:S(2)}, u32[]{:S(2)}) %collective-permute-start.9) | collective-permute-done | bytes 262176 | tf_op jit(solution)/shard_map/ppermute | solution.py:116
  103.4 1.1 copy-done.15
  105.5 1.6 %shard_map.72 = (f32[384,512]{1,0:T(8,128)S(1)}, f32[128,512]{1,0:T(8,128)S(1)}) custom-call(f32[384,512]{1,0:T(8,128)S(1)} %copy-done.15, f32[128,512]{1,0:T(8,128)} %collective-permute-done.9.va, bf16[384,128]{1,0:T(8,128)(2,1)S(1)} %get-tuple-element.127.xa, s32[384,128]{1,0:T(8,128)S(1)} %copy-done.34), custom_call_target="tpu_custom_call" | custom-call | flops 150994944 | bytes 1343488 | tf_op jit(solution)/shard_map/pallas_call | solution.py:99
  107.1 1.9 %collective-permute-done.10.vb = f32[128,512]{1,0:T(8,128)S(1)} collective-permute-done((f32[128,512]{1,0:T(8,128)}, f32[128,512]{1,0:T(8,128)S(1)}, u32[]{:S(2)}, u32[]{:S(2)}) %collective-permute-start.10) | collective-permute-done | bytes 262176 | tf_op jit(solution)/shard_map/ppermute | solution.py:116
  110.8 1.7 %shard_map.73 = (f32[384,512]{1,0:T(8,128)S(1)}, f32[128,512]{1,0:T(8,128)}, bf16[384,128]{1,0:T(8,128)(2,1)S(1)}, bf16[384,128]{1,0:T(8,128)(2,1)S(1)}) custom-call(f32[384,512]{1,0:T(8,128)S(1)} %copy-done.15, f32[384,512]{1,0:T(8,128)S(1)} %get-tuple-element.129.grad_u, f32[128,512]{1,0:T(8,128)S(1)} %get-tuple-element.130.va1, ...), custom_call_target="tpu_custom_call" | custom-call | flops 201326592 | bytes 2686976 | tf_op jit(solution)/shard_map/pallas_call | solution.py:99
  112.6 1.9 %shard_map.74 = (f32[128,512]{1,0:T(8,128)}, f32[384,512]{1,0:T(8,128)S(1)}, bf16[384,128]{1,0:T(8,128)(2,1)S(1)}, s32[384,128]{1,0:T(8,128)S(1)}, bf16[384,128]{1,0:T(8,128)(2,1)S(1)}, /*index=5*/s32[384,128]{1,0:T(8,128)S(1)}) custom-call(s32[1]{0:T(128)} %bitcast.1.first, f32[384,512]{1,0:T(8,128)S(1)} %copy-done.15, ...), custom_call_target="tpu_custom_call" | custom-call | flops 251658240 | bytes 4194304 | tf_op jit(solution)/shard_map/pallas_call | solution.py:99
  117.3 6.9 %collective-permute-done.11.va = f32[128,512]{1,0:T(8,128)} collective-permute-done((f32[128,512]{1,0:T(8,128)}, f32[128,512]{1,0:T(8,128)}, u32[]{:S(2)}, u32[]{:S(2)}) %collective-permute-start.11) | collective-permute-done | bytes 262176 | tf_op jit(solution)/shard_map/ppermute | solution.py:116
  124.3 1.1 copy-done.17
  126.3 1.6 %shard_map.75 = (f32[384,512]{1,0:T(8,128)S(1)}, f32[128,512]{1,0:T(8,128)S(1)}) custom-call(f32[384,512]{1,0:T(8,128)S(1)} %copy-done.17, f32[128,512]{1,0:T(8,128)} %collective-permute-done.11.va, bf16[384,128]{1,0:T(8,128)(2,1)S(1)} %get-tuple-element.139.xa, s32[384,128]{1,0:T(8,128)S(1)} %copy-done.28), custom_call_target="tpu_custom_call" | custom-call | flops 150994944 | bytes 1343488 | tf_op jit(solution)/shard_map/pallas_call | solution.py:99
  127.9 1.0 collective-permute-done.12.vb
  131.9 1.9 %copy-done.2 = s32[384,2048]{1,0:T(8,128)S(1)} copy-done((s32[384,2048]{1,0:T(8,128)S(1)}, s32[384,2048]{1,0:T(8,128)}, u32[]{:S(2)}) %copy-start.2) | copy-done | bytes 3145752
  133.7 2.0 %shard_map.77 = (f32[128,512]{1,0:T(8,128)S(1)}, f32[384,512]{1,0:T(8,128)S(1)}, bf16[384,128]{1,0:T(8,128)(2,1)}, s32[384,128]{1,0:T(8,128)}, bf16[384,128]{1,0:T(8,128)(2,1)}, /*index=5*/s32[384,128]{1,0:T(8,128)}) custom-call(s32[1]{0:T(128)} %bitcast.first, f32[384,512]{1,0:T(8,128)S(1)} %copy-done.17, f32[384,512]{1,0:T(8,128)S(1)} %get-tuple-element.146.u1, ...), custom_call_target="tpu_custom_call" | custom-call | flops 251658240 | bytes 4194304 | tf_op jit(solution)/shard_map/pallas_call | solution.py:99
  135.8 1.5 collective-permute-done.13
  137.4 1.5 collective-permute-start.14
  138.9 4.1 %collective-permute-done.14 = f32[64,512]{1,0:T(8,128)S(1)} collective-permute-done((f32[64,512]{1,0:T(8,128)S(1)}, f32[64,512]{1,0:T(8,128)S(1)}, u32[]{:S(2)}, u32[]{:S(2)}) %collective-permute-start.14) | collective-permute-done | bytes 131104 | tf_op jit(solution)/shard_map/ppermute | solution.py:116
  143.1 1.4 collective-permute-start.16
  144.5 9.9 %collective-permute-done.15 = f32[64,512]{1,0:T(8,128)S(1)} collective-permute-done((f32[64,512]{1,0:T(8,128)S(1)}, f32[64,512]{1,0:T(8,128)S(1)}, u32[]{:S(2)}, u32[]{:S(2)}) %collective-permute-start.15) | collective-permute-done | bytes 131104 | tf_op jit(solution)/shard_map/ppermute | solution.py:116
  154.4 1.8 %collective-permute-done.16 = f32[64,512]{1,0:T(8,128)S(1)} collective-permute-done((f32[64,512]{1,0:T(8,128)S(1)}, f32[64,512]{1,0:T(8,128)S(1)}, u32[]{:S(2)}, u32[]{:S(2)}) %collective-permute-start.16) | collective-permute-done | bytes 131104 | tf_op jit(solution)/shard_map/ppermute | solution.py:116
  (151 shorter events, 42.9 us)
Async XLA Ops:
  0.7 1.9 %copy-start = (s32[384,2048]{1,0:T(8,128)S(1)}, s32[384,2048]{1,0:T(8,128)}, u32[]{:S(2)}) copy-start(s32[384,2048]{1,0:T(8,128)} %m_hbm.13) | copy-start | bytes 9437188
  2.5 1.4 copy-start.3
  4.0 1.1 copy-start.24
  5.1 1.0 copy-start.49
  6.4 4.8 %copy-start.47 = (s32[384,128]{1,0:T(8,128)}, s32[384,128]{1,0:T(8,128)S(1)}, u32[]{:S(2)}) copy-start(s32[384,128]{1,0:T(8,128)S(1)} %get-tuple-element.85.mb) | copy-start | bytes 589828
  6.4 4.8 %copy-start.60 = (bf16[384,128]{1,0:T(8,128)(2,1)}, bf16[384,128]{1,0:T(8,128)(2,1)S(1)}, u32[]{:S(2)}) copy-start(bf16[384,128]{1,0:T(8,128)(2,1)S(1)} %get-tuple-element.84.xb) | copy-start | bytes 294916
  6.4 7.7 %copy-start.1 = (s32[384,2048]{1,0:T(8,128)S(1)}, s32[384,2048]{1,0:T(8,128)}, u32[]{:S(2)}) copy-start(s32[384,2048]{1,0:T(8,128)} %m_hbm.13) | copy-start | bytes 9437188
  7.1 1.9 %copy-start.22 = (f32[128,512]{1,0:T(8,128)}, f32[128,512]{1,0:T(8,128)S(1)}, u32[]{:S(2)}) copy-start(f32[128,512]{1,0:T(8,128)S(1)} %get-tuple-element.82.va1) | copy-start | bytes 786436
  11.2 17.5 %collective-permute-start = (f32[128,512]{1,0:T(8,128)}, f32[128,512]{1,0:T(8,128)}, u32[]{:S(2)}, u32[]{:S(2)}) collective-permute-start(f32[128,512]{1,0:T(8,128)} %get-tuple-element.90), channel_id=1, source_target_pairs={{0,4},{1,5},{2,6},{3,7},{4,8},{5,9},{6,10},{7,11},{8,12},{9,13},{1... | collective-permute-start | bytes 786440 | tf_op jit(solution)/shard_map/ppermute | solution.py:116
  14.2 1.4 copy-start.4
  15.6 1.1 copy-start.21
  16.7 0.9 copy-start.23
  17.7 1.1 copy-start.36
  27.1 10.7 %collective-permute-start.1 = (f32[128,512]{1,0:T(8,128)}, f32[128,512]{1,0:T(8,128)S(1)}, u32[]{:S(2)}, u32[]{:S(2)}) collective-permute-start(f32[128,512]{1,0:T(8,128)} %get-tuple-element.95), channel_id=1, source_target_pairs={{0,4},{1,5},{2,6},{3,7},{4,8},{5,9},{6,10},{7,11},{8,12},{9,13},{1... | collective-permute-start | bytes 786440 | tf_op jit(solution)/shard_map/ppermute | solution.py:116
  28.7 12.7 %copy-start.5 = (bf16[384,2048]{1,0:T(8,128)(2,1)S(1)}, bf16[384,2048]{1,0:T(8,128)(2,1)}, u32[]{:S(2)}) copy-start(bf16[384,2048]{1,0:T(8,128)(2,1)} %x_hbm.13) | copy-start | bytes 4718596
  28.7 1.3 copy-start.13
  37.8 0.9 copy-start.40
  41.4 10.7 %collective-permute-start.2 = (f32[128,512]{1,0:T(8,128)}, f32[128,512]{1,0:T(8,128)}, u32[]{:S(2)}, u32[]{:S(2)}) collective-permute-start(f32[128,512]{1,0:T(8,128)} %get-tuple-element.102), channel_id=1, source_target_pairs={{0,4},{1,5},{2,6},{3,7},{4,8},{5,9},{6,10},{7,11},{8,12},{9,13},{1... | collective-permute-start | bytes 786440 | tf_op jit(solution)/shard_map/ppermute | solution.py:116
  46.1 10.6 %collective-permute-start.3 = (f32[128,512]{1,0:T(8,128)}, f32[128,512]{1,0:T(8,128)S(1)}, u32[]{:S(2)}, u32[]{:S(2)}) collective-permute-start(f32[128,512]{1,0:T(8,128)} %get-tuple-element.107), channel_id=1, source_target_pairs={{0,4},{1,5},{2,6},{3,7},{4,8},{5,9},{6,10},{7,11},{8,12},{9,13},{1... | collective-permute-start | bytes 786440 | tf_op jit(solution)/shard_map/ppermute | solution.py:116
  47.4 12.3 %copy-start.6 = (bf16[384,2048]{1,0:T(8,128)(2,1)S(1)}, bf16[384,2048]{1,0:T(8,128)(2,1)}, u32[]{:S(2)}) copy-start(bf16[384,2048]{1,0:T(8,128)(2,1)} %x_hbm.13) | copy-start | bytes 4718596
  52.0 1.1 copy-start.19
  56.8 0.9 copy-start.46
  59.6 1.9 %copy-start.62 = (f32[128,512]{1,0:T(8,128)}, f32[128,512]{1,0:T(8,128)S(1)}, u32[]{:S(2)}) copy-start(f32[128,512]{1,0:T(8,128)S(1)} %get-tuple-element.114) | copy-start | bytes 786436
  64.4 1.9 %collective-permute-start.4 = (f32[128,512]{1,0:T(8,128)}, f32[128,512]{1,0:T(8,128)}, u32[]{:S(2)}, u32[]{:S(2)}) collective-permute-start(f32[128,512]{1,0:T(8,128)} %get-tuple-element.115), channel_id=1, source_target_pairs={{0,1},{1,0},{2,3},{3,2},{4,5},{5,4},{6,7},{7,6},{8,9},{9,8},{10,11... | collective-permute-start | bytes 786440 | tf_op jit(solution)/shard_map/ppermute | solution.py:116
  67.4 5.6 %collective-permute-start.5 = (f32[64,512]{1,0:T(8,128)S(1)}, f32[64,512]{1,0:T(8,128)S(1)}, u32[]{:S(2)}, u32[]{:S(2)}) collective-permute-start(f32[64,512]{1,0:T(8,128)S(1)} %slice_select_fusion.1), channel_id=1, source_target_pairs={{0,2},{1,3},{2,0},{3,1},{4,6},{5,7},{6,4},{7,5},{8,10},{9,11},{10,... | collective-permute-start | bytes 393224 | tf_op jit(solution)/shard_map/ppermute | solution.py:116
  73.0 9.8 %collective-permute-start.6 = (f32[64,512]{1,0:T(8,128)S(1)}, f32[64,512]{1,0:T(8,128)S(1)}, u32[]{:S(2)}, u32[]{:S(2)}) collective-permute-start(f32[64,512]{1,0:T(8,128)S(1)} %add_multiply_fusion.1), channel_id=1, source_target_pairs={{0,6},{1,7},{2,4},{3,5},{4,10},{5,11},{6,8},{7,9},{8,14},{9,15},{1... | collective-permute-start | bytes 393224 | tf_op jit(solution)/shard_map/ppermute | solution.py:116
  73.1 11.1 %collective-permute-start.7 = (f32[64,512]{1,0:T(8,128)S(1)}, f32[64,512]{1,0:T(8,128)S(1)}, u32[]{:S(2)}, u32[]{:S(2)}) collective-permute-start(f32[64,512]{1,0:T(8,128)S(1)} %add_multiply_fusion.1), channel_id=1, source_target_pairs={{0,4},{1,5},{2,6},{3,7},{4,8},{5,9},{6,10},{7,11},{8,12},{9,13},{1... | collective-permute-start | bytes 393224 | tf_op jit(solution)/shard_map/ppermute | solution.py:116
  84.2 3.0 %collective-permute-start.8 = (f32[128,512]{1,0:T(8,128)S(1)}, f32[128,512]{1,0:T(8,128)}, u32[]{:S(2)}, u32[]{:S(2)}) collective-permute-start(f32[128,512]{1,0:T(8,128)S(1)} %maximum_select_fusion.1.va), channel_id=1, source_target_pairs={{0,1},{1,0},{2,3},{3,2},{4,5},{5,4},{6,7},{7,6},{8,9},{9,8},{10,11... | collective-permute-start | bytes 786440 | tf_op jit(solution)/shard_map/ppermute | solution.py:116
  84.3 7.4 %copy-start.7 = (bf16[384,2048]{1,0:T(8,128)(2,1)S(1)}, bf16[384,2048]{1,0:T(8,128)(2,1)}, u32[]{:S(2)}) copy-start(bf16[384,2048]{1,0:T(8,128)(2,1)} %x_hbm.13) | copy-start | bytes 4718596
  84.4 1.3 copy-start.11
  85.6 0.9 copy-start.26
  87.2 0.9 copy-start.38
  91.7 11.7 %collective-permute-start.9 = (f32[128,512]{1,0:T(8,128)}, f32[128,512]{1,0:T(8,128)}, u32[]{:S(2)}, u32[]{:S(2)}) collective-permute-start(f32[128,512]{1,0:T(8,128)} %get-tuple-element.126), channel_id=1, source_target_pairs={{0,4},{1,5},{2,6},{3,7},{4,8},{5,9},{6,10},{7,11},{8,12},{9,13},{1... | collective-permute-start | bytes 786440 | tf_op jit(solution)/shard_map/ppermute | solution.py:116
  97.4 11.6 %collective-permute-start.10 = (f32[128,512]{1,0:T(8,128)}, f32[128,512]{1,0:T(8,128)S(1)}, u32[]{:S(2)}, u32[]{:S(2)}) collective-permute-start(f32[128,512]{1,0:T(8,128)} %get-tuple-element.131), channel_id=1, source_target_pairs={{0,4},{1,5},{2,6},{3,7},{4,8},{5,9},{6,10},{7,11},{8,12},{9,13},{1... | collective-permute-start | bytes 786440 | tf_op jit(solution)/shard_map/ppermute | solution.py:116
  97.4 15.1 %copy-start.8 = (bf16[384,2048]{1,0:T(8,128)(2,1)S(1)}, bf16[384,2048]{1,0:T(8,128)(2,1)}, u32[]{:S(2)}) copy-start(bf16[384,2048]{1,0:T(8,128)(2,1)} %x_hbm.13) | copy-start | bytes 4718596
  103.4 1.1 copy-start.15
  109.0 0.9 copy-start.42
  112.6 11.7 %collective-permute-start.11 = (f32[128,512]{1,0:T(8,128)}, f32[128,512]{1,0:T(8,128)}, u32[]{:S(2)}, u32[]{:S(2)}) collective-permute-start(f32[128,512]{1,0:T(8,128)} %get-tuple-element.138), channel_id=1, source_target_pairs={{0,4},{1,5},{2,6},{3,7},{4,8},{5,9},{6,10},{7,11},{8,12},{9,13},{1... | collective-permute-start | bytes 786440 | tf_op jit(solution)/shard_map/ppermute | solution.py:116
  117.3 14.5 %copy-start.9 = (bf16[384,2048]{1,0:T(8,128)(2,1)S(1)}, bf16[384,2048]{1,0:T(8,128)(2,1)}, u32[]{:S(2)}) copy-start(bf16[384,2048]{1,0:T(8,128)(2,1)} %x_hbm.13) | copy-start | bytes 4718596
  117.3 11.7 %collective-permute-start.12 = (f32[128,512]{1,0:T(8,128)}, f32[128,512]{1,0:T(8,128)S(1)}, u32[]{:S(2)}, u32[]{:S(2)}) collective-permute-start(f32[128,512]{1,0:T(8,128)} %get-tuple-element.143), channel_id=1, source_target_pairs={{0,4},{1,5},{2,6},{3,7},{4,8},{5,9},{6,10},{7,11},{8,12},{9,13},{1... | collective-permute-start | bytes 786440 | tf_op jit(solution)/shard_map/ppermute | solution.py:116
  124.3 1.1 copy-start.17
  129.0 0.9 copy-start.44
  131.8 1.9 %copy-start.2 = (s32[384,2048]{1,0:T(8,128)S(1)}, s32[384,2048]{1,0:T(8,128)}, u32[]{:S(2)}) copy-start(s32[384,2048]{1,0:T(8,128)} %m_hbm.13) | copy-start | bytes 9437188
  135.7 1.6 %collective-permute-start.13 = (f32[128,512]{1,0:T(8,128)S(1)}, f32[128,512]{1,0:T(8,128)S(1)}, u32[]{:S(2)}, u32[]{:S(2)}) collective-permute-start(f32[128,512]{1,0:T(8,128)S(1)} %get-tuple-element.151), channel_id=1, source_target_pairs={{0,1},{1,0},{2,3},{3,2},{4,5},{5,4},{6,7},{7,6},{8,9},{9,8},{10,11... | collective-permute-start | bytes 786440 | tf_op jit(solution)/shard_map/ppermute | solution.py:116
  137.4 5.6 %collective-permute-start.14 = (f32[64,512]{1,0:T(8,128)S(1)}, f32[64,512]{1,0:T(8,128)S(1)}, u32[]{:S(2)}, u32[]{:S(2)}) collective-permute-start(f32[64,512]{1,0:T(8,128)S(1)} %slice_select_fusion), channel_id=1, source_target_pairs={{0,2},{1,3},{2,0},{3,1},{4,6},{5,7},{6,4},{7,5},{8,10},{9,11},{10,... | collective-permute-start | bytes 393224 | tf_op jit(solution)/shard_map/ppermute | solution.py:116
  143.0 11.4 %collective-permute-start.15 = (f32[64,512]{1,0:T(8,128)S(1)}, f32[64,512]{1,0:T(8,128)S(1)}, u32[]{:S(2)}, u32[]{:S(2)}) collective-permute-start(f32[64,512]{1,0:T(8,128)S(1)} %add_multiply_fusion), channel_id=1, source_target_pairs={{0,14},{1,15},{2,12},{3,13},{4,18},{5,19},{6,16},{7,17},{8,22},{9,... | collective-permute-start | bytes 393224 | tf_op jit(solution)/shard_map/ppermute | solution.py:116
  143.1 13.1 %collective-permute-start.16 = (f32[64,512]{1,0:T(8,128)S(1)}, f32[64,512]{1,0:T(8,128)S(1)}, u32[]{:S(2)}, u32[]{:S(2)}) collective-permute-start(f32[64,512]{1,0:T(8,128)S(1)} %add_multiply_fusion), channel_id=1, source_target_pairs={{0,12},{1,13},{2,14},{3,15},{4,16},{5,17},{6,18},{7,19},{8,20},{9,... | collective-permute-start | bytes 393224 | tf_op jit(solution)/shard_map/ppermute | solution.py:116
  156.3 1.6 %collective-permute-start.17 = (f32[128,512]{1,0:T(8,128)S(1)}, f32[128,512]{1,0:T(8,128)S(1)}, u32[]{:S(2)}, u32[]{:S(2)}) collective-permute-start(f32[128,512]{1,0:T(8,128)S(1)} %maximum_select_fusion.2), channel_id=1, source_target_pairs={{0,1},{1,0},{2,3},{3,2},{4,5},{5,4},{6,7},{7,6},{8,9},{9,8},{10,11... | collective-permute-start | bytes 786440 | tf_op jit(solution)/shard_map/ppermute | solution.py:116
  (37 other events, 29.2 us)

commit v3 on v2

--- a/solution.py
+++ b/solution.py
@@ -24,26 +24,30 @@
     return jnp.dot(a, b, preferred_element_type=F32)
 
 
-def residue(x_ref, m_ref, cell_half, locus_half):
-    difference = x_ref[...].astype(F32) - across(cell_half, locus_half)
-    return (m_ref[...].astype(F32) * difference).astype(HALF)
-
-
-def tile_copies(first, x_hbm, m_hbm, xa, ma, xb, mb, sems):
-    width = xa.shape[1]
+def residue(tile, mask, place, cell_half, locus_half):
+    width = locus_half.shape[0]
+    columns = slice(place * width, (place + 1) * width)
+    difference = tile[:, columns].astype(F32) - across(cell_half, locus_half)
+    return (mask[:, columns].astype(F32) * difference).astype(HALF)
+
+
+def tile_copies(first, x_hbm, m_hbm, tile, mask, sems):
+    width = tile.shape[1] // 2
     copies = []
-    for place, (x_out, m_out) in enumerate(((xa, ma), (xb, mb))):
-        column = first if place == 0 else first + 1 - 2 * (first % 2)
-        columns = pl.ds(pl.multiple_of(column * width, width), width)
-        copies.append(pltpu.make_async_copy(x_hbm.at[:, columns], x_out, sems.at[2 * place]))
-        copies.append(pltpu.make_async_copy(m_hbm.at[:, columns], m_out, sems.at[2 * place + 1]))
+    for place, column in enumerate((first, first + 1 - 2 * (first % 2))):
+        source = pl.ds(pl.multiple_of(column * width, width), width)
+        target = pl.ds(place * width, width)
+        for i, (whole, part) in enumerate(((x_hbm, tile), (m_hbm, mask))):
+            copies.append(
+                pltpu.make_async_copy(whole.at[:, source], part.at[:, target], sems.at[2 * place + i])
+            )
     return copies
 
 
-def load_body(first, x_hbm, m_hbm, u_hbm, v_hbm, xa, ma, xb, mb, u, va, vb, sems):
+def load_body(first, x_hbm, m_hbm, u_hbm, v_hbm, tile, mask, u, va, vb, sems):
     rows = va.shape[0]
     half = first[0] % 2
-    copies = tile_copies(first[0], x_hbm, m_hbm, xa, ma, xb, mb, sems)
+    copies = tile_copies(first[0], x_hbm, m_hbm, tile, mask, sems)
     copies.append(pltpu.make_async_copy(u_hbm, u, sems.at[4]))
     for place, (out, index) in enumerate(((va, half), (vb, 1 - half))):
         at = pl.ds(pl.multiple_of(index * rows, rows), rows)
@@ -54,55 +58,57 @@
         copy.wait()
 
 
-def open_body(steps, u, va, xa, ma, grad_u, va1):
+def open_body(steps, u, va, tile, mask, grad_u, va1):
     cell_half, locus_half = u[...].astype(HALF), va[...].astype(HALF)
-    r = residue(xa, ma, cell_half, locus_half)
+    r = residue(tile, mask, 0, cell_half, locus_half)
     grad_u[...] = times(r, locus_half)
     va1[...] = va[...] + steps[1] * along(r, cell_half)
 
 
-def turn_body(steps, u, grad_u, va1, vb, xa, ma, xb, mb, u1, va2, r1b, r2a):
+def turn_body(steps, u, grad_u, va1, vb, tile, mask, u1, va2, rest):
+    width = vb.shape[0]
     cell_half, locus_half = u[...].astype(HALF), vb[...].astype(HALF)
-    r = residue(xb, mb, cell_half, locus_half)
-    r1b[...] = r
+    r = residue(tile, mask, 1, cell_half, locus_half)
+    rest[:, width:] = r
     moved_u = u[...] + steps[0] * (grad_u[...] + times(r, locus_half))
     u1[...] = moved_u
     cell_half, locus_half = moved_u.astype(HALF), va1[...].astype(HALF)
-    r = residue(xa, ma, cell_half, locus_half)
-    r2a[...] = r
+    r = residue(tile, mask, 0, cell_half, locus_half)
+    rest[:, :width] = r
     va2[...] = va1[...] + steps[1] * along(r, cell_half)
 
 
 def close_body(
-    steps, first, u, u1, r1b, r2a, va1, vb, xb, mb, x_hbm, m_hbm,
-    vb2, u2, xa_next, ma_next, xb_next, mb_next, sems,
+    steps, first, u, u1, rest, va1, vb, tile, mask, x_hbm, m_hbm, vb2, u2, tile_next, mask_next, sems
 ):
-    copies = tile_copies(first[0], x_hbm, m_hbm, xa_next, ma_next, xb_next, mb_next, sems)
+    width = vb.shape[0]
+    copies = tile_copies(first[0], x_hbm, m_hbm, tile_next, mask_next, sems)
     for copy in copies:
         copy.start()
-    vb1 = vb[...] + steps[1] * along(r1b[...], u[...].astype(HALF))
+    vb1 = vb[...] + steps[1] * along(rest[:, width:], u[...].astype(HALF))
     cell_half, locus_half = u1[...].astype(HALF), vb1.astype(HALF)
-    r = residue(xb, mb, cell_half, locus_half)
+    r = residue(tile, mask, 1, cell_half, locus_half)
     vb2[...] = vb1 + steps[1] * along(r, cell_half)
-    u2[...] = u1[...] + steps[0] * (times(r2a[...], va1[...].astype(HALF)) + times(r, locus_half))
+    grad_u = times(rest[:, :width], va1[...].astype(HALF)) + times(r, locus_half)
+    u2[...] = u1[...] + steps[0] * grad_u
     for copy in copies:
         copy.wait()
 
 
 def call(body, args, spaces, outs, sems=0, flops=0):
-    kinds = {"v": pltpu.VMEM, "h": pl.ANY, "s": pltpu.SMEM}
+    kinds = {"v": pltpu.VMEM, "h": pltpu.HBM, "s": pltpu.SMEM}
     pinned = [
-        pltpu.with_memory_space_constraint(a, pltpu.VMEM) if s == "v" else a
+        a if s == "s" else pltpu.with_memory_space_constraint(a, kinds[s])
         for a, s in zip(args, spaces)
     ]
     moved_bytes = sum(a.size * a.dtype.itemsize for a in args) if sems == 0 else 4 << 20
     return pl.pallas_call(
         body,
-        out_shape=[pltpu.VMEM(shape, dtype) for shape, dtype in outs],
+        out_shape=[jax.ShapeDtypeStruct(shape, dtype) for shape, dtype in outs],
         in_specs=[pl.BlockSpec(memory_space=kinds[s]) for s in spaces],
         out_specs=[pl.BlockSpec(memory_space=pltpu.VMEM) for _ in outs],
         scratch_shapes=[pltpu.SemaphoreType.DMA((sems,))] if sems else [],
-        compiler_params=pltpu.CompilerParams(vmem_limit_bytes=24 << 20),
+        compiler_params=pltpu.CompilerParams(vmem_limit_bytes=8 << 20),
         cost_estimate=pl.CostEstimate(flops=flops, bytes_accessed=moved_bytes, transcendentals=0),
     )(*pinned)
 
@@ -150,14 +156,13 @@
         rows = locus_factors.shape[0] // 2
         steps = (2.0 / (2 * rows + rank), 2.0 / (cells + rank))
         wide, tall = ((cells, rank), F32), ((rows, rank), F32)
-        tiles = [((cells, rows), HALF), ((cells, rows), jnp.int32)] * 2
-        small = ((cells, rows), HALF)
+        tiles = [((cells, 2 * rows), HALF), ((cells, 2 * rows), jnp.int32)]
         work = 2 * cells * rows * rank
 
         def first(hop):
             return ((position - hop) % blocks * 2 + side).reshape(1).astype(jnp.int32)
 
-        xa, ma, xb, mb, u, va, vb = call(
+        tile, mask, u, va, vb = call(
             load_body,
             (first(0), expression, observed, cell_factors, locus_factors),
             "shhhh",
@@ -166,20 +171,20 @@
         )
         for hop in range(HOPS):
             grad_u, va1 = call(
-                functools.partial(open_body, steps), (u, va, xa, ma), "vvvv", [wide, tall], 0, 3 * work
-            )
-            u1, va2, r1b, r2a = call(
+                functools.partial(open_body, steps), (u, va, tile, mask), "vvvv", [wide, tall], 0, 3 * work
+            )
+            u1, va2, rest = call(
                 functools.partial(turn_body, steps),
-                (u, grad_u, va1, vb, xa, ma, xb, mb),
-                "vvvvvvvv",
-                [wide, tall, small, small],
+                (u, grad_u, va1, vb, tile, mask),
+                "vvvvvv",
+                [wide, tall, ((cells, 2 * rows), HALF)],
                 0,
                 4 * work,
             )
-            vb2, u, xa, ma, xb, mb = call(
+            vb2, u, tile, mask = call(
                 functools.partial(close_body, steps),
-                (first(hop + 1), u, u1, r1b, r2a, va1, vb, xb, mb, expression, observed),
-                "svvvvvvvvhh",
+                (first(hop + 1), u, u1, rest, va1, vb, tile, mask, expression, observed),
+                "svvvvvvvhh",
                 [tall, wide] + tiles,
                 4,
                 5 * work,

time: 160 us -> 127 us (0.79)
  local copies, waits for them, and re-layouts: 52.7 us -> 3.61 us
  waiting for transfers between devices: 61.7 us -> 83.4 us
  Pallas kernels: 30.2 us -> 28 us
    unnamed x135 -> x8, local copies, waits for them, and re-layouts: 52.7 us -> 3.61 us
    ppermute x18, waiting for transfers between devices: 61.7 us -> 83.4 us  [moved(): return lax.ppermute(block, AXES, route)]
    pallas_call x19, Pallas kernels: 30.2 us -> 28 us  [call(): pl.pallas_call(body, out_shape=[jax.ShapeDtypeStruct(shape, dtype) for sh...]
  transfers between devices with their start and end apart: 18 -> 18, of which waited for: 16 -> 18; matrix products, arithmetic and copies ran while one was open for 1% -> 0% of each run, Pallas kernels for 10% -> 9%
where the time goes in v3:
time: 127 us
  waiting for transfers between devices  83.4 us (66%)
  Pallas kernels  28 us (22%)
  starting transfers between devices  10 us (8%)
  local copies, waits for them, and re-layouts  3.61 us (3%)
    ppermute x18, waiting for transfers between devices, moved(): return lax.ppermute(block, AXES, route)  83.4 us
    pallas_call x19, Pallas kernels, call(): pl.pallas_call(body, out_shape=[jax.ShapeDtypeStruct(shape, dtype) for sh...  28 us
    ppermute x18, starting transfers between devices, moved(): return lax.ppermute(block, AXES, route)  10 us
    unnamed x8, local copies, waits for them, and re-layouts  3.61 us
  transfers between devices with their start and end apart: 18, of which 18 were waited for; matrix products, arithmetic and copies ran while one was open for 0% of the time, Pallas kernels for 9%

profile of v3, /device:TPU:0, one launch (start us, length us, event | category | flops | bytes accessed | tf_op | source)
XLA Modules:
  0.0 127.1 jit_solution(10407273124197086300)
XLA Ops:
  0.7 1.6 %shard_map.59 = (bf16[384,256]{1,0:T(8,128)(2,1)S(1)}, s32[384,256]{1,0:T(8,128)S(1)}, f32[384,512]{1,0:T(8,128)S(1)}, f32[128,512]{1,0:T(8,128)S(1)}, f32[128,512]{1,0:T(8,128)S(1)}) custom-call(s32[1]{0:T(128)} %bitcast.6.first, bf16[384,2048]{1,0:T(8,128)(2,1)} %x_hbm.13, s32[384,2048]{1,0:T(8,128)} %m_hbm.13, f32[384,512]{1,0:T(8,128)} %u_hbm.1, ...), custom_call_target="tpu_custom_call" | custom-call | bytes 4194304 | tf_op jit(solution)/shard_map/pallas_call | solution.py:105
  2.3 0.7 shard_map.60
  3.0 1.7 %shard_map.61 = (f32[384,512]{1,0:T(8,128)S(1)}, f32[128,512]{1,0:T(8,128)}, bf16[384,256]{1,0:T(8,128)(2,1)S(1)}) custom-call(f32[384,512]{1,0:T(8,128)S(1)} %get-tuple-element.59.u, f32[384,512]{1,0:T(8,128)S(1)} %get-tuple-element.63.grad_u, f32[128,512]{1,0:T(8,128)S(1)} %get-tuple-element.64.va1, f32[128,512]{1,0:T(8,128)S(1)} %get-tuple-element.65.vb, ...), custom_call_target="tpu_custom_call" | custom-call | flops 201326592 | bytes 2686976 | tf_op jit(solution)/shard_map/pallas_call | solution.py:105
  4.7 0.9 copy-done
  5.6 0.7 copy-done.2
  6.3 3.0 %collective-permute-start = (f32[128,512]{1,0:T(8,128)}, f32[128,512]{1,0:T(8,128)S(1)}, u32[]{:S(2)}, u32[]{:S(2)}) collective-permute-start(f32[128,512]{1,0:T(8,128)} %get-tuple-element.69), channel_id=1, source_target_pairs={{0,4},{1,5},{2,6},{3,7},{4,8},{5,9},{6,10},{7,11},{8,12},{9,13},{1... | collective-permute-start | bytes 786440 | tf_op jit(solution)/shard_map/ppermute | solution.py:122
  9.2 1.1 copy-done.1
  10.4 0.9 copy-done.3
  11.3 2.7 %shard_map.62 = (f32[128,512]{1,0:T(8,128)}, f32[384,512]{1,0:T(8,128)S(1)}, bf16[384,256]{1,0:T(8,128)(2,1)S(1)}, s32[384,256]{1,0:T(8,128)S(1)}) custom-call(s32[1]{0:T(128)} %bitcast.5.first, f32[384,512]{1,0:T(8,128)S(1)} %get-tuple-element.59.u, f32[384,512]{1,0:T(8,128)S(1)} %copy-done.1, bf16[384,256]{1,0:T(8,128)(2,1)S(1)} %copy-done.3, ...), custom_call_target="tpu_custom_call" | custom-call | flops 251658240 | bytes 4194304 | tf_op jit(solution)/shard_map/pallas_call | solution.py:105
  14.0 1.6 %collective-permute-start.1 = (f32[128,512]{1,0:T(8,128)}, f32[128,512]{1,0:T(8,128)S(1)}, u32[]{:S(2)}, u32[]{:S(2)}) collective-permute-start(f32[128,512]{1,0:T(8,128)} %get-tuple-element.74), channel_id=1, source_target_pairs={{0,4},{1,5},{2,6},{3,7},{4,8},{5,9},{6,10},{7,11},{8,12},{9,13},{1... | collective-permute-start | bytes 786440 | tf_op jit(solution)/shard_map/ppermute | solution.py:122
  15.5 3.2 %collective-permute-done.va = f32[128,512]{1,0:T(8,128)S(1)} collective-permute-done((f32[128,512]{1,0:T(8,128)}, f32[128,512]{1,0:T(8,128)S(1)}, u32[]{:S(2)}, u32[]{:S(2)}) %collective-permute-start) | collective-permute-done | bytes 262176 | tf_op jit(solution)/shard_map/ppermute | solution.py:122
  18.8 0.7 shard_map.63
  19.4 5.3 %collective-permute-done.1.vb = f32[128,512]{1,0:T(8,128)S(1)} collective-permute-done((f32[128,512]{1,0:T(8,128)}, f32[128,512]{1,0:T(8,128)S(1)}, u32[]{:S(2)}, u32[]{:S(2)}) %collective-permute-start.1) | collective-permute-done | bytes 262176 | tf_op jit(solution)/shard_map/ppermute | solution.py:122
  24.7 1.7 %shard_map.64 = (f32[384,512]{1,0:T(8,128)S(1)}, f32[128,512]{1,0:T(8,128)}, bf16[384,256]{1,0:T(8,128)(2,1)S(1)}) custom-call(f32[384,512]{1,0:T(8,128)S(1)} %get-tuple-element.68.u, f32[384,512]{1,0:T(8,128)S(1)} %get-tuple-element.72.grad_u, f32[128,512]{1,0:T(8,128)S(1)} %get-tuple-element.73.va1, f32[128,512]{1,0:T(8,128)S(1)} %collective-permute-done.1.vb, ...), custom_call_target="tpu_custom_call" | custom-call | flops 201326592 | bytes 2686976 | tf_op jit(solution)/shard_map/pallas_call | solution.py:105
  26.4 1.9 %shard_map.65 = (f32[128,512]{1,0:T(8,128)S(1)}, f32[384,512]{1,0:T(8,128)S(1)}, bf16[384,256]{1,0:T(8,128)(2,1)S(1)}, s32[384,256]{1,0:T(8,128)S(1)}) custom-call(s32[1]{0:T(128)} %bitcast.4.first, f32[384,512]{1,0:T(8,128)S(1)} %get-tuple-element.68.u, f32[384,512]{1,0:T(8,128)S(1)} %get-tuple-element.75.u1, bf16[384,256]{1,0:T(8,128)(2,1)S(1)} %get-tuple-element.76.rest, ...), custom_call_target="tpu_custom_call" | custom-call | flops 251658240 | bytes 4194304 | tf_op jit(solution)/shard_map/pallas_call | solution.py:105
  28.4 1.3 %collective-permute-start.3 = (f32[128,512]{1,0:T(8,128)S(1)}, f32[128,512]{1,0:T(8,128)S(1)}, u32[]{:S(2)}, u32[]{:S(2)}) collective-permute-start(f32[128,512]{1,0:T(8,128)S(1)} %get-tuple-element.83), channel_id=1, source_target_pairs={{0,4},{1,5},{2,6},{3,7},{4,8},{5,9},{6,10},{7,11},{8,12},{9,13},{1... | collective-permute-start | bytes 786440 | tf_op jit(solution)/shard_map/ppermute | solution.py:122
  29.7 8.9 %collective-permute-done.2.va = f32[128,512]{1,0:T(8,128)S(1)} collective-permute-done((f32[128,512]{1,0:T(8,128)}, f32[128,512]{1,0:T(8,128)S(1)}, u32[]{:S(2)}, u32[]{:S(2)}) %collective-permute-start.2) | collective-permute-done | bytes 262176 | tf_op jit(solution)/shard_map/ppermute | solution.py:122
  38.6 0.7 shard_map.66
  39.2 2.6 %collective-permute-done.3.vb = f32[128,512]{1,0:T(8,128)S(1)} collective-permute-done((f32[128,512]{1,0:T(8,128)S(1)}, f32[128,512]{1,0:T(8,128)S(1)}, u32[]{:S(2)}, u32[]{:S(2)}) %collective-permute-start.3) | collective-permute-done | bytes 262176 | tf_op jit(solution)/shard_map/ppermute | solution.py:122
  41.8 1.0 shard_map.67
  42.9 1.9 %shard_map.68 = (f32[128,512]{1,0:T(8,128)S(1)}, f32[384,512]{1,0:T(8,128)S(1)}, bf16[384,256]{1,0:T(8,128)(2,1)S(1)}, s32[384,256]{1,0:T(8,128)S(1)}) custom-call(s32[1]{0:T(128)} %bitcast.3.first, f32[384,512]{1,0:T(8,128)S(1)} %get-tuple-element.77.u, f32[384,512]{1,0:T(8,128)S(1)} %get-tuple-element.84.u1, bf16[384,256]{1,0:T(8,128)(2,1)S(1)} %get-tuple-element.85.rest, ...), custom_call_target="tpu_custom_call" | custom-call | flops 251658240 | bytes 4194304 | tf_op jit(solution)/shard_map/pallas_call | solution.py:105
  44.9 1.5 %collective-permute-done.4 = f32[128,512]{1,0:T(8,128)S(1)} collective-permute-done((f32[128,512]{1,0:T(8,128)S(1)}, f32[128,512]{1,0:T(8,128)S(1)}, u32[]{:S(2)}, u32[]{:S(2)}) %collective-permute-start.4) | collective-permute-done | bytes 262176 | tf_op jit(solution)/shard_map/ppermute | solution.py:122
  46.5 1.5 %collective-permute-start.5 = (f32[64,512]{1,0:T(8,128)S(1)}, f32[64,512]{1,0:T(8,128)S(1)}, u32[]{:S(2)}, u32[]{:S(2)}) collective-permute-start(f32[64,512]{1,0:T(8,128)S(1)} %slice_select_fusion.1), channel_id=1, source_target_pairs={{0,2},{1,3},{2,0},{3,1},{4,6},{5,7},{6,4},{7,5},{8,10},{9,11},{10,... | collective-permute-start | bytes 393224 | tf_op jit(solution)/shard_map/ppermute | solution.py:122
  48.0 4.1 %collective-permute-done.5 = f32[64,512]{1,0:T(8,128)S(1)} collective-permute-done((f32[64,512]{1,0:T(8,128)S(1)}, f32[64,512]{1,0:T(8,128)S(1)}, u32[]{:S(2)}, u32[]{:S(2)}) %collective-permute-start.5) | collective-permute-done | bytes 131104 | tf_op jit(solution)/shard_map/ppermute | solution.py:122
  52.2 0.4 collective-permute-start.7
  52.5 9.4 %collective-permute-done.6 = f32[64,512]{1,0:T(8,128)S(1)} collective-permute-done((f32[64,512]{1,0:T(8,128)S(1)}, f32[64,512]{1,0:T(8,128)S(1)}, u32[]{:S(2)}, u32[]{:S(2)}) %collective-permute-start.6) | collective-permute-done | bytes 131104 | tf_op jit(solution)/shard_map/ppermute | solution.py:122
  61.9 1.4 %collective-permute-done.7 = f32[64,512]{1,0:T(8,128)S(1)} collective-permute-done((f32[64,512]{1,0:T(8,128)S(1)}, f32[64,512]{1,0:T(8,128)S(1)}, u32[]{:S(2)}, u32[]{:S(2)}) %collective-permute-start.7) | collective-permute-done | bytes 131104 | tf_op jit(solution)/shard_map/ppermute | solution.py:122
  63.4 0.7 shard_map.69
  64.1 0.8 collective-permute-done.8.vb
  64.9 1.7 %shard_map.70 = (f32[384,512]{1,0:T(8,128)S(1)}, f32[128,512]{1,0:T(8,128)}, bf16[384,256]{1,0:T(8,128)(2,1)S(1)}) custom-call(f32[384,512]{1,0:T(8,128)S(1)} %get-tuple-element.86.u, f32[384,512]{1,0:T(8,128)S(1)} %get-tuple-element.91.grad_u, f32[128,512]{1,0:T(8,128)S(1)} %get-tuple-element.92.va1, f32[128,512]{1,0:T(8,128)S(1)} %collective-permute-done.8.vb, ...), custom_call_target="tpu_custom_call" | custom-call | flops 201326592 | bytes 2686976 | tf_op jit(solution)/shard_map/pallas_call | solution.py:105
  66.7 1.9 %shard_map.71 = (f32[128,512]{1,0:T(8,128)S(1)}, f32[384,512]{1,0:T(8,128)S(1)}, bf16[384,256]{1,0:T(8,128)(2,1)S(1)}, s32[384,256]{1,0:T(8,128)S(1)}) custom-call(s32[1]{0:T(128)} %bitcast.2.first, f32[384,512]{1,0:T(8,128)S(1)} %get-tuple-element.86.u, f32[384,512]{1,0:T(8,128)S(1)} %get-tuple-element.93.u1, bf16[384,256]{1,0:T(8,128)(2,1)S(1)} %get-tuple-element.94.rest, ...), custom_call_target="tpu_custom_call" | custom-call | flops 251658240 | bytes 4194304 | tf_op jit(solution)/shard_map/pallas_call | solution.py:105
  68.7 10.0 %collective-permute-done.9.va = f32[128,512]{1,0:T(8,128)S(1)} collective-permute-done((f32[128,512]{1,0:T(8,128)}, f32[128,512]{1,0:T(8,128)S(1)}, u32[]{:S(2)}, u32[]{:S(2)}) %collective-permute-start.9) | collective-permute-done | bytes 262176 | tf_op jit(solution)/shard_map/ppermute | solution.py:122
  78.7 0.7 shard_map.72
  79.4 4.2 %collective-permute-done.10.vb = f32[128,512]{1,0:T(8,128)S(1)} collective-permute-done((f32[128,512]{1,0:T(8,128)S(1)}, f32[128,512]{1,0:T(8,128)S(1)}, u32[]{:S(2)}, u32[]{:S(2)}) %collective-permute-start.10) | collective-permute-done | bytes 262176 | tf_op jit(solution)/shard_map/ppermute | solution.py:122
  83.5 1.7 %shard_map.73 = (f32[384,512]{1,0:T(8,128)S(1)}, f32[128,512]{1,0:T(8,128)}, bf16[384,256]{1,0:T(8,128)(2,1)S(1)}) custom-call(f32[384,512]{1,0:T(8,128)S(1)} %get-tuple-element.95.u, f32[384,512]{1,0:T(8,128)S(1)} %get-tuple-element.99.grad_u, f32[128,512]{1,0:T(8,128)S(1)} %get-tuple-element.100.va1, f32[128,512]{1,0:T(8,128)S(1)} %collective-permute-done.10.vb, ...), custom_call_target="tpu_custom_call" | custom-call | flops 201326592 | bytes 2686976 | tf_op jit(solution)/shard_map/pallas_call | solution.py:105
  85.3 1.9 %shard_map.74 = (f32[128,512]{1,0:T(8,128)S(1)}, f32[384,512]{1,0:T(8,128)S(1)}, bf16[384,256]{1,0:T(8,128)(2,1)S(1)}, s32[384,256]{1,0:T(8,128)S(1)}) custom-call(s32[1]{0:T(128)} %bitcast.1.first, f32[384,512]{1,0:T(8,128)S(1)} %get-tuple-element.95.u, f32[384,512]{1,0:T(8,128)S(1)} %get-tuple-element.102.u1, ...), custom_call_target="tpu_custom_call" | custom-call | flops 251658240 | bytes 4194304 | tf_op jit(solution)/shard_map/pallas_call | solution.py:105
  87.5 9.9 %collective-permute-done.11.va = f32[128,512]{1,0:T(8,128)S(1)} collective-permute-done((f32[128,512]{1,0:T(8,128)}, f32[128,512]{1,0:T(8,128)S(1)}, u32[]{:S(2)}, u32[]{:S(2)}) %collective-permute-start.11) | collective-permute-done | bytes 262176 | tf_op jit(solution)/shard_map/ppermute | solution.py:122
  97.4 0.7 shard_map.75
  98.1 3.2 %collective-permute-done.12.vb = f32[128,512]{1,0:T(8,128)S(1)} collective-permute-done((f32[128,512]{1,0:T(8,128)S(1)}, f32[128,512]{1,0:T(8,128)S(1)}, u32[]{:S(2)}, u32[]{:S(2)}) %collective-permute-start.12) | collective-permute-done | bytes 262176 | tf_op jit(solution)/shard_map/ppermute | solution.py:122
  101.3 1.0 shard_map.76
  102.3 3.0 %shard_map.77 = (f32[128,512]{1,0:T(8,128)S(1)}, f32[384,512]{1,0:T(8,128)}, bf16[384,256]{1,0:T(8,128)(2,1)}, s32[384,256]{1,0:T(8,128)}) custom-call(s32[1]{0:T(128)} %bitcast.first, f32[384,512]{1,0:T(8,128)S(1)} %get-tuple-element.104.u, f32[384,512]{1,0:T(8,128)S(1)} %get-tuple-element.111.u1, bf16[384,256]{1,0:T(8,128)(2,1)S(1)} %get-tuple-element.112.rest, ...), custom_call_target="tpu_custom_call" | custom-call | flops 251658240 | bytes 4194304 | tf_op jit(solution)/shard_map/pallas_call | solution.py:105
  105.5 1.5 %collective-permute-done.13 = f32[128,512]{1,0:T(8,128)S(1)} collective-permute-done((f32[128,512]{1,0:T(8,128)S(1)}, f32[128,512]{1,0:T(8,128)S(1)}, u32[]{:S(2)}, u32[]{:S(2)}) %collective-permute-start.13) | collective-permute-done | bytes 262176 | tf_op jit(solution)/shard_map/ppermute | solution.py:122
  107.1 1.5 %collective-permute-start.14 = (f32[64,512]{1,0:T(8,128)S(1)}, f32[64,512]{1,0:T(8,128)S(1)}, u32[]{:S(2)}, u32[]{:S(2)}) collective-permute-start(f32[64,512]{1,0:T(8,128)S(1)} %slice_select_fusion), channel_id=1, source_target_pairs={{0,2},{1,3},{2,0},{3,1},{4,6},{5,7},{6,4},{7,5},{8,10},{9,11},{10,... | collective-permute-start | bytes 393224 | tf_op jit(solution)/shard_map/ppermute | solution.py:122
  108.6 4.1 %collective-permute-done.14 = f32[64,512]{1,0:T(8,128)S(1)} collective-permute-done((f32[64,512]{1,0:T(8,128)S(1)}, f32[64,512]{1,0:T(8,128)S(1)}, u32[]{:S(2)}, u32[]{:S(2)}) %collective-permute-start.14) | collective-permute-done | bytes 131104 | tf_op jit(solution)/shard_map/ppermute | solution.py:122
  112.8 10.0 %collective-permute-done.15 = f32[64,512]{1,0:T(8,128)S(1)} collective-permute-done((f32[64,512]{1,0:T(8,128)S(1)}, f32[64,512]{1,0:T(8,128)S(1)}, u32[]{:S(2)}, u32[]{:S(2)}) %collective-permute-start.15) | collective-permute-done | bytes 131104 | tf_op jit(solution)/shard_map/ppermute | solution.py:122
  122.9 1.7 %collective-permute-done.16 = f32[64,512]{1,0:T(8,128)S(1)} collective-permute-done((f32[64,512]{1,0:T(8,128)S(1)}, f32[64,512]{1,0:T(8,128)S(1)}, u32[]{:S(2)}, u32[]{:S(2)}) %collective-permute-start.16) | collective-permute-done | bytes 131104 | tf_op jit(solution)/shard_map/ppermute | solution.py:122
  124.7 1.5 %collective-permute-done.17 = f32[128,512]{1,0:T(8,128)S(1)} collective-permute-done((f32[128,512]{1,0:T(8,128)S(1)}, f32[128,512]{1,0:T(8,128)S(1)}, u32[]{:S(2)}, u32[]{:S(2)}) %collective-permute-start.17) | collective-permute-done | bytes 262176 | tf_op jit(solution)/shard_map/ppermute | solution.py:122
  126.2 0.8 maximum_select_fusion
  (24 shorter events, 1.0 us)
Async XLA Ops:
  4.7 0.9 copy-start
  5.6 0.7 copy-start.2
  6.3 12.5 %collective-permute-start = (f32[128,512]{1,0:T(8,128)}, f32[128,512]{1,0:T(8,128)S(1)}, u32[]{:S(2)}, u32[]{:S(2)}) collective-permute-start(f32[128,512]{1,0:T(8,128)} %get-tuple-element.69), channel_id=1, source_target_pairs={{0,4},{1,5},{2,6},{3,7},{4,8},{5,9},{6,10},{7,11},{8,12},{9,13},{1... | collective-permute-start | bytes 786440 | tf_op jit(solution)/shard_map/ppermute | solution.py:122
  9.2 1.1 copy-start.1
  10.4 0.9 copy-start.3
  14.0 10.7 %collective-permute-start.1 = (f32[128,512]{1,0:T(8,128)}, f32[128,512]{1,0:T(8,128)S(1)}, u32[]{:S(2)}, u32[]{:S(2)}) collective-permute-start(f32[128,512]{1,0:T(8,128)} %get-tuple-element.74), channel_id=1, source_target_pairs={{0,4},{1,5},{2,6},{3,7},{4,8},{5,9},{6,10},{7,11},{8,12},{9,13},{1... | collective-permute-start | bytes 786440 | tf_op jit(solution)/shard_map/ppermute | solution.py:122
  26.4 12.2 %collective-permute-start.2 = (f32[128,512]{1,0:T(8,128)}, f32[128,512]{1,0:T(8,128)S(1)}, u32[]{:S(2)}, u32[]{:S(2)}) collective-permute-start(f32[128,512]{1,0:T(8,128)} %get-tuple-element.78), channel_id=1, source_target_pairs={{0,4},{1,5},{2,6},{3,7},{4,8},{5,9},{6,10},{7,11},{8,12},{9,13},{1... | collective-permute-start | bytes 786440 | tf_op jit(solution)/shard_map/ppermute | solution.py:122
  28.4 13.4 %collective-permute-start.3 = (f32[128,512]{1,0:T(8,128)S(1)}, f32[128,512]{1,0:T(8,128)S(1)}, u32[]{:S(2)}, u32[]{:S(2)}) collective-permute-start(f32[128,512]{1,0:T(8,128)S(1)} %get-tuple-element.83), channel_id=1, source_target_pairs={{0,4},{1,5},{2,6},{3,7},{4,8},{5,9},{6,10},{7,11},{8,12},{9,13},{1... | collective-permute-start | bytes 786440 | tf_op jit(solution)/shard_map/ppermute | solution.py:122
  44.8 1.6 %collective-permute-start.4 = (f32[128,512]{1,0:T(8,128)S(1)}, f32[128,512]{1,0:T(8,128)S(1)}, u32[]{:S(2)}, u32[]{:S(2)}) collective-permute-start(f32[128,512]{1,0:T(8,128)S(1)} %get-tuple-element.88), channel_id=1, source_target_pairs={{0,1},{1,0},{2,3},{3,2},{4,5},{5,4},{6,7},{7,6},{8,9},{9,8},{10,11... | collective-permute-start | bytes 786440 | tf_op jit(solution)/shard_map/ppermute | solution.py:122
  46.5 5.6 %collective-permute-start.5 = (f32[64,512]{1,0:T(8,128)S(1)}, f32[64,512]{1,0:T(8,128)S(1)}, u32[]{:S(2)}, u32[]{:S(2)}) collective-permute-start(f32[64,512]{1,0:T(8,128)S(1)} %slice_select_fusion.1), channel_id=1, source_target_pairs={{0,2},{1,3},{2,0},{3,1},{4,6},{5,7},{6,4},{7,5},{8,10},{9,11},{10,... | collective-permute-start | bytes 393224 | tf_op jit(solution)/shard_map/ppermute | solution.py:122
  52.1 9.8 %collective-permute-start.6 = (f32[64,512]{1,0:T(8,128)S(1)}, f32[64,512]{1,0:T(8,128)S(1)}, u32[]{:S(2)}, u32[]{:S(2)}) collective-permute-start(f32[64,512]{1,0:T(8,128)S(1)} %add_multiply_fusion.1), channel_id=1, source_target_pairs={{0,6},{1,7},{2,4},{3,5},{4,10},{5,11},{6,8},{7,9},{8,14},{9,15},{1... | collective-permute-start | bytes 393224 | tf_op jit(solution)/shard_map/ppermute | solution.py:122
  52.2 11.1 %collective-permute-start.7 = (f32[64,512]{1,0:T(8,128)S(1)}, f32[64,512]{1,0:T(8,128)S(1)}, u32[]{:S(2)}, u32[]{:S(2)}) collective-permute-start(f32[64,512]{1,0:T(8,128)S(1)} %add_multiply_fusion.1), channel_id=1, source_target_pairs={{0,4},{1,5},{2,6},{3,7},{4,8},{5,9},{6,10},{7,11},{8,12},{9,13},{1... | collective-permute-start | bytes 393224 | tf_op jit(solution)/shard_map/ppermute | solution.py:122
  63.3 1.6 %collective-permute-start.8 = (f32[128,512]{1,0:T(8,128)S(1)}, f32[128,512]{1,0:T(8,128)S(1)}, u32[]{:S(2)}, u32[]{:S(2)}) collective-permute-start(f32[128,512]{1,0:T(8,128)S(1)} %maximum_select_fusion.1.va), channel_id=1, source_target_pairs={{0,1},{1,0},{2,3},{3,2},{4,5},{5,4},{6,7},{7,6},{8,9},{9,8},{10,11... | collective-permute-start | bytes 786440 | tf_op jit(solution)/shard_map/ppermute | solution.py:122
  66.7 12.1 %collective-permute-start.9 = (f32[128,512]{1,0:T(8,128)}, f32[128,512]{1,0:T(8,128)S(1)}, u32[]{:S(2)}, u32[]{:S(2)}) collective-permute-start(f32[128,512]{1,0:T(8,128)} %get-tuple-element.96), channel_id=1, source_target_pairs={{0,4},{1,5},{2,6},{3,7},{4,8},{5,9},{6,10},{7,11},{8,12},{9,13},{1... | collective-permute-start | bytes 786440 | tf_op jit(solution)/shard_map/ppermute | solution.py:122
  68.6 14.9 %collective-permute-start.10 = (f32[128,512]{1,0:T(8,128)S(1)}, f32[128,512]{1,0:T(8,128)S(1)}, u32[]{:S(2)}, u32[]{:S(2)}) collective-permute-start(f32[128,512]{1,0:T(8,128)S(1)} %get-tuple-element.101), channel_id=1, source_target_pairs={{0,4},{1,5},{2,6},{3,7},{4,8},{5,9},{6,10},{7,11},{8,12},{9,13},{1... | collective-permute-start | bytes 786440 | tf_op jit(solution)/shard_map/ppermute | solution.py:122
  85.3 12.2 %collective-permute-start.11 = (f32[128,512]{1,0:T(8,128)}, f32[128,512]{1,0:T(8,128)S(1)}, u32[]{:S(2)}, u32[]{:S(2)}) collective-permute-start(f32[128,512]{1,0:T(8,128)} %get-tuple-element.105), channel_id=1, source_target_pairs={{0,4},{1,5},{2,6},{3,7},{4,8},{5,9},{6,10},{7,11},{8,12},{9,13},{1... | collective-permute-start | bytes 786440 | tf_op jit(solution)/shard_map/ppermute | solution.py:122
  87.2 14.1 %collective-permute-start.12 = (f32[128,512]{1,0:T(8,128)S(1)}, f32[128,512]{1,0:T(8,128)S(1)}, u32[]{:S(2)}, u32[]{:S(2)}) collective-permute-start(f32[128,512]{1,0:T(8,128)S(1)} %get-tuple-element.110), channel_id=1, source_target_pairs={{0,4},{1,5},{2,6},{3,7},{4,8},{5,9},{6,10},{7,11},{8,12},{9,13},{1... | collective-permute-start | bytes 786440 | tf_op jit(solution)/shard_map/ppermute | solution.py:122
  105.4 1.6 %collective-permute-start.13 = (f32[128,512]{1,0:T(8,128)S(1)}, f32[128,512]{1,0:T(8,128)S(1)}, u32[]{:S(2)}, u32[]{:S(2)}) collective-permute-start(f32[128,512]{1,0:T(8,128)S(1)} %get-tuple-element.115), channel_id=1, source_target_pairs={{0,1},{1,0},{2,3},{3,2},{4,5},{5,4},{6,7},{7,6},{8,9},{9,8},{10,11... | collective-permute-start | bytes 786440 | tf_op jit(solution)/shard_map/ppermute | solution.py:122
  107.1 5.6 %collective-permute-start.14 = (f32[64,512]{1,0:T(8,128)S(1)}, f32[64,512]{1,0:T(8,128)S(1)}, u32[]{:S(2)}, u32[]{:S(2)}) collective-permute-start(f32[64,512]{1,0:T(8,128)S(1)} %slice_select_fusion), channel_id=1, source_target_pairs={{0,2},{1,3},{2,0},{3,1},{4,6},{5,7},{6,4},{7,5},{8,10},{9,11},{10,... | collective-permute-start | bytes 393224 | tf_op jit(solution)/shard_map/ppermute | solution.py:122
  112.7 10.2 %collective-permute-start.15 = (f32[64,512]{1,0:T(8,128)S(1)}, f32[64,512]{1,0:T(8,128)S(1)}, u32[]{:S(2)}, u32[]{:S(2)}) collective-permute-start(f32[64,512]{1,0:T(8,128)S(1)} %add_multiply_fusion), channel_id=1, source_target_pairs={{0,14},{1,15},{2,12},{3,13},{4,18},{5,19},{6,16},{7,17},{8,22},{9,... | collective-permute-start | bytes 393224 | tf_op jit(solution)/shard_map/ppermute | solution.py:122
  112.8 11.8 %collective-permute-start.16 = (f32[64,512]{1,0:T(8,128)S(1)}, f32[64,512]{1,0:T(8,128)S(1)}, u32[]{:S(2)}, u32[]{:S(2)}) collective-permute-start(f32[64,512]{1,0:T(8,128)S(1)} %add_multiply_fusion), channel_id=1, source_target_pairs={{0,12},{1,13},{2,14},{3,15},{4,16},{5,17},{6,18},{7,19},{8,20},{9,... | collective-permute-start | bytes 393224 | tf_op jit(solution)/shard_map/ppermute | solution.py:122
  124.6 1.6 %collective-permute-start.17 = (f32[128,512]{1,0:T(8,128)S(1)}, f32[128,512]{1,0:T(8,128)S(1)}, u32[]{:S(2)}, u32[]{:S(2)}) collective-permute-start(f32[128,512]{1,0:T(8,128)S(1)} %maximum_select_fusion.2), channel_id=1, source_target_pairs={{0,1},{1,0},{2,3},{3,2},{4,5},{5,4},{6,7},{7,6},{8,9},{9,8},{10,11... | collective-permute-start | bytes 786440 | tf_op jit(solution)/shard_map/ppermute | solution.py:122

commit v4 on v3

--- a/solution.py
+++ b/solution.py
@@ -44,14 +44,20 @@
     return copies
 
 
-def load_body(first, x_hbm, m_hbm, u_hbm, v_hbm, tile, mask, u, va, vb, sems):
+def first_columns(place, blocks, hop, flip):
+    block = lax.rem(place[0] + (blocks * HOPS - hop), blocks)
+    side = 1 - place[1] if flip else place[1]
+    return 2 * block + side
+
+
+def load_body(blocks, place, x_hbm, m_hbm, u_hbm, v_hbm, tile, mask, u, va, vb, sems):
     rows = va.shape[0]
-    half = first[0] % 2
-    copies = tile_copies(first[0], x_hbm, m_hbm, tile, mask, sems)
+    half = place[1]
+    copies = tile_copies(first_columns(place, blocks, 0, False), x_hbm, m_hbm, tile, mask, sems)
     copies.append(pltpu.make_async_copy(u_hbm, u, sems.at[4]))
-    for place, (out, index) in enumerate(((va, half), (vb, 1 - half))):
+    for order, (out, index) in enumerate(((va, half), (vb, 1 - half))):
         at = pl.ds(pl.multiple_of(index * rows, rows), rows)
-        copies.append(pltpu.make_async_copy(v_hbm.at[at], out, sems.at[5 + place]))
+        copies.append(pltpu.make_async_copy(v_hbm.at[at], out, sems.at[5 + order]))
     for copy in copies:
         copy.start()
     for copy in copies:
@@ -78,19 +84,27 @@
     va2[...] = va1[...] + steps[1] * along(r, cell_half)
 
 
-def close_body(
-    steps, first, u, u1, rest, va1, vb, tile, mask, x_hbm, m_hbm, vb2, u2, tile_next, mask_next, sems
-):
+def close_body(steps, u, u1, rest, vb, tile, mask, vb2, vb1_half, r2b):
     width = vb.shape[0]
-    copies = tile_copies(first[0], x_hbm, m_hbm, tile_next, mask_next, sems)
-    for copy in copies:
-        copy.start()
     vb1 = vb[...] + steps[1] * along(rest[:, width:], u[...].astype(HALF))
     cell_half, locus_half = u1[...].astype(HALF), vb1.astype(HALF)
     r = residue(tile, mask, 1, cell_half, locus_half)
     vb2[...] = vb1 + steps[1] * along(r, cell_half)
-    grad_u = times(rest[:, :width], va1[...].astype(HALF)) + times(r, locus_half)
+    vb1_half[...] = locus_half
+    r2b[...] = r
+
+
+def settle(steps, u1, rest, va1, vb1_half, r2b, u2):
+    width = r2b.shape[1]
+    grad_u = times(rest[:, :width], va1[...].astype(HALF)) + times(r2b[...], vb1_half[...])
     u2[...] = u1[...] + steps[0] * grad_u
+
+
+def settle_body(steps, blocks, hop, flip, place, u1, rest, va1, vb1_half, r2b, x_hbm, m_hbm, u2, tile, mask, sems):
+    copies = tile_copies(first_columns(place, blocks, hop, flip), x_hbm, m_hbm, tile, mask, sems)
+    for copy in copies:
+        copy.start()
+    settle(steps, u1, rest, va1, vb1_half, r2b, u2)
     for copy in copies:
         copy.wait()
 
@@ -122,15 +136,17 @@
     return lax.ppermute(block, AXES, route)
 
 
-def average(part_a, part_b, blocks, groups, distance):
+def average(part_a, part_b, pending, blocks, groups, distance):
     member = lax.axis_index("group")
     bits = [1 << i for i in range(1, groups.bit_length() - 1)]
-    share = part_a + moved(part_b, blocks, groups, 0, 1)
+    share = part_b + moved(part_a, blocks, groups, 0, 1)
     for bit in bits:
         rows = share.shape[0] // 2
         upper = (member & bit) != 0
         low, high = share[:rows], share[rows:]
-        share = jnp.where(upper, high, low) + moved(jnp.where(upper, low, high), blocks, groups, 0, bit)
+        received = moved(jnp.where(upper, low, high), blocks, groups, 0, bit)
+        received, *pending = lax.optimization_barrier((received, *pending))
+        share = jnp.where(upper, high, low) + received
     share = share / groups
     for place, bit in enumerate(reversed(bits)):
         upper = (member & bit) != 0
@@ -143,7 +159,7 @@
         share = jnp.where(
             upper, jnp.concatenate([other, mine], 0), jnp.concatenate([mine, other], 0)
         )
-    return share, moved(share, blocks, groups, 0, 1)
+    return share, moved(share, blocks, groups, 0, 1), pending
 
 
 def solution(mesh):
@@ -158,13 +174,11 @@
         wide, tall = ((cells, rank), F32), ((rows, rank), F32)
         tiles = [((cells, 2 * rows), HALF), ((cells, 2 * rows), jnp.int32)]
         work = 2 * cells * rows * rank
-
-        def first(hop):
-            return ((position - hop) % blocks * 2 + side).reshape(1).astype(jnp.int32)
+        place = jnp.stack([position, side]).astype(jnp.int32)
 
         tile, mask, u, va, vb = call(
-            load_body,
-            (first(0), expression, observed, cell_factors, locus_factors),
+            functools.partial(load_body, blocks),
+            (place, expression, observed, cell_factors, locus_factors),
             "shhhh",
             tiles + [wide, tall, tall],
             7,
@@ -181,17 +195,30 @@
                 0,
                 4 * work,
             )
-            vb2, u, tile, mask = call(
+            vb2, vb1_half, r2b = call(
                 functools.partial(close_body, steps),
-                (first(hop + 1), u, u1, rest, va1, vb, tile, mask, expression, observed),
-                "svvvvvvvhh",
-                [tall, wide] + tiles,
-                4,
-                5 * work,
-            )
+                (u, u1, rest, vb, tile, mask),
+                "vvvvvv",
+                [tall, ((rows, rank), HALF), ((cells, rows), HALF)],
+                0,
+                3 * work,
+            )
+            if hop < HOPS - 1:
+                u, tile, mask = call(
+                    functools.partial(settle_body, steps, blocks, hop + 1, hop + 1 >= HOPS // 2),
+                    (place, u1, rest, va1, vb1_half, r2b, expression, observed),
+                    "svvvvvhh",
+                    [wide] + tiles,
+                    4,
+                    2 * work,
+                )
+            else:
+                (u,) = call(
+                    functools.partial(settle, steps), (u1, rest, va1, vb1_half, r2b), "vvvvv", [wide], 0, 2 * work
+                )
             if hop == HOPS // 2 - 1 or hop == HOPS - 1:
                 distance = 1 if hop < HOPS - 1 else 1 - HOPS
-                va, vb = average(va2, vb2, blocks, groups, distance)
+                va, vb, (u, tile, mask) = average(va2, vb2, (u, tile, mask), blocks, groups, distance)
             else:
                 va, vb = (moved(part, blocks, groups, 1) for part in (va2, vb2))
         whole = jnp.where(side == 0, jnp.concatenate([va, vb], 0), jnp.concatenate([vb, va], 0))

time: 127 us -> 117 us (0.921)
  waiting for transfers between devices: 83.4 us -> 79 us
  local copies, waits for them, and re-layouts: 3.61 us -> 0 us
    ppermute x18, waiting for transfers between devices: 83.4 us -> 79 us  [moved(): return lax.ppermute(block, AXES, route)]
    unnamed x8 -> x0, local copies, waits for them, and re-layouts: 3.61 us -> none
    pallas_call x19 -> x25, Pallas kernels: 28 us -> 27.1 us  [call(): pl.pallas_call(body, out_shape=[jax.ShapeDtypeStruct(shape, dtype) for sh...]
  transfers between devices with their start and end apart: 18 -> 18, of which waited for: 18 -> 18; matrix products, arithmetic and copies ran while one was open for 0% -> 0% of each run, Pallas kernels for 9% -> 15%
where the time goes in v4:
time: 117 us
  waiting for transfers between devices  79 us (68%)
  Pallas kernels  27.1 us (23%)
  starting transfers between devices  8.91 us (8%)
    ppermute x18, waiting for transfers between devices, moved(): return lax.ppermute(block, AXES, route)  79 us
    pallas_call x25, Pallas kernels, call(): pl.pallas_call(body, out_shape=[jax.ShapeDtypeStruct(shape, dtype) for sh...  27.1 us
    ppermute x18, starting transfers between devices, moved(): return lax.ppermute(block, AXES, route)  8.91 us
  transfers between devices with their start and end apart: 18, of which 18 were waited for; matrix products, arithmetic and copies ran while one was open for 0% of the time, Pallas kernels for 15%

profile of v4, /device:TPU:0, one launch (start us, length us, event | category | flops | bytes accessed | tf_op | source)
XLA Modules:
  0.0 117.2 jit_solution(12822298170672307253)
XLA Ops:
  0.7 2.2 %shard_map.59 = (bf16[384,256]{1,0:T(8,128)(2,1)S(1)}, s32[384,256]{1,0:T(8,128)S(1)}, f32[384,512]{1,0:T(8,128)S(1)}, f32[128,512]{1,0:T(8,128)S(1)}, f32[128,512]{1,0:T(8,128)S(1)}) custom-call(s32[2]{0:T(128)S(1)} %pad_add_fusion.place, bf16[384,2048]{1,0:T(8,128)(2,1)} %x_hbm.11, s32[384,2048]{1,0:T(8,128)} %m_hbm.11, f32[384,512]{1,0:T(8,128)} %u_hbm.1, ...), custom_call_target="tpu_custom_call" | custom-call | bytes 4194304 | tf_op jit(solution)/shard_map/pallas_call | solution.py:119
  3.6 1.0 shard_map.61
  4.6 3.0 %collective-permute-start = (f32[128,512]{1,0:T(8,128)S(1)}, f32[128,512]{1,0:T(8,128)S(1)}, u32[]{:S(2)}, u32[]{:S(2)}) collective-permute-start(f32[128,512]{1,0:T(8,128)S(1)} %get-tuple-element.88), channel_id=1, source_target_pairs={{0,4},{1,5},{2,6},{3,7},{4,8},{5,9},{6,10},{7,11},{8,12},{9,13},{1... | collective-permute-start | bytes 786440 | tf_op jit(solution)/shard_map/ppermute | solution.py:136
  7.6 0.8 shard_map.62
  8.4 1.6 %collective-permute-start.1 = (f32[128,512]{1,0:T(8,128)S(1)}, f32[128,512]{1,0:T(8,128)S(1)}, u32[]{:S(2)}, u32[]{:S(2)}) collective-permute-start(f32[128,512]{1,0:T(8,128)S(1)} %get-tuple-element.93), channel_id=1, source_target_pairs={{0,4},{1,5},{2,6},{3,7},{4,8},{5,9},{6,10},{7,11},{8,12},{9,13},{1... | collective-permute-start | bytes 786440 | tf_op jit(solution)/shard_map/ppermute | solution.py:136
  10.0 1.7 %shard_map.63 = (f32[384,512]{1,0:T(8,128)S(1)}, bf16[384,256]{1,0:T(8,128)(2,1)S(1)}, s32[384,256]{1,0:T(8,128)S(1)}) custom-call(s32[2]{0:T(128)S(1)} %pad_add_fusion.place, f32[384,512]{1,0:T(8,128)S(1)} %get-tuple-element.83.u1, bf16[384,256]{1,0:T(8,128)(2,1)S(1)} %get-tuple-element.84.rest, f32[128,512]{1,0:T(8,128)S(1)} %get-tuple-element.81.va1, ...), custom_call_target="tpu_custom_call" | custom-call | flops 100663296 | bytes 4194304 | tf_op jit(solution)/shard_map/pallas_call | solution.py:119
  11.8 6.0 %collective-permute-done.va = f32[128,512]{1,0:T(8,128)S(1)} collective-permute-done((f32[128,512]{1,0:T(8,128)S(1)}, f32[128,512]{1,0:T(8,128)S(1)}, u32[]{:S(2)}, u32[]{:S(2)}) %collective-permute-start) | collective-permute-done | bytes 262176 | tf_op jit(solution)/shard_map/ppermute | solution.py:136
  17.8 0.7 shard_map.64
  18.5 4.1 %collective-permute-done.1.vb = f32[128,512]{1,0:T(8,128)S(1)} collective-permute-done((f32[128,512]{1,0:T(8,128)S(1)}, f32[128,512]{1,0:T(8,128)S(1)}, u32[]{:S(2)}, u32[]{:S(2)}) %collective-permute-start.1) | collective-permute-done | bytes 262176 | tf_op jit(solution)/shard_map/ppermute | solution.py:136
  22.6 1.1 shard_map.65
  23.7 0.8 shard_map.66
  24.5 1.2 collective-permute-start.3
  25.7 1.7 %shard_map.67 = (f32[384,512]{1,0:T(8,128)S(1)}, bf16[384,256]{1,0:T(8,128)(2,1)S(1)}, s32[384,256]{1,0:T(8,128)S(1)}) custom-call(s32[2]{0:T(128)S(1)} %pad_add_fusion.place, f32[384,512]{1,0:T(8,128)S(1)} %get-tuple-element.94.u1, bf16[384,256]{1,0:T(8,128)(2,1)S(1)} %get-tuple-element.95.rest, f32[128,512]{1,0:T(8,128)S(1)} %get-tuple-element.92.va1, ...), custom_call_target="tpu_custom_call" | custom-call | flops 100663296 | bytes 4194304 | tf_op jit(solution)/shard_map/pallas_call | solution.py:119
  27.4 8.2 %collective-permute-done.2.va = f32[128,512]{1,0:T(8,128)S(1)} collective-permute-done((f32[128,512]{1,0:T(8,128)S(1)}, f32[128,512]{1,0:T(8,128)S(1)}, u32[]{:S(2)}, u32[]{:S(2)}) %collective-permute-start.2) | collective-permute-done | bytes 262176 | tf_op jit(solution)/shard_map/ppermute | solution.py:136
  35.6 0.7 shard_map.68
  36.3 3.2 %collective-permute-done.3.vb = f32[128,512]{1,0:T(8,128)S(1)} collective-permute-done((f32[128,512]{1,0:T(8,128)S(1)}, f32[128,512]{1,0:T(8,128)S(1)}, u32[]{:S(2)}, u32[]{:S(2)}) %collective-permute-start.3) | collective-permute-done | bytes 262176 | tf_op jit(solution)/shard_map/ppermute | solution.py:136
  39.5 1.0 shard_map.69
  40.6 0.8 shard_map.70
  41.5 0.7 collective-permute-done.4
  42.2 1.4 %collective-permute-start.5 = (f32[64,512]{1,0:T(8,128)S(1)}, f32[64,512]{1,0:T(8,128)S(1)}, u32[]{:S(2)}, u32[]{:S(2)}) collective-permute-start(f32[64,512]{1,0:T(8,128)S(1)} %slice_select_fusion.1), channel_id=1, source_target_pairs={{0,2},{1,3},{2,0},{3,1},{4,6},{5,7},{6,4},{7,5},{8,10},{9,11},{10,... | collective-permute-start | bytes 393224 | tf_op jit(solution)/shard_map/ppermute | solution.py:136
  43.6 1.7 %shard_map.71 = (f32[384,512]{1,0:T(8,128)S(1)}, bf16[384,256]{1,0:T(8,128)(2,1)S(1)}, s32[384,256]{1,0:T(8,128)S(1)}) custom-call(s32[2]{0:T(128)S(1)} %pad_add_fusion.place, f32[384,512]{1,0:T(8,128)S(1)} %get-tuple-element.105.u1, bf16[384,256]{1,0:T(8,128)(2,1)S(1)} %get-tuple-element.106.rest, f32[128,512]{1,0:T(8,128)S(1)} %get-tuple-element.103.va1, ...), custom_call_target="tpu_custom_call" | custom-call | flops 100663296 | bytes 4194304 | tf_op jit(solution)/shard_map/pallas_call | solution.py:119
  45.3 2.5 %collective-permute-done.5 = f32[64,512]{1,0:T(8,128)S(1)} collective-permute-done((f32[64,512]{1,0:T(8,128)S(1)}, f32[64,512]{1,0:T(8,128)S(1)}, u32[]{:S(2)}, u32[]{:S(2)}) %collective-permute-start.5) | collective-permute-done | bytes 131104 | tf_op jit(solution)/shard_map/ppermute | solution.py:136
  48.0 9.1 %collective-permute-done.7 = f32[64,512]{1,0:T(8,128)S(1)} collective-permute-done((f32[64,512]{1,0:T(8,128)S(1)}, f32[64,512]{1,0:T(8,128)S(1)}, u32[]{:S(2)}, u32[]{:S(2)}) %collective-permute-start.7) | collective-permute-done | bytes 131104 | tf_op jit(solution)/shard_map/ppermute | solution.py:136
  57.0 1.8 %collective-permute-done.6 = f32[64,512]{1,0:T(8,128)S(1)} collective-permute-done((f32[64,512]{1,0:T(8,128)S(1)}, f32[64,512]{1,0:T(8,128)S(1)}, u32[]{:S(2)}, u32[]{:S(2)}) %collective-permute-start.6) | collective-permute-done | bytes 131104 | tf_op jit(solution)/shard_map/ppermute | solution.py:136
  59.0 0.7 shard_map.72
  59.6 0.9 collective-permute-done.8.vb
  60.5 1.0 shard_map.73
  61.6 0.8 shard_map.74
  62.5 1.7 %shard_map.75 = (f32[384,512]{1,0:T(8,128)S(1)}, bf16[384,256]{1,0:T(8,128)(2,1)S(1)}, s32[384,256]{1,0:T(8,128)S(1)}) custom-call(s32[2]{0:T(128)S(1)} %pad_add_fusion.place, f32[384,512]{1,0:T(8,128)S(1)} %get-tuple-element.120.u1, bf16[384,256]{1,0:T(8,128)(2,1)S(1)} %get-tuple-element.121.rest, f32[128,512]{1,0:T(8,128)S(1)} %get-tuple-element.119.va1, ...), custom_call_target="tpu_custom_call" | custom-call | flops 100663296 | bytes 4194304 | tf_op jit(solution)/shard_map/pallas_call | solution.py:119
  64.2 9.2 %collective-permute-done.9.va = f32[128,512]{1,0:T(8,128)S(1)} collective-permute-done((f32[128,512]{1,0:T(8,128)S(1)}, f32[128,512]{1,0:T(8,128)S(1)}, u32[]{:S(2)}, u32[]{:S(2)}) %collective-permute-start.9) | collective-permute-done | bytes 262176 | tf_op jit(solution)/shard_map/ppermute | solution.py:136
  73.5 0.7 shard_map.76
  74.1 4.2 %collective-permute-done.10.vb = f32[128,512]{1,0:T(8,128)S(1)} collective-permute-done((f32[128,512]{1,0:T(8,128)S(1)}, f32[128,512]{1,0:T(8,128)S(1)}, u32[]{:S(2)}, u32[]{:S(2)}) %collective-permute-start.10) | collective-permute-done | bytes 262176 | tf_op jit(solution)/shard_map/ppermute | solution.py:136
  78.3 1.0 shard_map.77
  79.4 0.8 shard_map.78
  80.5 1.7 %shard_map.79 = (f32[384,512]{1,0:T(8,128)S(1)}, bf16[384,256]{1,0:T(8,128)(2,1)S(1)}, s32[384,256]{1,0:T(8,128)S(1)}) custom-call(s32[2]{0:T(128)S(1)} %pad_add_fusion.place, f32[384,512]{1,0:T(8,128)S(1)} %get-tuple-element.131.u1, bf16[384,256]{1,0:T(8,128)(2,1)S(1)} %get-tuple-element.132.rest, f32[128,512]{1,0:T(8,128)S(1)} %get-tuple-element.129.va1, ...), custom_call_target="tpu_custom_call" | custom-call | flops 100663296 | bytes 4194304 | tf_op jit(solution)/shard_map/pallas_call | solution.py:119
  82.2 9.1 %collective-permute-done.11.va = f32[128,512]{1,0:T(8,128)S(1)} collective-permute-done((f32[128,512]{1,0:T(8,128)S(1)}, f32[128,512]{1,0:T(8,128)S(1)}, u32[]{:S(2)}, u32[]{:S(2)}) %collective-permute-start.11) | collective-permute-done | bytes 262176 | tf_op jit(solution)/shard_map/ppermute | solution.py:136
  91.3 0.7 shard_map.80
  92.0 3.2 %collective-permute-done.12.vb = f32[128,512]{1,0:T(8,128)S(1)} collective-permute-done((f32[128,512]{1,0:T(8,128)S(1)}, f32[128,512]{1,0:T(8,128)S(1)}, u32[]{:S(2)}, u32[]{:S(2)}) %collective-permute-start.12) | collective-permute-done | bytes 262176 | tf_op jit(solution)/shard_map/ppermute | solution.py:136
  95.2 1.0 shard_map.81
  96.3 0.8 shard_map.82
  97.2 0.7 collective-permute-done.13
  97.9 0.8 collective-permute-start.14
  98.7 1.2 %shard_map.83 = f32[384,512]{1,0:T(8,128)} custom-call(f32[384,512]{1,0:T(8,128)S(1)} %get-tuple-element.142.u1, bf16[384,256]{1,0:T(8,128)(2,1)S(1)} %get-tuple-element.143.rest, f32[128,512]{1,0:T(8,128)S(1)} %get-tuple-element.140.va1, bf16[128,512]{1,0:T(8,128)(2,1)S(1)} %get-tuple-element.146.vb1_half, bf16[384,128]{1,0:T(8,128)(2,1)S(1)} %get-tuple-element.147.r2b), custom_call_target="tpu_custom_call" | custom-call | flops 100663296 | bytes 1474560 | tf_op jit(solution)/shard_map/pallas_call | solution.py:119
  99.9 3.6 %collective-permute-done.14 = f32[64,512]{1,0:T(8,128)S(1)} collective-permute-done((f32[64,512]{1,0:T(8,128)S(1)}, f32[64,512]{1,0:T(8,128)S(1)}, u32[]{:S(2)}, u32[]{:S(2)}) %collective-permute-start.14) | collective-permute-done | bytes 131104 | tf_op jit(solution)/shard_map/ppermute | solution.py:136
  103.7 8.1 %collective-permute-done.16 = f32[64,512]{1,0:T(8,128)S(1)} collective-permute-done((f32[64,512]{1,0:T(8,128)S(1)}, f32[64,512]{1,0:T(8,128)S(1)}, u32[]{:S(2)}, u32[]{:S(2)}) %collective-permute-start.16) | collective-permute-done | bytes 131104 | tf_op jit(solution)/shard_map/ppermute | solution.py:136
  111.8 2.9 %collective-permute-done.15 = f32[64,512]{1,0:T(8,128)S(1)} collective-permute-done((f32[64,512]{1,0:T(8,128)S(1)}, f32[64,512]{1,0:T(8,128)S(1)}, u32[]{:S(2)}, u32[]{:S(2)}) %collective-permute-start.15) | collective-permute-done | bytes 131104 | tf_op jit(solution)/shard_map/ppermute | solution.py:136
  114.8 1.5 %collective-permute-done.17 = f32[128,512]{1,0:T(8,128)S(1)} collective-permute-done((f32[128,512]{1,0:T(8,128)S(1)}, f32[128,512]{1,0:T(8,128)S(1)}, u32[]{:S(2)}, u32[]{:S(2)}) %collective-permute-start.17) | collective-permute-done | bytes 262176 | tf_op jit(solution)/shard_map/ppermute | solution.py:136
  116.3 0.8 maximum_select_fusion
  (23 shorter events, 1.9 us)
Async XLA Ops:
  4.6 13.2 %collective-permute-start = (f32[128,512]{1,0:T(8,128)S(1)}, f32[128,512]{1,0:T(8,128)S(1)}, u32[]{:S(2)}, u32[]{:S(2)}) collective-permute-start(f32[128,512]{1,0:T(8,128)S(1)} %get-tuple-element.88), channel_id=1, source_target_pairs={{0,4},{1,5},{2,6},{3,7},{4,8},{5,9},{6,10},{7,11},{8,12},{9,13},{1... | collective-permute-start | bytes 786440 | tf_op jit(solution)/shard_map/ppermute | solution.py:136
  8.4 14.1 %collective-permute-start.1 = (f32[128,512]{1,0:T(8,128)S(1)}, f32[128,512]{1,0:T(8,128)S(1)}, u32[]{:S(2)}, u32[]{:S(2)}) collective-permute-start(f32[128,512]{1,0:T(8,128)S(1)} %get-tuple-element.93), channel_id=1, source_target_pairs={{0,4},{1,5},{2,6},{3,7},{4,8},{5,9},{6,10},{7,11},{8,12},{9,13},{1... | collective-permute-start | bytes 786440 | tf_op jit(solution)/shard_map/ppermute | solution.py:136
  23.7 12.0 %collective-permute-start.2 = (f32[128,512]{1,0:T(8,128)S(1)}, f32[128,512]{1,0:T(8,128)S(1)}, u32[]{:S(2)}, u32[]{:S(2)}) collective-permute-start(f32[128,512]{1,0:T(8,128)S(1)} %get-tuple-element.99), channel_id=1, source_target_pairs={{0,4},{1,5},{2,6},{3,7},{4,8},{5,9},{6,10},{7,11},{8,12},{9,13},{1... | collective-permute-start | bytes 786440 | tf_op jit(solution)/shard_map/ppermute | solution.py:136
  24.5 15.0 %collective-permute-start.3 = (f32[128,512]{1,0:T(8,128)S(1)}, f32[128,512]{1,0:T(8,128)S(1)}, u32[]{:S(2)}, u32[]{:S(2)}) collective-permute-start(f32[128,512]{1,0:T(8,128)S(1)} %get-tuple-element.104), channel_id=1, source_target_pairs={{0,4},{1,5},{2,6},{3,7},{4,8},{5,9},{6,10},{7,11},{8,12},{9,13},{1... | collective-permute-start | bytes 786440 | tf_op jit(solution)/shard_map/ppermute | solution.py:136
  40.5 1.6 %collective-permute-start.4 = (f32[128,512]{1,0:T(8,128)S(1)}, f32[128,512]{1,0:T(8,128)S(1)}, u32[]{:S(2)}, u32[]{:S(2)}) collective-permute-start(f32[128,512]{1,0:T(8,128)S(1)} %get-tuple-element.108), channel_id=1, source_target_pairs={{0,1},{1,0},{2,3},{3,2},{4,5},{5,4},{6,7},{7,6},{8,9},{9,8},{10,11... | collective-permute-start | bytes 786440 | tf_op jit(solution)/shard_map/ppermute | solution.py:136
  42.2 5.6 %collective-permute-start.5 = (f32[64,512]{1,0:T(8,128)S(1)}, f32[64,512]{1,0:T(8,128)S(1)}, u32[]{:S(2)}, u32[]{:S(2)}) collective-permute-start(f32[64,512]{1,0:T(8,128)S(1)} %slice_select_fusion.1), channel_id=1, source_target_pairs={{0,2},{1,3},{2,0},{3,1},{4,6},{5,7},{6,4},{7,5},{8,10},{9,11},{10,... | collective-permute-start | bytes 393224 | tf_op jit(solution)/shard_map/ppermute | solution.py:136
  47.9 9.2 %collective-permute-start.7 = (f32[64,512]{1,0:T(8,128)S(1)}, f32[64,512]{1,0:T(8,128)S(1)}, u32[]{:S(2)}, u32[]{:S(2)}) collective-permute-start(f32[64,512]{1,0:T(8,128)S(1)} %add_multiply_fusion.1), channel_id=1, source_target_pairs={{0,4},{1,5},{2,6},{3,7},{4,8},{5,9},{6,10},{7,11},{8,12},{9,13},{1... | collective-permute-start | bytes 393224 | tf_op jit(solution)/shard_map/ppermute | solution.py:136
  47.9 11.0 %collective-permute-start.6 = (f32[64,512]{1,0:T(8,128)S(1)}, f32[64,512]{1,0:T(8,128)S(1)}, u32[]{:S(2)}, u32[]{:S(2)}) collective-permute-start(f32[64,512]{1,0:T(8,128)S(1)} %add_multiply_fusion.1), channel_id=1, source_target_pairs={{0,6},{1,7},{2,4},{3,5},{4,10},{5,11},{6,8},{7,9},{8,14},{9,15},{1... | collective-permute-start | bytes 393224 | tf_op jit(solution)/shard_map/ppermute | solution.py:136
  58.9 1.6 %collective-permute-start.8 = (f32[128,512]{1,0:T(8,128)S(1)}, f32[128,512]{1,0:T(8,128)S(1)}, u32[]{:S(2)}, u32[]{:S(2)}) collective-permute-start(f32[128,512]{1,0:T(8,128)S(1)} %maximum_select_fusion.1.va), channel_id=1, source_target_pairs={{0,1},{1,0},{2,3},{3,2},{4,5},{5,4},{6,7},{7,6},{8,9},{9,8},{10,11... | collective-permute-start | bytes 786440 | tf_op jit(solution)/shard_map/ppermute | solution.py:136
  61.6 11.9 %collective-permute-start.9 = (f32[128,512]{1,0:T(8,128)S(1)}, f32[128,512]{1,0:T(8,128)S(1)}, u32[]{:S(2)}, u32[]{:S(2)}) collective-permute-start(f32[128,512]{1,0:T(8,128)S(1)} %get-tuple-element.125), channel_id=1, source_target_pairs={{0,4},{1,5},{2,6},{3,7},{4,8},{5,9},{6,10},{7,11},{8,12},{9,13},{1... | collective-permute-start | bytes 786440 | tf_op jit(solution)/shard_map/ppermute | solution.py:136
  62.4 15.8 %collective-permute-start.10 = (f32[128,512]{1,0:T(8,128)S(1)}, f32[128,512]{1,0:T(8,128)S(1)}, u32[]{:S(2)}, u32[]{:S(2)}) collective-permute-start(f32[128,512]{1,0:T(8,128)S(1)} %get-tuple-element.130), channel_id=1, source_target_pairs={{0,4},{1,5},{2,6},{3,7},{4,8},{5,9},{6,10},{7,11},{8,12},{9,13},{1... | collective-permute-start | bytes 786440 | tf_op jit(solution)/shard_map/ppermute | solution.py:136
  79.3 12.0 %collective-permute-start.11 = (f32[128,512]{1,0:T(8,128)S(1)}, f32[128,512]{1,0:T(8,128)S(1)}, u32[]{:S(2)}, u32[]{:S(2)}) collective-permute-start(f32[128,512]{1,0:T(8,128)S(1)} %get-tuple-element.136), channel_id=1, source_target_pairs={{0,4},{1,5},{2,6},{3,7},{4,8},{5,9},{6,10},{7,11},{8,12},{9,13},{1... | collective-permute-start | bytes 786440 | tf_op jit(solution)/shard_map/ppermute | solution.py:136
  80.2 15.0 %collective-permute-start.12 = (f32[128,512]{1,0:T(8,128)S(1)}, f32[128,512]{1,0:T(8,128)S(1)}, u32[]{:S(2)}, u32[]{:S(2)}) collective-permute-start(f32[128,512]{1,0:T(8,128)S(1)} %get-tuple-element.141), channel_id=1, source_target_pairs={{0,4},{1,5},{2,6},{3,7},{4,8},{5,9},{6,10},{7,11},{8,12},{9,13},{1... | collective-permute-start | bytes 786440 | tf_op jit(solution)/shard_map/ppermute | solution.py:136
  96.3 1.6 %collective-permute-start.13 = (f32[128,512]{1,0:T(8,128)S(1)}, f32[128,512]{1,0:T(8,128)S(1)}, u32[]{:S(2)}, u32[]{:S(2)}) collective-permute-start(f32[128,512]{1,0:T(8,128)S(1)} %get-tuple-element.145), channel_id=1, source_target_pairs={{0,1},{1,0},{2,3},{3,2},{4,5},{5,4},{6,7},{7,6},{8,9},{9,8},{10,11... | collective-permute-start | bytes 786440 | tf_op jit(solution)/shard_map/ppermute | solution.py:136
  97.9 5.6 %collective-permute-start.14 = (f32[64,512]{1,0:T(8,128)S(1)}, f32[64,512]{1,0:T(8,128)S(1)}, u32[]{:S(2)}, u32[]{:S(2)}) collective-permute-start(f32[64,512]{1,0:T(8,128)S(1)} %slice_select_fusion), channel_id=1, source_target_pairs={{0,2},{1,3},{2,0},{3,1},{4,6},{5,7},{6,4},{7,5},{8,10},{9,11},{10,... | collective-permute-start | bytes 393224 | tf_op jit(solution)/shard_map/ppermute | solution.py:136
  103.6 8.3 %collective-permute-start.16 = (f32[64,512]{1,0:T(8,128)S(1)}, f32[64,512]{1,0:T(8,128)S(1)}, u32[]{:S(2)}, u32[]{:S(2)}) collective-permute-start(f32[64,512]{1,0:T(8,128)S(1)} %add_multiply_fusion), channel_id=1, source_target_pairs={{0,12},{1,13},{2,14},{3,15},{4,16},{5,17},{6,18},{7,19},{8,20},{9,... | collective-permute-start | bytes 393224 | tf_op jit(solution)/shard_map/ppermute | solution.py:136
  103.6 11.1 %collective-permute-start.15 = (f32[64,512]{1,0:T(8,128)S(1)}, f32[64,512]{1,0:T(8,128)S(1)}, u32[]{:S(2)}, u32[]{:S(2)}) collective-permute-start(f32[64,512]{1,0:T(8,128)S(1)} %add_multiply_fusion), channel_id=1, source_target_pairs={{0,14},{1,15},{2,12},{3,13},{4,18},{5,19},{6,16},{7,17},{8,22},{9,... | collective-permute-start | bytes 393224 | tf_op jit(solution)/shard_map/ppermute | solution.py:136
  114.7 1.6 %collective-permute-start.17 = (f32[128,512]{1,0:T(8,128)S(1)}, f32[128,512]{1,0:T(8,128)S(1)}, u32[]{:S(2)}, u32[]{:S(2)}) collective-permute-start(f32[128,512]{1,0:T(8,128)S(1)} %maximum_select_fusion.2), channel_id=1, source_target_pairs={{0,1},{1,0},{2,3},{3,2},{4,5},{5,4},{6,7},{7,6},{8,9},{9,8},{10,11... | collective-permute-start | bytes 786440 | tf_op jit(solution)/shard_map/ppermute | solution.py:136

commit v5 on v4

--- a/solution.py
+++ b/solution.py
@@ -45,14 +45,14 @@
 
 
 def first_columns(place, blocks, hop, flip):
-    block = lax.rem(place[0] + (blocks * HOPS - hop), blocks)
-    side = 1 - place[1] if flip else place[1]
-    return 2 * block + side
+    block = lax.rem(place[0] // 2 + (blocks * HOPS - hop), blocks)
+    side = place[0] % 2
+    return 2 * block + (1 - side if flip else side)
 
 
 def load_body(blocks, place, x_hbm, m_hbm, u_hbm, v_hbm, tile, mask, u, va, vb, sems):
     rows = va.shape[0]
-    half = place[1]
+    half = place[0] % 2
     copies = tile_copies(first_columns(place, blocks, 0, False), x_hbm, m_hbm, tile, mask, sems)
     copies.append(pltpu.make_async_copy(u_hbm, u, sems.at[4]))
     for order, (out, index) in enumerate(((va, half), (vb, 1 - half))):
@@ -98,6 +98,12 @@
     width = r2b.shape[1]
     grad_u = times(rest[:, :width], va1[...].astype(HALF)) + times(r2b[...], vb1_half[...])
     u2[...] = u1[...] + steps[0] * grad_u
+
+
+def hold_body(steps, blocks, hop, place, u1, rest, va1, vb1_half, r2b, va2, vb2, x_hbm, m_hbm, u2, tile, mask, va, vb, sems):
+    va[...] = va2[...]
+    vb[...] = vb2[...]
+    settle_body(steps, blocks, hop, hop >= HOPS // 2, place, u1, rest, va1, vb1_half, r2b, x_hbm, m_hbm, u2, tile, mask, sems)
 
 
 def settle_body(steps, blocks, hop, flip, place, u1, rest, va1, vb1_half, r2b, x_hbm, m_hbm, u2, tile, mask, sems):
@@ -127,13 +133,21 @@
     )(*pinned)
 
 
-def moved(block, blocks, groups, distance, flip=0):
+def moved(block, blocks, groups, distance, flip=0, cores=(0, 1)):
     route = [
         (b * groups + g, (b + distance) % blocks * groups + (g ^ flip))
         for b in range(blocks)
         for g in range(groups)
+        if g % 2 in cores
     ]
     return lax.ppermute(block, AXES, route)
+
+
+def in_turns(parts, later, blocks, groups):
+    first = [moved(part, blocks, groups, 1, cores=(0,)) for part in parts]
+    second = [moved(part, blocks, groups, 1, cores=(1,)) for part in later]
+    first = lax.optimization_barrier(first)
+    return zip(first, second)
 
 
 def average(part_a, part_b, pending, blocks, groups, distance):
@@ -174,7 +188,7 @@
         wide, tall = ((cells, rank), F32), ((rows, rank), F32)
         tiles = [((cells, 2 * rows), HALF), ((cells, 2 * rows), jnp.int32)]
         work = 2 * cells * rows * rank
-        place = jnp.stack([position, side]).astype(jnp.int32)
+        place = (2 * position + side).reshape(1).astype(jnp.int32)
 
         tile, mask, u, va, vb = call(
             functools.partial(load_body, blocks),
@@ -187,6 +201,9 @@
             grad_u, va1 = call(
                 functools.partial(open_body, steps), (u, va, tile, mask), "vvvv", [wide, tall], 0, 3 * work
             )
+            if vb is None:
+                va1, *pair_b = lax.optimization_barrier((va1, *pair_b))
+                vb = jnp.where(side == 0, *pair_b)
             u1, va2, rest = call(
                 functools.partial(turn_body, steps),
                 (u, grad_u, va1, vb, tile, mask),
@@ -203,7 +220,17 @@
                 0,
                 3 * work,
             )
-            if hop < HOPS - 1:
+            turns = hop % (HOPS // 2) == 0
+            if turns:
+                u, tile, mask, *later = call(
+                    functools.partial(hold_body, steps, blocks, hop + 1),
+                    (place, u1, rest, va1, vb1_half, r2b, va2, vb2, expression, observed),
+                    "svvvvvvvhh",
+                    [wide] + tiles + [tall, tall],
+                    4,
+                    2 * work,
+                )
+            elif hop < HOPS - 1:
                 u, tile, mask = call(
                     functools.partial(settle_body, steps, blocks, hop + 1, hop + 1 >= HOPS // 2),
                     (place, u1, rest, va1, vb1_half, r2b, expression, observed),
@@ -219,6 +246,9 @@
             if hop == HOPS // 2 - 1 or hop == HOPS - 1:
                 distance = 1 if hop < HOPS - 1 else 1 - HOPS
                 va, vb, (u, tile, mask) = average(va2, vb2, (u, tile, mask), blocks, groups, distance)
+            elif turns:
+                pair_a, pair_b = in_turns((va2, vb2), later, blocks, groups)
+                va, vb = jnp.where(side == 0, *pair_a), None
             else:
                 va, vb = (moved(part, blocks, groups, 1) for part in (va2, vb2))
         whole = jnp.where(side == 0, jnp.concatenate([va, vb], 0), jnp.concatenate([vb, va], 0))

time: 117 us -> 123 us (1.051)
  starting transfers between devices: 8.91 us -> 20.7 us
  waiting for transfers between devices: 79 us -> 74.9 us
  Pallas kernels: 27.1 us -> 24.6 us
    ppermute x18 -> x22, starting transfers between devices: 8.91 us -> 20.7 us  [moved(): return lax.ppermute(block, AXES, route)]
    ppermute x18 -> x22, waiting for transfers between devices: 79 us -> 74.9 us  [moved(): return lax.ppermute(block, AXES, route)]
    pallas_call x25, Pallas kernels: 27.1 us -> 24.6 us  [call(): pl.pallas_call(body, out_shape=[jax.ShapeDtypeStruct(shape, dtype) for sh...]
  transfers between devices with their start and end apart: 18 -> 22, of which waited for: 18 -> 18; matrix products, arithmetic and copies ran while one was open for 0% -> 0% of each run, Pallas kernels for 15% -> 13%
where the time goes in v5:
time: 123 us; the launch traced here: 122 us
  waiting for transfers between devices  74.9 us (61%)
  Pallas kernels  24.6 us (20%)
  starting transfers between devices  20.7 us (17%)
    ppermute x22, waiting for transfers between devices, moved(): return lax.ppermute(block, AXES, route)  74.9 us
    pallas_call x25, Pallas kernels, call(): pl.pallas_call(body, out_shape=[jax.ShapeDtypeStruct(shape, dtype) for sh...  24.6 us
    ppermute x22, starting transfers between devices, moved(): return lax.ppermute(block, AXES, route)  20.7 us
  transfers between devices with their start and end apart: 22, of which 18 were waited for; matrix products, arithmetic and copies ran while one was open for 0% of the time, Pallas kernels for 13%

profile of v5, /device:TPU:0, one launch (start us, length us, event | category | flops | bytes accessed | tf_op | source)
XLA Modules:
  0.0 122.4 jit_solution(7469736890241010840)
XLA Ops:
  0.6 1.6 %shard_map.59 = (bf16[384,256]{1,0:T(8,128)(2,1)S(1)}, s32[384,256]{1,0:T(8,128)S(1)}, f32[384,512]{1,0:T(8,128)S(1)}, f32[128,512]{1,0:T(8,128)S(1)}, f32[128,512]{1,0:T(8,128)S(1)}) custom-call(s32[1]{0:T(128)} %bitcast.place, bf16[384,2048]{1,0:T(8,128)(2,1)} %x_hbm.11, s32[384,2048]{1,0:T(8,128)} %m_hbm.11, f32[384,512]{1,0:T(8,128)} %u_hbm.1, ...), custom_call_target="tpu_custom_call" | custom-call | bytes 4194304 | tf_op jit(solution)/shard_map/pallas_call | solution.py:125
  2.3 0.7 shard_map.60
  3.0 1.0 shard_map.61
  4.0 4.9 %collective-permute-start = (f32[128,512]{1,0:T(8,128)S(1)}, f32[128,512]{1,0:T(8,128)S(1)}, u32[]{:S(2)}, u32[]{:S(2)}) collective-permute-start(f32[128,512]{1,0:T(8,128)S(1)} %get-tuple-element.101.va2), channel_id=1, source_target_pairs={{0,4},{2,6},{4,8},{6,10},{8,12},{10,14},{12,16},{14,18},{16,20},{1... | collective-permute-start | bytes 786440 | tf_op jit(solution)/shard_map/ppermute | solution.py:143
  8.9 0.8 shard_map.62
  9.7 3.4 %collective-permute-start.1 = (f32[128,512]{1,0:T(8,128)S(1)}, f32[128,512]{1,0:T(8,128)S(1)}, u32[]{:S(2)}, u32[]{:S(2)}) collective-permute-start(f32[128,512]{1,0:T(8,128)S(1)} %get-tuple-element.102.vb2), channel_id=1, source_target_pairs={{0,4},{2,6},{4,8},{6,10},{8,12},{10,14},{12,16},{14,18},{16,20},{1... | collective-permute-start | bytes 786440 | tf_op jit(solution)/shard_map/ppermute | solution.py:143
  13.2 1.5 %shard_map.63 = (f32[384,512]{1,0:T(8,128)S(1)}, bf16[384,256]{1,0:T(8,128)(2,1)S(1)}, s32[384,256]{1,0:T(8,128)S(1)}, f32[128,512]{1,0:T(8,128)S(1)}, f32[128,512]{1,0:T(8,128)S(1)}) custom-call(s32[1]{0:T(128)} %bitcast.place, f32[384,512]{1,0:T(8,128)S(1)} %get-tuple-element.97.u1, bf16[384,256]{1,0:T(8,128)(2,1)S(1)} %get-tuple-element.98.rest, ...), custom_call_target="tpu_custom_call" | custom-call | flops 100663296 | bytes 4194304 | tf_op jit(solution)/shard_map/pallas_call | solution.py:125
  14.7 0.7 collective-permute-start.2
  15.3 0.7 collective-permute-start.3
  16.3 7.3 %collective-permute-done.1 = f32[128,512]{1,0:T(8,128)S(1)} collective-permute-done((f32[128,512]{1,0:T(8,128)S(1)}, f32[128,512]{1,0:T(8,128)S(1)}, u32[]{:S(2)}, u32[]{:S(2)}) %collective-permute-start.1) | collective-permute-done | bytes 262176 | tf_op jit(solution)/shard_map/ppermute | solution.py:143
  24.3 1.0 shard_map.65
  25.4 0.8 shard_map.66
  26.3 1.3 %collective-permute-start.5 = (f32[128,512]{1,0:T(8,128)S(1)}, f32[128,512]{1,0:T(8,128)S(1)}, u32[]{:S(2)}, u32[]{:S(2)}) collective-permute-start(f32[128,512]{1,0:T(8,128)S(1)} %get-tuple-element.125), channel_id=1, source_target_pairs={{0,4},{1,5},{2,6},{3,7},{4,8},{5,9},{6,10},{7,11},{8,12},{9,13},{1... | collective-permute-start | bytes 786440 | tf_op jit(solution)/shard_map/ppermute | solution.py:143
  27.6 1.2 shard_map.67
  28.8 8.5 %collective-permute-done.4.va = f32[128,512]{1,0:T(8,128)S(1)} collective-permute-done((f32[128,512]{1,0:T(8,128)S(1)}, f32[128,512]{1,0:T(8,128)S(1)}, u32[]{:S(2)}, u32[]{:S(2)}) %collective-permute-start.4) | collective-permute-done | bytes 262176 | tf_op jit(solution)/shard_map/ppermute | solution.py:143
  37.9 4.3 %collective-permute-done.5.vb = f32[128,512]{1,0:T(8,128)S(1)} collective-permute-done((f32[128,512]{1,0:T(8,128)S(1)}, f32[128,512]{1,0:T(8,128)S(1)}, u32[]{:S(2)}, u32[]{:S(2)}) %collective-permute-start.5) | collective-permute-done | bytes 262176 | tf_op jit(solution)/shard_map/ppermute | solution.py:143
  42.2 1.0 shard_map.69
  43.3 0.8 shard_map.70
  44.2 0.7 collective-permute-done.6
  44.9 1.7 %collective-permute-start.7 = (f32[64,512]{1,0:T(8,128)S(1)}, f32[64,512]{1,0:T(8,128)S(1)}, u32[]{:S(2)}, u32[]{:S(2)}) collective-permute-start(f32[64,512]{1,0:T(8,128)S(1)} %slice_select_fusion.1), channel_id=1, source_target_pairs={{0,2},{1,3},{2,0},{3,1},{4,6},{5,7},{6,4},{7,5},{8,10},{9,11},{10,... | collective-permute-start | bytes 393224 | tf_op jit(solution)/shard_map/ppermute | solution.py:143
  46.6 1.2 shard_map.71
  47.8 2.7 %collective-permute-done.7 = f32[64,512]{1,0:T(8,128)S(1)} collective-permute-done((f32[64,512]{1,0:T(8,128)S(1)}, f32[64,512]{1,0:T(8,128)S(1)}, u32[]{:S(2)}, u32[]{:S(2)}) %collective-permute-start.7) | collective-permute-done | bytes 131104 | tf_op jit(solution)/shard_map/ppermute | solution.py:143
  51.1 8.6 %collective-permute-done.9 = f32[64,512]{1,0:T(8,128)S(1)} collective-permute-done((f32[64,512]{1,0:T(8,128)S(1)}, f32[64,512]{1,0:T(8,128)S(1)}, u32[]{:S(2)}, u32[]{:S(2)}) %collective-permute-start.9) | collective-permute-done | bytes 131104 | tf_op jit(solution)/shard_map/ppermute | solution.py:143
  59.7 2.1 %collective-permute-done.8 = f32[64,512]{1,0:T(8,128)S(1)} collective-permute-done((f32[64,512]{1,0:T(8,128)S(1)}, f32[64,512]{1,0:T(8,128)S(1)}, u32[]{:S(2)}, u32[]{:S(2)}) %collective-permute-start.8) | collective-permute-done | bytes 131104 | tf_op jit(solution)/shard_map/ppermute | solution.py:143
  62.6 0.9 collective-permute-done.10.vb
  63.5 1.0 shard_map.73
  64.5 1.9 %collective-permute-start.11 = (f32[128,512]{1,0:T(8,128)S(1)}, f32[128,512]{1,0:T(8,128)S(1)}, u32[]{:S(2)}, u32[]{:S(2)}) collective-permute-start(f32[128,512]{1,0:T(8,128)S(1)} %get-tuple-element.145.va2), channel_id=1, source_target_pairs={{0,4},{2,6},{4,8},{6,10},{8,12},{10,14},{12,16},{14,18},{16,20},{1... | collective-permute-start | bytes 786440 | tf_op jit(solution)/shard_map/ppermute | solution.py:143
  66.5 0.8 shard_map.74
  67.3 1.9 %collective-permute-start.12 = (f32[128,512]{1,0:T(8,128)S(1)}, f32[128,512]{1,0:T(8,128)S(1)}, u32[]{:S(2)}, u32[]{:S(2)}) collective-permute-start(f32[128,512]{1,0:T(8,128)S(1)} %get-tuple-element.146.vb2), channel_id=1, source_target_pairs={{0,4},{2,6},{4,8},{6,10},{8,12},{10,14},{12,16},{14,18},{16,20},{1... | collective-permute-start | bytes 786440 | tf_op jit(solution)/shard_map/ppermute | solution.py:143
  69.2 1.5 %shard_map.75 = (f32[384,512]{1,0:T(8,128)S(1)}, bf16[384,256]{1,0:T(8,128)(2,1)S(1)}, s32[384,256]{1,0:T(8,128)S(1)}, f32[128,512]{1,0:T(8,128)S(1)}, f32[128,512]{1,0:T(8,128)S(1)}) custom-call(s32[1]{0:T(128)} %bitcast.place, f32[384,512]{1,0:T(8,128)S(1)} %get-tuple-element.141.u1, bf16[384,256]{1,0:T(8,128)(2,1)S(1)} %get-tuple-element.142.rest, ...), custom_call_target="tpu_custom_call" | custom-call | flops 100663296 | bytes 4194304 | tf_op jit(solution)/shard_map/pallas_call | solution.py:125
  70.7 0.7 collective-permute-start.13
  71.4 0.7 collective-permute-start.14
  72.1 3.4 %collective-permute-done.11 = f32[128,512]{1,0:T(8,128)S(1)} collective-permute-done((f32[128,512]{1,0:T(8,128)S(1)}, f32[128,512]{1,0:T(8,128)S(1)}, u32[]{:S(2)}, u32[]{:S(2)}) %collective-permute-start.11) | collective-permute-done | bytes 262176 | tf_op jit(solution)/shard_map/ppermute | solution.py:143
  75.5 5.5 %collective-permute-done.12 = f32[128,512]{1,0:T(8,128)S(1)} collective-permute-done((f32[128,512]{1,0:T(8,128)S(1)}, f32[128,512]{1,0:T(8,128)S(1)}, u32[]{:S(2)}, u32[]{:S(2)}) %collective-permute-start.12) | collective-permute-done | bytes 262176 | tf_op jit(solution)/shard_map/ppermute | solution.py:143
  81.8 1.0 shard_map.77
  82.9 0.8 shard_map.78
  84.0 1.2 shard_map.79
  85.2 8.5 %collective-permute-done.15.va = f32[128,512]{1,0:T(8,128)S(1)} collective-permute-done((f32[128,512]{1,0:T(8,128)S(1)}, f32[128,512]{1,0:T(8,128)S(1)}, u32[]{:S(2)}, u32[]{:S(2)}) %collective-permute-start.15) | collective-permute-done | bytes 262176 | tf_op jit(solution)/shard_map/ppermute | solution.py:143
  94.4 5.0 %collective-permute-done.16.vb = f32[128,512]{1,0:T(8,128)S(1)} collective-permute-done((f32[128,512]{1,0:T(8,128)S(1)}, f32[128,512]{1,0:T(8,128)S(1)}, u32[]{:S(2)}, u32[]{:S(2)}) %collective-permute-start.16) | collective-permute-done | bytes 262176 | tf_op jit(solution)/shard_map/ppermute | solution.py:143
  99.3 1.1 shard_map.81
  100.4 1.0 collective-permute-start.17
  101.3 0.8 shard_map.82
  103.2 1.2 %shard_map.83 = f32[384,512]{1,0:T(8,128)} custom-call(f32[384,512]{1,0:T(8,128)S(1)} %get-tuple-element.170.u1, bf16[384,256]{1,0:T(8,128)(2,1)S(1)} %get-tuple-element.171.rest, f32[128,512]{1,0:T(8,128)S(1)} %get-tuple-element.168.va1, bf16[128,512]{1,0:T(8,128)(2,1)S(1)} %get-tuple-element.174.vb1_half, bf16[384,128]{1,0:T(8,128)(2,1)S(1)} %get-tuple-element.175.r2b), custom_call_target="tpu_custom_call" | custom-call | flops 100663296 | bytes 1474560 | tf_op jit(solution)/shard_map/pallas_call | solution.py:125
  104.4 4.0 %collective-permute-done.18 = f32[64,512]{1,0:T(8,128)S(1)} collective-permute-done((f32[64,512]{1,0:T(8,128)S(1)}, f32[64,512]{1,0:T(8,128)S(1)}, u32[]{:S(2)}, u32[]{:S(2)}) %collective-permute-start.18) | collective-permute-done | bytes 131104 | tf_op jit(solution)/shard_map/ppermute | solution.py:143
  108.6 8.7 %collective-permute-done.20 = f32[64,512]{1,0:T(8,128)S(1)} collective-permute-done((f32[64,512]{1,0:T(8,128)S(1)}, f32[64,512]{1,0:T(8,128)S(1)}, u32[]{:S(2)}, u32[]{:S(2)}) %collective-permute-start.20) | collective-permute-done | bytes 131104 | tf_op jit(solution)/shard_map/ppermute | solution.py:143
  117.3 2.7 %collective-permute-done.19 = f32[64,512]{1,0:T(8,128)S(1)} collective-permute-done((f32[64,512]{1,0:T(8,128)S(1)}, f32[64,512]{1,0:T(8,128)S(1)}, u32[]{:S(2)}, u32[]{:S(2)}) %collective-permute-start.19) | collective-permute-done | bytes 131104 | tf_op jit(solution)/shard_map/ppermute | solution.py:143
  120.1 1.5 %collective-permute-done.21 = f32[128,512]{1,0:T(8,128)S(1)} collective-permute-done((f32[128,512]{1,0:T(8,128)S(1)}, f32[128,512]{1,0:T(8,128)S(1)}, u32[]{:S(2)}, u32[]{:S(2)}) %collective-permute-start.21) | collective-permute-done | bytes 262176 | tf_op jit(solution)/shard_map/ppermute | solution.py:143
  121.6 0.8 maximum_select_fusion
  (34 shorter events, 6.1 us)
Async XLA Ops:
  4.0 12.3 %collective-permute-start = (f32[128,512]{1,0:T(8,128)S(1)}, f32[128,512]{1,0:T(8,128)S(1)}, u32[]{:S(2)}, u32[]{:S(2)}) collective-permute-start(f32[128,512]{1,0:T(8,128)S(1)} %get-tuple-element.101.va2), channel_id=1, source_target_pairs={{0,4},{2,6},{4,8},{6,10},{8,12},{10,14},{12,16},{14,18},{16,20},{1... | collective-permute-start | bytes 786440 | tf_op jit(solution)/shard_map/ppermute | solution.py:143
  9.7 13.8 %collective-permute-start.1 = (f32[128,512]{1,0:T(8,128)S(1)}, f32[128,512]{1,0:T(8,128)S(1)}, u32[]{:S(2)}, u32[]{:S(2)}) collective-permute-start(f32[128,512]{1,0:T(8,128)S(1)} %get-tuple-element.102.vb2), channel_id=1, source_target_pairs={{0,4},{2,6},{4,8},{6,10},{8,12},{10,14},{12,16},{14,18},{16,20},{1... | collective-permute-start | bytes 786440 | tf_op jit(solution)/shard_map/ppermute | solution.py:143
  14.7 8.9 %collective-permute-start.2 = (f32[128,512]{1,0:T(8,128)S(1)}, f32[128,512]{1,0:T(8,128)S(1)}, u32[]{:S(2)}, u32[]{:S(2)}) collective-permute-start(f32[128,512]{1,0:T(8,128)S(1)} %get-tuple-element.105), channel_id=1, source_target_pairs={{1,5},{3,7},{5,9},{7,11},{9,13},{11,15},{13,17},{15,19},{17,21},{1... | collective-permute-start | bytes 786440 | tf_op jit(solution)/shard_map/ppermute | solution.py:143
  15.3 8.9 %collective-permute-start.3 = (f32[128,512]{1,0:T(8,128)S(1)}, f32[128,512]{1,0:T(8,128)S(1)}, u32[]{:S(2)}, u32[]{:S(2)}) collective-permute-start(f32[128,512]{1,0:T(8,128)S(1)} %get-tuple-element.111), channel_id=1, source_target_pairs={{1,5},{3,7},{5,9},{7,11},{9,13},{11,15},{13,17},{15,19},{17,21},{1... | collective-permute-start | bytes 786440 | tf_op jit(solution)/shard_map/ppermute | solution.py:143
  25.4 11.9 %collective-permute-start.4 = (f32[128,512]{1,0:T(8,128)S(1)}, f32[128,512]{1,0:T(8,128)S(1)}, u32[]{:S(2)}, u32[]{:S(2)}) collective-permute-start(f32[128,512]{1,0:T(8,128)S(1)} %get-tuple-element.120), channel_id=1, source_target_pairs={{0,4},{1,5},{2,6},{3,7},{4,8},{5,9},{6,10},{7,11},{8,12},{9,13},{1... | collective-permute-start | bytes 786440 | tf_op jit(solution)/shard_map/ppermute | solution.py:143
  26.3 16.0 %collective-permute-start.5 = (f32[128,512]{1,0:T(8,128)S(1)}, f32[128,512]{1,0:T(8,128)S(1)}, u32[]{:S(2)}, u32[]{:S(2)}) collective-permute-start(f32[128,512]{1,0:T(8,128)S(1)} %get-tuple-element.125), channel_id=1, source_target_pairs={{0,4},{1,5},{2,6},{3,7},{4,8},{5,9},{6,10},{7,11},{8,12},{9,13},{1... | collective-permute-start | bytes 786440 | tf_op jit(solution)/shard_map/ppermute | solution.py:143
  43.3 1.6 %collective-permute-start.6 = (f32[128,512]{1,0:T(8,128)S(1)}, f32[128,512]{1,0:T(8,128)S(1)}, u32[]{:S(2)}, u32[]{:S(2)}) collective-permute-start(f32[128,512]{1,0:T(8,128)S(1)} %get-tuple-element.129), channel_id=1, source_target_pairs={{0,1},{1,0},{2,3},{3,2},{4,5},{5,4},{6,7},{7,6},{8,9},{9,8},{10,11... | collective-permute-start | bytes 786440 | tf_op jit(solution)/shard_map/ppermute | solution.py:143
  44.9 5.6 %collective-permute-start.7 = (f32[64,512]{1,0:T(8,128)S(1)}, f32[64,512]{1,0:T(8,128)S(1)}, u32[]{:S(2)}, u32[]{:S(2)}) collective-permute-start(f32[64,512]{1,0:T(8,128)S(1)} %slice_select_fusion.1), channel_id=1, source_target_pairs={{0,2},{1,3},{2,0},{3,1},{4,6},{5,7},{6,4},{7,5},{8,10},{9,11},{10,... | collective-permute-start | bytes 393224 | tf_op jit(solution)/shard_map/ppermute | solution.py:143
  50.6 9.2 %collective-permute-start.9 = (f32[64,512]{1,0:T(8,128)S(1)}, f32[64,512]{1,0:T(8,128)S(1)}, u32[]{:S(2)}, u32[]{:S(2)}) collective-permute-start(f32[64,512]{1,0:T(8,128)S(1)} %add_multiply_fusion.1), channel_id=1, source_target_pairs={{0,4},{1,5},{2,6},{3,7},{4,8},{5,9},{6,10},{7,11},{8,12},{9,13},{1... | collective-permute-start | bytes 393224 | tf_op jit(solution)/shard_map/ppermute | solution.py:143
  50.6 11.3 %collective-permute-start.8 = (f32[64,512]{1,0:T(8,128)S(1)}, f32[64,512]{1,0:T(8,128)S(1)}, u32[]{:S(2)}, u32[]{:S(2)}) collective-permute-start(f32[64,512]{1,0:T(8,128)S(1)} %add_multiply_fusion.1), channel_id=1, source_target_pairs={{0,6},{1,7},{2,4},{3,5},{4,10},{5,11},{6,8},{7,9},{8,14},{9,15},{1... | collective-permute-start | bytes 393224 | tf_op jit(solution)/shard_map/ppermute | solution.py:143
  61.9 1.6 %collective-permute-start.10 = (f32[128,512]{1,0:T(8,128)S(1)}, f32[128,512]{1,0:T(8,128)S(1)}, u32[]{:S(2)}, u32[]{:S(2)}) collective-permute-start(f32[128,512]{1,0:T(8,128)S(1)} %maximum_select_fusion.1.va), channel_id=1, source_target_pairs={{0,1},{1,0},{2,3},{3,2},{4,5},{5,4},{6,7},{7,6},{8,9},{9,8},{10,11... | collective-permute-start | bytes 786440 | tf_op jit(solution)/shard_map/ppermute | solution.py:143
  64.5 11.0 %collective-permute-start.11 = (f32[128,512]{1,0:T(8,128)S(1)}, f32[128,512]{1,0:T(8,128)S(1)}, u32[]{:S(2)}, u32[]{:S(2)}) collective-permute-start(f32[128,512]{1,0:T(8,128)S(1)} %get-tuple-element.145.va2), channel_id=1, source_target_pairs={{0,4},{2,6},{4,8},{6,10},{8,12},{10,14},{12,16},{14,18},{16,20},{1... | collective-permute-start | bytes 786440 | tf_op jit(solution)/shard_map/ppermute | solution.py:143
  67.3 13.7 %collective-permute-start.12 = (f32[128,512]{1,0:T(8,128)S(1)}, f32[128,512]{1,0:T(8,128)S(1)}, u32[]{:S(2)}, u32[]{:S(2)}) collective-permute-start(f32[128,512]{1,0:T(8,128)S(1)} %get-tuple-element.146.vb2), channel_id=1, source_target_pairs={{0,4},{2,6},{4,8},{6,10},{8,12},{10,14},{12,16},{14,18},{16,20},{1... | collective-permute-start | bytes 786440 | tf_op jit(solution)/shard_map/ppermute | solution.py:143
  70.7 10.3 %collective-permute-start.13 = (f32[128,512]{1,0:T(8,128)S(1)}, f32[128,512]{1,0:T(8,128)S(1)}, u32[]{:S(2)}, u32[]{:S(2)}) collective-permute-start(f32[128,512]{1,0:T(8,128)S(1)} %get-tuple-element.149), channel_id=1, source_target_pairs={{1,5},{3,7},{5,9},{7,11},{9,13},{11,15},{13,17},{15,19},{17,21},{1... | collective-permute-start | bytes 786440 | tf_op jit(solution)/shard_map/ppermute | solution.py:143
  71.4 10.3 %collective-permute-start.14 = (f32[128,512]{1,0:T(8,128)S(1)}, f32[128,512]{1,0:T(8,128)S(1)}, u32[]{:S(2)}, u32[]{:S(2)}) collective-permute-start(f32[128,512]{1,0:T(8,128)S(1)} %get-tuple-element.155), channel_id=1, source_target_pairs={{1,5},{3,7},{5,9},{7,11},{9,13},{11,15},{13,17},{15,19},{17,21},{1... | collective-permute-start | bytes 786440 | tf_op jit(solution)/shard_map/ppermute | solution.py:143
  82.8 10.9 %collective-permute-start.15 = (f32[128,512]{1,0:T(8,128)S(1)}, f32[128,512]{1,0:T(8,128)S(1)}, u32[]{:S(2)}, u32[]{:S(2)}) collective-permute-start(f32[128,512]{1,0:T(8,128)S(1)} %get-tuple-element.164), channel_id=1, source_target_pairs={{0,4},{1,5},{2,6},{3,7},{4,8},{5,9},{6,10},{7,11},{8,12},{9,13},{1... | collective-permute-start | bytes 786440 | tf_op jit(solution)/shard_map/ppermute | solution.py:143
  83.7 15.6 %collective-permute-start.16 = (f32[128,512]{1,0:T(8,128)S(1)}, f32[128,512]{1,0:T(8,128)S(1)}, u32[]{:S(2)}, u32[]{:S(2)}) collective-permute-start(f32[128,512]{1,0:T(8,128)S(1)} %get-tuple-element.169), channel_id=1, source_target_pairs={{0,4},{1,5},{2,6},{3,7},{4,8},{5,9},{6,10},{7,11},{8,12},{9,13},{1... | collective-permute-start | bytes 786440 | tf_op jit(solution)/shard_map/ppermute | solution.py:143
  100.4 2.1 %collective-permute-start.17 = (f32[128,512]{1,0:T(8,128)S(1)}, f32[128,512]{1,0:T(8,128)S(1)}, u32[]{:S(2)}, u32[]{:S(2)}) collective-permute-start(f32[128,512]{1,0:T(8,128)S(1)} %get-tuple-element.173), channel_id=1, source_target_pairs={{0,1},{1,0},{2,3},{3,2},{4,5},{5,4},{6,7},{7,6},{8,9},{9,8},{10,11... | collective-permute-start | bytes 786440 | tf_op jit(solution)/shard_map/ppermute | solution.py:143
  102.6 5.8 %collective-permute-start.18 = (f32[64,512]{1,0:T(8,128)S(1)}, f32[64,512]{1,0:T(8,128)S(1)}, u32[]{:S(2)}, u32[]{:S(2)}) collective-permute-start(f32[64,512]{1,0:T(8,128)S(1)} %slice_select_fusion), channel_id=1, source_target_pairs={{0,2},{1,3},{2,0},{3,1},{4,6},{5,7},{6,4},{7,5},{8,10},{9,11},{10,... | collective-permute-start | bytes 393224 | tf_op jit(solution)/shard_map/ppermute | solution.py:143
  108.4 8.8 %collective-permute-start.20 = (f32[64,512]{1,0:T(8,128)S(1)}, f32[64,512]{1,0:T(8,128)S(1)}, u32[]{:S(2)}, u32[]{:S(2)}) collective-permute-start(f32[64,512]{1,0:T(8,128)S(1)} %add_multiply_fusion), channel_id=1, source_target_pairs={{0,12},{1,13},{2,14},{3,15},{4,16},{5,17},{6,18},{7,19},{8,20},{9,... | collective-permute-start | bytes 393224 | tf_op jit(solution)/shard_map/ppermute | solution.py:143
  108.5 11.5 %collective-permute-start.19 = (f32[64,512]{1,0:T(8,128)S(1)}, f32[64,512]{1,0:T(8,128)S(1)}, u32[]{:S(2)}, u32[]{:S(2)}) collective-permute-start(f32[64,512]{1,0:T(8,128)S(1)} %add_multiply_fusion), channel_id=1, source_target_pairs={{0,14},{1,15},{2,12},{3,13},{4,18},{5,19},{6,16},{7,17},{8,22},{9,... | collective-permute-start | bytes 393224 | tf_op jit(solution)/shard_map/ppermute | solution.py:143
  120.0 1.6 %collective-permute-start.21 = (f32[128,512]{1,0:T(8,128)S(1)}, f32[128,512]{1,0:T(8,128)S(1)}, u32[]{:S(2)}, u32[]{:S(2)}) collective-permute-start(f32[128,512]{1,0:T(8,128)S(1)} %maximum_select_fusion.2), channel_id=1, source_target_pairs={{0,1},{1,0},{2,3},{3,2},{4,5},{5,4},{6,7},{7,6},{8,9},{9,8},{10,11... | collective-permute-start | bytes 786440 | tf_op jit(solution)/shard_map/ppermute | solution.py:143

commit v6 on v1

v6 whole, which is shorter than its diff:
```python
import functools

import jax
import jax.numpy as jnp
from jax import lax
from jax.experimental import pallas as pl
from jax.experimental.pallas import tpu as pltpu
from jax.sharding import PartitionSpec as P

HOPS = 6
AXES = ("blk", "group")
F32, HALF = jnp.float32, jnp.bfloat16


def across(a, b):
    return lax.dot_general(a, b, (((1,), (1,)), ((), ())), preferred_element_type=F32)


def along(a, b):
    return lax.dot_general(a, b, (((0,), (0,)), ((), ())), preferred_element_type=F32)


def times(a, b):
    return jnp.dot(a, b, preferred_element_type=F32)


def first_columns(place, blocks, hop, flip):
    block = lax.rem(place[0] // 2 + (blocks * HOPS - hop), blocks)
    side = place[0] % 2
    return 2 * block + (1 - side if flip else side)


def tile_copies(first, x_hbm, m_hbm, tile, mask, sems):
    width = tile.shape[1] // 2
    copies = []
    for order, column in enumerate((first, first + 1 - 2 * (first % 2))):
        source = pl.ds(pl.multiple_of(column * width, width), width)
        target = pl.ds(order * width, width)
        for i, (whole, part) in enumerate(((x_hbm, tile), (m_hbm, mask))):
            copies.append(
                pltpu.make_async_copy(whole.at[:, source], part.at[:, target], sems.at[2 * order + i])
            )
    return copies


def residue(tile, mask, cell_half, locus_half):
    return (mask[...] * (tile[...] - across(locus_half, cell_half))).astype(HALF)


def visit(steps, cells, loci, tile, mask, u1, v1_half, r2, v2):
    cell_half, locus_half = cells.astype(HALF), loci.astype(HALF)
    r = residue(tile, mask, cell_half, locus_half)
    cells = cells + steps[0] * along(r, locus_half)
    u1[...] = cells
    loci = loci + steps[1] * times(r, cell_half)
    cell_half, locus_half = cells.astype(HALF), loci.astype(HALF)
    v1_half[...] = locus_half
    r = residue(tile, mask, cell_half, locus_half)
    r2[...] = r
    loci = loci + steps[1] * times(r, cell_half)
    row = 0
    for out in v2:
        out[...] = loci[row : row + out.shape[0]]
        row += out.shape[0]


def start_body(steps, blocks, place, x_hbm, m_hbm, u_hbm, v_hbm, u1, v1_half, r2, v2, tile, mask, x, m, u, v, sems):
    rows = v.shape[0] // 2
    side = place[0] % 2
    copies = tile_copies(first_columns(place, blocks, 0, False), x_hbm, m_hbm, x, m, sems)
    inputs = [pltpu.make_async_copy(u_hbm, u, sems.at[4])]
    for order, index in enumerate((side, 1 - side)):
        source = pl.ds(pl.multiple_of(index * rows, rows), rows)
        target = pl.ds(order * rows, rows)
        inputs.append(pltpu.make_async_copy(v_hbm.at[source], v.at[target], sems.at[5 + order]))
    for copy in copies + inputs:
        copy.start()
    for copy in copies:
        copy.wait()
    tile[...] = x[...].astype(F32).T
    mask[...] = m[...].astype(F32).T
    for copy in inputs:
        copy.wait()
    visit(steps, u[...], v[...], tile, mask, u1, v1_half, r2, (v2,))


def visit_body(steps, parts, u, *refs):
    loci = jnp.concatenate([part[...] for part in refs[:parts]], 0)
    tile, mask, u1, v1_half, r2, *v2 = refs[parts:]
    visit(steps, u[...], loci, tile, mask, u1, v1_half, r2, v2)


def settle(steps, u1, v1_half, r2, u2):
    u2[...] = u1[...] + steps[0] * along(r2[...], v1_half[...])


def settle_body(steps, blocks, hop, flip, place, u1, v1_half, r2, x_hbm, m_hbm, u2, tile, mask, x, m, sems):
    copies = tile_copies(first_columns(place, blocks, hop, flip), x_hbm, m_hbm, x, m, sems)
    for copy in copies:
        copy.start()
    settle(steps, u1, v1_half, r2, u2)
    for copy in copies:
        copy.wait()
    tile[...] = x[...].astype(F32).T
    mask[...] = m[...].astype(F32).T


def call(body, args, spaces, outs, scratch=(), flops=0):
    kinds = {"v": pltpu.VMEM, "h": pltpu.HBM, "s": pltpu.SMEM}
    placed = [
        a if s == "s" else pltpu.with_memory_space_constraint(a, kinds[s])
        for a, s in zip(args, spaces)
    ]
    return pl.pallas_call(
        body,
        out_shape=[jax.ShapeDtypeStruct(shape, dtype) for shape, dtype in outs],
        in_specs=[pl.BlockSpec(memory_space=kinds[s]) for s in spaces],
        out_specs=[pl.BlockSpec(memory_space=pltpu.VMEM) for _ in outs],
        scratch_shapes=list(scratch),
        compiler_params=pltpu.CompilerParams(vmem_limit_bytes=12 << 20),
        cost_estimate=pl.CostEstimate(flops=flops, bytes_accessed=4 << 20, transcendentals=0),
    )(*placed)


def moved(block, blocks, groups, distance, flip=0):
    route = [
        (b * groups + g, (b + distance) % blocks * groups + (g ^ flip))
        for b in range(blocks)
        for g in range(groups)
    ]
    return lax.ppermute(block, AXES, route)


def average(part_a, part_b, pending, blocks, groups, distance):
    member = lax.axis_index("group")
    bits = [1 << i for i in range(1, groups.bit_length() - 1)]
    share = part_b + moved(part_a, blocks, groups, 0, 1)
    for bit in bits:
        rows = share.shape[0] // 2
        upper = (member & bit) != 0
        low, high = share[:rows], share[rows:]
        received = moved(jnp.where(upper, low, high), blocks, groups, 0, bit)
        received, *pending = lax.optimization_barrier((received, *pending))
        share = jnp.where(upper, high, low) + received
    share = share / groups
    for place, bit in enumerate(reversed(bits)):
        upper = (member & bit) != 0
        if place == 0:
            mine = moved(share, blocks, groups, distance)
            other = moved(share, blocks, groups, distance, bit)
        else:
            mine = share
            other = moved(share, blocks, groups, 0, bit)
        share = jnp.where(
            upper, jnp.concatenate([other, mine], 0), jnp.concatenate([mine, other], 0)
        )
    return share, moved(share, blocks, groups, 0, 1), pending


def solution(mesh):
    blocks, groups = mesh.shape["blk"], mesh.shape["group"]

    def on_device(expression, observed, cell_factors, locus_factors):
        position = lax.axis_index("blk")
        side = lax.axis_index("group") % 2
        cells, rank = cell_factors.shape
        loci = locus_factors.shape[0]
        steps = (2.0 / (loci + rank), 2.0 / (cells + rank))
        work = 2 * cells * loci * rank
        place = (2 * position + side).reshape(1).astype(jnp.int32)
        wide, tall, turned = ((cells, rank), F32), ((loci, rank), F32), ((loci, cells), F32)
        part = ((loci // 2, rank), F32)
        state = [wide, ((loci, rank), HALF), ((loci, cells), HALF)]
        fetched = [pltpu.VMEM((cells, loci), HALF), pltpu.VMEM((cells, loci), jnp.int32)]

        for hop in range(HOPS):
            averaged = (hop + 1) % (HOPS // 2) == 0
            if hop == 0:
                u1, v1_half, r2, v2 = call(
                    functools.partial(start_body, steps, blocks),
                    (place, expression, observed, cell_factors, locus_factors),
                    "shhhh",
                    state + [tall],
                    [
                        pltpu.VMEM(turned[0], F32),
                        pltpu.VMEM(turned[0], F32),
                        *fetched,
                        pltpu.VMEM(wide[0], F32),
                        pltpu.VMEM(tall[0], F32),
                        pltpu.SemaphoreType.DMA((7,)),
                    ],
                    5 * work,
                )
                v2 = [v2]
            else:
                u1, v1_half, r2, *v2 = call(
                    functools.partial(visit_body, steps, len(parts)),
                    (u, *parts, tile, mask),
                    "v" * (3 + len(parts)),
                    state + ([part, part] if averaged else [tall]),
                    (),
                    5 * work,
                )
            if hop < HOPS - 1:
                u, tile, mask = call(
                    functools.partial(settle_body, steps, blocks, hop + 1, hop + 1 >= HOPS // 2),
                    (place, u1, v1_half, r2, expression, observed),
                    "svvvhh",
                    [wide, turned, turned],
                    fetched + [pltpu.SemaphoreType.DMA((4,))],
                    work,
                )
                pending = (u, tile, mask)
            else:
                pending = call(functools.partial(settle, steps), (u1, v1_half, r2), "vvv", [wide], (), work)
            if averaged:
                distance = 1 if hop < HOPS - 1 else 1 - HOPS
                *parts, pending = average(*v2, pending, blocks, groups, distance)
                u, *rest = pending
                if rest:
                    tile, mask = rest
            else:
                parts = [moved(v2[0], blocks, groups, 1)]
        low, high = parts
        return u, jnp.where(side == 0, jnp.concatenate([low, high], 0), jnp.concatenate([high, low], 0))

    split = P(AXES, None)
    return jax.shard_map(
        on_device,
        mesh=mesh,
        in_specs=(split, split, split, P("blk", None)),
        out_specs=(split, P("blk", None)),
        check_vma=False,
    )
```

time: 138 us -> 117 us (0.85)
  matrix products: 39.6 us -> 0 us
  Pallas kernels: 0 us -> 17.1 us
  waiting for transfers between devices: 81.6 us -> 91.9 us
  other arithmetic: 5.03 us -> 1.06 us
  starting transfers between devices: 8.62 us -> 5.88 us
    dot_general x72 -> x0, matrix products: 39.6 us -> none  [the longest x24 16 us: visit(): term = jnp.dot(residue, half, preferred_element_type=jnp.float32)]
    pallas_call x0 -> x12, Pallas kernels: none -> 17.1 us  [call(): pl.pallas_call(body, out_shape=[jax.ShapeDtypeStruct(shape, dtype) for sh...]
    ppermute x18 -> x14, waiting for transfers between devices: 81.6 us -> 91.9 us  [moved(): return lax.ppermute(block, AXES, route)]
    ppermute x18 -> x14, starting transfers between devices: 8.62 us -> 5.88 us  [moved(): return lax.ppermute(block, AXES, route)]
  transfers between devices with their start and end apart: 18 -> 14, of which waited for: 18 -> 14; matrix products, arithmetic and copies ran while one was open for 12% -> 0% of each run, Pallas kernels for 0% -> 7%
where the time goes in v6:
time: 117 us
  waiting for transfers between devices  91.9 us (79%)
  Pallas kernels  17.1 us (15%)
  starting transfers between devices  5.88 us (5%)
    ppermute x14, waiting for transfers between devices, moved(): return lax.ppermute(block, AXES, route)  91.9 us
    pallas_call x12, Pallas kernels, call(): pl.pallas_call(body, out_shape=[jax.ShapeDtypeStruct(shape, dtype) for sh...  17.1 us
    ppermute x14, starting transfers between devices, moved(): return lax.ppermute(block, AXES, route)  5.88 us
  transfers between devices with their start and end apart: 14, of which 14 were waited for; matrix products, arithmetic and copies ran while one was open for 0% of the time, Pallas kernels for 7%

profile of v6, /device:TPU:0, one launch (start us, length us, event | category | flops | bytes accessed | tf_op | source)
XLA Modules:
  0.0 116.8 jit_solution(452492329197214418)
XLA Ops:
  0.6 2.8 %shard_map.59 = (f32[384,512]{1,0:T(8,128)S(1)}, bf16[256,512]{1,0:T(8,128)(2,1)S(1)}, bf16[256,384]{1,0:T(8,128)(2,1)S(1)}, f32[256,512]{1,0:T(8,128)S(1)}) custom-call(s32[1]{0:T(128)} %bitcast.place, bf16[384,2048]{1,0:T(8,128)(2,1)} %x_hbm.11, s32[384,2048]{1,0:T(8,128)} %m_hbm.11, f32[384,512]{1,0:T(8,128)} %u_hbm.1, f32[256,512]{1,0:T(8,128)} %v_hbm.1), custom_call_target="tpu_custom_call" | custom-call | flops 503316480 | bytes 4194304 | tf_op jit(solution)/shard_map/pallas_call | solution.py:114
  3.5 3.0 %collective-permute-start = (f32[256,512]{1,0:T(8,128)S(1)}, f32[256,512]{1,0:T(8,128)S(1)}, u32[]{:S(2)}, u32[]{:S(2)}) collective-permute-start(f32[256,512]{1,0:T(8,128)S(1)} %get-tuple-element.53), channel_id=1, source_target_pairs={{0,4},{1,5},{2,6},{3,7},{4,8},{5,9},{6,10},{7,11},{8,12},{9,13},{1... | collective-permute-start | bytes 1572872 | tf_op jit(solution)/shard_map/ppermute | solution.py:131
  6.5 1.4 %shard_map.60 = (f32[384,512]{1,0:T(8,128)S(1)}, f32[256,384]{1,0:T(8,128)S(1)}, f32[256,384]{1,0:T(8,128)S(1)}) custom-call(s32[1]{0:T(128)} %bitcast.place, f32[384,512]{1,0:T(8,128)S(1)} %get-tuple-element.49.u1, bf16[256,512]{1,0:T(8,128)(2,1)S(1)} %get-tuple-element.50.v1_half, bf16[256,384]{1,0:T(8,128)(2,1)S(1)} %get-tuple-element.51.r2, ...), custom_call_target="tpu_custom_call" | custom-call | flops 100663296 | bytes 4194304 | tf_op jit(solution)/shard_map/pallas_call | solution.py:114
  8.0 13.5 %collective-permute-done.refs_0_ = f32[256,512]{1,0:T(8,128)S(1)} collective-permute-done((f32[256,512]{1,0:T(8,128)S(1)}, f32[256,512]{1,0:T(8,128)S(1)}, u32[]{:S(2)}, u32[]{:S(2)}) %collective-permute-start) | collective-permute-done | bytes 524320 | tf_op jit(solution)/shard_map/ppermute | solution.py:131
  21.5 1.2 %shard_map.61 = (f32[384,512]{1,0:T(8,128)S(1)}, bf16[256,512]{1,0:T(8,128)(2,1)S(1)}, bf16[256,384]{1,0:T(8,128)(2,1)S(1)}, f32[256,512]{1,0:T(8,128)S(1)}) custom-call(f32[384,512]{1,0:T(8,128)S(1)} %get-tuple-element.52.u, f32[256,512]{1,0:T(8,128)S(1)} %collective-permute-done.refs_0_, f32[256,384]{1,0:T(8,128)S(1)} %get-tuple-element.54.refs_1_, ...), custom_call_target="tpu_custom_call" | custom-call | flops 503316480 | bytes 4194304 | tf_op jit(solution)/shard_map/pallas_call | solution.py:114
  22.7 0.1 collective-permute-start.1
  22.7 1.4 %shard_map.62 = (f32[384,512]{1,0:T(8,128)S(1)}, f32[256,384]{1,0:T(8,128)S(1)}, f32[256,384]{1,0:T(8,128)S(1)}) custom-call(s32[1]{0:T(128)} %bitcast.place, f32[384,512]{1,0:T(8,128)S(1)} %get-tuple-element.56.u1, bf16[256,512]{1,0:T(8,128)(2,1)S(1)} %get-tuple-element.57.v1_half, bf16[256,384]{1,0:T(8,128)(2,1)S(1)} %get-tuple-element.58.r2, ...), custom_call_target="tpu_custom_call" | custom-call | flops 100663296 | bytes 4194304 | tf_op jit(solution)/shard_map/pallas_call | solution.py:114
  24.2 14.4 %collective-permute-done.1.refs_0_ = f32[256,512]{1,0:T(8,128)S(1)} collective-permute-done((f32[256,512]{1,0:T(8,128)S(1)}, f32[256,512]{1,0:T(8,128)S(1)}, u32[]{:S(2)}, u32[]{:S(2)}) %collective-permute-start.1) | collective-permute-done | bytes 524320 | tf_op jit(solution)/shard_map/ppermute | solution.py:131
  38.5 1.2 %shard_map.63 = (f32[384,512]{1,0:T(8,128)S(1)}, bf16[256,512]{1,0:T(8,128)(2,1)S(1)}, bf16[256,384]{1,0:T(8,128)(2,1)S(1)}, f32[128,512]{1,0:T(8,128)S(1)}, f32[128,512]{1,0:T(8,128)S(1)}) custom-call(f32[384,512]{1,0:T(8,128)S(1)} %get-tuple-element.59.u, f32[256,512]{1,0:T(8,128)S(1)} %collective-permute-done.1.refs_0_, ...), custom_call_target="tpu_custom_call" | custom-call | flops 503316480 | bytes 4194304 | tf_op jit(solution)/shard_map/pallas_call | solution.py:114
  39.7 0.1 collective-permute-start.2
  39.8 1.5 %collective-permute-done.2 = f32[128,512]{1,0:T(8,128)S(1)} collective-permute-done((f32[128,512]{1,0:T(8,128)S(1)}, f32[128,512]{1,0:T(8,128)S(1)}, u32[]{:S(2)}, u32[]{:S(2)}) %collective-permute-start.2) | collective-permute-done | bytes 262176 | tf_op jit(solution)/shard_map/ppermute | solution.py:131
  41.4 1.4 %collective-permute-start.3 = (f32[64,512]{1,0:T(8,128)S(1)}, f32[64,512]{1,0:T(8,128)S(1)}, u32[]{:S(2)}, u32[]{:S(2)}) collective-permute-start(f32[64,512]{1,0:T(8,128)S(1)} %slice_select_fusion.1), channel_id=1, source_target_pairs={{0,2},{1,3},{2,0},{3,1},{4,6},{5,7},{6,4},{7,5},{8,10},{9,11},{10,... | collective-permute-start | bytes 393224 | tf_op jit(solution)/shard_map/ppermute | solution.py:131
  42.8 1.4 %shard_map.64 = (f32[384,512]{1,0:T(8,128)S(1)}, f32[256,384]{1,0:T(8,128)S(1)}, f32[256,384]{1,0:T(8,128)S(1)}) custom-call(s32[1]{0:T(128)} %bitcast.place, f32[384,512]{1,0:T(8,128)S(1)} %get-tuple-element.65.u1, bf16[256,512]{1,0:T(8,128)(2,1)S(1)} %get-tuple-element.66.v1_half, bf16[256,384]{1,0:T(8,128)(2,1)S(1)} %get-tuple-element.67.r2, ...), custom_call_target="tpu_custom_call" | custom-call | flops 100663296 | bytes 4194304 | tf_op jit(solution)/shard_map/pallas_call | solution.py:114
  44.2 2.8 %collective-permute-done.3 = f32[64,512]{1,0:T(8,128)S(1)} collective-permute-done((f32[64,512]{1,0:T(8,128)S(1)}, f32[64,512]{1,0:T(8,128)S(1)}, u32[]{:S(2)}, u32[]{:S(2)}) %collective-permute-start.3) | collective-permute-done | bytes 131104 | tf_op jit(solution)/shard_map/ppermute | solution.py:131
  47.0 0.1 collective-permute-start.5
  47.1 0.1 collective-permute-start.4
  47.2 9.1 %collective-permute-done.5 = f32[64,512]{1,0:T(8,128)S(1)} collective-permute-done((f32[64,512]{1,0:T(8,128)S(1)}, f32[64,512]{1,0:T(8,128)S(1)}, u32[]{:S(2)}, u32[]{:S(2)}) %collective-permute-start.5) | collective-permute-done | bytes 131104 | tf_op jit(solution)/shard_map/ppermute | solution.py:131
  56.2 1.8 %collective-permute-done.4 = f32[64,512]{1,0:T(8,128)S(1)} collective-permute-done((f32[64,512]{1,0:T(8,128)S(1)}, f32[64,512]{1,0:T(8,128)S(1)}, u32[]{:S(2)}, u32[]{:S(2)}) %collective-permute-start.4) | collective-permute-done | bytes 131104 | tf_op jit(solution)/shard_map/ppermute | solution.py:131
  58.1 0.1 collective-permute-start.6
  58.2 1.5 %collective-permute-done.6.refs_1_ = f32[128,512]{1,0:T(8,128)S(1)} collective-permute-done((f32[128,512]{1,0:T(8,128)S(1)}, f32[128,512]{1,0:T(8,128)S(1)}, u32[]{:S(2)}, u32[]{:S(2)}) %collective-permute-start.6) | collective-permute-done | bytes 262176 | tf_op jit(solution)/shard_map/ppermute | solution.py:131
  59.7 1.2 %shard_map.65 = (f32[384,512]{1,0:T(8,128)S(1)}, bf16[256,512]{1,0:T(8,128)(2,1)S(1)}, bf16[256,384]{1,0:T(8,128)(2,1)S(1)}, f32[256,512]{1,0:T(8,128)S(1)}) custom-call(f32[384,512]{1,0:T(8,128)S(1)} %get-tuple-element.71.u, f32[128,512]{1,0:T(8,128)S(1)} %maximum_select_fusion.1.refs_0_, f32[128,512]{1,0:T(8,128)S(1)} %collective-permute-done.6.refs_1_, ...), custom_call_target="tpu_custom_call" | custom-call | flops 503316480 | bytes 4194304 | tf_op jit(solution)/shard_map/pallas_call | solution.py:114
  60.9 0.1 collective-permute-start.7
  61.0 1.4 %shard_map.66 = (f32[384,512]{1,0:T(8,128)S(1)}, f32[256,384]{1,0:T(8,128)S(1)}, f32[256,384]{1,0:T(8,128)S(1)}) custom-call(s32[1]{0:T(128)} %bitcast.place, f32[384,512]{1,0:T(8,128)S(1)} %get-tuple-element.75.u1, bf16[256,512]{1,0:T(8,128)(2,1)S(1)} %get-tuple-element.76.v1_half, bf16[256,384]{1,0:T(8,128)(2,1)S(1)} %get-tuple-element.77.r2, ...), custom_call_target="tpu_custom_call" | custom-call | flops 100663296 | bytes 4194304 | tf_op jit(solution)/shard_map/pallas_call | solution.py:114
  62.4 15.2 %collective-permute-done.7.refs_0_ = f32[256,512]{1,0:T(8,128)S(1)} collective-permute-done((f32[256,512]{1,0:T(8,128)S(1)}, f32[256,512]{1,0:T(8,128)S(1)}, u32[]{:S(2)}, u32[]{:S(2)}) %collective-permute-start.7) | collective-permute-done | bytes 524320 | tf_op jit(solution)/shard_map/ppermute | solution.py:131
  77.6 1.2 %shard_map.67 = (f32[384,512]{1,0:T(8,128)S(1)}, bf16[256,512]{1,0:T(8,128)(2,1)S(1)}, bf16[256,384]{1,0:T(8,128)(2,1)S(1)}, f32[256,512]{1,0:T(8,128)S(1)}) custom-call(f32[384,512]{1,0:T(8,128)S(1)} %get-tuple-element.78.u, f32[256,512]{1,0:T(8,128)S(1)} %collective-permute-done.7.refs_0_, f32[256,384]{1,0:T(8,128)S(1)} %get-tuple-element.80.refs_1_, ...), custom_call_target="tpu_custom_call" | custom-call | flops 503316480 | bytes 4194304 | tf_op jit(solution)/shard_map/pallas_call | solution.py:114
  78.8 0.1 collective-permute-start.8
  78.9 1.4 %shard_map.68 = (f32[384,512]{1,0:T(8,128)S(1)}, f32[256,384]{1,0:T(8,128)S(1)}, f32[256,384]{1,0:T(8,128)S(1)}) custom-call(s32[1]{0:T(128)} %bitcast.place, f32[384,512]{1,0:T(8,128)S(1)} %get-tuple-element.82.u1, bf16[256,512]{1,0:T(8,128)(2,1)S(1)} %get-tuple-element.83.v1_half, bf16[256,384]{1,0:T(8,128)(2,1)S(1)} %get-tuple-element.84.r2, ...), custom_call_target="tpu_custom_call" | custom-call | flops 100663296 | bytes 4194304 | tf_op jit(solution)/shard_map/pallas_call | solution.py:114
  80.3 14.4 %collective-permute-done.8.refs_0_ = f32[256,512]{1,0:T(8,128)S(1)} collective-permute-done((f32[256,512]{1,0:T(8,128)S(1)}, f32[256,512]{1,0:T(8,128)S(1)}, u32[]{:S(2)}, u32[]{:S(2)}) %collective-permute-start.8) | collective-permute-done | bytes 524320 | tf_op jit(solution)/shard_map/ppermute | solution.py:131
  94.7 1.2 %shard_map.69 = (f32[384,512]{1,0:T(8,128)S(1)}, bf16[256,512]{1,0:T(8,128)(2,1)S(1)}, bf16[256,384]{1,0:T(8,128)(2,1)S(1)}, f32[128,512]{1,0:T(8,128)S(1)}, f32[128,512]{1,0:T(8,128)S(1)}) custom-call(f32[384,512]{1,0:T(8,128)S(1)} %get-tuple-element.85.u, f32[256,512]{1,0:T(8,128)S(1)} %collective-permute-done.8.refs_0_, ...), custom_call_target="tpu_custom_call" | custom-call | flops 503316480 | bytes 4194304 | tf_op jit(solution)/shard_map/pallas_call | solution.py:114
  95.9 0.1 collective-permute-start.9
  96.0 1.5 %collective-permute-done.9 = f32[128,512]{1,0:T(8,128)S(1)} collective-permute-done((f32[128,512]{1,0:T(8,128)S(1)}, f32[128,512]{1,0:T(8,128)S(1)}, u32[]{:S(2)}, u32[]{:S(2)}) %collective-permute-start.9) | collective-permute-done | bytes 262176 | tf_op jit(solution)/shard_map/ppermute | solution.py:131
  97.5 0.8 collective-permute-start.10
  98.3 1.2 %shard_map.70 = f32[384,512]{1,0:T(8,128)} custom-call(f32[384,512]{1,0:T(8,128)S(1)} %get-tuple-element.91.u1, bf16[256,512]{1,0:T(8,128)(2,1)S(1)} %get-tuple-element.92.v1_half, bf16[256,384]{1,0:T(8,128)(2,1)S(1)} %get-tuple-element.93.r2), custom_call_target="tpu_custom_call" | custom-call | flops 100663296 | bytes 4194304 | tf_op jit(solution)/shard_map/pallas_call | solution.py:114
  99.5 3.7 %collective-permute-done.10 = f32[64,512]{1,0:T(8,128)S(1)} collective-permute-done((f32[64,512]{1,0:T(8,128)S(1)}, f32[64,512]{1,0:T(8,128)S(1)}, u32[]{:S(2)}, u32[]{:S(2)}) %collective-permute-start.10) | collective-permute-done | bytes 131104 | tf_op jit(solution)/shard_map/ppermute | solution.py:131
  103.2 0.1 collective-permute-start.12
  103.2 0.1 collective-permute-start.11
  103.3 8.2 %collective-permute-done.12 = f32[64,512]{1,0:T(8,128)S(1)} collective-permute-done((f32[64,512]{1,0:T(8,128)S(1)}, f32[64,512]{1,0:T(8,128)S(1)}, u32[]{:S(2)}, u32[]{:S(2)}) %collective-permute-start.12) | collective-permute-done | bytes 131104 | tf_op jit(solution)/shard_map/ppermute | solution.py:131
  111.5 2.9 %collective-permute-done.11 = f32[64,512]{1,0:T(8,128)S(1)} collective-permute-done((f32[64,512]{1,0:T(8,128)S(1)}, f32[64,512]{1,0:T(8,128)S(1)}, u32[]{:S(2)}, u32[]{:S(2)}) %collective-permute-start.11) | collective-permute-done | bytes 131104 | tf_op jit(solution)/shard_map/ppermute | solution.py:131
  114.4 0.1 collective-permute-start.13
  114.4 1.5 %collective-permute-done.13 = f32[128,512]{1,0:T(8,128)S(1)} collective-permute-done((f32[128,512]{1,0:T(8,128)S(1)}, f32[128,512]{1,0:T(8,128)S(1)}, u32[]{:S(2)}, u32[]{:S(2)}) %collective-permute-start.13) | collective-permute-done | bytes 262176 | tf_op jit(solution)/shard_map/ppermute | solution.py:131
  116.0 0.8 maximum_select_fusion
  (8 shorter events, 0.2 us)
Async XLA Ops:
  3.5 18.0 %collective-permute-start = (f32[256,512]{1,0:T(8,128)S(1)}, f32[256,512]{1,0:T(8,128)S(1)}, u32[]{:S(2)}, u32[]{:S(2)}) collective-permute-start(f32[256,512]{1,0:T(8,128)S(1)} %get-tuple-element.53), channel_id=1, source_target_pairs={{0,4},{1,5},{2,6},{3,7},{4,8},{5,9},{6,10},{7,11},{8,12},{9,13},{1... | collective-permute-start | bytes 1572872 | tf_op jit(solution)/shard_map/ppermute | solution.py:131
  22.7 15.9 %collective-permute-start.1 = (f32[256,512]{1,0:T(8,128)S(1)}, f32[256,512]{1,0:T(8,128)S(1)}, u32[]{:S(2)}, u32[]{:S(2)}) collective-permute-start(f32[256,512]{1,0:T(8,128)S(1)} %get-tuple-element.60), channel_id=1, source_target_pairs={{0,4},{1,5},{2,6},{3,7},{4,8},{5,9},{6,10},{7,11},{8,12},{9,13},{1... | collective-permute-start | bytes 1572872 | tf_op jit(solution)/shard_map/ppermute | solution.py:131
  39.7 1.6 %collective-permute-start.2 = (f32[128,512]{1,0:T(8,128)S(1)}, f32[128,512]{1,0:T(8,128)S(1)}, u32[]{:S(2)}, u32[]{:S(2)}) collective-permute-start(f32[128,512]{1,0:T(8,128)S(1)} %get-tuple-element.64), channel_id=1, source_target_pairs={{0,1},{1,0},{2,3},{3,2},{4,5},{5,4},{6,7},{7,6},{8,9},{9,8},{10,11... | collective-permute-start | bytes 786440 | tf_op jit(solution)/shard_map/ppermute | solution.py:131
  41.4 5.6 %collective-permute-start.3 = (f32[64,512]{1,0:T(8,128)S(1)}, f32[64,512]{1,0:T(8,128)S(1)}, u32[]{:S(2)}, u32[]{:S(2)}) collective-permute-start(f32[64,512]{1,0:T(8,128)S(1)} %slice_select_fusion.1), channel_id=1, source_target_pairs={{0,2},{1,3},{2,0},{3,1},{4,6},{5,7},{6,4},{7,5},{8,10},{9,11},{10,... | collective-permute-start | bytes 393224 | tf_op jit(solution)/shard_map/ppermute | solution.py:131
  47.0 9.2 %collective-permute-start.5 = (f32[64,512]{1,0:T(8,128)S(1)}, f32[64,512]{1,0:T(8,128)S(1)}, u32[]{:S(2)}, u32[]{:S(2)}) collective-permute-start(f32[64,512]{1,0:T(8,128)S(1)} %add_multiply_fusion.1), channel_id=1, source_target_pairs={{0,4},{1,5},{2,6},{3,7},{4,8},{5,9},{6,10},{7,11},{8,12},{9,13},{1... | collective-permute-start | bytes 393224 | tf_op jit(solution)/shard_map/ppermute | solution.py:131
  47.1 11.0 %collective-permute-start.4 = (f32[64,512]{1,0:T(8,128)S(1)}, f32[64,512]{1,0:T(8,128)S(1)}, u32[]{:S(2)}, u32[]{:S(2)}) collective-permute-start(f32[64,512]{1,0:T(8,128)S(1)} %add_multiply_fusion.1), channel_id=1, source_target_pairs={{0,6},{1,7},{2,4},{3,5},{4,10},{5,11},{6,8},{7,9},{8,14},{9,15},{1... | collective-permute-start | bytes 393224 | tf_op jit(solution)/shard_map/ppermute | solution.py:131
  58.1 1.6 %collective-permute-start.6 = (f32[128,512]{1,0:T(8,128)S(1)}, f32[128,512]{1,0:T(8,128)S(1)}, u32[]{:S(2)}, u32[]{:S(2)}) collective-permute-start(f32[128,512]{1,0:T(8,128)S(1)} %maximum_select_fusion.1.refs_0_), channel_id=1, source_target_pairs={{0,1},{1,0},{2,3},{3,2},{4,5},{5,4},{6,7},{7,6},{8,9},{9,8},{10,11... | collective-permute-start | bytes 786440 | tf_op jit(solution)/shard_map/ppermute | solution.py:131
  60.9 16.7 %collective-permute-start.7 = (f32[256,512]{1,0:T(8,128)S(1)}, f32[256,512]{1,0:T(8,128)S(1)}, u32[]{:S(2)}, u32[]{:S(2)}) collective-permute-start(f32[256,512]{1,0:T(8,128)S(1)} %get-tuple-element.79), channel_id=1, source_target_pairs={{0,4},{1,5},{2,6},{3,7},{4,8},{5,9},{6,10},{7,11},{8,12},{9,13},{1... | collective-permute-start | bytes 1572872 | tf_op jit(solution)/shard_map/ppermute | solution.py:131
  78.8 15.9 %collective-permute-start.8 = (f32[256,512]{1,0:T(8,128)S(1)}, f32[256,512]{1,0:T(8,128)S(1)}, u32[]{:S(2)}, u32[]{:S(2)}) collective-permute-start(f32[256,512]{1,0:T(8,128)S(1)} %get-tuple-element.86), channel_id=1, source_target_pairs={{0,4},{1,5},{2,6},{3,7},{4,8},{5,9},{6,10},{7,11},{8,12},{9,13},{1... | collective-permute-start | bytes 1572872 | tf_op jit(solution)/shard_map/ppermute | solution.py:131
  95.9 1.6 %collective-permute-start.9 = (f32[128,512]{1,0:T(8,128)S(1)}, f32[128,512]{1,0:T(8,128)S(1)}, u32[]{:S(2)}, u32[]{:S(2)}) collective-permute-start(f32[128,512]{1,0:T(8,128)S(1)} %get-tuple-element.90), channel_id=1, source_target_pairs={{0,1},{1,0},{2,3},{3,2},{4,5},{5,4},{6,7},{7,6},{8,9},{9,8},{10,11... | collective-permute-start | bytes 786440 | tf_op jit(solution)/shard_map/ppermute | solution.py:131
  97.5 5.6 %collective-permute-start.10 = (f32[64,512]{1,0:T(8,128)S(1)}, f32[64,512]{1,0:T(8,128)S(1)}, u32[]{:S(2)}, u32[]{:S(2)}) collective-permute-start(f32[64,512]{1,0:T(8,128)S(1)} %slice_select_fusion), channel_id=1, source_target_pairs={{0,2},{1,3},{2,0},{3,1},{4,6},{5,7},{6,4},{7,5},{8,10},{9,11},{10,... | collective-permute-start | bytes 393224 | tf_op jit(solution)/shard_map/ppermute | solution.py:131
  103.2 8.3 %collective-permute-start.12 = (f32[64,512]{1,0:T(8,128)S(1)}, f32[64,512]{1,0:T(8,128)S(1)}, u32[]{:S(2)}, u32[]{:S(2)}) collective-permute-start(f32[64,512]{1,0:T(8,128)S(1)} %add_multiply_fusion), channel_id=1, source_target_pairs={{0,12},{1,13},{2,14},{3,15},{4,16},{5,17},{6,18},{7,19},{8,20},{9,... | collective-permute-start | bytes 393224 | tf_op jit(solution)/shard_map/ppermute | solution.py:131
  103.2 11.1 %collective-permute-start.11 = (f32[64,512]{1,0:T(8,128)S(1)}, f32[64,512]{1,0:T(8,128)S(1)}, u32[]{:S(2)}, u32[]{:S(2)}) collective-permute-start(f32[64,512]{1,0:T(8,128)S(1)} %add_multiply_fusion), channel_id=1, source_target_pairs={{0,14},{1,15},{2,12},{3,13},{4,18},{5,19},{6,16},{7,17},{8,22},{9,... | collective-permute-start | bytes 393224 | tf_op jit(solution)/shard_map/ppermute | solution.py:131
  114.4 1.6 %collective-permute-start.13 = (f32[128,512]{1,0:T(8,128)S(1)}, f32[128,512]{1,0:T(8,128)S(1)}, u32[]{:S(2)}, u32[]{:S(2)}) collective-permute-start(f32[128,512]{1,0:T(8,128)S(1)} %maximum_select_fusion.2), channel_id=1, source_target_pairs={{0,1},{1,0},{2,3},{3,2},{4,5},{5,4},{6,7},{7,6},{8,9},{9,8},{10,11... | collective-permute-start | bytes 786440 | tf_op jit(solution)/shard_map/ppermute | solution.py:131

commit v7 on v6

--- a/solution.py
+++ b/solution.py
@@ -64,45 +64,76 @@
         row += out.shape[0]
 
 
-def start_body(steps, blocks, place, x_hbm, m_hbm, u_hbm, v_hbm, u1, v1_half, r2, v2, tile, mask, x, m, u, v, sems):
-    rows = v.shape[0] // 2
-    side = place[0] % 2
-    copies = tile_copies(first_columns(place, blocks, 0, False), x_hbm, m_hbm, x, m, sems)
-    inputs = [pltpu.make_async_copy(u_hbm, u, sems.at[4])]
-    for order, index in enumerate((side, 1 - side)):
-        source = pl.ds(pl.multiple_of(index * rows, rows), rows)
-        target = pl.ds(order * rows, rows)
-        inputs.append(pltpu.make_async_copy(v_hbm.at[source], v.at[target], sems.at[5 + order]))
-    for copy in copies + inputs:
+def parity(place):
+    return place[0] // 2 % 2
+
+
+def start_body(steps, blocks, turn, place, x_hbm, m_hbm, u_hbm, v_hbm, u1, v1_half, r2, v2, tile, mask, x, m, u, v, sems):
+    @pl.when(parity(place) == turn)
+    def _():
+        rows = v.shape[0] // 2
+        side = place[0] % 2
+        copies = tile_copies(first_columns(place, blocks, 0, False), x_hbm, m_hbm, x, m, sems)
+        inputs = [pltpu.make_async_copy(u_hbm, u, sems.at[4])]
+        for order, index in enumerate((side, 1 - side)):
+            source = pl.ds(pl.multiple_of(index * rows, rows), rows)
+            target = pl.ds(order * rows, rows)
+            inputs.append(pltpu.make_async_copy(v_hbm.at[source], v.at[target], sems.at[5 + order]))
+        for copy in copies + inputs:
+            copy.start()
+        for copy in copies:
+            copy.wait()
+        tile[...] = x[...].astype(F32).T
+        mask[...] = m[...].astype(F32).T
+        for copy in inputs:
+            copy.wait()
+        visit(steps, u[...], v[...], tile, mask, u1, v1_half, r2, (v2,))
+
+
+def turn_body(steps, turn, parts, place, u, *refs):
+    @pl.when(parity(place) == turn)
+    def _():
+        loci = jnp.concatenate([part[...] for part in refs[:parts]], 0)
+        tile, mask, u1, v1_half, r2, *v2 = refs[parts:]
+        visit(steps, u[...], loci, tile, mask, u1, v1_half, r2, v2)
+
+
+def visit_body(steps, place, u, even, odd, tile, mask, u1, v1_half, r2, *v2):
+    @pl.when(parity(place) == 0)
+    def _():
+        visit(steps, u[...], even[...], tile, mask, u1, v1_half, r2, v2)
+
+    @pl.when(parity(place) == 1)
+    def _():
+        visit(steps, u[...], odd[...], tile, mask, u1, v1_half, r2, v2)
+
+
+def settle(steps, place, states, u2):
+    for turn, (u1, v1_half, r2) in enumerate(states):
+
+        @pl.when(parity(place) == turn)
+        def _():
+            u2[...] = u1[...] + steps[0] * along(r2[...], v1_half[...])
+
+
+def settle_body(steps, blocks, hop, flip, count, place, *refs):
+    states, (x_hbm, m_hbm, u2, tile, mask, x, m, sems) = refs[: 3 * count], refs[3 * count :]
+    copies = tile_copies(first_columns(place, blocks, hop, flip), x_hbm, m_hbm, x, m, sems)
+    for copy in copies:
         copy.start()
+    if count == 1:
+        u1, v1_half, r2 = states
+        u2[...] = u1[...] + steps[0] * along(r2[...], v1_half[...])
+    else:
+        settle(steps, place, (states[:3], states[3:]), u2)
     for copy in copies:
         copy.wait()
     tile[...] = x[...].astype(F32).T
     mask[...] = m[...].astype(F32).T
-    for copy in inputs:
-        copy.wait()
-    visit(steps, u[...], v[...], tile, mask, u1, v1_half, r2, (v2,))
-
-
-def visit_body(steps, parts, u, *refs):
-    loci = jnp.concatenate([part[...] for part in refs[:parts]], 0)
-    tile, mask, u1, v1_half, r2, *v2 = refs[parts:]
-    visit(steps, u[...], loci, tile, mask, u1, v1_half, r2, v2)
-
-
-def settle(steps, u1, v1_half, r2, u2):
+
+
+def finish_body(steps, u1, v1_half, r2, u2):
     u2[...] = u1[...] + steps[0] * along(r2[...], v1_half[...])
-
-
-def settle_body(steps, blocks, hop, flip, place, u1, v1_half, r2, x_hbm, m_hbm, u2, tile, mask, x, m, sems):
-    copies = tile_copies(first_columns(place, blocks, hop, flip), x_hbm, m_hbm, x, m, sems)
-    for copy in copies:
-        copy.start()
-    settle(steps, u1, v1_half, r2, u2)
-    for copy in copies:
-        copy.wait()
-    tile[...] = x[...].astype(F32).T
-    mask[...] = m[...].astype(F32).T
 
 
 def call(body, args, spaces, outs, scratch=(), flops=0):
@@ -122,11 +153,12 @@
     )(*placed)
 
 
-def moved(block, blocks, groups, distance, flip=0):
+def moved(block, blocks, groups, distance, flip=0, senders=(0, 1)):
     route = [
         (b * groups + g, (b + distance) % blocks * groups + (g ^ flip))
         for b in range(blocks)
         for g in range(groups)
+        if b % 2 in senders
     ]
     return lax.ppermute(block, AXES, route)
 
@@ -173,55 +205,73 @@
         state = [wide, ((loci, rank), HALF), ((loci, cells), HALF)]
         fetched = [pltpu.VMEM((cells, loci), HALF), pltpu.VMEM((cells, loci), jnp.int32)]
 
+        def turns(u, parts, tile, mask):
+            states, gots = [], []
+            for turn in (1, 0):
+                if u is None:
+                    *state_of, v2 = call(
+                        functools.partial(start_body, steps, blocks, turn),
+                        (place, expression, observed, cell_factors, locus_factors),
+                        "shhhh",
+                        state + [tall],
+                        [
+                            pltpu.VMEM(turned[0], F32),
+                            pltpu.VMEM(turned[0], F32),
+                            *fetched,
+                            pltpu.VMEM(wide[0], F32),
+                            pltpu.VMEM(tall[0], F32),
+                            pltpu.SemaphoreType.DMA((7,)),
+                        ],
+                        5 * work,
+                    )
+                else:
+                    mine = parts[turn]
+                    *state_of, v2 = call(
+                        functools.partial(turn_body, steps, turn, len(mine)),
+                        (place, u, *mine, tile, mask),
+                        "s" + "v" * (3 + len(mine)),
+                        state + [tall],
+                        (),
+                        5 * work,
+                    )
+                states.append(state_of)
+                gots.append(moved(v2, blocks, groups, 1, senders=(turn,)))
+            return states[1] + states[0], gots
+
+        def settled(hop, states):
+            return call(
+                functools.partial(settle_body, steps, blocks, hop, hop >= HOPS // 2, len(states) // 3),
+                (place, *states, expression, observed),
+                "s" + "v" * len(states) + "hh",
+                [wide, turned, turned],
+                fetched + [pltpu.SemaphoreType.DMA((4,))],
+                work,
+            )
+
+        u = tile = mask = parts = None
         for hop in range(HOPS):
-            averaged = (hop + 1) % (HOPS // 2) == 0
-            if hop == 0:
-                u1, v1_half, r2, v2 = call(
-                    functools.partial(start_body, steps, blocks),
-                    (place, expression, observed, cell_factors, locus_factors),
-                    "shhhh",
-                    state + [tall],
-                    [
-                        pltpu.VMEM(turned[0], F32),
-                        pltpu.VMEM(turned[0], F32),
-                        *fetched,
-                        pltpu.VMEM(wide[0], F32),
-                        pltpu.VMEM(tall[0], F32),
-                        pltpu.SemaphoreType.DMA((7,)),
-                    ],
-                    5 * work,
-                )
-                v2 = [v2]
+            if (hop + 1) % (HOPS // 2):
+                states, (even, odd) = turns(u, parts, tile, mask)
+                u, tile, mask = settled(hop + 1, states)
+                parts = [even], [odd]
+                continue
+            u1, v1_half, r2, *v2 = call(
+                functools.partial(visit_body, steps),
+                (place, u, even, odd, tile, mask),
+                "svvvvv",
+                state + [part, part],
+                (),
+                5 * work,
+            )
+            if hop < HOPS - 1:
+                pending = settled(hop + 1, (u1, v1_half, r2))
             else:
-                u1, v1_half, r2, *v2 = call(
-                    functools.partial(visit_body, steps, len(parts)),
-                    (u, *parts, tile, mask),
-                    "v" * (3 + len(parts)),
-                    state + ([part, part] if averaged else [tall]),
-                    (),
-                    5 * work,
-                )
+                pending = call(functools.partial(finish_body, steps), (u1, v1_half, r2), "vvv", [wide], (), work)
+            distance = 1 if hop < HOPS - 1 else 1 - HOPS
+            *parts, pending = average(*v2, pending, blocks, groups, distance)
             if hop < HOPS - 1:
-                u, tile, mask = call(
-                    functools.partial(settle_body, steps, blocks, hop + 1, hop + 1 >= HOPS // 2),
-                    (place, u1, v1_half, r2, expression, observed),
-                    "svvvhh",
-                    [wide, turned, turned],
-                    fetched + [pltpu.SemaphoreType.DMA((4,))],
-                    work,
-                )
-                pending = (u, tile, mask)
-            else:
-                pending = call(functools.partial(settle, steps), (u1, v1_half, r2), "vvv", [wide], (), work)
-            if averaged:
-                distance = 1 if hop < HOPS - 1 else 1 - HOPS
-                *parts, pending = average(*v2, pending, blocks, groups, distance)
-                u, *rest = pending
-                if rest:
-                    tile, mask = rest
-            else:
-                parts = [moved(v2[0], blocks, groups, 1)]
-        low, high = parts
+                (u, tile, mask), parts = pending, (parts, parts)
+        (u,), (low, high) = pending, parts
         return u, jnp.where(side == 0, jnp.concatenate([low, high], 0), jnp.concatenate([high, low], 0))
 
     split = P(AXES, None)

time: 117 us -> 119 us (1.017)
  starting transfers between devices: 5.88 us -> 20.2 us
  waiting for transfers between devices: 91.9 us -> 79.1 us
    ppermute x14 -> x18, starting transfers between devices: 5.88 us -> 20.2 us  [moved(): return lax.ppermute(block, AXES, route)]
    ppermute x14 -> x18, waiting for transfers between devices: 91.9 us -> 79.1 us  [moved(): return lax.ppermute(block, AXES, route)]
    pallas_call x12 -> x16, Pallas kernels: 17.1 us -> 17.2 us  [call(): pl.pallas_call(body, out_shape=[jax.ShapeDtypeStruct(shape, dtype) for sh...]
  transfers between devices with their start and end apart: 14 -> 18, of which waited for: 14 -> 18; matrix products, arithmetic and copies ran while one was open for 0% -> 0% of each run, Pallas kernels for 7% -> 9%
where the time goes in v7:
time: 119 us; the launch traced here: 118 us
  waiting for transfers between devices  79.1 us (66%)
  starting transfers between devices  20.2 us (17%)
  Pallas kernels  17.2 us (14%)
    ppermute x18, waiting for transfers between devices, moved(): return lax.ppermute(block, AXES, route)  79.1 us
    ppermute x18, starting transfers between devices, moved(): return lax.ppermute(block, AXES, route)  20.2 us
    pallas_call x16, Pallas kernels, call(): pl.pallas_call(body, out_shape=[jax.ShapeDtypeStruct(shape, dtype) for sh...  17.2 us
  transfers between devices with their start and end apart: 18, of which 18 were waited for; matrix products, arithmetic and copies ran while one was open for 0% of the time, Pallas kernels for 9%

profile of v7, /device:TPU:0, one launch (start us, length us, event | category | flops | bytes accessed | tf_op | source)
XLA Modules:
  0.0 118.5 jit_solution(4552445513718016444)
XLA Ops:
  0.6 2.9 %shard_map.59 = (f32[384,512]{1,0:T(8,128)S(1)}, bf16[256,512]{1,0:T(8,128)(2,1)S(1)}, bf16[256,384]{1,0:T(8,128)(2,1)S(1)}, f32[256,512]{1,0:T(8,128)S(1)}) custom-call(s32[1]{0:T(128)} %bitcast.place, bf16[384,2048]{1,0:T(8,128)(2,1)} %refs_6_.7, s32[384,2048]{1,0:T(8,128)} %refs_7_.7, f32[384,512]{1,0:T(8,128)} %u_hbm.3, f32[256,512]{1,0:T(8,128)} %v_hbm.3), custom_call_target="tpu_custom_call" | custom-call | flops 503316480 | bytes 4194304 | tf_op jit(solution)/shard_map/pallas_call | solution.py:145
  3.5 2.1 %collective-permute-start.1 = (f32[256,512]{1,0:T(8,128)S(1)}, f32[256,512]{1,0:T(8,128)S(1)}, u32[]{:S(2)}, u32[]{:S(2)}) collective-permute-start(f32[256,512]{1,0:T(8,128)S(1)} %get-tuple-element.78), channel_id=1, source_target_pairs={{0,4},{1,5},{2,6},{3,7},{8,12},{9,13},{10,14},{11,15},{16,20},{17,... | collective-permute-start | bytes 1572872 | tf_op jit(solution)/shard_map/ppermute | solution.py:163
  5.6 0.1 shard_map.60
  5.7 1.3 %collective-permute-start = (f32[256,512]{1,0:T(8,128)S(1)}, f32[256,512]{1,0:T(8,128)S(1)}, u32[]{:S(2)}, u32[]{:S(2)}) collective-permute-start(f32[256,512]{1,0:T(8,128)S(1)} %get-tuple-element.72), channel_id=1, source_target_pairs={{4,8},{5,9},{6,10},{7,11},{12,16},{13,17},{14,18},{15,19},{20,24},... | collective-permute-start | bytes 1572872 | tf_op jit(solution)/shard_map/ppermute | solution.py:163
  7.0 1.4 %shard_map.61 = (f32[384,512]{1,0:T(8,128)S(1)}, f32[256,384]{1,0:T(8,128)S(1)}, f32[256,384]{1,0:T(8,128)S(1)}) custom-call(s32[1]{0:T(128)} %bitcast.place, f32[384,512]{1,0:T(8,128)S(1)} %get-tuple-element.65.refs_0_, bf16[256,512]{1,0:T(8,128)(2,1)S(1)} %get-tuple-element.66.refs_1_, bf16[256,384]{1,0:T(8,128)(2,1)S(1)} %get-tuple-element.67.refs_2_, ...), custom_call_target="tpu_custom_call" | custom-call | flops 100663296 | bytes 4194304 | tf_op jit(solution)/shard_map/pallas_call | solution.py:145
  8.5 8.4 %collective-permute-done.1.refs_0_ = f32[256,512]{1,0:T(8,128)S(1)} collective-permute-done((f32[256,512]{1,0:T(8,128)S(1)}, f32[256,512]{1,0:T(8,128)S(1)}, u32[]{:S(2)}, u32[]{:S(2)}) %collective-permute-start.1) | collective-permute-done | bytes 524320 | tf_op jit(solution)/shard_map/ppermute | solution.py:163
  16.9 1.3 %collective-permute-start.2 = (f32[256,512]{1,0:T(8,128)S(1)}, f32[256,512]{1,0:T(8,128)S(1)}, u32[]{:S(2)}, u32[]{:S(2)}) collective-permute-start(f32[256,512]{1,0:T(8,128)S(1)} %get-tuple-element.83), channel_id=1, source_target_pairs={{4,8},{5,9},{6,10},{7,11},{12,16},{13,17},{14,18},{15,19},{20,24},... | collective-permute-start | bytes 1572872 | tf_op jit(solution)/shard_map/ppermute | solution.py:163
  18.2 5.9 %collective-permute-done.refs_0_ = f32[256,512]{1,0:T(8,128)S(1)} collective-permute-done((f32[256,512]{1,0:T(8,128)S(1)}, f32[256,512]{1,0:T(8,128)S(1)}, u32[]{:S(2)}, u32[]{:S(2)}) %collective-permute-start) | collective-permute-done | bytes 524320 | tf_op jit(solution)/shard_map/ppermute | solution.py:163
  24.1 1.2 shard_map.62
  25.3 1.3 %collective-permute-start.3 = (f32[256,512]{1,0:T(8,128)S(1)}, f32[256,512]{1,0:T(8,128)S(1)}, u32[]{:S(2)}, u32[]{:S(2)}) collective-permute-start(f32[256,512]{1,0:T(8,128)S(1)} %get-tuple-element.84), channel_id=1, source_target_pairs={{0,4},{1,5},{2,6},{3,7},{8,12},{9,13},{10,14},{11,15},{16,20},{17,... | collective-permute-start | bytes 1572872 | tf_op jit(solution)/shard_map/ppermute | solution.py:163
  26.6 1.4 %shard_map.64 = (f32[384,512]{1,0:T(8,128)S(1)}, f32[256,384]{1,0:T(8,128)S(1)}, f32[256,384]{1,0:T(8,128)S(1)}) custom-call(s32[1]{0:T(128)} %bitcast.place, f32[384,512]{1,0:T(8,128)S(1)} %get-tuple-element.75.refs_0_, bf16[256,512]{1,0:T(8,128)(2,1)S(1)} %get-tuple-element.76.refs_1_, bf16[256,384]{1,0:T(8,128)(2,1)S(1)} %get-tuple-element.77.refs_2_, ...), custom_call_target="tpu_custom_call" | custom-call | flops 100663296 | bytes 4194304 | tf_op jit(solution)/shard_map/pallas_call | solution.py:145
  28.0 9.0 %collective-permute-done.2.even = f32[256,512]{1,0:T(8,128)S(1)} collective-permute-done((f32[256,512]{1,0:T(8,128)S(1)}, f32[256,512]{1,0:T(8,128)S(1)}, u32[]{:S(2)}, u32[]{:S(2)}) %collective-permute-start.2) | collective-permute-done | bytes 524320 | tf_op jit(solution)/shard_map/ppermute | solution.py:163
  37.1 0.2 collective-permute-done.3.odd
  37.3 1.2 %shard_map.65 = (f32[384,512]{1,0:T(8,128)S(1)}, bf16[256,512]{1,0:T(8,128)(2,1)S(1)}, bf16[256,384]{1,0:T(8,128)(2,1)S(1)}, f32[128,512]{1,0:T(8,128)S(1)}, f32[128,512]{1,0:T(8,128)S(1)}) custom-call(s32[1]{0:T(128)} %bitcast.place, f32[384,512]{1,0:T(8,128)S(1)} %get-tuple-element.82.u, f32[256,512]{1,0:T(8,128)S(1)} %collective-permute-done.2.even, ...), custom_call_target="tpu_custom_call" | custom-call | flops 503316480 | bytes 4194304 | tf_op jit(solution)/shard_map/pallas_call | solution.py:145
  38.6 1.5 %collective-permute-done.4 = f32[128,512]{1,0:T(8,128)S(1)} collective-permute-done((f32[128,512]{1,0:T(8,128)S(1)}, f32[128,512]{1,0:T(8,128)S(1)}, u32[]{:S(2)}, u32[]{:S(2)}) %collective-permute-start.4) | collective-permute-done | bytes 262176 | tf_op jit(solution)/shard_map/ppermute | solution.py:163
  40.2 1.9 %collective-permute-start.5 = (f32[64,512]{1,0:T(8,128)S(1)}, f32[64,512]{1,0:T(8,128)S(1)}, u32[]{:S(2)}, u32[]{:S(2)}) collective-permute-start(f32[64,512]{1,0:T(8,128)S(1)} %slice_select_fusion.1), channel_id=1, source_target_pairs={{0,2},{1,3},{2,0},{3,1},{4,6},{5,7},{6,4},{7,5},{8,10},{9,11},{10,... | collective-permute-start | bytes 393224 | tf_op jit(solution)/shard_map/ppermute | solution.py:163
  42.1 1.4 %shard_map.66 = (f32[384,512]{1,0:T(8,128)S(1)}, f32[256,384]{1,0:T(8,128)S(1)}, f32[256,384]{1,0:T(8,128)S(1)}) custom-call(s32[1]{0:T(128)} %bitcast.place, f32[384,512]{1,0:T(8,128)S(1)} %get-tuple-element.89.refs_0_, bf16[256,512]{1,0:T(8,128)(2,1)S(1)} %get-tuple-element.90.refs_1_, bf16[256,384]{1,0:T(8,128)(2,1)S(1)} %get-tuple-element.91.refs_2_, ...), custom_call_target="tpu_custom_call" | custom-call | flops 100663296 | bytes 4194304 | tf_op jit(solution)/shard_map/pallas_call | solution.py:145
  43.6 2.4 %collective-permute-done.5 = f32[64,512]{1,0:T(8,128)S(1)} collective-permute-done((f32[64,512]{1,0:T(8,128)S(1)}, f32[64,512]{1,0:T(8,128)S(1)}, u32[]{:S(2)}, u32[]{:S(2)}) %collective-permute-start.5) | collective-permute-done | bytes 131104 | tf_op jit(solution)/shard_map/ppermute | solution.py:163
  45.9 2.5 %collective-permute-start.7 = (f32[64,512]{1,0:T(8,128)S(1)}, f32[64,512]{1,0:T(8,128)S(1)}, u32[]{:S(2)}, u32[]{:S(2)}) collective-permute-start(f32[64,512]{1,0:T(8,128)S(1)} %add_multiply_fusion.1), channel_id=1, source_target_pairs={{0,4},{1,5},{2,6},{3,7},{4,8},{5,9},{6,10},{7,11},{8,12},{9,13},{1... | collective-permute-start | bytes 393224 | tf_op jit(solution)/shard_map/ppermute | solution.py:163
  48.5 1.2 %collective-permute-start.6 = (f32[64,512]{1,0:T(8,128)S(1)}, f32[64,512]{1,0:T(8,128)S(1)}, u32[]{:S(2)}, u32[]{:S(2)}) collective-permute-start(f32[64,512]{1,0:T(8,128)S(1)} %add_multiply_fusion.1), channel_id=1, source_target_pairs={{0,6},{1,7},{2,4},{3,5},{4,10},{5,11},{6,8},{7,9},{8,14},{9,15},{1... | collective-permute-start | bytes 393224 | tf_op jit(solution)/shard_map/ppermute | solution.py:163
  49.7 4.0 %collective-permute-done.7 = f32[64,512]{1,0:T(8,128)S(1)} collective-permute-done((f32[64,512]{1,0:T(8,128)S(1)}, f32[64,512]{1,0:T(8,128)S(1)}, u32[]{:S(2)}, u32[]{:S(2)}) %collective-permute-start.7) | collective-permute-done | bytes 131104 | tf_op jit(solution)/shard_map/ppermute | solution.py:163
  53.7 4.0 %collective-permute-done.6 = f32[64,512]{1,0:T(8,128)S(1)} collective-permute-done((f32[64,512]{1,0:T(8,128)S(1)}, f32[64,512]{1,0:T(8,128)S(1)}, u32[]{:S(2)}, u32[]{:S(2)}) %collective-permute-start.6) | collective-permute-done | bytes 131104 | tf_op jit(solution)/shard_map/ppermute | solution.py:163
  57.7 0.1 collective-permute-start.8
  57.8 1.5 %collective-permute-done.8.refs_1_ = f32[128,512]{1,0:T(8,128)S(1)} collective-permute-done((f32[128,512]{1,0:T(8,128)S(1)}, f32[128,512]{1,0:T(8,128)S(1)}, u32[]{:S(2)}, u32[]{:S(2)}) %collective-permute-start.8) | collective-permute-done | bytes 262176 | tf_op jit(solution)/shard_map/ppermute | solution.py:163
  59.3 1.2 %shard_map.67 = (f32[384,512]{1,0:T(8,128)S(1)}, bf16[256,512]{1,0:T(8,128)(2,1)S(1)}, bf16[256,384]{1,0:T(8,128)(2,1)S(1)}, f32[256,512]{1,0:T(8,128)S(1)}) custom-call(s32[1]{0:T(128)} %bitcast.place, f32[384,512]{1,0:T(8,128)S(1)} %get-tuple-element.95.u, f32[128,512]{1,0:T(8,128)S(1)} %maximum_select_fusion.1.refs_0_, ...), custom_call_target="tpu_custom_call" | custom-call | flops 503316480 | bytes 4194304 | tf_op jit(solution)/shard_map/pallas_call | solution.py:145
  60.5 1.3 %collective-permute-start.10 = (f32[256,512]{1,0:T(8,128)S(1)}, f32[256,512]{1,0:T(8,128)S(1)}, u32[]{:S(2)}, u32[]{:S(2)}) collective-permute-start(f32[256,512]{1,0:T(8,128)S(1)} %get-tuple-element.112), channel_id=1, source_target_pairs={{0,4},{1,5},{2,6},{3,7},{8,12},{9,13},{10,14},{11,15},{16,20},{17,... | collective-permute-start | bytes 1572872 | tf_op jit(solution)/shard_map/ppermute | solution.py:163
  61.8 1.3 %collective-permute-start.9 = (f32[256,512]{1,0:T(8,128)S(1)}, f32[256,512]{1,0:T(8,128)S(1)}, u32[]{:S(2)}, u32[]{:S(2)}) collective-permute-start(f32[256,512]{1,0:T(8,128)S(1)} %get-tuple-element.106), channel_id=1, source_target_pairs={{4,8},{5,9},{6,10},{7,11},{12,16},{13,17},{14,18},{15,19},{20,24},... | collective-permute-start | bytes 1572872 | tf_op jit(solution)/shard_map/ppermute | solution.py:163
  63.1 1.4 %shard_map.69 = (f32[384,512]{1,0:T(8,128)S(1)}, f32[256,384]{1,0:T(8,128)S(1)}, f32[256,384]{1,0:T(8,128)S(1)}) custom-call(s32[1]{0:T(128)} %bitcast.place, f32[384,512]{1,0:T(8,128)S(1)} %get-tuple-element.99.refs_0_, bf16[256,512]{1,0:T(8,128)(2,1)S(1)} %get-tuple-element.100.refs_1_, bf16[256,384]{1,0:T(8,128)(2,1)S(1)} %get-tuple-element.101.refs_2_, ...), custom_call_target="tpu_custom_call" | custom-call | flops 100663296 | bytes 4194304 | tf_op jit(solution)/shard_map/pallas_call | solution.py:145
  64.6 9.0 %collective-permute-done.10.refs_0_ = f32[256,512]{1,0:T(8,128)S(1)} collective-permute-done((f32[256,512]{1,0:T(8,128)S(1)}, f32[256,512]{1,0:T(8,128)S(1)}, u32[]{:S(2)}, u32[]{:S(2)}) %collective-permute-start.10) | collective-permute-done | bytes 524320 | tf_op jit(solution)/shard_map/ppermute | solution.py:163
  73.5 1.3 %collective-permute-start.11 = (f32[256,512]{1,0:T(8,128)S(1)}, f32[256,512]{1,0:T(8,128)S(1)}, u32[]{:S(2)}, u32[]{:S(2)}) collective-permute-start(f32[256,512]{1,0:T(8,128)S(1)} %get-tuple-element.117), channel_id=1, source_target_pairs={{4,8},{5,9},{6,10},{7,11},{12,16},{13,17},{14,18},{15,19},{20,24},... | collective-permute-start | bytes 1572872 | tf_op jit(solution)/shard_map/ppermute | solution.py:163
  74.8 5.6 %collective-permute-done.9.refs_0_ = f32[256,512]{1,0:T(8,128)S(1)} collective-permute-done((f32[256,512]{1,0:T(8,128)S(1)}, f32[256,512]{1,0:T(8,128)S(1)}, u32[]{:S(2)}, u32[]{:S(2)}) %collective-permute-start.9) | collective-permute-done | bytes 524320 | tf_op jit(solution)/shard_map/ppermute | solution.py:163
  80.4 1.2 %shard_map.70 = (f32[384,512]{1,0:T(8,128)S(1)}, bf16[256,512]{1,0:T(8,128)(2,1)S(1)}, bf16[256,384]{1,0:T(8,128)(2,1)S(1)}, f32[256,512]{1,0:T(8,128)S(1)}) custom-call(s32[1]{0:T(128)} %bitcast.place, f32[384,512]{1,0:T(8,128)S(1)} %get-tuple-element.105.u, f32[256,512]{1,0:T(8,128)S(1)} %collective-permute-done.9.refs_0_, ...), custom_call_target="tpu_custom_call" | custom-call | flops 503316480 | bytes 4194304 | tf_op jit(solution)/shard_map/pallas_call | solution.py:145
  81.6 1.3 %collective-permute-start.12 = (f32[256,512]{1,0:T(8,128)S(1)}, f32[256,512]{1,0:T(8,128)S(1)}, u32[]{:S(2)}, u32[]{:S(2)}) collective-permute-start(f32[256,512]{1,0:T(8,128)S(1)} %get-tuple-element.118), channel_id=1, source_target_pairs={{0,4},{1,5},{2,6},{3,7},{8,12},{9,13},{10,14},{11,15},{16,20},{17,... | collective-permute-start | bytes 1572872 | tf_op jit(solution)/shard_map/ppermute | solution.py:163
  82.9 1.4 %shard_map.72 = (f32[384,512]{1,0:T(8,128)S(1)}, f32[256,384]{1,0:T(8,128)S(1)}, f32[256,384]{1,0:T(8,128)S(1)}) custom-call(s32[1]{0:T(128)} %bitcast.place, f32[384,512]{1,0:T(8,128)S(1)} %get-tuple-element.109.refs_0_, bf16[256,512]{1,0:T(8,128)(2,1)S(1)} %get-tuple-element.110.refs_1_, bf16[256,384]{1,0:T(8,128)(2,1)S(1)} %get-tuple-element.111.refs_2_, ...), custom_call_target="tpu_custom_call" | custom-call | flops 100663296 | bytes 4194304 | tf_op jit(solution)/shard_map/pallas_call | solution.py:145
  84.3 7.3 %collective-permute-done.11.even = f32[256,512]{1,0:T(8,128)S(1)} collective-permute-done((f32[256,512]{1,0:T(8,128)S(1)}, f32[256,512]{1,0:T(8,128)S(1)}, u32[]{:S(2)}, u32[]{:S(2)}) %collective-permute-start.11) | collective-permute-done | bytes 524320 | tf_op jit(solution)/shard_map/ppermute | solution.py:163
  91.6 2.2 %collective-permute-done.12.odd = f32[256,512]{1,0:T(8,128)S(1)} collective-permute-done((f32[256,512]{1,0:T(8,128)S(1)}, f32[256,512]{1,0:T(8,128)S(1)}, u32[]{:S(2)}, u32[]{:S(2)}) %collective-permute-start.12) | collective-permute-done | bytes 524320 | tf_op jit(solution)/shard_map/ppermute | solution.py:163
  93.8 1.2 %shard_map.73 = (f32[384,512]{1,0:T(8,128)S(1)}, bf16[256,512]{1,0:T(8,128)(2,1)S(1)}, bf16[256,384]{1,0:T(8,128)(2,1)S(1)}, f32[128,512]{1,0:T(8,128)S(1)}, f32[128,512]{1,0:T(8,128)S(1)}) custom-call(s32[1]{0:T(128)} %bitcast.place, f32[384,512]{1,0:T(8,128)S(1)} %get-tuple-element.116.u, f32[256,512]{1,0:T(8,128)S(1)} %collective-permute-done.11.even, ...), custom_call_target="tpu_custom_call" | custom-call | flops 503316480 | bytes 4194304 | tf_op jit(solution)/shard_map/pallas_call | solution.py:145
  95.0 0.1 collective-permute-start.13
  95.1 1.5 %collective-permute-done.13 = f32[128,512]{1,0:T(8,128)S(1)} collective-permute-done((f32[128,512]{1,0:T(8,128)S(1)}, f32[128,512]{1,0:T(8,128)S(1)}, u32[]{:S(2)}, u32[]{:S(2)}) %collective-permute-start.13) | collective-permute-done | bytes 262176 | tf_op jit(solution)/shard_map/ppermute | solution.py:163
  96.7 1.2 %collective-permute-start.14 = (f32[64,512]{1,0:T(8,128)S(1)}, f32[64,512]{1,0:T(8,128)S(1)}, u32[]{:S(2)}, u32[]{:S(2)}) collective-permute-start(f32[64,512]{1,0:T(8,128)S(1)} %slice_select_fusion), channel_id=1, source_target_pairs={{0,2},{1,3},{2,0},{3,1},{4,6},{5,7},{6,4},{7,5},{8,10},{9,11},{10,... | collective-permute-start | bytes 393224 | tf_op jit(solution)/shard_map/ppermute | solution.py:163
  97.9 1.2 shard_map.74
  99.1 3.2 %collective-permute-done.14 = f32[64,512]{1,0:T(8,128)S(1)} collective-permute-done((f32[64,512]{1,0:T(8,128)S(1)}, f32[64,512]{1,0:T(8,128)S(1)}, u32[]{:S(2)}, u32[]{:S(2)}) %collective-permute-start.14) | collective-permute-done | bytes 131104 | tf_op jit(solution)/shard_map/ppermute | solution.py:163
  102.4 1.8 %collective-permute-start.15 = (f32[64,512]{1,0:T(8,128)S(1)}, f32[64,512]{1,0:T(8,128)S(1)}, u32[]{:S(2)}, u32[]{:S(2)}) collective-permute-start(f32[64,512]{1,0:T(8,128)S(1)} %add_multiply_fusion), channel_id=1, source_target_pairs={{0,14},{1,15},{2,12},{3,13},{4,18},{5,19},{6,16},{7,17},{8,22},{9,... | collective-permute-start | bytes 393224 | tf_op jit(solution)/shard_map/ppermute | solution.py:163
  104.2 8.6 %collective-permute-done.16 = f32[64,512]{1,0:T(8,128)S(1)} collective-permute-done((f32[64,512]{1,0:T(8,128)S(1)}, f32[64,512]{1,0:T(8,128)S(1)}, u32[]{:S(2)}, u32[]{:S(2)}) %collective-permute-start.16) | collective-permute-done | bytes 131104 | tf_op jit(solution)/shard_map/ppermute | solution.py:163
  112.7 3.3 %collective-permute-done.15 = f32[64,512]{1,0:T(8,128)S(1)} collective-permute-done((f32[64,512]{1,0:T(8,128)S(1)}, f32[64,512]{1,0:T(8,128)S(1)}, u32[]{:S(2)}, u32[]{:S(2)}) %collective-permute-start.15) | collective-permute-done | bytes 131104 | tf_op jit(solution)/shard_map/ppermute | solution.py:163
  116.0 0.1 collective-permute-start.17
  116.1 1.5 %collective-permute-done.17 = f32[128,512]{1,0:T(8,128)S(1)} collective-permute-done((f32[128,512]{1,0:T(8,128)S(1)}, f32[128,512]{1,0:T(8,128)S(1)}, u32[]{:S(2)}, u32[]{:S(2)}) %collective-permute-start.17) | collective-permute-done | bytes 262176 | tf_op jit(solution)/shard_map/ppermute | solution.py:163
  117.6 0.8 maximum_select_fusion
  (13 shorter events, 0.4 us)
Async XLA Ops:
  3.5 13.4 %collective-permute-start.1 = (f32[256,512]{1,0:T(8,128)S(1)}, f32[256,512]{1,0:T(8,128)S(1)}, u32[]{:S(2)}, u32[]{:S(2)}) collective-permute-start(f32[256,512]{1,0:T(8,128)S(1)} %get-tuple-element.78), channel_id=1, source_target_pairs={{0,4},{1,5},{2,6},{3,7},{8,12},{9,13},{10,14},{11,15},{16,20},{17,... | collective-permute-start | bytes 1572872 | tf_op jit(solution)/shard_map/ppermute | solution.py:163
  5.7 18.4 %collective-permute-start = (f32[256,512]{1,0:T(8,128)S(1)}, f32[256,512]{1,0:T(8,128)S(1)}, u32[]{:S(2)}, u32[]{:S(2)}) collective-permute-start(f32[256,512]{1,0:T(8,128)S(1)} %get-tuple-element.72), channel_id=1, source_target_pairs={{4,8},{5,9},{6,10},{7,11},{12,16},{13,17},{14,18},{15,19},{20,24},... | collective-permute-start | bytes 1572872 | tf_op jit(solution)/shard_map/ppermute | solution.py:163
  16.9 20.2 %collective-permute-start.2 = (f32[256,512]{1,0:T(8,128)S(1)}, f32[256,512]{1,0:T(8,128)S(1)}, u32[]{:S(2)}, u32[]{:S(2)}) collective-permute-start(f32[256,512]{1,0:T(8,128)S(1)} %get-tuple-element.83), channel_id=1, source_target_pairs={{4,8},{5,9},{6,10},{7,11},{12,16},{13,17},{14,18},{15,19},{20,24},... | collective-permute-start | bytes 1572872 | tf_op jit(solution)/shard_map/ppermute | solution.py:163
  25.3 12.0 %collective-permute-start.3 = (f32[256,512]{1,0:T(8,128)S(1)}, f32[256,512]{1,0:T(8,128)S(1)}, u32[]{:S(2)}, u32[]{:S(2)}) collective-permute-start(f32[256,512]{1,0:T(8,128)S(1)} %get-tuple-element.84), channel_id=1, source_target_pairs={{0,4},{1,5},{2,6},{3,7},{8,12},{9,13},{10,14},{11,15},{16,20},{17,... | collective-permute-start | bytes 1572872 | tf_op jit(solution)/shard_map/ppermute | solution.py:163
  38.5 1.6 %collective-permute-start.4 = (f32[128,512]{1,0:T(8,128)S(1)}, f32[128,512]{1,0:T(8,128)S(1)}, u32[]{:S(2)}, u32[]{:S(2)}) collective-permute-start(f32[128,512]{1,0:T(8,128)S(1)} %get-tuple-element.88), channel_id=1, source_target_pairs={{0,1},{1,0},{2,3},{3,2},{4,5},{5,4},{6,7},{7,6},{8,9},{9,8},{10,11... | collective-permute-start | bytes 786440 | tf_op jit(solution)/shard_map/ppermute | solution.py:163
  40.2 5.7 %collective-permute-start.5 = (f32[64,512]{1,0:T(8,128)S(1)}, f32[64,512]{1,0:T(8,128)S(1)}, u32[]{:S(2)}, u32[]{:S(2)}) collective-permute-start(f32[64,512]{1,0:T(8,128)S(1)} %slice_select_fusion.1), channel_id=1, source_target_pairs={{0,2},{1,3},{2,0},{3,1},{4,6},{5,7},{6,4},{7,5},{8,10},{9,11},{10,... | collective-permute-start | bytes 393224 | tf_op jit(solution)/shard_map/ppermute | solution.py:163
  45.9 7.7 %collective-permute-start.7 = (f32[64,512]{1,0:T(8,128)S(1)}, f32[64,512]{1,0:T(8,128)S(1)}, u32[]{:S(2)}, u32[]{:S(2)}) collective-permute-start(f32[64,512]{1,0:T(8,128)S(1)} %add_multiply_fusion.1), channel_id=1, source_target_pairs={{0,4},{1,5},{2,6},{3,7},{4,8},{5,9},{6,10},{7,11},{8,12},{9,13},{1... | collective-permute-start | bytes 393224 | tf_op jit(solution)/shard_map/ppermute | solution.py:163
  48.5 9.2 %collective-permute-start.6 = (f32[64,512]{1,0:T(8,128)S(1)}, f32[64,512]{1,0:T(8,128)S(1)}, u32[]{:S(2)}, u32[]{:S(2)}) collective-permute-start(f32[64,512]{1,0:T(8,128)S(1)} %add_multiply_fusion.1), channel_id=1, source_target_pairs={{0,6},{1,7},{2,4},{3,5},{4,10},{5,11},{6,8},{7,9},{8,14},{9,15},{1... | collective-permute-start | bytes 393224 | tf_op jit(solution)/shard_map/ppermute | solution.py:163
  57.7 1.6 %collective-permute-start.8 = (f32[128,512]{1,0:T(8,128)S(1)}, f32[128,512]{1,0:T(8,128)S(1)}, u32[]{:S(2)}, u32[]{:S(2)}) collective-permute-start(f32[128,512]{1,0:T(8,128)S(1)} %maximum_select_fusion.1.refs_0_), channel_id=1, source_target_pairs={{0,1},{1,0},{2,3},{3,2},{4,5},{5,4},{6,7},{7,6},{8,9},{9,8},{10,11... | collective-permute-start | bytes 786440 | tf_op jit(solution)/shard_map/ppermute | solution.py:163
  60.5 13.0 %collective-permute-start.10 = (f32[256,512]{1,0:T(8,128)S(1)}, f32[256,512]{1,0:T(8,128)S(1)}, u32[]{:S(2)}, u32[]{:S(2)}) collective-permute-start(f32[256,512]{1,0:T(8,128)S(1)} %get-tuple-element.112), channel_id=1, source_target_pairs={{0,4},{1,5},{2,6},{3,7},{8,12},{9,13},{10,14},{11,15},{16,20},{17,... | collective-permute-start | bytes 1572872 | tf_op jit(solution)/shard_map/ppermute | solution.py:163
  61.8 18.6 %collective-permute-start.9 = (f32[256,512]{1,0:T(8,128)S(1)}, f32[256,512]{1,0:T(8,128)S(1)}, u32[]{:S(2)}, u32[]{:S(2)}) collective-permute-start(f32[256,512]{1,0:T(8,128)S(1)} %get-tuple-element.106), channel_id=1, source_target_pairs={{4,8},{5,9},{6,10},{7,11},{12,16},{13,17},{14,18},{15,19},{20,24},... | collective-permute-start | bytes 1572872 | tf_op jit(solution)/shard_map/ppermute | solution.py:163
  73.5 18.1 %collective-permute-start.11 = (f32[256,512]{1,0:T(8,128)S(1)}, f32[256,512]{1,0:T(8,128)S(1)}, u32[]{:S(2)}, u32[]{:S(2)}) collective-permute-start(f32[256,512]{1,0:T(8,128)S(1)} %get-tuple-element.117), channel_id=1, source_target_pairs={{4,8},{5,9},{6,10},{7,11},{12,16},{13,17},{14,18},{15,19},{20,24},... | collective-permute-start | bytes 1572872 | tf_op jit(solution)/shard_map/ppermute | solution.py:163
  81.6 12.2 %collective-permute-start.12 = (f32[256,512]{1,0:T(8,128)S(1)}, f32[256,512]{1,0:T(8,128)S(1)}, u32[]{:S(2)}, u32[]{:S(2)}) collective-permute-start(f32[256,512]{1,0:T(8,128)S(1)} %get-tuple-element.118), channel_id=1, source_target_pairs={{0,4},{1,5},{2,6},{3,7},{8,12},{9,13},{10,14},{11,15},{16,20},{17,... | collective-permute-start | bytes 1572872 | tf_op jit(solution)/shard_map/ppermute | solution.py:163
  95.0 1.6 %collective-permute-start.13 = (f32[128,512]{1,0:T(8,128)S(1)}, f32[128,512]{1,0:T(8,128)S(1)}, u32[]{:S(2)}, u32[]{:S(2)}) collective-permute-start(f32[128,512]{1,0:T(8,128)S(1)} %get-tuple-element.122), channel_id=1, source_target_pairs={{0,1},{1,0},{2,3},{3,2},{4,5},{5,4},{6,7},{7,6},{8,9},{9,8},{10,11... | collective-permute-start | bytes 786440 | tf_op jit(solution)/shard_map/ppermute | solution.py:163
  96.7 5.6 %collective-permute-start.14 = (f32[64,512]{1,0:T(8,128)S(1)}, f32[64,512]{1,0:T(8,128)S(1)}, u32[]{:S(2)}, u32[]{:S(2)}) collective-permute-start(f32[64,512]{1,0:T(8,128)S(1)} %slice_select_fusion), channel_id=1, source_target_pairs={{0,2},{1,3},{2,0},{3,1},{4,6},{5,7},{6,4},{7,5},{8,10},{9,11},{10,... | collective-permute-start | bytes 393224 | tf_op jit(solution)/shard_map/ppermute | solution.py:163
  102.3 10.4 %collective-permute-start.16 = (f32[64,512]{1,0:T(8,128)S(1)}, f32[64,512]{1,0:T(8,128)S(1)}, u32[]{:S(2)}, u32[]{:S(2)}) collective-permute-start(f32[64,512]{1,0:T(8,128)S(1)} %add_multiply_fusion), channel_id=1, source_target_pairs={{0,12},{1,13},{2,14},{3,15},{4,16},{5,17},{6,18},{7,19},{8,20},{9,... | collective-permute-start | bytes 393224 | tf_op jit(solution)/shard_map/ppermute | solution.py:163
  102.4 13.6 %collective-permute-start.15 = (f32[64,512]{1,0:T(8,128)S(1)}, f32[64,512]{1,0:T(8,128)S(1)}, u32[]{:S(2)}, u32[]{:S(2)}) collective-permute-start(f32[64,512]{1,0:T(8,128)S(1)} %add_multiply_fusion), channel_id=1, source_target_pairs={{0,14},{1,15},{2,12},{3,13},{4,18},{5,19},{6,16},{7,17},{8,22},{9,... | collective-permute-start | bytes 393224 | tf_op jit(solution)/shard_map/ppermute | solution.py:163
  116.0 1.6 %collective-permute-start.17 = (f32[128,512]{1,0:T(8,128)S(1)}, f32[128,512]{1,0:T(8,128)S(1)}, u32[]{:S(2)}, u32[]{:S(2)}) collective-permute-start(f32[128,512]{1,0:T(8,128)S(1)} %maximum_select_fusion.2), channel_id=1, source_target_pairs={{0,1},{1,0},{2,3},{3,2},{4,5},{5,4},{6,7},{7,6},{8,9},{9,8},{10,11... | collective-permute-start | bytes 786440 | tf_op jit(solution)/shard_map/ppermute | solution.py:163

commit v8 on v6

--- a/solution.py
+++ b/solution.py
@@ -43,25 +43,34 @@
     return copies
 
 
-def residue(tile, mask, cell_half, locus_half):
-    return (mask[...] * (tile[...] - across(locus_half, cell_half))).astype(HALF)
-
-
-def visit(steps, cells, loci, tile, mask, u1, v1_half, r2, v2):
+def residue(tile, mask, predicted):
+    return (mask * (tile - predicted)).astype(HALF)
+
+
+def visit(steps, cells, loci, tile, mask, u1, v1_half, r2, v2, fetch=lambda: None):
     cell_half, locus_half = cells.astype(HALF), loci.astype(HALF)
-    r = residue(tile, mask, cell_half, locus_half)
+    predicted = across(locus_half, cell_half)
+    fetch()
+    r = residue(tile[...], mask[...], predicted)
     cells = cells + steps[0] * along(r, locus_half)
     u1[...] = cells
     loci = loci + steps[1] * times(r, cell_half)
     cell_half, locus_half = cells.astype(HALF), loci.astype(HALF)
     v1_half[...] = locus_half
-    r = residue(tile, mask, cell_half, locus_half)
+    rows = v2[0].shape[0]
+    r = residue(tile[:rows], mask[:rows], across(locus_half[:rows], cell_half))
     r2[...] = r
-    loci = loci + steps[1] * times(r, cell_half)
-    row = 0
-    for out in v2:
-        out[...] = loci[row : row + out.shape[0]]
-        row += out.shape[0]
+    v2[0][...] = loci[:rows] + steps[1] * times(r, cell_half)
+    for v1 in v2[1:]:
+        v1[...] = loci[rows:]
+
+
+def rest_body(steps, u1, v1_half, v1, tile, mask, r2, v2):
+    rows = v1.shape[0]
+    cell_half = u1[...].astype(HALF)
+    r = residue(tile[rows:], mask[rows:], across(v1_half[rows:], cell_half))
+    r2[...] = r
+    v2[...] = v1[...] + steps[1] * times(r, cell_half)
 
 
 def start_body(steps, blocks, place, x_hbm, m_hbm, u_hbm, v_hbm, u1, v1_half, r2, v2, tile, mask, x, m, u, v, sems):
@@ -73,15 +82,18 @@
         source = pl.ds(pl.multiple_of(index * rows, rows), rows)
         target = pl.ds(order * rows, rows)
         inputs.append(pltpu.make_async_copy(v_hbm.at[source], v.at[target], sems.at[5 + order]))
-    for copy in copies + inputs:
+    for copy in inputs + copies:
         copy.start()
-    for copy in copies:
-        copy.wait()
-    tile[...] = x[...].astype(F32).T
-    mask[...] = m[...].astype(F32).T
+
+    def fetch():
+        for copy in copies:
+            copy.wait()
+        tile[...] = x[...].astype(F32).T
+        mask[...] = m[...].astype(F32).T
+
     for copy in inputs:
         copy.wait()
-    visit(steps, u[...], v[...], tile, mask, u1, v1_half, r2, (v2,))
+    visit(steps, u[...], v[...], tile, mask, u1, v1_half, r2, (v2,), fetch)
 
 
 def visit_body(steps, parts, u, *refs):
@@ -90,22 +102,42 @@
     visit(steps, u[...], loci, tile, mask, u1, v1_half, r2, v2)
 
 
-def settle(steps, u1, v1_half, r2, u2):
-    u2[...] = u1[...] + steps[0] * along(r2[...], v1_half[...])
-
-
-def settle_body(steps, blocks, hop, flip, place, u1, v1_half, r2, x_hbm, m_hbm, u2, tile, mask, x, m, sems):
+def settle(steps, u1, v1_half, residues, u2):
+    r2 = residues[0][...] if len(residues) == 1 else jnp.concatenate([r[...] for r in residues], 0)
+    u2[...] = u1[...] + steps[0] * along(r2, v1_half[...])
+
+
+def settle_body(steps, blocks, hop, flip, place, u1, v1_half, *refs):
+    *residues, x_hbm, m_hbm, u2, tile, mask, x, m, sems = refs
     copies = tile_copies(first_columns(place, blocks, hop, flip), x_hbm, m_hbm, x, m, sems)
     for copy in copies:
         copy.start()
-    settle(steps, u1, v1_half, r2, u2)
+    settle(steps, u1, v1_half, residues, u2)
     for copy in copies:
         copy.wait()
     tile[...] = x[...].astype(F32).T
     mask[...] = m[...].astype(F32).T
 
 
-def call(body, args, spaces, outs, scratch=(), flops=0):
+def finish_body(steps, u1, v1_half, *refs):
+    *residues, u2 = refs
+    settle(steps, u1, v1_half, residues, u2)
+
+
+def store_body(place, first, second, out, sems):
+    rows = first.shape[0]
+    side = place[0] % 2
+    copies = []
+    for order, (half, index) in enumerate(((first, side), (second, 1 - side))):
+        target = pl.ds(pl.multiple_of(index * rows, rows), rows)
+        copies.append(pltpu.make_async_copy(half, out.at[target], sems.at[order]))
+    for copy in copies:
+        copy.start()
+    for copy in copies:
+        copy.wait()
+
+
+def call(body, args, spaces, outs, scratch=(), flops=0, made=pltpu.VMEM):
     kinds = {"v": pltpu.VMEM, "h": pltpu.HBM, "s": pltpu.SMEM}
     placed = [
         a if s == "s" else pltpu.with_memory_space_constraint(a, kinds[s])
@@ -115,7 +147,7 @@
         body,
         out_shape=[jax.ShapeDtypeStruct(shape, dtype) for shape, dtype in outs],
         in_specs=[pl.BlockSpec(memory_space=kinds[s]) for s in spaces],
-        out_specs=[pl.BlockSpec(memory_space=pltpu.VMEM) for _ in outs],
+        out_specs=[pl.BlockSpec(memory_space=made) for _ in outs],
         scratch_shapes=list(scratch),
         compiler_params=pltpu.CompilerParams(vmem_limit_bytes=12 << 20),
         cost_estimate=pl.CostEstimate(flops=flops, bytes_accessed=4 << 20, transcendentals=0),
@@ -193,6 +225,10 @@
                 )
                 v2 = [v2]
             else:
+                if averaged:
+                    state = [wide, ((loci, rank), HALF), ((loci // 2, cells), HALF)]
+                else:
+                    state = [wide, ((loci, rank), HALF), ((loci, cells), HALF)]
                 u1, v1_half, r2, *v2 = call(
                     functools.partial(visit_body, steps, len(parts)),
                     (u, *parts, tile, mask),
@@ -201,18 +237,31 @@
                     (),
                     5 * work,
                 )
+            residues = [r2]
+            if averaged:
+                va2, vb1 = v2
+                r2b, vb2 = call(
+                    functools.partial(rest_body, steps),
+                    (u1, v1_half, vb1, tile, mask),
+                    "vvvvv",
+                    [((loci // 2, cells), HALF), part],
+                    (),
+                    work,
+                )
+                v2 = [va2, vb2]
+                residues = [r2, r2b]
             if hop < HOPS - 1:
                 u, tile, mask = call(
                     functools.partial(settle_body, steps, blocks, hop + 1, hop + 1 >= HOPS // 2),
-                    (place, u1, v1_half, r2, expression, observed),
-                    "svvvhh",
+                    (place, u1, v1_half, *residues, expression, observed),
+                    "svv" + "v" * len(residues) + "hh",
                     [wide, turned, turned],
                     fetched + [pltpu.SemaphoreType.DMA((4,))],
                     work,
                 )
                 pending = (u, tile, mask)
             else:
-                pending = call(functools.partial(settle, steps), (u1, v1_half, r2), "vvv", [wide], (), work)
+                pending = call(functools.partial(finish_body, steps), (u1, v1_half, *residues), "vvvv", [wide], (), work)
             if averaged:
                 distance = 1 if hop < HOPS - 1 else 1 - HOPS
                 *parts, pending = average(*v2, pending, blocks, groups, distance)
@@ -221,8 +270,10 @@
                     tile, mask = rest
             else:
                 parts = [moved(v2[0], blocks, groups, 1)]
-        low, high = parts
-        return u, jnp.where(side == 0, jnp.concatenate([low, high], 0), jnp.concatenate([high, low], 0))
+        (whole,) = call(
+            store_body, (place, *parts), "svv", [tall], [pltpu.SemaphoreType.DMA((2,))], made=pltpu.HBM
+        )
+        return u, whole
 
     split = P(AXES, None)
     return jax.shard_map(

time: 117 us -> 117 us (level)
  Pallas kernels: 17.1 us -> 18.7 us
    pallas_call x12 -> x15, Pallas kernels: 17.1 us -> 18.7 us  [call(): pl.pallas_call(body, out_shape=[jax.ShapeDtypeStruct(shape, dtype) for sh...]
  transfers between devices with their start and end apart: 14 -> 14, of which waited for: 14 -> 14; matrix products, arithmetic and copies ran while one was open for 0% -> 0% of each run, Pallas kernels for 7% -> 8%
where the time goes in v8:
time: 117 us; the launch traced here: 116 us
  waiting for transfers between devices  90.9 us (78%)
  Pallas kernels  18.7 us (16%)
  starting transfers between devices  5.88 us (5%)
    ppermute x14, waiting for transfers between devices, moved(): return lax.ppermute(block, AXES, route)  90.9 us
    pallas_call x15, Pallas kernels, call(): pl.pallas_call(body, out_shape=[jax.ShapeDtypeStruct(shape, dtype) for sh...  18.7 us
    ppermute x14, starting transfers between devices, moved(): return lax.ppermute(block, AXES, route)  5.88 us
  transfers between devices with their start and end apart: 14, of which 14 were waited for; matrix products, arithmetic and copies ran while one was open for 0% of the time, Pallas kernels for 8%

profile of v8, /device:TPU:0, one launch (start us, length us, event | category | flops | bytes accessed | tf_op | source)
XLA Modules:
  0.0 116.5 jit_solution(8345286548879882297)
XLA Ops:
  0.6 2.8 %shard_map.59 = (f32[384,512]{1,0:T(8,128)S(1)}, bf16[256,512]{1,0:T(8,128)(2,1)S(1)}, bf16[256,384]{1,0:T(8,128)(2,1)S(1)}, f32[256,512]{1,0:T(8,128)S(1)}) custom-call(s32[1]{0:T(128)} %bitcast.place, bf16[384,2048]{1,0:T(8,128)(2,1)} %refs_1_.7, s32[384,2048]{1,0:T(8,128)} %refs_2_.9, f32[384,512]{1,0:T(8,128)} %u_hbm.1, f32[256,512]{1,0:T(8,128)} %v_hbm.1), custom_call_target="tpu_custom_call" | custom-call | flops 503316480 | bytes 4194304 | tf_op jit(solution)/shard_map/pallas_call | solution.py:146
  3.4 3.0 %collective-permute-start = (f32[256,512]{1,0:T(8,128)S(1)}, f32[256,512]{1,0:T(8,128)S(1)}, u32[]{:S(2)}, u32[]{:S(2)}) collective-permute-start(f32[256,512]{1,0:T(8,128)S(1)} %get-tuple-element.57), channel_id=1, source_target_pairs={{0,4},{1,5},{2,6},{3,7},{4,8},{5,9},{6,10},{7,11},{8,12},{9,13},{1... | collective-permute-start | bytes 1572872 | tf_op jit(solution)/shard_map/ppermute | solution.py:163
  6.5 1.4 %shard_map.60 = (f32[384,512]{1,0:T(8,128)S(1)}, f32[256,384]{1,0:T(8,128)S(1)}, f32[256,384]{1,0:T(8,128)S(1)}) custom-call(s32[1]{0:T(128)} %bitcast.place, f32[384,512]{1,0:T(8,128)S(1)} %get-tuple-element.53.u1, bf16[256,512]{1,0:T(8,128)(2,1)S(1)} %get-tuple-element.54.v1_half, bf16[256,384]{1,0:T(8,128)(2,1)S(1)} %get-tuple-element.55.refs_0_, ...), custom_call_target="tpu_custom_call" | custom-call | flops 100663296 | bytes 4194304 | tf_op jit(solution)/shard_map/pallas_call | solution.py:146
  7.9 13.5 %collective-permute-done.refs_0_ = f32[256,512]{1,0:T(8,128)S(1)} collective-permute-done((f32[256,512]{1,0:T(8,128)S(1)}, f32[256,512]{1,0:T(8,128)S(1)}, u32[]{:S(2)}, u32[]{:S(2)}) %collective-permute-start) | collective-permute-done | bytes 524320 | tf_op jit(solution)/shard_map/ppermute | solution.py:163
  21.4 1.2 %shard_map.61 = (f32[384,512]{1,0:T(8,128)S(1)}, bf16[256,512]{1,0:T(8,128)(2,1)S(1)}, bf16[256,384]{1,0:T(8,128)(2,1)S(1)}, f32[256,512]{1,0:T(8,128)S(1)}) custom-call(f32[384,512]{1,0:T(8,128)S(1)} %get-tuple-element.56.u, f32[256,512]{1,0:T(8,128)S(1)} %collective-permute-done.refs_0_, f32[256,384]{1,0:T(8,128)S(1)} %get-tuple-element.58.refs_1_, ...), custom_call_target="tpu_custom_call" | custom-call | flops 503316480 | bytes 4194304 | tf_op jit(solution)/shard_map/pallas_call | solution.py:146
  22.6 0.1 collective-permute-start.1
  22.7 1.4 %shard_map.62 = (f32[384,512]{1,0:T(8,128)S(1)}, f32[256,384]{1,0:T(8,128)S(1)}, f32[256,384]{1,0:T(8,128)S(1)}) custom-call(s32[1]{0:T(128)} %bitcast.place, f32[384,512]{1,0:T(8,128)S(1)} %get-tuple-element.60.u1, bf16[256,512]{1,0:T(8,128)(2,1)S(1)} %get-tuple-element.61.v1_half, bf16[256,384]{1,0:T(8,128)(2,1)S(1)} %get-tuple-element.62.refs_0_, ...), custom_call_target="tpu_custom_call" | custom-call | flops 100663296 | bytes 4194304 | tf_op jit(solution)/shard_map/pallas_call | solution.py:146
  24.1 14.3 %collective-permute-done.1.refs_0_ = f32[256,512]{1,0:T(8,128)S(1)} collective-permute-done((f32[256,512]{1,0:T(8,128)S(1)}, f32[256,512]{1,0:T(8,128)S(1)}, u32[]{:S(2)}, u32[]{:S(2)}) %collective-permute-start.1) | collective-permute-done | bytes 524320 | tf_op jit(solution)/shard_map/ppermute | solution.py:163
  38.4 1.1 shard_map.63
  39.5 0.1 collective-permute-start.2
  39.6 0.5 shard_map.64
  40.1 1.0 collective-permute-done.2
  41.2 1.4 %collective-permute-start.3 = (f32[64,512]{1,0:T(8,128)S(1)}, f32[64,512]{1,0:T(8,128)S(1)}, u32[]{:S(2)}, u32[]{:S(2)}) collective-permute-start(f32[64,512]{1,0:T(8,128)S(1)} %slice_select_fusion.1), channel_id=1, source_target_pairs={{0,2},{1,3},{2,0},{3,1},{4,6},{5,7},{6,4},{7,5},{8,10},{9,11},{10,... | collective-permute-start | bytes 393224 | tf_op jit(solution)/shard_map/ppermute | solution.py:163
  42.6 1.4 %shard_map.65 = (f32[384,512]{1,0:T(8,128)S(1)}, f32[256,384]{1,0:T(8,128)S(1)}, f32[256,384]{1,0:T(8,128)S(1)}) custom-call(s32[1]{0:T(128)} %bitcast.place, f32[384,512]{1,0:T(8,128)S(1)} %get-tuple-element.67.u1, bf16[256,512]{1,0:T(8,128)(2,1)S(1)} %get-tuple-element.68.v1_half, bf16[128,384]{1,0:T(8,128)(2,1)S(1)} %get-tuple-element.72.refs_0_, ...), custom_call_target="tpu_custom_call" | custom-call | flops 100663296 | bytes 4194304 | tf_op jit(solution)/shard_map/pallas_call | solution.py:146
  44.1 2.7 %collective-permute-done.3 = f32[64,512]{1,0:T(8,128)S(1)} collective-permute-done((f32[64,512]{1,0:T(8,128)S(1)}, f32[64,512]{1,0:T(8,128)S(1)}, u32[]{:S(2)}, u32[]{:S(2)}) %collective-permute-start.3) | collective-permute-done | bytes 131104 | tf_op jit(solution)/shard_map/ppermute | solution.py:163
  46.8 0.1 collective-permute-start.5
  46.9 0.1 collective-permute-start.4
  47.0 9.1 %collective-permute-done.5 = f32[64,512]{1,0:T(8,128)S(1)} collective-permute-done((f32[64,512]{1,0:T(8,128)S(1)}, f32[64,512]{1,0:T(8,128)S(1)}, u32[]{:S(2)}, u32[]{:S(2)}) %collective-permute-start.5) | collective-permute-done | bytes 131104 | tf_op jit(solution)/shard_map/ppermute | solution.py:163
  56.0 1.9 %collective-permute-done.4 = f32[64,512]{1,0:T(8,128)S(1)} collective-permute-done((f32[64,512]{1,0:T(8,128)S(1)}, f32[64,512]{1,0:T(8,128)S(1)}, u32[]{:S(2)}, u32[]{:S(2)}) %collective-permute-start.4) | collective-permute-done | bytes 131104 | tf_op jit(solution)/shard_map/ppermute | solution.py:163
  57.9 0.1 collective-permute-start.6
  58.0 1.5 %collective-permute-done.6.refs_1_ = f32[128,512]{1,0:T(8,128)S(1)} collective-permute-done((f32[128,512]{1,0:T(8,128)S(1)}, f32[128,512]{1,0:T(8,128)S(1)}, u32[]{:S(2)}, u32[]{:S(2)}) %collective-permute-start.6) | collective-permute-done | bytes 262176 | tf_op jit(solution)/shard_map/ppermute | solution.py:163
  59.5 1.2 %shard_map.66 = (f32[384,512]{1,0:T(8,128)S(1)}, bf16[256,512]{1,0:T(8,128)(2,1)S(1)}, bf16[256,384]{1,0:T(8,128)(2,1)S(1)}, f32[256,512]{1,0:T(8,128)S(1)}) custom-call(f32[384,512]{1,0:T(8,128)S(1)} %get-tuple-element.77.u, f32[128,512]{1,0:T(8,128)S(1)} %maximum_select_fusion.refs_0_, f32[128,512]{1,0:T(8,128)S(1)} %collective-permute-done.6.refs_1_, ...), custom_call_target="tpu_custom_call" | custom-call | flops 503316480 | bytes 4194304 | tf_op jit(solution)/shard_map/pallas_call | solution.py:146
  60.7 0.1 collective-permute-start.7
  60.8 1.4 %shard_map.67 = (f32[384,512]{1,0:T(8,128)S(1)}, f32[256,384]{1,0:T(8,128)S(1)}, f32[256,384]{1,0:T(8,128)S(1)}) custom-call(s32[1]{0:T(128)} %bitcast.place, f32[384,512]{1,0:T(8,128)S(1)} %get-tuple-element.81.u1, bf16[256,512]{1,0:T(8,128)(2,1)S(1)} %get-tuple-element.82.v1_half, bf16[256,384]{1,0:T(8,128)(2,1)S(1)} %get-tuple-element.83.refs_0_, ...), custom_call_target="tpu_custom_call" | custom-call | flops 100663296 | bytes 4194304 | tf_op jit(solution)/shard_map/pallas_call | solution.py:146
  62.2 15.2 %collective-permute-done.7.refs_0_ = f32[256,512]{1,0:T(8,128)S(1)} collective-permute-done((f32[256,512]{1,0:T(8,128)S(1)}, f32[256,512]{1,0:T(8,128)S(1)}, u32[]{:S(2)}, u32[]{:S(2)}) %collective-permute-start.7) | collective-permute-done | bytes 524320 | tf_op jit(solution)/shard_map/ppermute | solution.py:163
  77.4 1.2 %shard_map.68 = (f32[384,512]{1,0:T(8,128)S(1)}, bf16[256,512]{1,0:T(8,128)(2,1)S(1)}, bf16[256,384]{1,0:T(8,128)(2,1)S(1)}, f32[256,512]{1,0:T(8,128)S(1)}) custom-call(f32[384,512]{1,0:T(8,128)S(1)} %get-tuple-element.84.u, f32[256,512]{1,0:T(8,128)S(1)} %collective-permute-done.7.refs_0_, f32[256,384]{1,0:T(8,128)S(1)} %get-tuple-element.86.refs_1_, ...), custom_call_target="tpu_custom_call" | custom-call | flops 503316480 | bytes 4194304 | tf_op jit(solution)/shard_map/pallas_call | solution.py:146
  78.7 0.1 collective-permute-start.8
  78.7 1.4 %shard_map.69 = (f32[384,512]{1,0:T(8,128)S(1)}, f32[256,384]{1,0:T(8,128)S(1)}, f32[256,384]{1,0:T(8,128)S(1)}) custom-call(s32[1]{0:T(128)} %bitcast.place, f32[384,512]{1,0:T(8,128)S(1)} %get-tuple-element.88.u1, bf16[256,512]{1,0:T(8,128)(2,1)S(1)} %get-tuple-element.89.v1_half, bf16[256,384]{1,0:T(8,128)(2,1)S(1)} %get-tuple-element.90.refs_0_, ...), custom_call_target="tpu_custom_call" | custom-call | flops 100663296 | bytes 4194304 | tf_op jit(solution)/shard_map/pallas_call | solution.py:146
  80.2 14.4 %collective-permute-done.8.refs_0_ = f32[256,512]{1,0:T(8,128)S(1)} collective-permute-done((f32[256,512]{1,0:T(8,128)S(1)}, f32[256,512]{1,0:T(8,128)S(1)}, u32[]{:S(2)}, u32[]{:S(2)}) %collective-permute-start.8) | collective-permute-done | bytes 524320 | tf_op jit(solution)/shard_map/ppermute | solution.py:163
  94.5 1.1 shard_map.70
  95.6 0.1 collective-permute-start.9
  95.7 0.5 shard_map.71
  96.2 1.0 collective-permute-done.9
  97.3 0.7 collective-permute-start.10
  98.1 1.2 %shard_map.72 = f32[384,512]{1,0:T(8,128)} custom-call(f32[384,512]{1,0:T(8,128)S(1)} %get-tuple-element.95.u1, bf16[256,512]{1,0:T(8,128)(2,1)S(1)} %get-tuple-element.96.v1_half, bf16[128,384]{1,0:T(8,128)(2,1)S(1)} %get-tuple-element.100.refs_0_, bf16[128,384]{1,0:T(8,128)(2,1)S(1)} %get-tuple-element.101.refs_1_), custom_call_target="tpu_custom_call" | custom-call | flops 100663296 | bytes 4194304 | tf_op jit(solution)/shard_map/pallas_call | solution.py:146
  99.2 3.7 %collective-permute-done.10 = f32[64,512]{1,0:T(8,128)S(1)} collective-permute-done((f32[64,512]{1,0:T(8,128)S(1)}, f32[64,512]{1,0:T(8,128)S(1)}, u32[]{:S(2)}, u32[]{:S(2)}) %collective-permute-start.10) | collective-permute-done | bytes 131104 | tf_op jit(solution)/shard_map/ppermute | solution.py:163
  103.0 0.1 collective-permute-start.12
  103.0 0.1 collective-permute-start.11
  103.1 8.1 %collective-permute-done.12 = f32[64,512]{1,0:T(8,128)S(1)} collective-permute-done((f32[64,512]{1,0:T(8,128)S(1)}, f32[64,512]{1,0:T(8,128)S(1)}, u32[]{:S(2)}, u32[]{:S(2)}) %collective-permute-start.12) | collective-permute-done | bytes 131104 | tf_op jit(solution)/shard_map/ppermute | solution.py:163
  111.2 2.8 %collective-permute-done.11 = f32[64,512]{1,0:T(8,128)S(1)} collective-permute-done((f32[64,512]{1,0:T(8,128)S(1)}, f32[64,512]{1,0:T(8,128)S(1)}, u32[]{:S(2)}, u32[]{:S(2)}) %collective-permute-start.11) | collective-permute-done | bytes 131104 | tf_op jit(solution)/shard_map/ppermute | solution.py:163
  114.1 0.1 collective-permute-start.13
  114.2 1.5 %collective-permute-done.13.second = f32[128,512]{1,0:T(8,128)S(1)} collective-permute-done((f32[128,512]{1,0:T(8,128)S(1)}, f32[128,512]{1,0:T(8,128)S(1)}, u32[]{:S(2)}, u32[]{:S(2)}) %collective-permute-start.13) | collective-permute-done | bytes 262176 | tf_op jit(solution)/shard_map/ppermute | solution.py:163
  115.7 0.8 shard_map.73
  (8 shorter events, 0.2 us)
Async XLA Ops:
  3.4 18.0 %collective-permute-start = (f32[256,512]{1,0:T(8,128)S(1)}, f32[256,512]{1,0:T(8,128)S(1)}, u32[]{:S(2)}, u32[]{:S(2)}) collective-permute-start(f32[256,512]{1,0:T(8,128)S(1)} %get-tuple-element.57), channel_id=1, source_target_pairs={{0,4},{1,5},{2,6},{3,7},{4,8},{5,9},{6,10},{7,11},{8,12},{9,13},{1... | collective-permute-start | bytes 1572872 | tf_op jit(solution)/shard_map/ppermute | solution.py:163
  22.6 15.8 %collective-permute-start.1 = (f32[256,512]{1,0:T(8,128)S(1)}, f32[256,512]{1,0:T(8,128)S(1)}, u32[]{:S(2)}, u32[]{:S(2)}) collective-permute-start(f32[256,512]{1,0:T(8,128)S(1)} %get-tuple-element.64), channel_id=1, source_target_pairs={{0,4},{1,5},{2,6},{3,7},{4,8},{5,9},{6,10},{7,11},{8,12},{9,13},{1... | collective-permute-start | bytes 1572872 | tf_op jit(solution)/shard_map/ppermute | solution.py:163
  39.5 1.6 %collective-permute-start.2 = (f32[128,512]{1,0:T(8,128)S(1)}, f32[128,512]{1,0:T(8,128)S(1)}, u32[]{:S(2)}, u32[]{:S(2)}) collective-permute-start(f32[128,512]{1,0:T(8,128)S(1)} %get-tuple-element.71), channel_id=1, source_target_pairs={{0,1},{1,0},{2,3},{3,2},{4,5},{5,4},{6,7},{7,6},{8,9},{9,8},{10,11... | collective-permute-start | bytes 786440 | tf_op jit(solution)/shard_map/ppermute | solution.py:163
  41.2 5.6 %collective-permute-start.3 = (f32[64,512]{1,0:T(8,128)S(1)}, f32[64,512]{1,0:T(8,128)S(1)}, u32[]{:S(2)}, u32[]{:S(2)}) collective-permute-start(f32[64,512]{1,0:T(8,128)S(1)} %slice_select_fusion.1), channel_id=1, source_target_pairs={{0,2},{1,3},{2,0},{3,1},{4,6},{5,7},{6,4},{7,5},{8,10},{9,11},{10,... | collective-permute-start | bytes 393224 | tf_op jit(solution)/shard_map/ppermute | solution.py:163
  46.8 9.2 %collective-permute-start.5 = (f32[64,512]{1,0:T(8,128)S(1)}, f32[64,512]{1,0:T(8,128)S(1)}, u32[]{:S(2)}, u32[]{:S(2)}) collective-permute-start(f32[64,512]{1,0:T(8,128)S(1)} %add_multiply_fusion.1), channel_id=1, source_target_pairs={{0,4},{1,5},{2,6},{3,7},{4,8},{5,9},{6,10},{7,11},{8,12},{9,13},{1... | collective-permute-start | bytes 393224 | tf_op jit(solution)/shard_map/ppermute | solution.py:163
  46.9 11.0 %collective-permute-start.4 = (f32[64,512]{1,0:T(8,128)S(1)}, f32[64,512]{1,0:T(8,128)S(1)}, u32[]{:S(2)}, u32[]{:S(2)}) collective-permute-start(f32[64,512]{1,0:T(8,128)S(1)} %add_multiply_fusion.1), channel_id=1, source_target_pairs={{0,6},{1,7},{2,4},{3,5},{4,10},{5,11},{6,8},{7,9},{8,14},{9,15},{1... | collective-permute-start | bytes 393224 | tf_op jit(solution)/shard_map/ppermute | solution.py:163
  57.9 1.6 %collective-permute-start.6 = (f32[128,512]{1,0:T(8,128)S(1)}, f32[128,512]{1,0:T(8,128)S(1)}, u32[]{:S(2)}, u32[]{:S(2)}) collective-permute-start(f32[128,512]{1,0:T(8,128)S(1)} %maximum_select_fusion.refs_0_), channel_id=1, source_target_pairs={{0,1},{1,0},{2,3},{3,2},{4,5},{5,4},{6,7},{7,6},{8,9},{9,8},{10,11... | collective-permute-start | bytes 786440 | tf_op jit(solution)/shard_map/ppermute | solution.py:163
  60.7 16.7 %collective-permute-start.7 = (f32[256,512]{1,0:T(8,128)S(1)}, f32[256,512]{1,0:T(8,128)S(1)}, u32[]{:S(2)}, u32[]{:S(2)}) collective-permute-start(f32[256,512]{1,0:T(8,128)S(1)} %get-tuple-element.85), channel_id=1, source_target_pairs={{0,4},{1,5},{2,6},{3,7},{4,8},{5,9},{6,10},{7,11},{8,12},{9,13},{1... | collective-permute-start | bytes 1572872 | tf_op jit(solution)/shard_map/ppermute | solution.py:163
  78.7 15.9 %collective-permute-start.8 = (f32[256,512]{1,0:T(8,128)S(1)}, f32[256,512]{1,0:T(8,128)S(1)}, u32[]{:S(2)}, u32[]{:S(2)}) collective-permute-start(f32[256,512]{1,0:T(8,128)S(1)} %get-tuple-element.92), channel_id=1, source_target_pairs={{0,4},{1,5},{2,6},{3,7},{4,8},{5,9},{6,10},{7,11},{8,12},{9,13},{1... | collective-permute-start | bytes 1572872 | tf_op jit(solution)/shard_map/ppermute | solution.py:163
  95.6 1.6 %collective-permute-start.9 = (f32[128,512]{1,0:T(8,128)S(1)}, f32[128,512]{1,0:T(8,128)S(1)}, u32[]{:S(2)}, u32[]{:S(2)}) collective-permute-start(f32[128,512]{1,0:T(8,128)S(1)} %get-tuple-element.99), channel_id=1, source_target_pairs={{0,1},{1,0},{2,3},{3,2},{4,5},{5,4},{6,7},{7,6},{8,9},{9,8},{10,11... | collective-permute-start | bytes 786440 | tf_op jit(solution)/shard_map/ppermute | solution.py:163
  97.3 5.6 %collective-permute-start.10 = (f32[64,512]{1,0:T(8,128)S(1)}, f32[64,512]{1,0:T(8,128)S(1)}, u32[]{:S(2)}, u32[]{:S(2)}) collective-permute-start(f32[64,512]{1,0:T(8,128)S(1)} %slice_select_fusion), channel_id=1, source_target_pairs={{0,2},{1,3},{2,0},{3,1},{4,6},{5,7},{6,4},{7,5},{8,10},{9,11},{10,... | collective-permute-start | bytes 393224 | tf_op jit(solution)/shard_map/ppermute | solution.py:163
  103.0 8.3 %collective-permute-start.12 = (f32[64,512]{1,0:T(8,128)S(1)}, f32[64,512]{1,0:T(8,128)S(1)}, u32[]{:S(2)}, u32[]{:S(2)}) collective-permute-start(f32[64,512]{1,0:T(8,128)S(1)} %add_multiply_fusion), channel_id=1, source_target_pairs={{0,12},{1,13},{2,14},{3,15},{4,16},{5,17},{6,18},{7,19},{8,20},{9,... | collective-permute-start | bytes 393224 | tf_op jit(solution)/shard_map/ppermute | solution.py:163
  103.0 11.0 %collective-permute-start.11 = (f32[64,512]{1,0:T(8,128)S(1)}, f32[64,512]{1,0:T(8,128)S(1)}, u32[]{:S(2)}, u32[]{:S(2)}) collective-permute-start(f32[64,512]{1,0:T(8,128)S(1)} %add_multiply_fusion), channel_id=1, source_target_pairs={{0,14},{1,15},{2,12},{3,13},{4,18},{5,19},{6,16},{7,17},{8,22},{9,... | collective-permute-start | bytes 393224 | tf_op jit(solution)/shard_map/ppermute | solution.py:163
  114.1 1.6 %collective-permute-start.13 = (f32[128,512]{1,0:T(8,128)S(1)}, f32[128,512]{1,0:T(8,128)S(1)}, u32[]{:S(2)}, u32[]{:S(2)}) collective-permute-start(f32[128,512]{1,0:T(8,128)S(1)} %maximum_select_fusion.1.first), channel_id=1, source_target_pairs={{0,1},{1,0},{2,3},{3,2},{4,5},{5,4},{6,7},{7,6},{8,9},{9,8},{10,11... | collective-permute-start | bytes 786440 | tf_op jit(solution)/shard_map/ppermute | solution.py:163

commit v9 on v8

--- a/solution.py
+++ b/solution.py
@@ -52,11 +52,13 @@
     predicted = across(locus_half, cell_half)
     fetch()
     r = residue(tile[...], mask[...], predicted)
-    cells = cells + steps[0] * along(r, locus_half)
+    loci = loci + steps[1] * times(r, cell_half)
+    grad_cells = along(r, locus_half)
+    locus_half = loci.astype(HALF)
+    v1_half[...] = locus_half
+    cells = cells + steps[0] * grad_cells
     u1[...] = cells
-    loci = loci + steps[1] * times(r, cell_half)
-    cell_half, locus_half = cells.astype(HALF), loci.astype(HALF)
-    v1_half[...] = locus_half
+    cell_half = cells.astype(HALF)
     rows = v2[0].shape[0]
     r = residue(tile[:rows], mask[:rows], across(locus_half[:rows], cell_half))
     r2[...] = r

time: 117 us -> 116 us (level)
  no operation moved by 1% of the time
where the time goes in v9:
time: 116 us
  waiting for transfers between devices  90.9 us (78%)
  Pallas kernels  18.2 us (16%)
  starting transfers between devices  5.89 us (5%)
    ppermute x14, waiting for transfers between devices, moved(): return lax.ppermute(block, AXES, route)  90.9 us
    pallas_call x15, Pallas kernels, call(): pl.pallas_call(body, out_shape=[jax.ShapeDtypeStruct(shape, dtype) for sh...  18.2 us
    ppermute x14, starting transfers between devices, moved(): return lax.ppermute(block, AXES, route)  5.89 us
  transfers between devices with their start and end apart: 14, of which 14 were waited for; matrix products, arithmetic and copies ran while one was open for 0% of the time, Pallas kernels for 8%

profile of v9, /device:TPU:0, one launch (start us, length us, event | category | flops | bytes accessed | tf_op | source)
XLA Modules:
  0.0 116.0 jit_solution(1173747326454469175)
XLA Ops:
  0.6 2.6 %shard_map.59 = (f32[384,512]{1,0:T(8,128)S(1)}, bf16[256,512]{1,0:T(8,128)(2,1)S(1)}, bf16[256,384]{1,0:T(8,128)(2,1)S(1)}, f32[256,512]{1,0:T(8,128)S(1)}) custom-call(s32[1]{0:T(128)} %bitcast.place, bf16[384,2048]{1,0:T(8,128)(2,1)} %refs_1_.7, s32[384,2048]{1,0:T(8,128)} %refs_2_.9, f32[384,512]{1,0:T(8,128)} %u_hbm.1, f32[256,512]{1,0:T(8,128)} %v_hbm.1), custom_call_target="tpu_custom_call" | custom-call | flops 503316480 | bytes 4194304 | tf_op jit(solution)/shard_map/pallas_call | solution.py:148
  3.3 3.0 %collective-permute-start = (f32[256,512]{1,0:T(8,128)S(1)}, f32[256,512]{1,0:T(8,128)S(1)}, u32[]{:S(2)}, u32[]{:S(2)}) collective-permute-start(f32[256,512]{1,0:T(8,128)S(1)} %get-tuple-element.57), channel_id=1, source_target_pairs={{0,4},{1,5},{2,6},{3,7},{4,8},{5,9},{6,10},{7,11},{8,12},{9,13},{1... | collective-permute-start | bytes 1572872 | tf_op jit(solution)/shard_map/ppermute | solution.py:165
  6.3 1.4 %shard_map.60 = (f32[384,512]{1,0:T(8,128)S(1)}, f32[256,384]{1,0:T(8,128)S(1)}, f32[256,384]{1,0:T(8,128)S(1)}) custom-call(s32[1]{0:T(128)} %bitcast.place, f32[384,512]{1,0:T(8,128)S(1)} %get-tuple-element.53.u1, bf16[256,512]{1,0:T(8,128)(2,1)S(1)} %get-tuple-element.54.v1_half, bf16[256,384]{1,0:T(8,128)(2,1)S(1)} %get-tuple-element.55.refs_0_, ...), custom_call_target="tpu_custom_call" | custom-call | flops 100663296 | bytes 4194304 | tf_op jit(solution)/shard_map/pallas_call | solution.py:148
  7.8 13.5 %collective-permute-done.refs_0_ = f32[256,512]{1,0:T(8,128)S(1)} collective-permute-done((f32[256,512]{1,0:T(8,128)S(1)}, f32[256,512]{1,0:T(8,128)S(1)}, u32[]{:S(2)}, u32[]{:S(2)}) %collective-permute-start) | collective-permute-done | bytes 524320 | tf_op jit(solution)/shard_map/ppermute | solution.py:165
  21.3 1.1 shard_map.61
  22.4 0.1 collective-permute-start.1
  22.5 1.4 %shard_map.62 = (f32[384,512]{1,0:T(8,128)S(1)}, f32[256,384]{1,0:T(8,128)S(1)}, f32[256,384]{1,0:T(8,128)S(1)}) custom-call(s32[1]{0:T(128)} %bitcast.place, f32[384,512]{1,0:T(8,128)S(1)} %get-tuple-element.60.u1, bf16[256,512]{1,0:T(8,128)(2,1)S(1)} %get-tuple-element.61.v1_half, bf16[256,384]{1,0:T(8,128)(2,1)S(1)} %get-tuple-element.62.refs_0_, ...), custom_call_target="tpu_custom_call" | custom-call | flops 100663296 | bytes 4194304 | tf_op jit(solution)/shard_map/pallas_call | solution.py:148
  23.9 14.3 %collective-permute-done.1.refs_0_ = f32[256,512]{1,0:T(8,128)S(1)} collective-permute-done((f32[256,512]{1,0:T(8,128)S(1)}, f32[256,512]{1,0:T(8,128)S(1)}, u32[]{:S(2)}, u32[]{:S(2)}) %collective-permute-start.1) | collective-permute-done | bytes 524320 | tf_op jit(solution)/shard_map/ppermute | solution.py:165
  38.3 1.0 shard_map.63
  39.3 0.1 collective-permute-start.2
  39.4 0.5 shard_map.64
  39.9 1.0 collective-permute-done.2
  41.0 1.4 %collective-permute-start.3 = (f32[64,512]{1,0:T(8,128)S(1)}, f32[64,512]{1,0:T(8,128)S(1)}, u32[]{:S(2)}, u32[]{:S(2)}) collective-permute-start(f32[64,512]{1,0:T(8,128)S(1)} %slice_select_fusion.1), channel_id=1, source_target_pairs={{0,2},{1,3},{2,0},{3,1},{4,6},{5,7},{6,4},{7,5},{8,10},{9,11},{10,... | collective-permute-start | bytes 393224 | tf_op jit(solution)/shard_map/ppermute | solution.py:165
  42.3 1.4 %shard_map.65 = (f32[384,512]{1,0:T(8,128)S(1)}, f32[256,384]{1,0:T(8,128)S(1)}, f32[256,384]{1,0:T(8,128)S(1)}) custom-call(s32[1]{0:T(128)} %bitcast.place, f32[384,512]{1,0:T(8,128)S(1)} %get-tuple-element.67.u1, bf16[256,512]{1,0:T(8,128)(2,1)S(1)} %get-tuple-element.68.v1_half, bf16[128,384]{1,0:T(8,128)(2,1)S(1)} %get-tuple-element.72.refs_0_, ...), custom_call_target="tpu_custom_call" | custom-call | flops 100663296 | bytes 4194304 | tf_op jit(solution)/shard_map/pallas_call | solution.py:148
  43.8 2.8 %collective-permute-done.3 = f32[64,512]{1,0:T(8,128)S(1)} collective-permute-done((f32[64,512]{1,0:T(8,128)S(1)}, f32[64,512]{1,0:T(8,128)S(1)}, u32[]{:S(2)}, u32[]{:S(2)}) %collective-permute-start.3) | collective-permute-done | bytes 131104 | tf_op jit(solution)/shard_map/ppermute | solution.py:165
  46.6 0.1 collective-permute-start.5
  46.7 0.1 collective-permute-start.4
  46.7 9.1 %collective-permute-done.5 = f32[64,512]{1,0:T(8,128)S(1)} collective-permute-done((f32[64,512]{1,0:T(8,128)S(1)}, f32[64,512]{1,0:T(8,128)S(1)}, u32[]{:S(2)}, u32[]{:S(2)}) %collective-permute-start.5) | collective-permute-done | bytes 131104 | tf_op jit(solution)/shard_map/ppermute | solution.py:165
  55.8 1.8 %collective-permute-done.4 = f32[64,512]{1,0:T(8,128)S(1)} collective-permute-done((f32[64,512]{1,0:T(8,128)S(1)}, f32[64,512]{1,0:T(8,128)S(1)}, u32[]{:S(2)}, u32[]{:S(2)}) %collective-permute-start.4) | collective-permute-done | bytes 131104 | tf_op jit(solution)/shard_map/ppermute | solution.py:165
  57.6 0.1 collective-permute-start.6
  57.7 1.5 %collective-permute-done.6.refs_1_ = f32[128,512]{1,0:T(8,128)S(1)} collective-permute-done((f32[128,512]{1,0:T(8,128)S(1)}, f32[128,512]{1,0:T(8,128)S(1)}, u32[]{:S(2)}, u32[]{:S(2)}) %collective-permute-start.6) | collective-permute-done | bytes 262176 | tf_op jit(solution)/shard_map/ppermute | solution.py:165
  59.2 1.1 shard_map.66
  60.4 0.1 collective-permute-start.7
  60.4 1.4 %shard_map.67 = (f32[384,512]{1,0:T(8,128)S(1)}, f32[256,384]{1,0:T(8,128)S(1)}, f32[256,384]{1,0:T(8,128)S(1)}) custom-call(s32[1]{0:T(128)} %bitcast.place, f32[384,512]{1,0:T(8,128)S(1)} %get-tuple-element.81.u1, bf16[256,512]{1,0:T(8,128)(2,1)S(1)} %get-tuple-element.82.v1_half, bf16[256,384]{1,0:T(8,128)(2,1)S(1)} %get-tuple-element.83.refs_0_, ...), custom_call_target="tpu_custom_call" | custom-call | flops 100663296 | bytes 4194304 | tf_op jit(solution)/shard_map/pallas_call | solution.py:148
  61.9 15.2 %collective-permute-done.7.refs_0_ = f32[256,512]{1,0:T(8,128)S(1)} collective-permute-done((f32[256,512]{1,0:T(8,128)S(1)}, f32[256,512]{1,0:T(8,128)S(1)}, u32[]{:S(2)}, u32[]{:S(2)}) %collective-permute-start.7) | collective-permute-done | bytes 524320 | tf_op jit(solution)/shard_map/ppermute | solution.py:165
  77.1 1.1 shard_map.68
  78.2 0.1 collective-permute-start.8
  78.3 1.4 %shard_map.69 = (f32[384,512]{1,0:T(8,128)S(1)}, f32[256,384]{1,0:T(8,128)S(1)}, f32[256,384]{1,0:T(8,128)S(1)}) custom-call(s32[1]{0:T(128)} %bitcast.place, f32[384,512]{1,0:T(8,128)S(1)} %get-tuple-element.88.u1, bf16[256,512]{1,0:T(8,128)(2,1)S(1)} %get-tuple-element.89.v1_half, bf16[256,384]{1,0:T(8,128)(2,1)S(1)} %get-tuple-element.90.refs_0_, ...), custom_call_target="tpu_custom_call" | custom-call | flops 100663296 | bytes 4194304 | tf_op jit(solution)/shard_map/pallas_call | solution.py:148
  79.7 14.4 %collective-permute-done.8.refs_0_ = f32[256,512]{1,0:T(8,128)S(1)} collective-permute-done((f32[256,512]{1,0:T(8,128)S(1)}, f32[256,512]{1,0:T(8,128)S(1)}, u32[]{:S(2)}, u32[]{:S(2)}) %collective-permute-start.8) | collective-permute-done | bytes 524320 | tf_op jit(solution)/shard_map/ppermute | solution.py:165
  94.1 1.0 shard_map.70
  95.1 0.1 collective-permute-start.9
  95.2 0.5 shard_map.71
  95.7 1.0 collective-permute-done.9
  96.8 0.8 collective-permute-start.10
  97.6 1.2 %shard_map.72 = f32[384,512]{1,0:T(8,128)} custom-call(f32[384,512]{1,0:T(8,128)S(1)} %get-tuple-element.95.u1, bf16[256,512]{1,0:T(8,128)(2,1)S(1)} %get-tuple-element.96.v1_half, bf16[128,384]{1,0:T(8,128)(2,1)S(1)} %get-tuple-element.100.refs_0_, bf16[128,384]{1,0:T(8,128)(2,1)S(1)} %get-tuple-element.101.refs_1_), custom_call_target="tpu_custom_call" | custom-call | flops 100663296 | bytes 4194304 | tf_op jit(solution)/shard_map/pallas_call | solution.py:148
  98.8 3.6 %collective-permute-done.10 = f32[64,512]{1,0:T(8,128)S(1)} collective-permute-done((f32[64,512]{1,0:T(8,128)S(1)}, f32[64,512]{1,0:T(8,128)S(1)}, u32[]{:S(2)}, u32[]{:S(2)}) %collective-permute-start.10) | collective-permute-done | bytes 131104 | tf_op jit(solution)/shard_map/ppermute | solution.py:165
  102.4 0.1 collective-permute-start.12
  102.5 0.1 collective-permute-start.11
  102.6 8.1 %collective-permute-done.12 = f32[64,512]{1,0:T(8,128)S(1)} collective-permute-done((f32[64,512]{1,0:T(8,128)S(1)}, f32[64,512]{1,0:T(8,128)S(1)}, u32[]{:S(2)}, u32[]{:S(2)}) %collective-permute-start.12) | collective-permute-done | bytes 131104 | tf_op jit(solution)/shard_map/ppermute | solution.py:165
  110.7 2.9 %collective-permute-done.11 = f32[64,512]{1,0:T(8,128)S(1)} collective-permute-done((f32[64,512]{1,0:T(8,128)S(1)}, f32[64,512]{1,0:T(8,128)S(1)}, u32[]{:S(2)}, u32[]{:S(2)}) %collective-permute-start.11) | collective-permute-done | bytes 131104 | tf_op jit(solution)/shard_map/ppermute | solution.py:165
  113.6 0.1 collective-permute-start.13
  113.7 1.5 %collective-permute-done.13.second = f32[128,512]{1,0:T(8,128)S(1)} collective-permute-done((f32[128,512]{1,0:T(8,128)S(1)}, f32[128,512]{1,0:T(8,128)S(1)}, u32[]{:S(2)}, u32[]{:S(2)}) %collective-permute-start.13) | collective-permute-done | bytes 262176 | tf_op jit(solution)/shard_map/ppermute | solution.py:165
  115.2 0.8 shard_map.73
  (8 shorter events, 0.2 us)
Async XLA Ops:
  3.3 18.0 %collective-permute-start = (f32[256,512]{1,0:T(8,128)S(1)}, f32[256,512]{1,0:T(8,128)S(1)}, u32[]{:S(2)}, u32[]{:S(2)}) collective-permute-start(f32[256,512]{1,0:T(8,128)S(1)} %get-tuple-element.57), channel_id=1, source_target_pairs={{0,4},{1,5},{2,6},{3,7},{4,8},{5,9},{6,10},{7,11},{8,12},{9,13},{1... | collective-permute-start | bytes 1572872 | tf_op jit(solution)/shard_map/ppermute | solution.py:165
  22.4 15.9 %collective-permute-start.1 = (f32[256,512]{1,0:T(8,128)S(1)}, f32[256,512]{1,0:T(8,128)S(1)}, u32[]{:S(2)}, u32[]{:S(2)}) collective-permute-start(f32[256,512]{1,0:T(8,128)S(1)} %get-tuple-element.64), channel_id=1, source_target_pairs={{0,4},{1,5},{2,6},{3,7},{4,8},{5,9},{6,10},{7,11},{8,12},{9,13},{1... | collective-permute-start | bytes 1572872 | tf_op jit(solution)/shard_map/ppermute | solution.py:165
  39.3 1.6 %collective-permute-start.2 = (f32[128,512]{1,0:T(8,128)S(1)}, f32[128,512]{1,0:T(8,128)S(1)}, u32[]{:S(2)}, u32[]{:S(2)}) collective-permute-start(f32[128,512]{1,0:T(8,128)S(1)} %get-tuple-element.71), channel_id=1, source_target_pairs={{0,1},{1,0},{2,3},{3,2},{4,5},{5,4},{6,7},{7,6},{8,9},{9,8},{10,11... | collective-permute-start | bytes 786440 | tf_op jit(solution)/shard_map/ppermute | solution.py:165
  41.0 5.6 %collective-permute-start.3 = (f32[64,512]{1,0:T(8,128)S(1)}, f32[64,512]{1,0:T(8,128)S(1)}, u32[]{:S(2)}, u32[]{:S(2)}) collective-permute-start(f32[64,512]{1,0:T(8,128)S(1)} %slice_select_fusion.1), channel_id=1, source_target_pairs={{0,2},{1,3},{2,0},{3,1},{4,6},{5,7},{6,4},{7,5},{8,10},{9,11},{10,... | collective-permute-start | bytes 393224 | tf_op jit(solution)/shard_map/ppermute | solution.py:165
  46.6 9.2 %collective-permute-start.5 = (f32[64,512]{1,0:T(8,128)S(1)}, f32[64,512]{1,0:T(8,128)S(1)}, u32[]{:S(2)}, u32[]{:S(2)}) collective-permute-start(f32[64,512]{1,0:T(8,128)S(1)} %add_multiply_fusion.1), channel_id=1, source_target_pairs={{0,4},{1,5},{2,6},{3,7},{4,8},{5,9},{6,10},{7,11},{8,12},{9,13},{1... | collective-permute-start | bytes 393224 | tf_op jit(solution)/shard_map/ppermute | solution.py:165
  46.7 10.9 %collective-permute-start.4 = (f32[64,512]{1,0:T(8,128)S(1)}, f32[64,512]{1,0:T(8,128)S(1)}, u32[]{:S(2)}, u32[]{:S(2)}) collective-permute-start(f32[64,512]{1,0:T(8,128)S(1)} %add_multiply_fusion.1), channel_id=1, source_target_pairs={{0,6},{1,7},{2,4},{3,5},{4,10},{5,11},{6,8},{7,9},{8,14},{9,15},{1... | collective-permute-start | bytes 393224 | tf_op jit(solution)/shard_map/ppermute | solution.py:165
  57.6 1.6 %collective-permute-start.6 = (f32[128,512]{1,0:T(8,128)S(1)}, f32[128,512]{1,0:T(8,128)S(1)}, u32[]{:S(2)}, u32[]{:S(2)}) collective-permute-start(f32[128,512]{1,0:T(8,128)S(1)} %maximum_select_fusion.refs_0_), channel_id=1, source_target_pairs={{0,1},{1,0},{2,3},{3,2},{4,5},{5,4},{6,7},{7,6},{8,9},{9,8},{10,11... | collective-permute-start | bytes 786440 | tf_op jit(solution)/shard_map/ppermute | solution.py:165
  60.4 16.7 %collective-permute-start.7 = (f32[256,512]{1,0:T(8,128)S(1)}, f32[256,512]{1,0:T(8,128)S(1)}, u32[]{:S(2)}, u32[]{:S(2)}) collective-permute-start(f32[256,512]{1,0:T(8,128)S(1)} %get-tuple-element.85), channel_id=1, source_target_pairs={{0,4},{1,5},{2,6},{3,7},{4,8},{5,9},{6,10},{7,11},{8,12},{9,13},{1... | collective-permute-start | bytes 1572872 | tf_op jit(solution)/shard_map/ppermute | solution.py:165
  78.2 15.9 %collective-permute-start.8 = (f32[256,512]{1,0:T(8,128)S(1)}, f32[256,512]{1,0:T(8,128)S(1)}, u32[]{:S(2)}, u32[]{:S(2)}) collective-permute-start(f32[256,512]{1,0:T(8,128)S(1)} %get-tuple-element.92), channel_id=1, source_target_pairs={{0,4},{1,5},{2,6},{3,7},{4,8},{5,9},{6,10},{7,11},{8,12},{9,13},{1... | collective-permute-start | bytes 1572872 | tf_op jit(solution)/shard_map/ppermute | solution.py:165
  95.1 1.6 %collective-permute-start.9 = (f32[128,512]{1,0:T(8,128)S(1)}, f32[128,512]{1,0:T(8,128)S(1)}, u32[]{:S(2)}, u32[]{:S(2)}) collective-permute-start(f32[128,512]{1,0:T(8,128)S(1)} %get-tuple-element.99), channel_id=1, source_target_pairs={{0,1},{1,0},{2,3},{3,2},{4,5},{5,4},{6,7},{7,6},{8,9},{9,8},{10,11... | collective-permute-start | bytes 786440 | tf_op jit(solution)/shard_map/ppermute | solution.py:165
  96.8 5.6 %collective-permute-start.10 = (f32[64,512]{1,0:T(8,128)S(1)}, f32[64,512]{1,0:T(8,128)S(1)}, u32[]{:S(2)}, u32[]{:S(2)}) collective-permute-start(f32[64,512]{1,0:T(8,128)S(1)} %slice_select_fusion), channel_id=1, source_target_pairs={{0,2},{1,3},{2,0},{3,1},{4,6},{5,7},{6,4},{7,5},{8,10},{9,11},{10,... | collective-permute-start | bytes 393224 | tf_op jit(solution)/shard_map/ppermute | solution.py:165
  102.4 8.3 %collective-permute-start.12 = (f32[64,512]{1,0:T(8,128)S(1)}, f32[64,512]{1,0:T(8,128)S(1)}, u32[]{:S(2)}, u32[]{:S(2)}) collective-permute-start(f32[64,512]{1,0:T(8,128)S(1)} %add_multiply_fusion), channel_id=1, source_target_pairs={{0,12},{1,13},{2,14},{3,15},{4,16},{5,17},{6,18},{7,19},{8,20},{9,... | collective-permute-start | bytes 393224 | tf_op jit(solution)/shard_map/ppermute | solution.py:165
  102.5 11.1 %collective-permute-start.11 = (f32[64,512]{1,0:T(8,128)S(1)}, f32[64,512]{1,0:T(8,128)S(1)}, u32[]{:S(2)}, u32[]{:S(2)}) collective-permute-start(f32[64,512]{1,0:T(8,128)S(1)} %add_multiply_fusion), channel_id=1, source_target_pairs={{0,14},{1,15},{2,12},{3,13},{4,18},{5,19},{6,16},{7,17},{8,22},{9,... | collective-permute-start | bytes 393224 | tf_op jit(solution)/shard_map/ppermute | solution.py:165
  113.6 1.6 %collective-permute-start.13 = (f32[128,512]{1,0:T(8,128)S(1)}, f32[128,512]{1,0:T(8,128)S(1)}, u32[]{:S(2)}, u32[]{:S(2)}) collective-permute-start(f32[128,512]{1,0:T(8,128)S(1)} %maximum_select_fusion.1.first), channel_id=1, source_target_pairs={{0,1},{1,0},{2,3},{3,2},{4,5},{5,4},{6,7},{7,6},{8,9},{9,8},{10,11... | collective-permute-start | bytes 786440 | tf_op jit(solution)/shard_map/ppermute | solution.py:165

commit v10 on v9

--- a/solution.py
+++ b/solution.py
@@ -126,20 +126,17 @@
     settle(steps, u1, v1_half, residues, u2)
 
 
-def store_body(place, first, second, out, sems):
-    rows = first.shape[0]
-    side = place[0] % 2
-    copies = []
-    for order, (half, index) in enumerate(((first, side), (second, 1 - side))):
-        target = pl.ds(pl.multiple_of(index * rows, rows), rows)
-        copies.append(pltpu.make_async_copy(half, out.at[target], sems.at[order]))
-    for copy in copies:
-        copy.start()
-    for copy in copies:
-        copy.wait()
-
-
-def call(body, args, spaces, outs, scratch=(), flops=0, made=pltpu.VMEM):
+def store_body(other, place, half, *refs):
+    *_, out, sems = refs
+    rows = half.shape[0]
+    index = 1 - place[0] % 2 if other else place[0] % 2
+    target = pl.ds(pl.multiple_of(index * rows, rows), rows)
+    copy = pltpu.make_async_copy(half, out.at[target], sems.at[0])
+    copy.start()
+    copy.wait()
+
+
+def call(body, args, spaces, outs, scratch=(), flops=0, made=pltpu.VMEM, aliases=None):
     kinds = {"v": pltpu.VMEM, "h": pltpu.HBM, "s": pltpu.SMEM}
     placed = [
         a if s == "s" else pltpu.with_memory_space_constraint(a, kinds[s])
@@ -151,6 +148,7 @@
         in_specs=[pl.BlockSpec(memory_space=kinds[s]) for s in spaces],
         out_specs=[pl.BlockSpec(memory_space=made) for _ in outs],
         scratch_shapes=list(scratch),
+        input_output_aliases=aliases or {},
         compiler_params=pltpu.CompilerParams(vmem_limit_bytes=12 << 20),
         cost_estimate=pl.CostEstimate(flops=flops, bytes_accessed=4 << 20, transcendentals=0),
     )(*placed)
@@ -272,8 +270,12 @@
                     tile, mask = rest
             else:
                 parts = [moved(v2[0], blocks, groups, 1)]
+        one = [pltpu.SemaphoreType.DMA((1,))]
         (whole,) = call(
-            store_body, (place, *parts), "svv", [tall], [pltpu.SemaphoreType.DMA((2,))], made=pltpu.HBM
+            functools.partial(store_body, False), (place, parts[0]), "sv", [tall], one, made=pltpu.HBM
+        )
+        (whole,) = call(
+            functools.partial(store_body, True), (place, parts[1], whole), "svh", [tall], one, made=pltpu.HBM, aliases={2: 0}
         )
         return u, whole
 

time: 116 us -> 116 us (level)
    pallas_call x15 -> x16, Pallas kernels: 18.2 us -> 18.8 us  [call(): pl.pallas_call(body, out_shape=[jax.ShapeDtypeStruct(shape, dtype) for sh...]
  transfers between devices with their start and end apart: 14 -> 14, of which waited for: 14 -> 14; matrix products, arithmetic and copies ran while one was open for 0% -> 0% of each run, Pallas kernels for 8% -> 9%
where the time goes in v10:
time: 116 us
  waiting for transfers between devices  90.1 us (78%)
  Pallas kernels  18.8 us (16%)
  starting transfers between devices  5.89 us (5%)
    ppermute x14, waiting for transfers between devices, moved(): return lax.ppermute(block, AXES, route)  90.1 us
    pallas_call x16, Pallas kernels, call(): pl.pallas_call(body, out_shape=[jax.ShapeDtypeStruct(shape, dtype) for sh...  18.8 us
    ppermute x14, starting transfers between devices, moved(): return lax.ppermute(block, AXES, route)  5.89 us
  transfers between devices with their start and end apart: 14, of which 14 were waited for; matrix products, arithmetic and copies ran while one was open for 0% of the time, Pallas kernels for 9%

profile of v10, /device:TPU:0, one launch (start us, length us, event | category | flops | bytes accessed | tf_op | source)
XLA Modules:
  0.0 115.9 jit_solution(2209650570584576164)
XLA Ops:
  0.6 2.6 %shard_map.59 = (f32[384,512]{1,0:T(8,128)S(1)}, bf16[256,512]{1,0:T(8,128)(2,1)S(1)}, bf16[256,384]{1,0:T(8,128)(2,1)S(1)}, f32[256,512]{1,0:T(8,128)S(1)}) custom-call(s32[1]{0:T(128)} %bitcast.place, bf16[384,2048]{1,0:T(8,128)(2,1)} %refs_1_.7, s32[384,2048]{1,0:T(8,128)} %refs_2_.9, f32[384,512]{1,0:T(8,128)} %u_hbm.1, f32[256,512]{1,0:T(8,128)} %v_hbm.1), custom_call_target="tpu_custom_call" | custom-call | flops 503316480 | bytes 4194304 | tf_op jit(solution)/shard_map/pallas_call | solution.py:145
  3.3 3.0 %collective-permute-start = (f32[256,512]{1,0:T(8,128)S(1)}, f32[256,512]{1,0:T(8,128)S(1)}, u32[]{:S(2)}, u32[]{:S(2)}) collective-permute-start(f32[256,512]{1,0:T(8,128)S(1)} %get-tuple-element.57), channel_id=1, source_target_pairs={{0,4},{1,5},{2,6},{3,7},{4,8},{5,9},{6,10},{7,11},{8,12},{9,13},{1... | collective-permute-start | bytes 1572872 | tf_op jit(solution)/shard_map/ppermute | solution.py:163
  6.3 1.4 %shard_map.60 = (f32[384,512]{1,0:T(8,128)S(1)}, f32[256,384]{1,0:T(8,128)S(1)}, f32[256,384]{1,0:T(8,128)S(1)}) custom-call(s32[1]{0:T(128)} %bitcast.place, f32[384,512]{1,0:T(8,128)S(1)} %get-tuple-element.53.u1, bf16[256,512]{1,0:T(8,128)(2,1)S(1)} %get-tuple-element.54.v1_half, bf16[256,384]{1,0:T(8,128)(2,1)S(1)} %get-tuple-element.55.refs_0_, ...), custom_call_target="tpu_custom_call" | custom-call | flops 100663296 | bytes 4194304 | tf_op jit(solution)/shard_map/pallas_call | solution.py:145
  7.8 13.5 %collective-permute-done.refs_0_ = f32[256,512]{1,0:T(8,128)S(1)} collective-permute-done((f32[256,512]{1,0:T(8,128)S(1)}, f32[256,512]{1,0:T(8,128)S(1)}, u32[]{:S(2)}, u32[]{:S(2)}) %collective-permute-start) | collective-permute-done | bytes 524320 | tf_op jit(solution)/shard_map/ppermute | solution.py:163
  21.3 1.1 shard_map.61
  22.4 0.1 collective-permute-start.1
  22.5 1.4 %shard_map.62 = (f32[384,512]{1,0:T(8,128)S(1)}, f32[256,384]{1,0:T(8,128)S(1)}, f32[256,384]{1,0:T(8,128)S(1)}) custom-call(s32[1]{0:T(128)} %bitcast.place, f32[384,512]{1,0:T(8,128)S(1)} %get-tuple-element.60.u1, bf16[256,512]{1,0:T(8,128)(2,1)S(1)} %get-tuple-element.61.v1_half, bf16[256,384]{1,0:T(8,128)(2,1)S(1)} %get-tuple-element.62.refs_0_, ...), custom_call_target="tpu_custom_call" | custom-call | flops 100663296 | bytes 4194304 | tf_op jit(solution)/shard_map/pallas_call | solution.py:145
  23.9 14.3 %collective-permute-done.1.refs_0_ = f32[256,512]{1,0:T(8,128)S(1)} collective-permute-done((f32[256,512]{1,0:T(8,128)S(1)}, f32[256,512]{1,0:T(8,128)S(1)}, u32[]{:S(2)}, u32[]{:S(2)}) %collective-permute-start.1) | collective-permute-done | bytes 524320 | tf_op jit(solution)/shard_map/ppermute | solution.py:163
  38.3 1.0 shard_map.63
  39.3 0.1 collective-permute-start.2
  39.4 0.5 shard_map.64
  39.9 1.0 collective-permute-done.2
  41.0 1.4 %collective-permute-start.3 = (f32[64,512]{1,0:T(8,128)S(1)}, f32[64,512]{1,0:T(8,128)S(1)}, u32[]{:S(2)}, u32[]{:S(2)}) collective-permute-start(f32[64,512]{1,0:T(8,128)S(1)} %slice_select_fusion.1), channel_id=1, source_target_pairs={{0,2},{1,3},{2,0},{3,1},{4,6},{5,7},{6,4},{7,5},{8,10},{9,11},{10,... | collective-permute-start | bytes 393224 | tf_op jit(solution)/shard_map/ppermute | solution.py:163
  42.3 1.4 %shard_map.65 = (f32[384,512]{1,0:T(8,128)S(1)}, f32[256,384]{1,0:T(8,128)S(1)}, f32[256,384]{1,0:T(8,128)S(1)}) custom-call(s32[1]{0:T(128)} %bitcast.place, f32[384,512]{1,0:T(8,128)S(1)} %get-tuple-element.67.u1, bf16[256,512]{1,0:T(8,128)(2,1)S(1)} %get-tuple-element.68.v1_half, bf16[128,384]{1,0:T(8,128)(2,1)S(1)} %get-tuple-element.72.refs_0_, ...), custom_call_target="tpu_custom_call" | custom-call | flops 100663296 | bytes 4194304 | tf_op jit(solution)/shard_map/pallas_call | solution.py:145
  43.8 2.8 %collective-permute-done.3 = f32[64,512]{1,0:T(8,128)S(1)} collective-permute-done((f32[64,512]{1,0:T(8,128)S(1)}, f32[64,512]{1,0:T(8,128)S(1)}, u32[]{:S(2)}, u32[]{:S(2)}) %collective-permute-start.3) | collective-permute-done | bytes 131104 | tf_op jit(solution)/shard_map/ppermute | solution.py:163
  46.6 0.1 collective-permute-start.5
  46.7 0.1 collective-permute-start.4
  46.7 9.1 %collective-permute-done.5 = f32[64,512]{1,0:T(8,128)S(1)} collective-permute-done((f32[64,512]{1,0:T(8,128)S(1)}, f32[64,512]{1,0:T(8,128)S(1)}, u32[]{:S(2)}, u32[]{:S(2)}) %collective-permute-start.5) | collective-permute-done | bytes 131104 | tf_op jit(solution)/shard_map/ppermute | solution.py:163
  55.8 1.8 %collective-permute-done.4 = f32[64,512]{1,0:T(8,128)S(1)} collective-permute-done((f32[64,512]{1,0:T(8,128)S(1)}, f32[64,512]{1,0:T(8,128)S(1)}, u32[]{:S(2)}, u32[]{:S(2)}) %collective-permute-start.4) | collective-permute-done | bytes 131104 | tf_op jit(solution)/shard_map/ppermute | solution.py:163
  57.6 0.1 collective-permute-start.6
  57.7 1.5 %collective-permute-done.6.refs_1_ = f32[128,512]{1,0:T(8,128)S(1)} collective-permute-done((f32[128,512]{1,0:T(8,128)S(1)}, f32[128,512]{1,0:T(8,128)S(1)}, u32[]{:S(2)}, u32[]{:S(2)}) %collective-permute-start.6) | collective-permute-done | bytes 262176 | tf_op jit(solution)/shard_map/ppermute | solution.py:163
  59.2 1.1 shard_map.66
  60.4 0.1 collective-permute-start.7
  60.4 1.4 %shard_map.67 = (f32[384,512]{1,0:T(8,128)S(1)}, f32[256,384]{1,0:T(8,128)S(1)}, f32[256,384]{1,0:T(8,128)S(1)}) custom-call(s32[1]{0:T(128)} %bitcast.place, f32[384,512]{1,0:T(8,128)S(1)} %get-tuple-element.81.u1, bf16[256,512]{1,0:T(8,128)(2,1)S(1)} %get-tuple-element.82.v1_half, bf16[256,384]{1,0:T(8,128)(2,1)S(1)} %get-tuple-element.83.refs_0_, ...), custom_call_target="tpu_custom_call" | custom-call | flops 100663296 | bytes 4194304 | tf_op jit(solution)/shard_map/pallas_call | solution.py:145
  61.9 15.2 %collective-permute-done.7.refs_0_ = f32[256,512]{1,0:T(8,128)S(1)} collective-permute-done((f32[256,512]{1,0:T(8,128)S(1)}, f32[256,512]{1,0:T(8,128)S(1)}, u32[]{:S(2)}, u32[]{:S(2)}) %collective-permute-start.7) | collective-permute-done | bytes 524320 | tf_op jit(solution)/shard_map/ppermute | solution.py:163
  77.1 1.1 shard_map.68
  78.2 0.1 collective-permute-start.8
  78.3 1.4 %shard_map.69 = (f32[384,512]{1,0:T(8,128)S(1)}, f32[256,384]{1,0:T(8,128)S(1)}, f32[256,384]{1,0:T(8,128)S(1)}) custom-call(s32[1]{0:T(128)} %bitcast.place, f32[384,512]{1,0:T(8,128)S(1)} %get-tuple-element.88.u1, bf16[256,512]{1,0:T(8,128)(2,1)S(1)} %get-tuple-element.89.v1_half, bf16[256,384]{1,0:T(8,128)(2,1)S(1)} %get-tuple-element.90.refs_0_, ...), custom_call_target="tpu_custom_call" | custom-call | flops 100663296 | bytes 4194304 | tf_op jit(solution)/shard_map/pallas_call | solution.py:145
  79.7 14.4 %collective-permute-done.8.refs_0_ = f32[256,512]{1,0:T(8,128)S(1)} collective-permute-done((f32[256,512]{1,0:T(8,128)S(1)}, f32[256,512]{1,0:T(8,128)S(1)}, u32[]{:S(2)}, u32[]{:S(2)}) %collective-permute-start.8) | collective-permute-done | bytes 524320 | tf_op jit(solution)/shard_map/ppermute | solution.py:163
  94.1 1.0 shard_map.70
  95.1 0.1 collective-permute-start.9
  95.2 0.5 shard_map.71
  95.7 1.0 collective-permute-done.9
  96.8 0.8 collective-permute-start.10
  97.6 1.2 %shard_map.72 = f32[384,512]{1,0:T(8,128)} custom-call(f32[384,512]{1,0:T(8,128)S(1)} %get-tuple-element.95.u1, bf16[256,512]{1,0:T(8,128)(2,1)S(1)} %get-tuple-element.96.v1_half, bf16[128,384]{1,0:T(8,128)(2,1)S(1)} %get-tuple-element.100.refs_0_, bf16[128,384]{1,0:T(8,128)(2,1)S(1)} %get-tuple-element.101.refs_1_), custom_call_target="tpu_custom_call" | custom-call | flops 100663296 | bytes 4194304 | tf_op jit(solution)/shard_map/pallas_call | solution.py:145
  98.8 3.6 %collective-permute-done.10 = f32[64,512]{1,0:T(8,128)S(1)} collective-permute-done((f32[64,512]{1,0:T(8,128)S(1)}, f32[64,512]{1,0:T(8,128)S(1)}, u32[]{:S(2)}, u32[]{:S(2)}) %collective-permute-start.10) | collective-permute-done | bytes 131104 | tf_op jit(solution)/shard_map/ppermute | solution.py:163
  102.4 0.1 collective-permute-start.12
  102.5 0.1 collective-permute-start.11
  102.6 8.1 %collective-permute-done.12 = f32[64,512]{1,0:T(8,128)S(1)} collective-permute-done((f32[64,512]{1,0:T(8,128)S(1)}, f32[64,512]{1,0:T(8,128)S(1)}, u32[]{:S(2)}, u32[]{:S(2)}) %collective-permute-start.12) | collective-permute-done | bytes 131104 | tf_op jit(solution)/shard_map/ppermute | solution.py:163
  110.7 2.9 %collective-permute-done.11 = f32[64,512]{1,0:T(8,128)S(1)} collective-permute-done((f32[64,512]{1,0:T(8,128)S(1)}, f32[64,512]{1,0:T(8,128)S(1)}, u32[]{:S(2)}, u32[]{:S(2)}) %collective-permute-start.11) | collective-permute-done | bytes 131104 | tf_op jit(solution)/shard_map/ppermute | solution.py:163
  113.6 0.1 collective-permute-start.13
  113.7 0.7 shard_map.73.refs_0_
  114.4 0.8 collective-permute-done.13.half
  115.2 0.7 shard_map.74
  (8 shorter events, 0.2 us)
Async XLA Ops:
  3.3 18.0 %collective-permute-start = (f32[256,512]{1,0:T(8,128)S(1)}, f32[256,512]{1,0:T(8,128)S(1)}, u32[]{:S(2)}, u32[]{:S(2)}) collective-permute-start(f32[256,512]{1,0:T(8,128)S(1)} %get-tuple-element.57), channel_id=1, source_target_pairs={{0,4},{1,5},{2,6},{3,7},{4,8},{5,9},{6,10},{7,11},{8,12},{9,13},{1... | collective-permute-start | bytes 1572872 | tf_op jit(solution)/shard_map/ppermute | solution.py:163
  22.4 15.9 %collective-permute-start.1 = (f32[256,512]{1,0:T(8,128)S(1)}, f32[256,512]{1,0:T(8,128)S(1)}, u32[]{:S(2)}, u32[]{:S(2)}) collective-permute-start(f32[256,512]{1,0:T(8,128)S(1)} %get-tuple-element.64), channel_id=1, source_target_pairs={{0,4},{1,5},{2,6},{3,7},{4,8},{5,9},{6,10},{7,11},{8,12},{9,13},{1... | collective-permute-start | bytes 1572872 | tf_op jit(solution)/shard_map/ppermute | solution.py:163
  39.3 1.6 %collective-permute-start.2 = (f32[128,512]{1,0:T(8,128)S(1)}, f32[128,512]{1,0:T(8,128)S(1)}, u32[]{:S(2)}, u32[]{:S(2)}) collective-permute-start(f32[128,512]{1,0:T(8,128)S(1)} %get-tuple-element.71), channel_id=1, source_target_pairs={{0,1},{1,0},{2,3},{3,2},{4,5},{5,4},{6,7},{7,6},{8,9},{9,8},{10,11... | collective-permute-start | bytes 786440 | tf_op jit(solution)/shard_map/ppermute | solution.py:163
  41.0 5.6 %collective-permute-start.3 = (f32[64,512]{1,0:T(8,128)S(1)}, f32[64,512]{1,0:T(8,128)S(1)}, u32[]{:S(2)}, u32[]{:S(2)}) collective-permute-start(f32[64,512]{1,0:T(8,128)S(1)} %slice_select_fusion.1), channel_id=1, source_target_pairs={{0,2},{1,3},{2,0},{3,1},{4,6},{5,7},{6,4},{7,5},{8,10},{9,11},{10,... | collective-permute-start | bytes 393224 | tf_op jit(solution)/shard_map/ppermute | solution.py:163
  46.6 9.2 %collective-permute-start.5 = (f32[64,512]{1,0:T(8,128)S(1)}, f32[64,512]{1,0:T(8,128)S(1)}, u32[]{:S(2)}, u32[]{:S(2)}) collective-permute-start(f32[64,512]{1,0:T(8,128)S(1)} %add_multiply_fusion.1), channel_id=1, source_target_pairs={{0,4},{1,5},{2,6},{3,7},{4,8},{5,9},{6,10},{7,11},{8,12},{9,13},{1... | collective-permute-start | bytes 393224 | tf_op jit(solution)/shard_map/ppermute | solution.py:163
  46.7 10.9 %collective-permute-start.4 = (f32[64,512]{1,0:T(8,128)S(1)}, f32[64,512]{1,0:T(8,128)S(1)}, u32[]{:S(2)}, u32[]{:S(2)}) collective-permute-start(f32[64,512]{1,0:T(8,128)S(1)} %add_multiply_fusion.1), channel_id=1, source_target_pairs={{0,6},{1,7},{2,4},{3,5},{4,10},{5,11},{6,8},{7,9},{8,14},{9,15},{1... | collective-permute-start | bytes 393224 | tf_op jit(solution)/shard_map/ppermute | solution.py:163
  57.6 1.6 %collective-permute-start.6 = (f32[128,512]{1,0:T(8,128)S(1)}, f32[128,512]{1,0:T(8,128)S(1)}, u32[]{:S(2)}, u32[]{:S(2)}) collective-permute-start(f32[128,512]{1,0:T(8,128)S(1)} %maximum_select_fusion.refs_0_), channel_id=1, source_target_pairs={{0,1},{1,0},{2,3},{3,2},{4,5},{5,4},{6,7},{7,6},{8,9},{9,8},{10,11... | collective-permute-start | bytes 786440 | tf_op jit(solution)/shard_map/ppermute | solution.py:163
  60.4 16.7 %collective-permute-start.7 = (f32[256,512]{1,0:T(8,128)S(1)}, f32[256,512]{1,0:T(8,128)S(1)}, u32[]{:S(2)}, u32[]{:S(2)}) collective-permute-start(f32[256,512]{1,0:T(8,128)S(1)} %get-tuple-element.85), channel_id=1, source_target_pairs={{0,4},{1,5},{2,6},{3,7},{4,8},{5,9},{6,10},{7,11},{8,12},{9,13},{1... | collective-permute-start | bytes 1572872 | tf_op jit(solution)/shard_map/ppermute | solution.py:163
  78.2 15.9 %collective-permute-start.8 = (f32[256,512]{1,0:T(8,128)S(1)}, f32[256,512]{1,0:T(8,128)S(1)}, u32[]{:S(2)}, u32[]{:S(2)}) collective-permute-start(f32[256,512]{1,0:T(8,128)S(1)} %get-tuple-element.92), channel_id=1, source_target_pairs={{0,4},{1,5},{2,6},{3,7},{4,8},{5,9},{6,10},{7,11},{8,12},{9,13},{1... | collective-permute-start | bytes 1572872 | tf_op jit(solution)/shard_map/ppermute | solution.py:163
  95.1 1.6 %collective-permute-start.9 = (f32[128,512]{1,0:T(8,128)S(1)}, f32[128,512]{1,0:T(8,128)S(1)}, u32[]{:S(2)}, u32[]{:S(2)}) collective-permute-start(f32[128,512]{1,0:T(8,128)S(1)} %get-tuple-element.99), channel_id=1, source_target_pairs={{0,1},{1,0},{2,3},{3,2},{4,5},{5,4},{6,7},{7,6},{8,9},{9,8},{10,11... | collective-permute-start | bytes 786440 | tf_op jit(solution)/shard_map/ppermute | solution.py:163
  96.8 5.6 %collective-permute-start.10 = (f32[64,512]{1,0:T(8,128)S(1)}, f32[64,512]{1,0:T(8,128)S(1)}, u32[]{:S(2)}, u32[]{:S(2)}) collective-permute-start(f32[64,512]{1,0:T(8,128)S(1)} %slice_select_fusion), channel_id=1, source_target_pairs={{0,2},{1,3},{2,0},{3,1},{4,6},{5,7},{6,4},{7,5},{8,10},{9,11},{10,... | collective-permute-start | bytes 393224 | tf_op jit(solution)/shard_map/ppermute | solution.py:163
  102.4 8.3 %collective-permute-start.12 = (f32[64,512]{1,0:T(8,128)S(1)}, f32[64,512]{1,0:T(8,128)S(1)}, u32[]{:S(2)}, u32[]{:S(2)}) collective-permute-start(f32[64,512]{1,0:T(8,128)S(1)} %add_multiply_fusion), channel_id=1, source_target_pairs={{0,12},{1,13},{2,14},{3,15},{4,16},{5,17},{6,18},{7,19},{8,20},{9,... | collective-permute-start | bytes 393224 | tf_op jit(solution)/shard_map/ppermute | solution.py:163
  102.5 11.1 %collective-permute-start.11 = (f32[64,512]{1,0:T(8,128)S(1)}, f32[64,512]{1,0:T(8,128)S(1)}, u32[]{:S(2)}, u32[]{:S(2)}) collective-permute-start(f32[64,512]{1,0:T(8,128)S(1)} %add_multiply_fusion), channel_id=1, source_target_pairs={{0,14},{1,15},{2,12},{3,13},{4,18},{5,19},{6,16},{7,17},{8,22},{9,... | collective-permute-start | bytes 393224 | tf_op jit(solution)/shard_map/ppermute | solution.py:163
  113.6 1.6 %collective-permute-start.13 = (f32[128,512]{1,0:T(8,128)S(1)}, f32[128,512]{1,0:T(8,128)S(1)}, u32[]{:S(2)}, u32[]{:S(2)}) collective-permute-start(f32[128,512]{1,0:T(8,128)S(1)} %maximum_select_fusion.1.half), channel_id=1, source_target_pairs={{0,1},{1,0},{2,3},{3,2},{4,5},{5,4},{6,7},{7,6},{8,9},{9,8},{10,11... | collective-permute-start | bytes 786440 | tf_op jit(solution)/shard_map/ppermute | solution.py:163

commit v11 on v10

--- a/solution.py
+++ b/solution.py
@@ -175,18 +175,23 @@
         received, *pending = lax.optimization_barrier((received, *pending))
         share = jnp.where(upper, high, low) + received
     share = share / groups
+    pieces = [share, share]
     for place, bit in enumerate(reversed(bits)):
         upper = (member & bit) != 0
         if place == 0:
             mine = moved(share, blocks, groups, distance)
             other = moved(share, blocks, groups, distance, bit)
         else:
-            mine = share
-            other = moved(share, blocks, groups, 0, bit)
-        share = jnp.where(
-            upper, jnp.concatenate([other, mine], 0), jnp.concatenate([mine, other], 0)
-        )
-    return share, moved(share, blocks, groups, 0, 1), pending
+            mine = pieces[0]
+            other = moved(pieces[0], blocks, groups, 0, bit)
+        last = place == len(bits) - 1
+        both = [(mine, other)]
+        if last:
+            both.append((moved(mine, blocks, groups, 0, 1), moved(other, blocks, groups, 0, 1)))
+        pieces = [
+            jnp.where(upper, jnp.concatenate([o, m], 0), jnp.concatenate([m, o], 0)) for m, o in both
+        ]
+    return pieces[0], pieces[1], pending
 
 
 def solution(mesh):

time: 116 us -> 116 us (level)
    ppermute x14 -> x16, waiting for transfers between devices: 90.1 us -> 89.7 us  [moved(): return lax.ppermute(block, AXES, route)]
    ppermute x14 -> x16, starting transfers between devices: 5.89 us -> 5.75 us  [moved(): return lax.ppermute(block, AXES, route)]
  transfers between devices with their start and end apart: 14 -> 16, of which waited for: 14 -> 14; matrix products, arithmetic and copies ran while one was open for 0% -> 0% of each run, Pallas kernels for 9% -> 9%
where the time goes in v11:
time: 116 us; the launch traced here: 115 us
  waiting for transfers between devices  89.7 us (77%)
  Pallas kernels  18.8 us (16%)
  starting transfers between devices  5.75 us (5%)
    ppermute x16, waiting for transfers between devices, moved(): return lax.ppermute(block, AXES, route)  89.7 us
    pallas_call x16, Pallas kernels, call(): pl.pallas_call(body, out_shape=[jax.ShapeDtypeStruct(shape, dtype) for sh...  18.8 us
    ppermute x16, starting transfers between devices, moved(): return lax.ppermute(block, AXES, route)  5.75 us
  transfers between devices with their start and end apart: 16, of which 14 were waited for; matrix products, arithmetic and copies ran while one was open for 0% of the time, Pallas kernels for 9%

profile of v11, /device:TPU:0, one launch (start us, length us, event | category | flops | bytes accessed | tf_op | source)
XLA Modules:
  0.0 115.5 jit_solution(9850845837939403233)
XLA Ops:
  0.6 2.6 %shard_map.59 = (f32[384,512]{1,0:T(8,128)S(1)}, bf16[256,512]{1,0:T(8,128)(2,1)S(1)}, bf16[256,384]{1,0:T(8,128)(2,1)S(1)}, f32[256,512]{1,0:T(8,128)S(1)}) custom-call(s32[1]{0:T(128)} %bitcast.place, bf16[384,2048]{1,0:T(8,128)(2,1)} %refs_1_.7, s32[384,2048]{1,0:T(8,128)} %refs_2_.9, f32[384,512]{1,0:T(8,128)} %u_hbm.1, f32[256,512]{1,0:T(8,128)} %v_hbm.1), custom_call_target="tpu_custom_call" | custom-call | flops 503316480 | bytes 4194304 | tf_op jit(solution)/shard_map/pallas_call | solution.py:145
  3.3 3.0 %collective-permute-start = (f32[256,512]{1,0:T(8,128)S(1)}, f32[256,512]{1,0:T(8,128)S(1)}, u32[]{:S(2)}, u32[]{:S(2)}) collective-permute-start(f32[256,512]{1,0:T(8,128)S(1)} %get-tuple-element.57), channel_id=1, source_target_pairs={{0,4},{1,5},{2,6},{3,7},{4,8},{5,9},{6,10},{7,11},{8,12},{9,13},{1... | collective-permute-start | bytes 1572872 | tf_op jit(solution)/shard_map/ppermute | solution.py:163
  6.3 1.4 %shard_map.60 = (f32[384,512]{1,0:T(8,128)S(1)}, f32[256,384]{1,0:T(8,128)S(1)}, f32[256,384]{1,0:T(8,128)S(1)}) custom-call(s32[1]{0:T(128)} %bitcast.place, f32[384,512]{1,0:T(8,128)S(1)} %get-tuple-element.53.u1, bf16[256,512]{1,0:T(8,128)(2,1)S(1)} %get-tuple-element.54.v1_half, bf16[256,384]{1,0:T(8,128)(2,1)S(1)} %get-tuple-element.55.refs_0_, ...), custom_call_target="tpu_custom_call" | custom-call | flops 100663296 | bytes 4194304 | tf_op jit(solution)/shard_map/pallas_call | solution.py:145
  7.8 13.5 %collective-permute-done.refs_0_ = f32[256,512]{1,0:T(8,128)S(1)} collective-permute-done((f32[256,512]{1,0:T(8,128)S(1)}, f32[256,512]{1,0:T(8,128)S(1)}, u32[]{:S(2)}, u32[]{:S(2)}) %collective-permute-start) | collective-permute-done | bytes 524320 | tf_op jit(solution)/shard_map/ppermute | solution.py:163
  21.3 1.1 shard_map.61
  22.4 0.1 collective-permute-start.1
  22.5 1.4 %shard_map.62 = (f32[384,512]{1,0:T(8,128)S(1)}, f32[256,384]{1,0:T(8,128)S(1)}, f32[256,384]{1,0:T(8,128)S(1)}) custom-call(s32[1]{0:T(128)} %bitcast.place, f32[384,512]{1,0:T(8,128)S(1)} %get-tuple-element.60.u1, bf16[256,512]{1,0:T(8,128)(2,1)S(1)} %get-tuple-element.61.v1_half, bf16[256,384]{1,0:T(8,128)(2,1)S(1)} %get-tuple-element.62.refs_0_, ...), custom_call_target="tpu_custom_call" | custom-call | flops 100663296 | bytes 4194304 | tf_op jit(solution)/shard_map/pallas_call | solution.py:145
  23.9 14.3 %collective-permute-done.1.refs_0_ = f32[256,512]{1,0:T(8,128)S(1)} collective-permute-done((f32[256,512]{1,0:T(8,128)S(1)}, f32[256,512]{1,0:T(8,128)S(1)}, u32[]{:S(2)}, u32[]{:S(2)}) %collective-permute-start.1) | collective-permute-done | bytes 524320 | tf_op jit(solution)/shard_map/ppermute | solution.py:163
  38.3 1.0 shard_map.63
  39.3 0.1 collective-permute-start.2
  39.4 0.5 shard_map.64
  39.9 1.0 collective-permute-done.2
  41.0 1.4 %collective-permute-start.3 = (f32[64,512]{1,0:T(8,128)S(1)}, f32[64,512]{1,0:T(8,128)S(1)}, u32[]{:S(2)}, u32[]{:S(2)}) collective-permute-start(f32[64,512]{1,0:T(8,128)S(1)} %slice_select_fusion.1), channel_id=1, source_target_pairs={{0,2},{1,3},{2,0},{3,1},{4,6},{5,7},{6,4},{7,5},{8,10},{9,11},{10,... | collective-permute-start | bytes 393224 | tf_op jit(solution)/shard_map/ppermute | solution.py:163
  42.3 1.4 %shard_map.65 = (f32[384,512]{1,0:T(8,128)S(1)}, f32[256,384]{1,0:T(8,128)S(1)}, f32[256,384]{1,0:T(8,128)S(1)}) custom-call(s32[1]{0:T(128)} %bitcast.place, f32[384,512]{1,0:T(8,128)S(1)} %get-tuple-element.67.u1, bf16[256,512]{1,0:T(8,128)(2,1)S(1)} %get-tuple-element.68.v1_half, bf16[128,384]{1,0:T(8,128)(2,1)S(1)} %get-tuple-element.72.refs_0_, ...), custom_call_target="tpu_custom_call" | custom-call | flops 100663296 | bytes 4194304 | tf_op jit(solution)/shard_map/pallas_call | solution.py:145
  43.8 2.8 %collective-permute-done.3 = f32[64,512]{1,0:T(8,128)S(1)} collective-permute-done((f32[64,512]{1,0:T(8,128)S(1)}, f32[64,512]{1,0:T(8,128)S(1)}, u32[]{:S(2)}, u32[]{:S(2)}) %collective-permute-start.3) | collective-permute-done | bytes 131104 | tf_op jit(solution)/shard_map/ppermute | solution.py:163
  46.6 0.1 collective-permute-start.5
  46.7 0.1 collective-permute-start.4
  46.7 9.1 %collective-permute-done.5 = f32[64,512]{1,0:T(8,128)S(1)} collective-permute-done((f32[64,512]{1,0:T(8,128)S(1)}, f32[64,512]{1,0:T(8,128)S(1)}, u32[]{:S(2)}, u32[]{:S(2)}) %collective-permute-start.5) | collective-permute-done | bytes 131104 | tf_op jit(solution)/shard_map/ppermute | solution.py:163
  55.8 0.0 collective-permute-start.7
  55.8 1.8 %collective-permute-done.4 = f32[64,512]{1,0:T(8,128)S(1)} collective-permute-done((f32[64,512]{1,0:T(8,128)S(1)}, f32[64,512]{1,0:T(8,128)S(1)}, u32[]{:S(2)}, u32[]{:S(2)}) %collective-permute-start.4) | collective-permute-done | bytes 131104 | tf_op jit(solution)/shard_map/ppermute | solution.py:163
  57.6 0.0 collective-permute-start.6
  57.6 0.0 collective-permute-done.7
  57.6 1.3 %collective-permute-done.6 = f32[64,512]{1,0:T(8,128)S(1)} collective-permute-done((f32[64,512]{1,0:T(8,128)S(1)}, f32[64,512]{1,0:T(8,128)S(1)}, u32[]{:S(2)}, u32[]{:S(2)}) %collective-permute-start.6) | collective-permute-done | bytes 131104 | tf_op jit(solution)/shard_map/ppermute | solution.py:163
  59.0 1.1 shard_map.66
  60.1 0.1 collective-permute-start.8
  60.2 1.4 %shard_map.67 = (f32[384,512]{1,0:T(8,128)S(1)}, f32[256,384]{1,0:T(8,128)S(1)}, f32[256,384]{1,0:T(8,128)S(1)}) custom-call(s32[1]{0:T(128)} %bitcast.place, f32[384,512]{1,0:T(8,128)S(1)} %get-tuple-element.81.u1, bf16[256,512]{1,0:T(8,128)(2,1)S(1)} %get-tuple-element.82.v1_half, bf16[256,384]{1,0:T(8,128)(2,1)S(1)} %get-tuple-element.83.refs_0_, ...), custom_call_target="tpu_custom_call" | custom-call | flops 100663296 | bytes 4194304 | tf_op jit(solution)/shard_map/pallas_call | solution.py:145
  61.6 15.2 %collective-permute-done.8.refs_0_ = f32[256,512]{1,0:T(8,128)S(1)} collective-permute-done((f32[256,512]{1,0:T(8,128)S(1)}, f32[256,512]{1,0:T(8,128)S(1)}, u32[]{:S(2)}, u32[]{:S(2)}) %collective-permute-start.8) | collective-permute-done | bytes 524320 | tf_op jit(solution)/shard_map/ppermute | solution.py:163
  76.8 1.1 shard_map.68
  78.0 0.1 collective-permute-start.9
  78.0 1.4 %shard_map.69 = (f32[384,512]{1,0:T(8,128)S(1)}, f32[256,384]{1,0:T(8,128)S(1)}, f32[256,384]{1,0:T(8,128)S(1)}) custom-call(s32[1]{0:T(128)} %bitcast.place, f32[384,512]{1,0:T(8,128)S(1)} %get-tuple-element.88.u1, bf16[256,512]{1,0:T(8,128)(2,1)S(1)} %get-tuple-element.89.v1_half, bf16[256,384]{1,0:T(8,128)(2,1)S(1)} %get-tuple-element.90.refs_0_, ...), custom_call_target="tpu_custom_call" | custom-call | flops 100663296 | bytes 4194304 | tf_op jit(solution)/shard_map/pallas_call | solution.py:145
  79.5 14.4 %collective-permute-done.9.refs_0_ = f32[256,512]{1,0:T(8,128)S(1)} collective-permute-done((f32[256,512]{1,0:T(8,128)S(1)}, f32[256,512]{1,0:T(8,128)S(1)}, u32[]{:S(2)}, u32[]{:S(2)}) %collective-permute-start.9) | collective-permute-done | bytes 524320 | tf_op jit(solution)/shard_map/ppermute | solution.py:163
  93.9 1.0 shard_map.70
  94.9 0.1 collective-permute-start.10
  95.0 0.5 shard_map.71
  95.5 1.0 collective-permute-done.10
  96.6 0.8 collective-permute-start.11
  97.3 1.2 %shard_map.72 = f32[384,512]{1,0:T(8,128)} custom-call(f32[384,512]{1,0:T(8,128)S(1)} %get-tuple-element.95.u1, bf16[256,512]{1,0:T(8,128)(2,1)S(1)} %get-tuple-element.96.v1_half, bf16[128,384]{1,0:T(8,128)(2,1)S(1)} %get-tuple-element.100.refs_0_, bf16[128,384]{1,0:T(8,128)(2,1)S(1)} %get-tuple-element.101.refs_1_), custom_call_target="tpu_custom_call" | custom-call | flops 100663296 | bytes 4194304 | tf_op jit(solution)/shard_map/pallas_call | solution.py:145
  98.5 3.6 %collective-permute-done.11 = f32[64,512]{1,0:T(8,128)S(1)} collective-permute-done((f32[64,512]{1,0:T(8,128)S(1)}, f32[64,512]{1,0:T(8,128)S(1)}, u32[]{:S(2)}, u32[]{:S(2)}) %collective-permute-start.11) | collective-permute-done | bytes 131104 | tf_op jit(solution)/shard_map/ppermute | solution.py:163
  102.2 0.1 collective-permute-start.14
  102.3 0.1 collective-permute-start.12
  102.3 8.1 %collective-permute-done.14 = f32[64,512]{1,0:T(8,128)S(1)} collective-permute-done((f32[64,512]{1,0:T(8,128)S(1)}, f32[64,512]{1,0:T(8,128)S(1)}, u32[]{:S(2)}, u32[]{:S(2)}) %collective-permute-start.14) | collective-permute-done | bytes 131104 | tf_op jit(solution)/shard_map/ppermute | solution.py:163
  110.5 0.0 collective-permute-start.15
  110.5 2.9 %collective-permute-done.12 = f32[64,512]{1,0:T(8,128)S(1)} collective-permute-done((f32[64,512]{1,0:T(8,128)S(1)}, f32[64,512]{1,0:T(8,128)S(1)}, u32[]{:S(2)}, u32[]{:S(2)}) %collective-permute-start.12) | collective-permute-done | bytes 131104 | tf_op jit(solution)/shard_map/ppermute | solution.py:163
  113.4 0.0 collective-permute-start.13
  113.4 0.7 shard_map.73.refs_0_
  114.1 0.0 collective-permute-done.15
  114.1 0.6 collective-permute-done.13
  114.7 0.7 shard_map.74
  (10 shorter events, 0.3 us)
Async XLA Ops:
  3.3 18.0 %collective-permute-start = (f32[256,512]{1,0:T(8,128)S(1)}, f32[256,512]{1,0:T(8,128)S(1)}, u32[]{:S(2)}, u32[]{:S(2)}) collective-permute-start(f32[256,512]{1,0:T(8,128)S(1)} %get-tuple-element.57), channel_id=1, source_target_pairs={{0,4},{1,5},{2,6},{3,7},{4,8},{5,9},{6,10},{7,11},{8,12},{9,13},{1... | collective-permute-start | bytes 1572872 | tf_op jit(solution)/shard_map/ppermute | solution.py:163
  22.4 15.9 %collective-permute-start.1 = (f32[256,512]{1,0:T(8,128)S(1)}, f32[256,512]{1,0:T(8,128)S(1)}, u32[]{:S(2)}, u32[]{:S(2)}) collective-permute-start(f32[256,512]{1,0:T(8,128)S(1)} %get-tuple-element.64), channel_id=1, source_target_pairs={{0,4},{1,5},{2,6},{3,7},{4,8},{5,9},{6,10},{7,11},{8,12},{9,13},{1... | collective-permute-start | bytes 1572872 | tf_op jit(solution)/shard_map/ppermute | solution.py:163
  39.3 1.6 %collective-permute-start.2 = (f32[128,512]{1,0:T(8,128)S(1)}, f32[128,512]{1,0:T(8,128)S(1)}, u32[]{:S(2)}, u32[]{:S(2)}) collective-permute-start(f32[128,512]{1,0:T(8,128)S(1)} %get-tuple-element.71), channel_id=1, source_target_pairs={{0,1},{1,0},{2,3},{3,2},{4,5},{5,4},{6,7},{7,6},{8,9},{9,8},{10,11... | collective-permute-start | bytes 786440 | tf_op jit(solution)/shard_map/ppermute | solution.py:163
  41.0 5.6 %collective-permute-start.3 = (f32[64,512]{1,0:T(8,128)S(1)}, f32[64,512]{1,0:T(8,128)S(1)}, u32[]{:S(2)}, u32[]{:S(2)}) collective-permute-start(f32[64,512]{1,0:T(8,128)S(1)} %slice_select_fusion.1), channel_id=1, source_target_pairs={{0,2},{1,3},{2,0},{3,1},{4,6},{5,7},{6,4},{7,5},{8,10},{9,11},{10,... | collective-permute-start | bytes 393224 | tf_op jit(solution)/shard_map/ppermute | solution.py:163
  46.6 9.2 %collective-permute-start.5 = (f32[64,512]{1,0:T(8,128)S(1)}, f32[64,512]{1,0:T(8,128)S(1)}, u32[]{:S(2)}, u32[]{:S(2)}) collective-permute-start(f32[64,512]{1,0:T(8,128)S(1)} %add_multiply_fusion.1), channel_id=1, source_target_pairs={{0,4},{1,5},{2,6},{3,7},{4,8},{5,9},{6,10},{7,11},{8,12},{9,13},{1... | collective-permute-start | bytes 393224 | tf_op jit(solution)/shard_map/ppermute | solution.py:163
  46.7 10.9 %collective-permute-start.4 = (f32[64,512]{1,0:T(8,128)S(1)}, f32[64,512]{1,0:T(8,128)S(1)}, u32[]{:S(2)}, u32[]{:S(2)}) collective-permute-start(f32[64,512]{1,0:T(8,128)S(1)} %add_multiply_fusion.1), channel_id=1, source_target_pairs={{0,6},{1,7},{2,4},{3,5},{4,10},{5,11},{6,8},{7,9},{8,14},{9,15},{1... | collective-permute-start | bytes 393224 | tf_op jit(solution)/shard_map/ppermute | solution.py:163
  55.8 1.9 %collective-permute-start.7 = (f32[64,512]{1,0:T(8,128)S(1)}, f32[64,512]{1,0:T(8,128)S(1)}, u32[]{:S(2)}, u32[]{:S(2)}) collective-permute-start(f32[64,512]{1,0:T(8,128)S(1)} %collective-permute-done.5), channel_id=1, source_target_pairs={{0,1},{1,0},{2,3},{3,2},{4,5},{5,4},{6,7},{7,6},{8,9},{9,8},{10,11... | collective-permute-start | bytes 393224 | tf_op jit(solution)/shard_map/ppermute | solution.py:163
  57.6 1.3 %collective-permute-start.6 = (f32[64,512]{1,0:T(8,128)S(1)}, f32[64,512]{1,0:T(8,128)S(1)}, u32[]{:S(2)}, u32[]{:S(2)}) collective-permute-start(f32[64,512]{1,0:T(8,128)S(1)} %collective-permute-done.4), channel_id=1, source_target_pairs={{0,1},{1,0},{2,3},{3,2},{4,5},{5,4},{6,7},{7,6},{8,9},{9,8},{10,11... | collective-permute-start | bytes 393224 | tf_op jit(solution)/shard_map/ppermute | solution.py:163
  60.1 16.7 %collective-permute-start.8 = (f32[256,512]{1,0:T(8,128)S(1)}, f32[256,512]{1,0:T(8,128)S(1)}, u32[]{:S(2)}, u32[]{:S(2)}) collective-permute-start(f32[256,512]{1,0:T(8,128)S(1)} %get-tuple-element.85), channel_id=1, source_target_pairs={{0,4},{1,5},{2,6},{3,7},{4,8},{5,9},{6,10},{7,11},{8,12},{9,13},{1... | collective-permute-start | bytes 1572872 | tf_op jit(solution)/shard_map/ppermute | solution.py:163
  78.0 15.9 %collective-permute-start.9 = (f32[256,512]{1,0:T(8,128)S(1)}, f32[256,512]{1,0:T(8,128)S(1)}, u32[]{:S(2)}, u32[]{:S(2)}) collective-permute-start(f32[256,512]{1,0:T(8,128)S(1)} %get-tuple-element.92), channel_id=1, source_target_pairs={{0,4},{1,5},{2,6},{3,7},{4,8},{5,9},{6,10},{7,11},{8,12},{9,13},{1... | collective-permute-start | bytes 1572872 | tf_op jit(solution)/shard_map/ppermute | solution.py:163
  94.9 1.6 %collective-permute-start.10 = (f32[128,512]{1,0:T(8,128)S(1)}, f32[128,512]{1,0:T(8,128)S(1)}, u32[]{:S(2)}, u32[]{:S(2)}) collective-permute-start(f32[128,512]{1,0:T(8,128)S(1)} %get-tuple-element.99), channel_id=1, source_target_pairs={{0,1},{1,0},{2,3},{3,2},{4,5},{5,4},{6,7},{7,6},{8,9},{9,8},{10,11... | collective-permute-start | bytes 786440 | tf_op jit(solution)/shard_map/ppermute | solution.py:163
  96.6 5.6 %collective-permute-start.11 = (f32[64,512]{1,0:T(8,128)S(1)}, f32[64,512]{1,0:T(8,128)S(1)}, u32[]{:S(2)}, u32[]{:S(2)}) collective-permute-start(f32[64,512]{1,0:T(8,128)S(1)} %slice_select_fusion), channel_id=1, source_target_pairs={{0,2},{1,3},{2,0},{3,1},{4,6},{5,7},{6,4},{7,5},{8,10},{9,11},{10,... | collective-permute-start | bytes 393224 | tf_op jit(solution)/shard_map/ppermute | solution.py:163
  102.2 8.3 %collective-permute-start.14 = (f32[64,512]{1,0:T(8,128)S(1)}, f32[64,512]{1,0:T(8,128)S(1)}, u32[]{:S(2)}, u32[]{:S(2)}) collective-permute-start(f32[64,512]{1,0:T(8,128)S(1)} %add_multiply_fusion), channel_id=1, source_target_pairs={{0,12},{1,13},{2,14},{3,15},{4,16},{5,17},{6,18},{7,19},{8,20},{9,... | collective-permute-start | bytes 393224 | tf_op jit(solution)/shard_map/ppermute | solution.py:163
  102.3 11.1 %collective-permute-start.12 = (f32[64,512]{1,0:T(8,128)S(1)}, f32[64,512]{1,0:T(8,128)S(1)}, u32[]{:S(2)}, u32[]{:S(2)}) collective-permute-start(f32[64,512]{1,0:T(8,128)S(1)} %add_multiply_fusion), channel_id=1, source_target_pairs={{0,14},{1,15},{2,12},{3,13},{4,18},{5,19},{6,16},{7,17},{8,22},{9,... | collective-permute-start | bytes 393224 | tf_op jit(solution)/shard_map/ppermute | solution.py:163
  110.5 3.7 %collective-permute-start.15 = (f32[64,512]{1,0:T(8,128)S(1)}, f32[64,512]{1,0:T(8,128)S(1)}, u32[]{:S(2)}, u32[]{:S(2)}) collective-permute-start(f32[64,512]{1,0:T(8,128)S(1)} %collective-permute-done.14), channel_id=1, source_target_pairs={{0,1},{1,0},{2,3},{3,2},{4,5},{5,4},{6,7},{7,6},{8,9},{9,8},{10,11... | collective-permute-start | bytes 393224 | tf_op jit(solution)/shard_map/ppermute | solution.py:163
  113.4 1.3 %collective-permute-start.13 = (f32[64,512]{1,0:T(8,128)S(1)}, f32[64,512]{1,0:T(8,128)S(1)}, u32[]{:S(2)}, u32[]{:S(2)}) collective-permute-start(f32[64,512]{1,0:T(8,128)S(1)} %collective-permute-done.12), channel_id=1, source_target_pairs={{0,1},{1,0},{2,3},{3,2},{4,5},{5,4},{6,7},{7,6},{8,9},{9,8},{10,11... | collective-permute-start | bytes 393224 | tf_op jit(solution)/shard_map/ppermute | solution.py:163

commit v12 on v11

--- a/solution.py
+++ b/solution.py
@@ -166,14 +166,22 @@
 def average(part_a, part_b, pending, blocks, groups, distance):
     member = lax.axis_index("group")
     bits = [1 << i for i in range(1, groups.bit_length() - 1)]
-    share = part_b + moved(part_a, blocks, groups, 0, 1)
+    share = None
     for bit in bits:
-        rows = share.shape[0] // 2
         upper = (member & bit) != 0
-        low, high = share[:rows], share[rows:]
-        received = moved(jnp.where(upper, low, high), blocks, groups, 0, bit)
+        rows = (part_b if share is None else share).shape[0] // 2
+
+        def split(block):
+            low, high = block[:rows], block[rows:]
+            return jnp.where(upper, low, high), jnp.where(upper, high, low)
+
+        if share is None:
+            send, keep = (b + moved(a, blocks, groups, 0, 1) for a, b in zip(split(part_a), split(part_b)))
+        else:
+            send, keep = split(share)
+        received = moved(send, blocks, groups, 0, bit)
         received, *pending = lax.optimization_barrier((received, *pending))
-        share = jnp.where(upper, high, low) + received
+        share = keep + received
     share = share / groups
     pieces = [share, share]
     for place, bit in enumerate(reversed(bits)):

time: 116 us -> 115 us (level)
    ppermute x16 -> x18, waiting for transfers between devices: 89.7 us -> 89.4 us  [moved(): return lax.ppermute(block, AXES, route)]
    ppermute x16 -> x18, starting transfers between devices: 5.75 us -> 5.75 us  [moved(): return lax.ppermute(block, AXES, route)]
  transfers between devices with their start and end apart: 16 -> 18, of which waited for: 14 -> 14; matrix products, arithmetic and copies ran while one was open for 0% -> 0% of each run, Pallas kernels for 9% -> 9%
where the time goes in v12:
time: 115 us
  waiting for transfers between devices  89.4 us (78%)
  Pallas kernels  18.8 us (16%)
  starting transfers between devices  5.75 us (5%)
    ppermute x18, waiting for transfers between devices, moved(): return lax.ppermute(block, AXES, route)  89.4 us
    pallas_call x16, Pallas kernels, call(): pl.pallas_call(body, out_shape=[jax.ShapeDtypeStruct(shape, dtype) for sh...  18.8 us
    ppermute x18, starting transfers between devices, moved(): return lax.ppermute(block, AXES, route)  5.75 us
  transfers between devices with their start and end apart: 18, of which 14 were waited for; matrix products, arithmetic and copies ran while one was open for 0% of the time, Pallas kernels for 9%

profile of v12, /device:TPU:0, one launch (start us, length us, event | category | flops | bytes accessed | tf_op | source)
XLA Modules:
  0.0 115.1 jit_solution(15567150551337160455)
XLA Ops:
  0.6 2.6 %shard_map.59 = (f32[384,512]{1,0:T(8,128)S(1)}, bf16[256,512]{1,0:T(8,128)(2,1)S(1)}, bf16[256,384]{1,0:T(8,128)(2,1)S(1)}, f32[256,512]{1,0:T(8,128)S(1)}) custom-call(s32[1]{0:T(128)} %bitcast.place, bf16[384,2048]{1,0:T(8,128)(2,1)} %refs_1_.7, s32[384,2048]{1,0:T(8,128)} %refs_2_.9, f32[384,512]{1,0:T(8,128)} %u_hbm.1, f32[256,512]{1,0:T(8,128)} %v_hbm.1), custom_call_target="tpu_custom_call" | custom-call | flops 503316480 | bytes 4194304 | tf_op jit(solution)/shard_map/pallas_call | solution.py:145
  3.3 3.0 %collective-permute-start = (f32[256,512]{1,0:T(8,128)S(1)}, f32[256,512]{1,0:T(8,128)S(1)}, u32[]{:S(2)}, u32[]{:S(2)}) collective-permute-start(f32[256,512]{1,0:T(8,128)S(1)} %get-tuple-element.57), channel_id=1, source_target_pairs={{0,4},{1,5},{2,6},{3,7},{4,8},{5,9},{6,10},{7,11},{8,12},{9,13},{1... | collective-permute-start | bytes 1572872 | tf_op jit(solution)/shard_map/ppermute | solution.py:163
  6.3 1.4 %shard_map.60 = (f32[384,512]{1,0:T(8,128)S(1)}, f32[256,384]{1,0:T(8,128)S(1)}, f32[256,384]{1,0:T(8,128)S(1)}) custom-call(s32[1]{0:T(128)} %bitcast.place, f32[384,512]{1,0:T(8,128)S(1)} %get-tuple-element.53.u1, bf16[256,512]{1,0:T(8,128)(2,1)S(1)} %get-tuple-element.54.v1_half, bf16[256,384]{1,0:T(8,128)(2,1)S(1)} %get-tuple-element.55.refs_0_, ...), custom_call_target="tpu_custom_call" | custom-call | flops 100663296 | bytes 4194304 | tf_op jit(solution)/shard_map/pallas_call | solution.py:145
  7.8 13.5 %collective-permute-done.refs_0_ = f32[256,512]{1,0:T(8,128)S(1)} collective-permute-done((f32[256,512]{1,0:T(8,128)S(1)}, f32[256,512]{1,0:T(8,128)S(1)}, u32[]{:S(2)}, u32[]{:S(2)}) %collective-permute-start) | collective-permute-done | bytes 524320 | tf_op jit(solution)/shard_map/ppermute | solution.py:163
  21.3 1.1 shard_map.61
  22.4 0.1 collective-permute-start.1
  22.5 1.4 %shard_map.62 = (f32[384,512]{1,0:T(8,128)S(1)}, f32[256,384]{1,0:T(8,128)S(1)}, f32[256,384]{1,0:T(8,128)S(1)}) custom-call(s32[1]{0:T(128)} %bitcast.place, f32[384,512]{1,0:T(8,128)S(1)} %get-tuple-element.60.u1, bf16[256,512]{1,0:T(8,128)(2,1)S(1)} %get-tuple-element.61.v1_half, bf16[256,384]{1,0:T(8,128)(2,1)S(1)} %get-tuple-element.62.refs_0_, ...), custom_call_target="tpu_custom_call" | custom-call | flops 100663296 | bytes 4194304 | tf_op jit(solution)/shard_map/pallas_call | solution.py:145
  23.9 14.3 %collective-permute-done.1.refs_0_ = f32[256,512]{1,0:T(8,128)S(1)} collective-permute-done((f32[256,512]{1,0:T(8,128)S(1)}, f32[256,512]{1,0:T(8,128)S(1)}, u32[]{:S(2)}, u32[]{:S(2)}) %collective-permute-start.1) | collective-permute-done | bytes 524320 | tf_op jit(solution)/shard_map/ppermute | solution.py:163
  38.3 1.0 shard_map.63
  39.3 0.1 collective-permute-start.2
  39.4 0.5 shard_map.64
  39.9 0.8 collective-permute-done.2
  40.8 1.4 %collective-permute-start.3 = (f32[64,512]{1,0:T(8,128)S(1)}, f32[64,512]{1,0:T(8,128)S(1)}, u32[]{:S(2)}, u32[]{:S(2)}) collective-permute-start(f32[64,512]{1,0:T(8,128)S(1)} %select_add_fusion.1), channel_id=1, source_target_pairs={{0,2},{1,3},{2,0},{3,1},{4,6},{5,7},{6,4},{7,5},{8,10},{9,11},{10,... | collective-permute-start | bytes 393224 | tf_op jit(solution)/shard_map/ppermute | solution.py:163
  42.1 0.0 collective-permute-start.4
  42.1 1.4 %shard_map.65 = (f32[384,512]{1,0:T(8,128)S(1)}, f32[256,384]{1,0:T(8,128)S(1)}, f32[256,384]{1,0:T(8,128)S(1)}) custom-call(s32[1]{0:T(128)} %bitcast.place, f32[384,512]{1,0:T(8,128)S(1)} %get-tuple-element.67.u1, bf16[256,512]{1,0:T(8,128)(2,1)S(1)} %get-tuple-element.68.v1_half, bf16[128,384]{1,0:T(8,128)(2,1)S(1)} %get-tuple-element.72.refs_0_, ...), custom_call_target="tpu_custom_call" | custom-call | flops 100663296 | bytes 4194304 | tf_op jit(solution)/shard_map/pallas_call | solution.py:145
  43.6 2.8 %collective-permute-done.3 = f32[64,512]{1,0:T(8,128)S(1)} collective-permute-done((f32[64,512]{1,0:T(8,128)S(1)}, f32[64,512]{1,0:T(8,128)S(1)}, u32[]{:S(2)}, u32[]{:S(2)}) %collective-permute-start.3) | collective-permute-done | bytes 131104 | tf_op jit(solution)/shard_map/ppermute | solution.py:163
  46.4 0.1 collective-permute-start.6
  46.5 0.1 collective-permute-start.5
  46.6 9.1 %collective-permute-done.6 = f32[64,512]{1,0:T(8,128)S(1)} collective-permute-done((f32[64,512]{1,0:T(8,128)S(1)}, f32[64,512]{1,0:T(8,128)S(1)}, u32[]{:S(2)}, u32[]{:S(2)}) %collective-permute-start.6) | collective-permute-done | bytes 131104 | tf_op jit(solution)/shard_map/ppermute | solution.py:163
  55.6 0.0 collective-permute-start.8
  55.6 1.8 %collective-permute-done.5 = f32[64,512]{1,0:T(8,128)S(1)} collective-permute-done((f32[64,512]{1,0:T(8,128)S(1)}, f32[64,512]{1,0:T(8,128)S(1)}, u32[]{:S(2)}, u32[]{:S(2)}) %collective-permute-start.5) | collective-permute-done | bytes 131104 | tf_op jit(solution)/shard_map/ppermute | solution.py:163
  57.5 0.0 collective-permute-done.8
  57.5 1.3 %collective-permute-done.7 = f32[64,512]{1,0:T(8,128)S(1)} collective-permute-done((f32[64,512]{1,0:T(8,128)S(1)}, f32[64,512]{1,0:T(8,128)S(1)}, u32[]{:S(2)}, u32[]{:S(2)}) %collective-permute-start.7) | collective-permute-done | bytes 131104 | tf_op jit(solution)/shard_map/ppermute | solution.py:163
  58.8 1.1 shard_map.66
  59.9 0.1 collective-permute-start.9
  60.0 1.4 %shard_map.67 = (f32[384,512]{1,0:T(8,128)S(1)}, f32[256,384]{1,0:T(8,128)S(1)}, f32[256,384]{1,0:T(8,128)S(1)}) custom-call(s32[1]{0:T(128)} %bitcast.place, f32[384,512]{1,0:T(8,128)S(1)} %get-tuple-element.81.u1, bf16[256,512]{1,0:T(8,128)(2,1)S(1)} %get-tuple-element.82.v1_half, bf16[256,384]{1,0:T(8,128)(2,1)S(1)} %get-tuple-element.83.refs_0_, ...), custom_call_target="tpu_custom_call" | custom-call | flops 100663296 | bytes 4194304 | tf_op jit(solution)/shard_map/pallas_call | solution.py:145
  61.5 15.2 %collective-permute-done.9.refs_0_ = f32[256,512]{1,0:T(8,128)S(1)} collective-permute-done((f32[256,512]{1,0:T(8,128)S(1)}, f32[256,512]{1,0:T(8,128)S(1)}, u32[]{:S(2)}, u32[]{:S(2)}) %collective-permute-start.9) | collective-permute-done | bytes 524320 | tf_op jit(solution)/shard_map/ppermute | solution.py:163
  76.7 1.1 shard_map.68
  77.8 0.1 collective-permute-start.10
  77.9 1.4 %shard_map.69 = (f32[384,512]{1,0:T(8,128)S(1)}, f32[256,384]{1,0:T(8,128)S(1)}, f32[256,384]{1,0:T(8,128)S(1)}) custom-call(s32[1]{0:T(128)} %bitcast.place, f32[384,512]{1,0:T(8,128)S(1)} %get-tuple-element.88.u1, bf16[256,512]{1,0:T(8,128)(2,1)S(1)} %get-tuple-element.89.v1_half, bf16[256,384]{1,0:T(8,128)(2,1)S(1)} %get-tuple-element.90.refs_0_, ...), custom_call_target="tpu_custom_call" | custom-call | flops 100663296 | bytes 4194304 | tf_op jit(solution)/shard_map/pallas_call | solution.py:145
  79.3 14.4 %collective-permute-done.10.refs_0_ = f32[256,512]{1,0:T(8,128)S(1)} collective-permute-done((f32[256,512]{1,0:T(8,128)S(1)}, f32[256,512]{1,0:T(8,128)S(1)}, u32[]{:S(2)}, u32[]{:S(2)}) %collective-permute-start.10) | collective-permute-done | bytes 524320 | tf_op jit(solution)/shard_map/ppermute | solution.py:163
  93.7 1.0 shard_map.70
  94.8 0.1 collective-permute-start.11
  94.8 0.5 shard_map.71
  95.3 0.8 collective-permute-done.11
  96.2 0.8 collective-permute-start.12
  97.0 0.0 collective-permute-start.13
  97.0 1.2 %shard_map.72 = f32[384,512]{1,0:T(8,128)} custom-call(f32[384,512]{1,0:T(8,128)S(1)} %get-tuple-element.95.u1, bf16[256,512]{1,0:T(8,128)(2,1)S(1)} %get-tuple-element.96.v1_half, bf16[128,384]{1,0:T(8,128)(2,1)S(1)} %get-tuple-element.100.refs_0_, bf16[128,384]{1,0:T(8,128)(2,1)S(1)} %get-tuple-element.101.refs_1_), custom_call_target="tpu_custom_call" | custom-call | flops 100663296 | bytes 4194304 | tf_op jit(solution)/shard_map/pallas_call | solution.py:145
  98.2 3.7 %collective-permute-done.12 = f32[64,512]{1,0:T(8,128)S(1)} collective-permute-done((f32[64,512]{1,0:T(8,128)S(1)}, f32[64,512]{1,0:T(8,128)S(1)}, u32[]{:S(2)}, u32[]{:S(2)}) %collective-permute-start.12) | collective-permute-done | bytes 131104 | tf_op jit(solution)/shard_map/ppermute | solution.py:163
  101.8 0.0 collective-permute-done.13
  101.9 0.1 collective-permute-start.16
  101.9 0.1 collective-permute-start.14
  102.0 8.2 %collective-permute-done.16 = f32[64,512]{1,0:T(8,128)S(1)} collective-permute-done((f32[64,512]{1,0:T(8,128)S(1)}, f32[64,512]{1,0:T(8,128)S(1)}, u32[]{:S(2)}, u32[]{:S(2)}) %collective-permute-start.16) | collective-permute-done | bytes 131104 | tf_op jit(solution)/shard_map/ppermute | solution.py:163
  110.2 2.9 %collective-permute-done.14 = f32[64,512]{1,0:T(8,128)S(1)} collective-permute-done((f32[64,512]{1,0:T(8,128)S(1)}, f32[64,512]{1,0:T(8,128)S(1)}, u32[]{:S(2)}, u32[]{:S(2)}) %collective-permute-start.14) | collective-permute-done | bytes 131104 | tf_op jit(solution)/shard_map/ppermute | solution.py:163
  113.0 0.0 collective-permute-start.15
  113.1 0.7 shard_map.73.refs_0_
  113.8 0.6 collective-permute-done.15
  114.4 0.7 shard_map.74
  (14 shorter events, 0.3 us)
Async XLA Ops:
  3.3 18.0 %collective-permute-start = (f32[256,512]{1,0:T(8,128)S(1)}, f32[256,512]{1,0:T(8,128)S(1)}, u32[]{:S(2)}, u32[]{:S(2)}) collective-permute-start(f32[256,512]{1,0:T(8,128)S(1)} %get-tuple-element.57), channel_id=1, source_target_pairs={{0,4},{1,5},{2,6},{3,7},{4,8},{5,9},{6,10},{7,11},{8,12},{9,13},{1... | collective-permute-start | bytes 1572872 | tf_op jit(solution)/shard_map/ppermute | solution.py:163
  22.4 15.9 %collective-permute-start.1 = (f32[256,512]{1,0:T(8,128)S(1)}, f32[256,512]{1,0:T(8,128)S(1)}, u32[]{:S(2)}, u32[]{:S(2)}) collective-permute-start(f32[256,512]{1,0:T(8,128)S(1)} %get-tuple-element.64), channel_id=1, source_target_pairs={{0,4},{1,5},{2,6},{3,7},{4,8},{5,9},{6,10},{7,11},{8,12},{9,13},{1... | collective-permute-start | bytes 1572872 | tf_op jit(solution)/shard_map/ppermute | solution.py:163
  39.3 1.4 %collective-permute-start.2 = (f32[64,512]{1,0:T(8,128)S(1)}, f32[64,512]{1,0:T(8,128)S(1)}, u32[]{:S(2)}, u32[]{:S(2)}) collective-permute-start(f32[64,512]{1,0:T(8,128)S(1)} %get-tuple-element.107), channel_id=1, source_target_pairs={{0,1},{1,0},{2,3},{3,2},{4,5},{5,4},{6,7},{7,6},{8,9},{9,8},{10,11... | collective-permute-start | bytes 393224 | tf_op jit(solution)/shard_map/ppermute | solution.py:163
  40.8 5.6 %collective-permute-start.3 = (f32[64,512]{1,0:T(8,128)S(1)}, f32[64,512]{1,0:T(8,128)S(1)}, u32[]{:S(2)}, u32[]{:S(2)}) collective-permute-start(f32[64,512]{1,0:T(8,128)S(1)} %select_add_fusion.1), channel_id=1, source_target_pairs={{0,2},{1,3},{2,0},{3,1},{4,6},{5,7},{6,4},{7,5},{8,10},{9,11},{10,... | collective-permute-start | bytes 393224 | tf_op jit(solution)/shard_map/ppermute | solution.py:163
  42.1 4.3 %collective-permute-start.4 = (f32[64,512]{1,0:T(8,128)S(1)}, f32[64,512]{1,0:T(8,128)S(1)}, u32[]{:S(2)}, u32[]{:S(2)}) collective-permute-start(f32[64,512]{1,0:T(8,128)S(1)} %get-tuple-element.106), channel_id=1, source_target_pairs={{0,1},{1,0},{2,3},{3,2},{4,5},{5,4},{6,7},{7,6},{8,9},{9,8},{10,11... | collective-permute-start | bytes 393224 | tf_op jit(solution)/shard_map/ppermute | solution.py:163
  46.4 9.2 %collective-permute-start.6 = (f32[64,512]{1,0:T(8,128)S(1)}, f32[64,512]{1,0:T(8,128)S(1)}, u32[]{:S(2)}, u32[]{:S(2)}) collective-permute-start(f32[64,512]{1,0:T(8,128)S(1)} %add_multiply_fusion.1), channel_id=1, source_target_pairs={{0,4},{1,5},{2,6},{3,7},{4,8},{5,9},{6,10},{7,11},{8,12},{9,13},{1... | collective-permute-start | bytes 393224 | tf_op jit(solution)/shard_map/ppermute | solution.py:163
  46.5 11.0 %collective-permute-start.5 = (f32[64,512]{1,0:T(8,128)S(1)}, f32[64,512]{1,0:T(8,128)S(1)}, u32[]{:S(2)}, u32[]{:S(2)}) collective-permute-start(f32[64,512]{1,0:T(8,128)S(1)} %add_multiply_fusion.1), channel_id=1, source_target_pairs={{0,6},{1,7},{2,4},{3,5},{4,10},{5,11},{6,8},{7,9},{8,14},{9,15},{1... | collective-permute-start | bytes 393224 | tf_op jit(solution)/shard_map/ppermute | solution.py:163
  55.6 1.9 %collective-permute-start.8 = (f32[64,512]{1,0:T(8,128)S(1)}, f32[64,512]{1,0:T(8,128)S(1)}, u32[]{:S(2)}, u32[]{:S(2)}) collective-permute-start(f32[64,512]{1,0:T(8,128)S(1)} %collective-permute-done.6), channel_id=1, source_target_pairs={{0,1},{1,0},{2,3},{3,2},{4,5},{5,4},{6,7},{7,6},{8,9},{9,8},{10,11... | collective-permute-start | bytes 393224 | tf_op jit(solution)/shard_map/ppermute | solution.py:163
  57.4 1.3 %collective-permute-start.7 = (f32[64,512]{1,0:T(8,128)S(1)}, f32[64,512]{1,0:T(8,128)S(1)}, u32[]{:S(2)}, u32[]{:S(2)}) collective-permute-start(f32[64,512]{1,0:T(8,128)S(1)} %collective-permute-done.5), channel_id=1, source_target_pairs={{0,1},{1,0},{2,3},{3,2},{4,5},{5,4},{6,7},{7,6},{8,9},{9,8},{10,11... | collective-permute-start | bytes 393224 | tf_op jit(solution)/shard_map/ppermute | solution.py:163
  59.9 16.7 %collective-permute-start.9 = (f32[256,512]{1,0:T(8,128)S(1)}, f32[256,512]{1,0:T(8,128)S(1)}, u32[]{:S(2)}, u32[]{:S(2)}) collective-permute-start(f32[256,512]{1,0:T(8,128)S(1)} %get-tuple-element.85), channel_id=1, source_target_pairs={{0,4},{1,5},{2,6},{3,7},{4,8},{5,9},{6,10},{7,11},{8,12},{9,13},{1... | collective-permute-start | bytes 1572872 | tf_op jit(solution)/shard_map/ppermute | solution.py:163
  77.8 15.9 %collective-permute-start.10 = (f32[256,512]{1,0:T(8,128)S(1)}, f32[256,512]{1,0:T(8,128)S(1)}, u32[]{:S(2)}, u32[]{:S(2)}) collective-permute-start(f32[256,512]{1,0:T(8,128)S(1)} %get-tuple-element.92), channel_id=1, source_target_pairs={{0,4},{1,5},{2,6},{3,7},{4,8},{5,9},{6,10},{7,11},{8,12},{9,13},{1... | collective-permute-start | bytes 1572872 | tf_op jit(solution)/shard_map/ppermute | solution.py:163
  94.8 1.4 %collective-permute-start.11 = (f32[64,512]{1,0:T(8,128)S(1)}, f32[64,512]{1,0:T(8,128)S(1)}, u32[]{:S(2)}, u32[]{:S(2)}) collective-permute-start(f32[64,512]{1,0:T(8,128)S(1)} %get-tuple-element.105), channel_id=1, source_target_pairs={{0,1},{1,0},{2,3},{3,2},{4,5},{5,4},{6,7},{7,6},{8,9},{9,8},{10,11... | collective-permute-start | bytes 393224 | tf_op jit(solution)/shard_map/ppermute | solution.py:163
  96.2 5.6 %collective-permute-start.12 = (f32[64,512]{1,0:T(8,128)S(1)}, f32[64,512]{1,0:T(8,128)S(1)}, u32[]{:S(2)}, u32[]{:S(2)}) collective-permute-start(f32[64,512]{1,0:T(8,128)S(1)} %select_add_fusion), channel_id=1, source_target_pairs={{0,2},{1,3},{2,0},{3,1},{4,6},{5,7},{6,4},{7,5},{8,10},{9,11},{10,... | collective-permute-start | bytes 393224 | tf_op jit(solution)/shard_map/ppermute | solution.py:163
  97.0 4.8 %collective-permute-start.13 = (f32[64,512]{1,0:T(8,128)S(1)}, f32[64,512]{1,0:T(8,128)S(1)}, u32[]{:S(2)}, u32[]{:S(2)}) collective-permute-start(f32[64,512]{1,0:T(8,128)S(1)} %get-tuple-element.104), channel_id=1, source_target_pairs={{0,1},{1,0},{2,3},{3,2},{4,5},{5,4},{6,7},{7,6},{8,9},{9,8},{10,11... | collective-permute-start | bytes 393224 | tf_op jit(solution)/shard_map/ppermute | solution.py:163
  101.9 8.3 %collective-permute-start.16 = (f32[64,512]{1,0:T(8,128)S(1)}, f32[64,512]{1,0:T(8,128)S(1)}, u32[]{:S(2)}, u32[]{:S(2)}) collective-permute-start(f32[64,512]{1,0:T(8,128)S(1)} %add_multiply_fusion), channel_id=1, source_target_pairs={{0,12},{1,13},{2,14},{3,15},{4,16},{5,17},{6,18},{7,19},{8,20},{9,... | collective-permute-start | bytes 393224 | tf_op jit(solution)/shard_map/ppermute | solution.py:163
  101.9 11.1 %collective-permute-start.14 = (f32[64,512]{1,0:T(8,128)S(1)}, f32[64,512]{1,0:T(8,128)S(1)}, u32[]{:S(2)}, u32[]{:S(2)}) collective-permute-start(f32[64,512]{1,0:T(8,128)S(1)} %add_multiply_fusion), channel_id=1, source_target_pairs={{0,14},{1,15},{2,12},{3,13},{4,18},{5,19},{6,16},{7,17},{8,22},{9,... | collective-permute-start | bytes 393224 | tf_op jit(solution)/shard_map/ppermute | solution.py:163
  110.2 3.6 %collective-permute-start.17 = (f32[64,512]{1,0:T(8,128)S(1)}, f32[64,512]{1,0:T(8,128)S(1)}, u32[]{:S(2)}, u32[]{:S(2)}) collective-permute-start(f32[64,512]{1,0:T(8,128)S(1)} %collective-permute-done.16), channel_id=1, source_target_pairs={{0,1},{1,0},{2,3},{3,2},{4,5},{5,4},{6,7},{7,6},{8,9},{9,8},{10,11... | collective-permute-start | bytes 393224 | tf_op jit(solution)/shard_map/ppermute | solution.py:163
  113.0 1.3 %collective-permute-start.15 = (f32[64,512]{1,0:T(8,128)S(1)}, f32[64,512]{1,0:T(8,128)S(1)}, u32[]{:S(2)}, u32[]{:S(2)}) collective-permute-start(f32[64,512]{1,0:T(8,128)S(1)} %collective-permute-done.14), channel_id=1, source_target_pairs={{0,1},{1,0},{2,3},{3,2},{4,5},{5,4},{6,7},{7,6},{8,9},{9,8},{10,11... | collective-permute-start | bytes 393224 | tf_op jit(solution)/shard_map/ppermute | solution.py:163
